TPU v7x, 32 devices: a whole 2x2x4 slice. The times are simulated.
32 devices in a mesh: grp: 2 (over y), feat: 8 (over z, x), tok: 2 (over core).
Axes of the slice: x: 2, y: 2, z: 4, core: 2. Of those that a mesh axis runs over, the one named last changes fastest.
Arguments:
- tokens: bfloat16 [32, 8192], P(('grp', 'feat'), 'tok'), parts along dimension 0, may hold values from -6 to 6
- b_pre: bfloat16 [16384], P(('grp', 'tok')), parts along dimension 0, may hold values from -3 to 3
- pre_codes: float32 [32, 64], P('grp'), parts along dimension 0, may hold values from -6 to 6
- top_idx: int32 [32, 64], P('grp'), parts along dimension 0, may hold values from 0 to 16777215, as said below
- blocks: int32 [16], P(('grp', 'feat')), parts along dimension 0, may hold values from 0 to 131071, as said below
- counts: int32 [16], P(('grp', 'feat')), parts along dimension 0, may hold values from 43 to 128, as said below
- dict_rows: bfloat16 [2048, 8192], P(('grp', 'feat'), 'tok'), parts along dimension 0, may hold values from -0.5 to 0.5
Outputs:
- grad_rows: bfloat16 [2048, 8192], P(('grp', 'feat'), 'tok'), parts along dimension 0
- grad_enc: bfloat16 [16384, 1024], P(('grp', 'tok'), 'feat'), parts along dimension 0
- grad_benc: float32 [2048], P(('grp', 'feat')), parts along dimension 0
There are 2 independent parts, one for each index of `grp`. A program takes and returns all parts, laid end to end along the dimension named above; each array names one. Nothing has to cross between parts.
Inputs may be any that keep to these rules, and one draw needn't show every extreme that they name: `blocks`: each index of feat holds a different block, block f lying in [f * 131072 / 8, (f + 1) * 131072 / 8). `counts`: some block has exactly 128 live slots and some exactly 43. `top_idx`: each row names 64 different latents, each of them a live slot's latent: blocks[f] * 128 + j with j < counts[f].
All inputs are finite; a program needn't handle non-finite values.
Results may differ from a plain program's by a relative error of at most 0.0064.
Values may be sent and summed in bfloat16 or wider, within the bound.
No kernel may reach another device: no remote copies, remote signals or barrier semaphores. Data moves between devices by JAX's collectives and lax.ppermute only.
A program may use at most 64 MiB of HBM per device.

v0:
```python
import jax
import jax.numpy as jnp
from jax import lax
from jax.sharding import PartitionSpec as P


def swapped(shard, axis, distance):
    return lax.ppermute(shard, axis, [(i, i ^ 1 << distance) for i in range(lax.axis_size(axis))])


def slot_codes(slot_ids, live_slots, top_idx, pre_codes):
    matches = (top_idx[:, :, None] == slot_ids[None, None, :]) & live_slots[None, None, :]
    positive = jnp.maximum(pre_codes, 0.0)
    code_block = jnp.sum(
        jnp.where(matches, positive[:, :, None], jnp.zeros_like(positive)[:, :, None]), axis=1
    )
    keep_mask = jnp.any(matches & (pre_codes > 0.0)[:, :, None], axis=1)
    return (code_block, keep_mask)


def local(tokens, b_pre, pre_codes, top_idx, blocks, counts, dict_rows):
    block_rows = dict_rows.shape[0]
    offsets = jnp.arange(block_rows, dtype=jnp.int32)
    slot_ids = blocks[0] * block_rows + offsets
    live_slots = offsets < counts[0]
    code_block, keep_mask = slot_codes(slot_ids, live_slots, top_idx, pre_codes)
    code_block = code_block.astype(jnp.bfloat16)
    centered_own = lax.optimization_barrier(
        (tokens.astype(jnp.float32) - b_pre.astype(jnp.float32)).astype(jnp.bfloat16)
    )
    centered = lax.all_gather(centered_own, "feat", axis=0, tiled=True)
    rebuilt_own = lax.psum_scatter(
        jnp.dot(code_block, dict_rows, preferred_element_type=jnp.float32),
        "feat",
        scatter_dimension=0,
        tiled=True,
    )
    scaled_own = (0.25 * (rebuilt_own - centered_own.astype(jnp.float32))).astype(jnp.bfloat16)
    scaled = lax.all_gather(scaled_own, "feat", axis=0, tiled=True)
    code_half = lax.dot_general(
        scaled, dict_rows, (((1,), (1,)), ((), ())), preferred_element_type=jnp.float32
    )
    code_grad = code_half + swapped(code_half, "tok", 0)
    pre_grad = jnp.where(keep_mask, code_grad, jnp.zeros_like(code_grad)).astype(jnp.bfloat16)
    grad_rows = lax.dot_general(
        code_block, scaled, (((0,), (0,)), ((), ())), preferred_element_type=jnp.float32
    ).astype(jnp.bfloat16)
    grad_enc = lax.dot_general(
        centered, pre_grad, (((0,), (0,)), ((), ())), preferred_element_type=jnp.float32
    ).astype(jnp.bfloat16)
    grad_benc = jnp.sum(pre_grad.astype(jnp.float32), axis=0)
    return (grad_rows, grad_enc, grad_benc)


def solution(mesh):
    return jax.shard_map(
        local,
        mesh=mesh,
        in_specs=(
            P(("grp", "feat"), "tok"),
            P(("grp", "tok")),
            P("grp", None),
            P("grp", None),
            P(("grp", "feat")),
            P(("grp", "feat")),
            P(("grp", "feat"), "tok"),
        ),
        out_specs=(P(("grp", "feat"), "tok"), P(("grp", "tok"), "feat"), P(("grp", "feat"))),
        check_vma=False,
    )
```

profile of v0, /device:TPU:0, one launch (start us, length us, event | category | flops | bytes accessed | tf_op | source)
XLA Modules:
  0.0 127.5 jit_solution(2646528047264367791)
XLA Ops:
  7.2 0.0 copy-start
  7.2 0.0 copy-start.4
  7.2 0.0 copy-start.3
  7.2 0.0 all-reduce.3.cloned.1.call-start
  8.6 0.7 broadcast_maximum_fusion
  9.3 1.0 select_reduce_fusion
  10.4 0.0 copy-done
  10.4 0.0 copy-start.5
  10.4 0.0 copy-start.1
  10.4 0.0 copy-start.2
  10.4 1.0 fusion.7
  11.4 0.0 all-reduce.3.cloned.1.call-update
  11.4 0.0 copy-done.4
  11.4 0.0 copy-done.3
  11.5 32.3 %all-gather.1 = bf16[8,2,4096]{2,1,0:T(2,128)(2,1)S(1)} all-gather(bf16[1,2,4096]{2,1,0:T(2,128)(2,1)S(1)} %bitcast.15), channel_id=1, replica_groups=mesh['grp'=2,'feat'=8,'tok'=2] {'feat'}, dimensions={0}, use_global_device_ids=true | all-gather | bytes 147456 | tf_op jit(solution)/shard_map/all_gather | solution.py:31
  43.8 0.1 reshape.23
  43.9 0.0 copy-done.5
  43.9 0.6 dynamic-slice
  45.1 0.0 copy-done.1
  45.2 0.0 copy-done.2
  45.2 0.4 and_reduce_fusion
  45.5 39.8 %all-reduce.3.cloned.1.call-done = f32[16,4096]{1,0:T(8,128)} async-done(((f32[16,4096]{1,0:T(8,128)}), f32[16,4096]{1,0:T(8,128)}) %all-reduce.3.cloned.1.call-update) | async-done | bytes 262160
  85.3 0.9 fusion.2
  86.2 30.5 %all-gather = bf16[8,2,4096]{2,1,0:T(2,128)(2,1)S(1)} all-gather(bf16[1,2,4096]{2,1,0:T(2,128)(2,1)S(1)} %fusion.2), channel_id=1, replica_groups=mesh['grp'=2,'feat'=8,'tok'=2] {'feat'}, dimensions={0}, use_global_device_ids=true | all-gather | bytes 147456 | tf_op jit(solution)/shard_map/all_gather | solution.py:39
  116.8 0.1 reshape.21
  116.8 0.4 fusion.6
  117.2 0.0 collective-permute-start
  117.2 1.4 %convolution_convert_fusion.1 = bf16[128,4096]{1,0:T(8,128)(2,1)} fusion(bf16[16,4096]{1,0:T(8,128)(2,1)S(1)} %reshape.21, bf16[16,128]{1,0:T(8,128)(2,1)S(1)} %select_reduce_fusion), kind=kOutput, calls=%fused_computation.1 | convolution fusion | flops 17301504 | bytes 1183744 | tf_op jit(solution)/shard_map/dot_general | solution.py:45
  118.7 0.0 collective-permute-done
  118.7 0.5 convert_reduce_fusion
  119.2 1.5 %convolution_convert_fusion = bf16[4096,128]{1,0:T(8,128)(2,1)} fusion(bf16[16,4096]{1,0:T(8,128)(2,1)S(1)} %reshape.23, bf16[16,128]{1,0:T(8,128)(2,1)S(1)} %get-tuple-element.4), kind=kOutput, calls=%fused_computation | convolution fusion | flops 17301504 | bytes 1183744 | tf_op jit(solution)/shard_map/dot_general | solution.py:48
  (5 shorter events, 0.0 us)
Async XLA Ops:
  7.2 3.2 %copy-start = (bf16[128,4096]{1,0:T(8,128)(2,1)S(1)}, bf16[128,4096]{1,0:T(8,128)(2,1)}, u32[]{:S(2)}) copy-start(bf16[128,4096]{1,0:T(8,128)(2,1)} %param.13) | copy-start | bytes 3145732
  7.2 4.2 %copy-start.4 = (bf16[4096]{0:T(1024)(128)(2,1)S(1)}, bf16[4096]{0:T(1024)(128)(2,1)}, u32[]{:S(2)}) copy-start(bf16[4096]{0:T(1024)(128)(2,1)} %param.8) | copy-start | bytes 24580
  7.2 4.3 %copy-start.3 = (bf16[2,4096]{1,0:T(2,128)(2,1)S(1)}, bf16[2,4096]{1,0:T(2,128)(2,1)}, u32[]{:S(2)}) copy-start(bf16[2,4096]{1,0:T(2,128)(2,1)} %param.7) | copy-start | bytes 49156
  7.2 78.1 %all-reduce.3.cloned.1.call-start = ((), (), s32[]{:S(2)}) async-start(), calls=%async_computation | async-start | bytes 524288
  10.4 33.5 %copy-start.5 = (u32[32]{0:T(128)S(1)}, u32[32]{0:T(128)}, u32[]{:S(2)}) copy-start(u32[32]{0:T(128)} %constant.17) | copy-start | bytes 388
  10.4 34.7 %copy-start.1 = (f32[16,64]{1,0:T(8,128)S(1)}, f32[16,64]{1,0:T(8,128)}, u32[]{:S(2)}) copy-start(f32[16,64]{1,0:T(8,128)} %param.9) | copy-start | bytes 12292
  10.4 34.7 %copy-start.2 = (s32[16,64]{1,0:T(8,128)S(1)}, s32[16,64]{1,0:T(8,128)}, u32[]{:S(2)}) copy-start(s32[16,64]{1,0:T(8,128)} %param.10) | copy-start | bytes 12292
  117.2 1.5 %collective-permute-start = (f32[16,128]{1,0:T(8,128)S(1)}, f32[16,128]{1,0:T(8,128)S(1)}, u32[]{:S(2)}, u32[]{:S(2)}) collective-permute-start(f32[16,128]{1,0:T(8,128)S(1)} %fusion.6), channel_id=1, source_target_pairs={{0,1},{1,0},{2,3},{3,2},{4,5},{5,4},{6,7},{7,6},{8,9},{9,8},{10,11... | collective-permute-start | bytes 24584 | tf_op jit(solution)/shard_map/ppermute | solution.py:8
Sparse Core Ops, SparseCore 0:
  12.0 73.3 all-reduce.2
where the time goes:
time: 128 us; the launch traced here: 127 us
  blocking collectives  62.9 us (49%)
  waiting for transfers between devices  39.8 us (31%)
  between operations  16.2 us (13%)
  matrix products  4.23 us (3%)
  other arithmetic  3.61 us (3%)
    unnamed x2, waiting for transfers between devices  39.8 us
    all_gather x1, blocking collectives, local(): centered = lax.all_gather(centered_own, 'feat', axis=0, tiled=True)  32.3 us
    all_gather x1, blocking collectives, local(): scaled = lax.all_gather(scaled_own, 'feat', axis=0, tiled=True)  30.5 us
  transfers between devices with their start and end apart: 2, of which 1 were waited for; matrix products, arithmetic and copies ran while one was open for 2% of the time, Pallas kernels for 0%

commit v1 on v0

--- a/solution.py
+++ b/solution.py
@@ -3,9 +3,44 @@
 from jax import lax
 from jax.sharding import PartitionSpec as P
 
+DIRECT = 8
+
 
 def swapped(shard, axis, distance):
-    return lax.ppermute(shard, axis, [(i, i ^ 1 << distance) for i in range(lax.axis_size(axis))])
+    return lax.ppermute(shard, axis, [(i, i ^ distance) for i in range(lax.axis_size(axis))])
+
+
+def is_direct(axis):
+    size = lax.axis_size(axis)
+    return size <= DIRECT and size & (size - 1) == 0
+
+
+def by_distance(array, axis):
+    size = lax.axis_size(axis)
+    if not is_direct(axis):
+        return array
+    blocks = array.reshape((size, array.shape[0] // size) + array.shape[1:])
+    order = lax.axis_index(axis) ^ jnp.arange(size, dtype=jnp.int32)
+    return blocks[order].reshape(array.shape)
+
+
+def gathered(own, axis):
+    if not is_direct(axis):
+        return lax.all_gather(own, axis, axis=0, tiled=True)
+    parts = [own] + [swapped(own, axis, k) for k in range(1, lax.axis_size(axis))]
+    return jnp.concatenate(parts, axis=0)
+
+
+def scattered_sum(whole, axis):
+    size = lax.axis_size(axis)
+    if not is_direct(axis):
+        return lax.psum_scatter(whole, axis, scatter_dimension=0, tiled=True)
+    rows = whole.shape[0] // size
+    total = whole[:rows]
+    for k in range(1, size):
+        part = whole[k * rows : (k + 1) * rows].astype(jnp.bfloat16)
+        total = total + swapped(part, axis, k).astype(jnp.float32)
+    return total
 
 
 def slot_codes(slot_ids, live_slots, top_idx, pre_codes):
@@ -20,27 +55,26 @@
 
 def local(tokens, b_pre, pre_codes, top_idx, blocks, counts, dict_rows):
     block_rows = dict_rows.shape[0]
+    centered_own = lax.optimization_barrier(
+        (tokens.astype(jnp.float32) - b_pre.astype(jnp.float32)).astype(jnp.bfloat16)
+    )
+    centered = gathered(centered_own, "feat")
     offsets = jnp.arange(block_rows, dtype=jnp.int32)
     slot_ids = blocks[0] * block_rows + offsets
     live_slots = offsets < counts[0]
-    code_block, keep_mask = slot_codes(slot_ids, live_slots, top_idx, pre_codes)
+    code_block, keep_mask = slot_codes(
+        slot_ids, live_slots, by_distance(top_idx, "feat"), by_distance(pre_codes, "feat")
+    )
     code_block = code_block.astype(jnp.bfloat16)
-    centered_own = lax.optimization_barrier(
-        (tokens.astype(jnp.float32) - b_pre.astype(jnp.float32)).astype(jnp.bfloat16)
-    )
-    centered = lax.all_gather(centered_own, "feat", axis=0, tiled=True)
-    rebuilt_own = lax.psum_scatter(
-        jnp.dot(code_block, dict_rows, preferred_element_type=jnp.float32),
-        "feat",
-        scatter_dimension=0,
-        tiled=True,
+    rebuilt_own = scattered_sum(
+        jnp.dot(code_block, dict_rows, preferred_element_type=jnp.float32), "feat"
     )
     scaled_own = (0.25 * (rebuilt_own - centered_own.astype(jnp.float32))).astype(jnp.bfloat16)
-    scaled = lax.all_gather(scaled_own, "feat", axis=0, tiled=True)
+    scaled = gathered(scaled_own, "feat")
     code_half = lax.dot_general(
         scaled, dict_rows, (((1,), (1,)), ((), ())), preferred_element_type=jnp.float32
     )
-    code_grad = code_half + swapped(code_half, "tok", 0)
+    code_grad = code_half + swapped(code_half, "tok", 1)
     pre_grad = jnp.where(keep_mask, code_grad, jnp.zeros_like(code_grad)).astype(jnp.bfloat16)
     grad_rows = lax.dot_general(
         code_block, scaled, (((0,), (0,)), ((), ())), preferred_element_type=jnp.float32

time: 128 us -> 48.3 us (0.38)
  blocking collectives: 62.9 us -> 0 us
  waiting for transfers between devices: 39.8 us -> 2.78 us
  starting transfers between devices: 0.04 us -> 35.1 us
  between operations: 16.2 us -> 2.17 us
  local copies, waits for them, and re-layouts: 0.73 us -> 3.07 us
  other arithmetic: 3.61 us -> 1.39 us
    all_gather x2 -> x0, blocking collectives: 62.9 us -> none  [the longest x1 32.3 us: local(): centered = lax.all_gather(centered_own, 'feat', axis=0, tiled=True)]
    unnamed x2 -> x0, waiting for transfers between devices: 39.8 us -> none
    ppermute x1 -> x22, starting transfers between devices: 0.01 us -> 35.1 us  [swapped(): lax.ppermute(shard, axis, [(i, i ^ distance) for i in range(lax.axis_size...]
    ppermute x1 -> x22, waiting for transfers between devices: 0.01 us -> 2.78 us  [swapped(): lax.ppermute(shard, axis, [(i, i ^ distance) for i in range(lax.axis_size...]
    gather x0 -> x2, local copies, waits for them, and re-layouts: none -> 2.54 us  [by_distance(): return blocks[order].reshape(array.shape)]
  transfers between devices with their start and end apart: 2 -> 22, of which waited for: 1 -> 3; matrix products, arithmetic and copies ran while one was open for 2% -> 4% of each run, Pallas kernels for 0% -> 0%
where the time goes in v1:
time: 48.3 us; the launch traced here: 48 us
  starting transfers between devices  35.1 us (73%)
  matrix products  3.52 us (7%)
  local copies, waits for them, and re-layouts  3.07 us (6%)
  waiting for transfers between devices  2.78 us (6%)
  between operations  2.17 us (4%)
  other arithmetic  1.39 us (3%)
    ppermute x22, starting transfers between devices, swapped(): lax.ppermute(shard, axis, [(i, i ^ distance) for i in range(lax.axis_size...  35.1 us
    ppermute x22, waiting for transfers between devices, swapped(): lax.ppermute(shard, axis, [(i, i ^ distance) for i in range(lax.axis_size...  2.78 us
    gather x2, local copies, waits for them, and re-layouts, by_distance(): return blocks[order].reshape(array.shape)  2.54 us
    dot_general x1, matrix products, local(): lax.dot_general(centered, pre_grad, (((0,), (0,)), ((), ())), preferred_e...  1.45 us
    dot_general x1, matrix products, local(): lax.dot_general(code_block, scaled, (((0,), (0,)), ((), ())), preferred_e...  1.44 us
  transfers between devices with their start and end apart: 22, of which 3 were waited for; matrix products, arithmetic and copies ran while one was open for 4% of the time, Pallas kernels for 0%

profile of v1, /device:TPU:0, one launch (start us, length us, event | category | flops | bytes accessed | tf_op | source)
XLA Modules:
  0.0 48.0 jit_solution(5845148933152467505)
XLA Ops:
  0.6 0.0 copy-start
  0.6 0.0 copy-start.2
  0.7 0.0 copy-start.1
  2.1 1.3 %gather_fusion.1 = f32[8,2,64]{2,1,0:T(2,128)S(1)} fusion(f32[8,2,64]{2,1,0:T(2,128)} %bitcast.20, s32[1024]{0:T(1024)S(1)} %pad_clamp_fusion), kind=kCustom, calls=%fused_computation.1 | custom fusion | bytes 8224 | tf_op jit(solution)/shard_map/gather | solution.py:24
  3.4 1.3 %gather_fusion = s32[8,2,64]{2,1,0:T(2,128)S(1)} fusion(s32[8,2,64]{2,1,0:T(2,128)} %bitcast.21, s32[1024]{0:T(1024)S(1)} %pad_clamp_fusion), kind=kCustom, calls=%fused_computation | custom fusion | bytes 8224 | tf_op jit(solution)/shard_map/gather | solution.py:24
  4.7 0.4 select_reduce_fusion
  5.0 0.0 copy-done
  5.0 0.3 fusion.10
  5.3 0.1 fusion.9
  5.4 3.0 %collective-permute-start = (bf16[2,4096]{1,0:T(2,128)(2,1)S(1)}, bf16[2,4096]{1,0:T(2,128)(2,1)S(1)}, u32[]{:S(2)}, u32[]{:S(2)}) collective-permute-start(bf16[2,4096]{1,0:T(2,128)(2,1)S(1)} %get-tuple-element.5), channel_id=1, source_target_pairs={{0,2},{2,0},{4,6},{6,4},{8,10},{10,8},{12,14},{14,12},{1,3},{3,1},... | collective-permute-start | bytes 49160 | tf_op jit(solution)/shard_map/ppermute | solution.py:10
  8.4 3.6 %collective-permute-start.6 = (bf16[2,4096]{1,0:T(2,128)(2,1)S(1)}, bf16[2,4096]{1,0:T(2,128)(2,1)S(1)}, u32[]{:S(2)}, u32[]{:S(2)}) collective-permute-start(bf16[2,4096]{1,0:T(2,128)(2,1)S(1)} %get-tuple-element.6), channel_id=1, source_target_pairs={{0,14},{2,12},{4,10},{6,8},{8,6},{10,4},{12,2},{14,0},{1,15},{3,13... | collective-permute-start | bytes 49160 | tf_op jit(solution)/shard_map/ppermute | solution.py:10
  12.0 0.0 collective-permute-start.5
  12.0 1.9 %collective-permute-start.4 = (bf16[2,4096]{1,0:T(2,128)(2,1)S(1)}, bf16[2,4096]{1,0:T(2,128)(2,1)S(1)}, u32[]{:S(2)}, u32[]{:S(2)}) collective-permute-start(bf16[2,4096]{1,0:T(2,128)(2,1)S(1)} %get-tuple-element.8), channel_id=1, source_target_pairs={{0,10},{2,8},{4,14},{6,12},{8,2},{10,0},{12,6},{14,4},{1,11},{3,9}... | collective-permute-start | bytes 49160 | tf_op jit(solution)/shard_map/ppermute | solution.py:10
  13.9 2.1 %collective-permute-start.3 = (bf16[2,4096]{1,0:T(2,128)(2,1)S(1)}, bf16[2,4096]{1,0:T(2,128)(2,1)S(1)}, u32[]{:S(2)}, u32[]{:S(2)}) collective-permute-start(bf16[2,4096]{1,0:T(2,128)(2,1)S(1)} %get-tuple-element.9), channel_id=1, source_target_pairs={{0,8},{2,10},{4,12},{6,14},{8,0},{10,2},{12,4},{14,6},{1,9},{3,11}... | collective-permute-start | bytes 49160 | tf_op jit(solution)/shard_map/ppermute | solution.py:10
  16.0 0.0 copy-done.2
  16.0 0.0 collective-permute-done
  16.0 1.3 %collective-permute-start.2 = (bf16[2,4096]{1,0:T(2,128)(2,1)S(1)}, bf16[2,4096]{1,0:T(2,128)(2,1)S(1)}, u32[]{:S(2)}, u32[]{:S(2)}) collective-permute-start(bf16[2,4096]{1,0:T(2,128)(2,1)S(1)} %get-tuple-element.10), channel_id=1, source_target_pairs={{0,6},{2,4},{4,2},{6,0},{8,14},{10,12},{12,10},{14,8},{1,7},{3,5},... | collective-permute-start | bytes 49160 | tf_op jit(solution)/shard_map/ppermute | solution.py:10
  17.3 0.0 collective-permute-done.6
  17.4 0.6 %collective-permute-start.1 = (bf16[2,4096]{1,0:T(2,128)(2,1)S(1)}, bf16[2,4096]{1,0:T(2,128)(2,1)S(1)}, u32[]{:S(2)}, u32[]{:S(2)}) collective-permute-start(bf16[2,4096]{1,0:T(2,128)(2,1)S(1)} %get-tuple-element.11), channel_id=1, source_target_pairs={{0,4},{2,6},{4,0},{6,2},{8,12},{10,14},{12,8},{14,10},{1,5},{3,7},... | collective-permute-start | bytes 49160 | tf_op jit(solution)/shard_map/ppermute | solution.py:10
  17.9 0.0 copy-done.1
  17.9 0.0 collective-permute-done.5
  18.0 4.8 %collective-permute-start.20 = (bf16[2,4096]{1,0:T(2,128)(2,1)S(1)}, bf16[2,4096]{1,0:T(2,128)(2,1)S(1)}, u32[]{:S(2)}, u32[]{:S(2)}) collective-permute-start(bf16[2,4096]{1,0:T(2,128)(2,1)S(1)} %subtract_convert_fusion), channel_id=1, source_target_pairs={{0,14},{2,12},{4,10},{6,8},{8,6},{10,4},{12,2},{14,0},{1,15},{3,13... | collective-permute-start | bytes 49160 | tf_op jit(solution)/shard_map/ppermute | solution.py:10
  22.7 0.0 collective-permute-done.4
  22.7 0.2 collective-permute-start.19
  23.0 0.0 collective-permute-done.3
  23.0 0.4 collective-permute-start.18
  23.4 0.0 collective-permute-done.2
  23.4 2.4 %collective-permute-start.17 = (bf16[2,4096]{1,0:T(2,128)(2,1)S(1)}, bf16[2,4096]{1,0:T(2,128)(2,1)S(1)}, u32[]{:S(2)}, u32[]{:S(2)}) collective-permute-start(bf16[2,4096]{1,0:T(2,128)(2,1)S(1)} %subtract_convert_fusion), channel_id=1, source_target_pairs={{0,8},{2,10},{4,12},{6,14},{8,0},{10,2},{12,4},{14,6},{1,9},{3,11}... | collective-permute-start | bytes 49160 | tf_op jit(solution)/shard_map/ppermute | solution.py:10
  25.8 0.0 collective-permute-done.1
  25.8 2.3 %collective-permute-start.16 = (bf16[2,4096]{1,0:T(2,128)(2,1)S(1)}, bf16[2,4096]{1,0:T(2,128)(2,1)S(1)}, u32[]{:S(2)}, u32[]{:S(2)}) collective-permute-start(bf16[2,4096]{1,0:T(2,128)(2,1)S(1)} %subtract_convert_fusion), channel_id=1, source_target_pairs={{0,6},{2,4},{4,2},{6,0},{8,14},{10,12},{12,10},{14,8},{1,7},{3,5},... | collective-permute-start | bytes 49160 | tf_op jit(solution)/shard_map/ppermute | solution.py:10
  28.1 0.1 multiply_convert_fusion
  28.2 0.0 collective-permute-done.20
  28.2 0.8 %collective-permute-start.15 = (bf16[2,4096]{1,0:T(2,128)(2,1)S(1)}, bf16[2,4096]{1,0:T(2,128)(2,1)S(1)}, u32[]{:S(2)}, u32[]{:S(2)}) collective-permute-start(bf16[2,4096]{1,0:T(2,128)(2,1)S(1)} %subtract_convert_fusion), channel_id=1, source_target_pairs={{0,4},{2,6},{4,0},{6,2},{8,12},{10,14},{12,8},{14,10},{1,5},{3,7},... | collective-permute-start | bytes 49160 | tf_op jit(solution)/shard_map/ppermute | solution.py:10
  29.0 0.0 collective-permute-done.19
  29.0 0.4 collective-permute-start.14
  29.4 0.0 collective-permute-done.18
  29.4 4.6 %collective-permute-start.13 = (bf16[2,4096]{1,0:T(2,128)(2,1)S(1)}, bf16[2,4096]{1,0:T(2,128)(2,1)S(1)}, u32[]{:S(2)}, u32[]{:S(2)}) collective-permute-start(bf16[2,4096]{1,0:T(2,128)(2,1)S(1)} %multiply_convert_fusion), channel_id=1, source_target_pairs={{0,14},{2,12},{4,10},{6,8},{8,6},{10,4},{12,2},{14,0},{1,15},{3,13... | collective-permute-start | bytes 49160 | tf_op jit(solution)/shard_map/ppermute | solution.py:10
  34.1 0.0 collective-permute-done.17
  34.1 0.2 collective-permute-start.12
  34.3 0.0 collective-permute-done.16
  34.3 0.5 collective-permute-start.11
  34.8 0.0 collective-permute-done.15
  34.8 2.4 %collective-permute-start.10 = (bf16[2,4096]{1,0:T(2,128)(2,1)S(1)}, bf16[2,4096]{1,0:T(2,128)(2,1)S(1)}, u32[]{:S(2)}, u32[]{:S(2)}) collective-permute-start(bf16[2,4096]{1,0:T(2,128)(2,1)S(1)} %multiply_convert_fusion), channel_id=1, source_target_pairs={{0,8},{2,10},{4,12},{6,14},{8,0},{10,2},{12,4},{14,6},{1,9},{3,11}... | collective-permute-start | bytes 49160 | tf_op jit(solution)/shard_map/ppermute | solution.py:10
  37.2 0.0 collective-permute-done.14
  37.2 2.3 %collective-permute-start.9 = (bf16[2,4096]{1,0:T(2,128)(2,1)S(1)}, bf16[2,4096]{1,0:T(2,128)(2,1)S(1)}, u32[]{:S(2)}, u32[]{:S(2)}) collective-permute-start(bf16[2,4096]{1,0:T(2,128)(2,1)S(1)} %multiply_convert_fusion), channel_id=1, source_target_pairs={{0,6},{2,4},{4,2},{6,0},{8,14},{10,12},{12,10},{14,8},{1,7},{3,5},... | collective-permute-start | bytes 49160 | tf_op jit(solution)/shard_map/ppermute | solution.py:10
  39.5 0.0 collective-permute-done.13
  39.5 0.7 %collective-permute-start.8 = (bf16[2,4096]{1,0:T(2,128)(2,1)S(1)}, bf16[2,4096]{1,0:T(2,128)(2,1)S(1)}, u32[]{:S(2)}, u32[]{:S(2)}) collective-permute-start(bf16[2,4096]{1,0:T(2,128)(2,1)S(1)} %multiply_convert_fusion), channel_id=1, source_target_pairs={{0,4},{2,6},{4,0},{6,2},{8,12},{10,14},{12,8},{14,10},{1,5},{3,7},... | collective-permute-start | bytes 49160 | tf_op jit(solution)/shard_map/ppermute | solution.py:10
  40.3 0.0 collective-permute-done.12
  40.3 0.4 collective-permute-start.7
  40.7 0.4 and_reduce_fusion
  41.0 0.2 concatenate.7
  41.2 0.0 collective-permute-done.11
  41.3 0.0 collective-permute-done.10
  41.3 0.6 %collective-permute-done.9 = bf16[2,4096]{1,0:T(2,128)(2,1)S(1)} collective-permute-done((bf16[2,4096]{1,0:T(2,128)(2,1)S(1)}, bf16[2,4096]{1,0:T(2,128)(2,1)S(1)}, u32[]{:S(2)}, u32[]{:S(2)}) %collective-permute-start.9) | collective-permute-done | bytes 16416 | tf_op jit(solution)/shard_map/ppermute | solution.py:10
  41.8 1.4 %collective-permute-done.8 = bf16[2,4096]{1,0:T(2,128)(2,1)S(1)} collective-permute-done((bf16[2,4096]{1,0:T(2,128)(2,1)S(1)}, bf16[2,4096]{1,0:T(2,128)(2,1)S(1)}, u32[]{:S(2)}, u32[]{:S(2)}) %collective-permute-start.8) | collective-permute-done | bytes 16416 | tf_op jit(solution)/shard_map/ppermute | solution.py:10
  43.3 0.7 %collective-permute-done.7 = bf16[2,4096]{1,0:T(2,128)(2,1)S(1)} collective-permute-done((bf16[2,4096]{1,0:T(2,128)(2,1)S(1)}, bf16[2,4096]{1,0:T(2,128)(2,1)S(1)}, u32[]{:S(2)}, u32[]{:S(2)}) %collective-permute-start.7) | collective-permute-done | bytes 16416 | tf_op jit(solution)/shard_map/ppermute | solution.py:10
  44.0 0.2 concatenate.6
  44.2 0.4 fusion.11
  44.6 0.0 collective-permute-start.21
  44.6 1.4 %convolution_convert_fusion.1 = bf16[128,4096]{1,0:T(8,128)(2,1)} fusion(bf16[16,4096]{1,0:T(8,128)(2,1)S(1)} %concatenate.6, bf16[16,128]{1,0:T(8,128)(2,1)S(1)} %select_reduce_fusion), kind=kOutput, calls=%fused_computation.3 | convolution fusion | flops 17301504 | bytes 1183744 | tf_op jit(solution)/shard_map/dot_general | solution.py:79
  46.0 0.0 collective-permute-done.21
  46.0 0.5 %convert_reduce_fusion = (f32[128]{0:T(128)}, bf16[16,128]{1,0:T(8,128)(2,1)S(1)}) fusion(pred[16,128]{1,0:T(8,128)(4,1)S(1)} %and_reduce_fusion, f32[16,128]{1,0:T(8,128)S(1)} %fusion.11, f32[16,128]{1,0:T(8,128)S(1)} %collective-permute-done.21), kind=kLoop, calls=%fused_computation.15 | loop fusion | flops 10112 | bytes 23040 | tf_op jit(solution)/shard_map/reduce_sum | solution.py:85
  46.6 1.5 %convolution_convert_fusion = bf16[4096,128]{1,0:T(8,128)(2,1)} fusion(bf16[16,4096]{1,0:T(8,128)(2,1)S(1)} %concatenate.7, bf16[16,128]{1,0:T(8,128)(2,1)S(1)} %get-tuple-element.4), kind=kOutput, calls=%fused_computation.2 | convolution fusion | flops 17301504 | bytes 1183744 | tf_op jit(solution)/shard_map/dot_general | solution.py:82
  (9 shorter events, 0.1 us)
Async XLA Ops:
  0.6 4.4 %copy-start = (bf16[128,4096]{1,0:T(8,128)(2,1)S(1)}, bf16[128,4096]{1,0:T(8,128)(2,1)}, u32[]{:S(2)}) copy-start(bf16[128,4096]{1,0:T(8,128)(2,1)} %param.13) | copy-start | bytes 3145732
  0.6 15.4 %copy-start.2 = (bf16[4096]{0:T(1024)(128)(2,1)S(1)}, bf16[4096]{0:T(1024)(128)(2,1)}, u32[]{:S(2)}) copy-start(bf16[4096]{0:T(1024)(128)(2,1)} %param.8) | copy-start | bytes 24580
  0.7 17.3 %copy-start.1 = (bf16[2,4096]{1,0:T(2,128)(2,1)S(1)}, bf16[2,4096]{1,0:T(2,128)(2,1)}, u32[]{:S(2)}) copy-start(bf16[2,4096]{1,0:T(2,128)(2,1)} %param.7) | copy-start | bytes 49156
  5.4 10.7 %collective-permute-start = (bf16[2,4096]{1,0:T(2,128)(2,1)S(1)}, bf16[2,4096]{1,0:T(2,128)(2,1)S(1)}, u32[]{:S(2)}, u32[]{:S(2)}) collective-permute-start(bf16[2,4096]{1,0:T(2,128)(2,1)S(1)} %get-tuple-element.5), channel_id=1, source_target_pairs={{0,2},{2,0},{4,6},{6,4},{8,10},{10,8},{12,14},{14,12},{1,3},{3,1},... | collective-permute-start | bytes 49160 | tf_op jit(solution)/shard_map/ppermute | solution.py:10
  8.4 9.0 %collective-permute-start.6 = (bf16[2,4096]{1,0:T(2,128)(2,1)S(1)}, bf16[2,4096]{1,0:T(2,128)(2,1)S(1)}, u32[]{:S(2)}, u32[]{:S(2)}) collective-permute-start(bf16[2,4096]{1,0:T(2,128)(2,1)S(1)} %get-tuple-element.6), channel_id=1, source_target_pairs={{0,14},{2,12},{4,10},{6,8},{8,6},{10,4},{12,2},{14,0},{1,15},{3,13... | collective-permute-start | bytes 49160 | tf_op jit(solution)/shard_map/ppermute | solution.py:10
  12.0 6.0 %collective-permute-start.5 = (bf16[2,4096]{1,0:T(2,128)(2,1)S(1)}, bf16[2,4096]{1,0:T(2,128)(2,1)S(1)}, u32[]{:S(2)}, u32[]{:S(2)}) collective-permute-start(bf16[2,4096]{1,0:T(2,128)(2,1)S(1)} %get-tuple-element.7), channel_id=1, source_target_pairs={{0,12},{2,14},{4,8},{6,10},{8,4},{10,6},{12,0},{14,2},{1,13},{3,15... | collective-permute-start | bytes 49160 | tf_op jit(solution)/shard_map/ppermute | solution.py:10
  12.0 10.8 %collective-permute-start.4 = (bf16[2,4096]{1,0:T(2,128)(2,1)S(1)}, bf16[2,4096]{1,0:T(2,128)(2,1)S(1)}, u32[]{:S(2)}, u32[]{:S(2)}) collective-permute-start(bf16[2,4096]{1,0:T(2,128)(2,1)S(1)} %get-tuple-element.8), channel_id=1, source_target_pairs={{0,10},{2,8},{4,14},{6,12},{8,2},{10,0},{12,6},{14,4},{1,11},{3,9}... | collective-permute-start | bytes 49160 | tf_op jit(solution)/shard_map/ppermute | solution.py:10
  13.9 9.1 %collective-permute-start.3 = (bf16[2,4096]{1,0:T(2,128)(2,1)S(1)}, bf16[2,4096]{1,0:T(2,128)(2,1)S(1)}, u32[]{:S(2)}, u32[]{:S(2)}) collective-permute-start(bf16[2,4096]{1,0:T(2,128)(2,1)S(1)} %get-tuple-element.9), channel_id=1, source_target_pairs={{0,8},{2,10},{4,12},{6,14},{8,0},{10,2},{12,4},{14,6},{1,9},{3,11}... | collective-permute-start | bytes 49160 | tf_op jit(solution)/shard_map/ppermute | solution.py:10
  16.0 7.4 %collective-permute-start.2 = (bf16[2,4096]{1,0:T(2,128)(2,1)S(1)}, bf16[2,4096]{1,0:T(2,128)(2,1)S(1)}, u32[]{:S(2)}, u32[]{:S(2)}) collective-permute-start(bf16[2,4096]{1,0:T(2,128)(2,1)S(1)} %get-tuple-element.10), channel_id=1, source_target_pairs={{0,6},{2,4},{4,2},{6,0},{8,14},{10,12},{12,10},{14,8},{1,7},{3,5},... | collective-permute-start | bytes 49160 | tf_op jit(solution)/shard_map/ppermute | solution.py:10
  17.4 8.4 %collective-permute-start.1 = (bf16[2,4096]{1,0:T(2,128)(2,1)S(1)}, bf16[2,4096]{1,0:T(2,128)(2,1)S(1)}, u32[]{:S(2)}, u32[]{:S(2)}) collective-permute-start(bf16[2,4096]{1,0:T(2,128)(2,1)S(1)} %get-tuple-element.11), channel_id=1, source_target_pairs={{0,4},{2,6},{4,0},{6,2},{8,12},{10,14},{12,8},{14,10},{1,5},{3,7},... | collective-permute-start | bytes 49160 | tf_op jit(solution)/shard_map/ppermute | solution.py:10
  18.0 10.3 %collective-permute-start.20 = (bf16[2,4096]{1,0:T(2,128)(2,1)S(1)}, bf16[2,4096]{1,0:T(2,128)(2,1)S(1)}, u32[]{:S(2)}, u32[]{:S(2)}) collective-permute-start(bf16[2,4096]{1,0:T(2,128)(2,1)S(1)} %subtract_convert_fusion), channel_id=1, source_target_pairs={{0,14},{2,12},{4,10},{6,8},{8,6},{10,4},{12,2},{14,0},{1,15},{3,13... | collective-permute-start | bytes 49160 | tf_op jit(solution)/shard_map/ppermute | solution.py:10
  22.7 6.3 %collective-permute-start.19 = (bf16[2,4096]{1,0:T(2,128)(2,1)S(1)}, bf16[2,4096]{1,0:T(2,128)(2,1)S(1)}, u32[]{:S(2)}, u32[]{:S(2)}) collective-permute-start(bf16[2,4096]{1,0:T(2,128)(2,1)S(1)} %subtract_convert_fusion), channel_id=1, source_target_pairs={{0,12},{2,14},{4,8},{6,10},{8,4},{10,6},{12,0},{14,2},{1,13},{3,15... | collective-permute-start | bytes 49160 | tf_op jit(solution)/shard_map/ppermute | solution.py:10
  23.0 6.5 %collective-permute-start.18 = (bf16[2,4096]{1,0:T(2,128)(2,1)S(1)}, bf16[2,4096]{1,0:T(2,128)(2,1)S(1)}, u32[]{:S(2)}, u32[]{:S(2)}) collective-permute-start(bf16[2,4096]{1,0:T(2,128)(2,1)S(1)} %subtract_convert_fusion), channel_id=1, source_target_pairs={{0,10},{2,8},{4,14},{6,12},{8,2},{10,0},{12,6},{14,4},{1,11},{3,9}... | collective-permute-start | bytes 49160 | tf_op jit(solution)/shard_map/ppermute | solution.py:10
  23.4 10.7 %collective-permute-start.17 = (bf16[2,4096]{1,0:T(2,128)(2,1)S(1)}, bf16[2,4096]{1,0:T(2,128)(2,1)S(1)}, u32[]{:S(2)}, u32[]{:S(2)}) collective-permute-start(bf16[2,4096]{1,0:T(2,128)(2,1)S(1)} %subtract_convert_fusion), channel_id=1, source_target_pairs={{0,8},{2,10},{4,12},{6,14},{8,0},{10,2},{12,4},{14,6},{1,9},{3,11}... | collective-permute-start | bytes 49160 | tf_op jit(solution)/shard_map/ppermute | solution.py:10
  25.8 8.6 %collective-permute-start.16 = (bf16[2,4096]{1,0:T(2,128)(2,1)S(1)}, bf16[2,4096]{1,0:T(2,128)(2,1)S(1)}, u32[]{:S(2)}, u32[]{:S(2)}) collective-permute-start(bf16[2,4096]{1,0:T(2,128)(2,1)S(1)} %subtract_convert_fusion), channel_id=1, source_target_pairs={{0,6},{2,4},{4,2},{6,0},{8,14},{10,12},{12,10},{14,8},{1,7},{3,5},... | collective-permute-start | bytes 49160 | tf_op jit(solution)/shard_map/ppermute | solution.py:10
  28.2 6.6 %collective-permute-start.15 = (bf16[2,4096]{1,0:T(2,128)(2,1)S(1)}, bf16[2,4096]{1,0:T(2,128)(2,1)S(1)}, u32[]{:S(2)}, u32[]{:S(2)}) collective-permute-start(bf16[2,4096]{1,0:T(2,128)(2,1)S(1)} %subtract_convert_fusion), channel_id=1, source_target_pairs={{0,4},{2,6},{4,0},{6,2},{8,12},{10,14},{12,8},{14,10},{1,5},{3,7},... | collective-permute-start | bytes 49160 | tf_op jit(solution)/shard_map/ppermute | solution.py:10
  29.0 8.2 %collective-permute-start.14 = (bf16[2,4096]{1,0:T(2,128)(2,1)S(1)}, bf16[2,4096]{1,0:T(2,128)(2,1)S(1)}, u32[]{:S(2)}, u32[]{:S(2)}) collective-permute-start(bf16[2,4096]{1,0:T(2,128)(2,1)S(1)} %subtract_convert_fusion), channel_id=1, source_target_pairs={{0,2},{2,0},{4,6},{6,4},{8,10},{10,8},{12,14},{14,12},{1,3},{3,1},... | collective-permute-start | bytes 49160 | tf_op jit(solution)/shard_map/ppermute | solution.py:10
  29.4 10.1 %collective-permute-start.13 = (bf16[2,4096]{1,0:T(2,128)(2,1)S(1)}, bf16[2,4096]{1,0:T(2,128)(2,1)S(1)}, u32[]{:S(2)}, u32[]{:S(2)}) collective-permute-start(bf16[2,4096]{1,0:T(2,128)(2,1)S(1)} %multiply_convert_fusion), channel_id=1, source_target_pairs={{0,14},{2,12},{4,10},{6,8},{8,6},{10,4},{12,2},{14,0},{1,15},{3,13... | collective-permute-start | bytes 49160 | tf_op jit(solution)/shard_map/ppermute | solution.py:10
  34.1 6.2 %collective-permute-start.12 = (bf16[2,4096]{1,0:T(2,128)(2,1)S(1)}, bf16[2,4096]{1,0:T(2,128)(2,1)S(1)}, u32[]{:S(2)}, u32[]{:S(2)}) collective-permute-start(bf16[2,4096]{1,0:T(2,128)(2,1)S(1)} %multiply_convert_fusion), channel_id=1, source_target_pairs={{0,12},{2,14},{4,8},{6,10},{8,4},{10,6},{12,0},{14,2},{1,13},{3,15... | collective-permute-start | bytes 49160 | tf_op jit(solution)/shard_map/ppermute | solution.py:10
  34.3 6.9 %collective-permute-start.11 = (bf16[2,4096]{1,0:T(2,128)(2,1)S(1)}, bf16[2,4096]{1,0:T(2,128)(2,1)S(1)}, u32[]{:S(2)}, u32[]{:S(2)}) collective-permute-start(bf16[2,4096]{1,0:T(2,128)(2,1)S(1)} %multiply_convert_fusion), channel_id=1, source_target_pairs={{0,10},{2,8},{4,14},{6,12},{8,2},{10,0},{12,6},{14,4},{1,11},{3,9}... | collective-permute-start | bytes 49160 | tf_op jit(solution)/shard_map/ppermute | solution.py:10
  34.8 6.5 %collective-permute-start.10 = (bf16[2,4096]{1,0:T(2,128)(2,1)S(1)}, bf16[2,4096]{1,0:T(2,128)(2,1)S(1)}, u32[]{:S(2)}, u32[]{:S(2)}) collective-permute-start(bf16[2,4096]{1,0:T(2,128)(2,1)S(1)} %multiply_convert_fusion), channel_id=1, source_target_pairs={{0,8},{2,10},{4,12},{6,14},{8,0},{10,2},{12,4},{14,6},{1,9},{3,11}... | collective-permute-start | bytes 49160 | tf_op jit(solution)/shard_map/ppermute | solution.py:10
  37.2 4.6 %collective-permute-start.9 = (bf16[2,4096]{1,0:T(2,128)(2,1)S(1)}, bf16[2,4096]{1,0:T(2,128)(2,1)S(1)}, u32[]{:S(2)}, u32[]{:S(2)}) collective-permute-start(bf16[2,4096]{1,0:T(2,128)(2,1)S(1)} %multiply_convert_fusion), channel_id=1, source_target_pairs={{0,6},{2,4},{4,2},{6,0},{8,14},{10,12},{12,10},{14,8},{1,7},{3,5},... | collective-permute-start | bytes 49160 | tf_op jit(solution)/shard_map/ppermute | solution.py:10
  39.5 3.7 %collective-permute-start.8 = (bf16[2,4096]{1,0:T(2,128)(2,1)S(1)}, bf16[2,4096]{1,0:T(2,128)(2,1)S(1)}, u32[]{:S(2)}, u32[]{:S(2)}) collective-permute-start(bf16[2,4096]{1,0:T(2,128)(2,1)S(1)} %multiply_convert_fusion), channel_id=1, source_target_pairs={{0,4},{2,6},{4,0},{6,2},{8,12},{10,14},{12,8},{14,10},{1,5},{3,7},... | collective-permute-start | bytes 49160 | tf_op jit(solution)/shard_map/ppermute | solution.py:10
  40.3 3.7 %collective-permute-start.7 = (bf16[2,4096]{1,0:T(2,128)(2,1)S(1)}, bf16[2,4096]{1,0:T(2,128)(2,1)S(1)}, u32[]{:S(2)}, u32[]{:S(2)}) collective-permute-start(bf16[2,4096]{1,0:T(2,128)(2,1)S(1)} %multiply_convert_fusion), channel_id=1, source_target_pairs={{0,2},{2,0},{4,6},{6,4},{8,10},{10,8},{12,14},{14,12},{1,3},{3,1},... | collective-permute-start | bytes 49160 | tf_op jit(solution)/shard_map/ppermute | solution.py:10
  44.6 1.4 %collective-permute-start.21 = (f32[16,128]{1,0:T(8,128)S(1)}, f32[16,128]{1,0:T(8,128)S(1)}, u32[]{:S(2)}, u32[]{:S(2)}) collective-permute-start(f32[16,128]{1,0:T(8,128)S(1)} %fusion.11), channel_id=1, source_target_pairs={{0,1},{1,0},{2,3},{3,2},{4,5},{5,4},{6,7},{7,6},{8,9},{9,8},{10,11... | collective-permute-start | bytes 24584 | tf_op jit(solution)/shard_map/ppermute | solution.py:10

commit v2 on v0

--- a/solution.py
+++ b/solution.py
@@ -6,6 +6,22 @@
 
 def swapped(shard, axis, distance):
     return lax.ppermute(shard, axis, [(i, i ^ 1 << distance) for i in range(lax.axis_size(axis))])
+
+
+def exchanged(blocks, axis):
+    return lax.all_to_all(blocks, axis, split_axis=0, concat_axis=0, tiled=True)
+
+
+def gathered(own, axis):
+    size = lax.axis_size(axis)
+    copies = jnp.broadcast_to(own[None], (size,) + own.shape)
+    return exchanged(copies, axis).reshape((size * own.shape[0],) + own.shape[1:])
+
+
+def scattered_sum(whole, axis):
+    size = lax.axis_size(axis)
+    parts = whole.astype(jnp.bfloat16).reshape((size, whole.shape[0] // size) + whole.shape[1:])
+    return jnp.sum(exchanged(parts, axis).astype(jnp.float32), axis=0)
 
 
 def slot_codes(slot_ids, live_slots, top_idx, pre_codes):
@@ -28,15 +44,12 @@
     centered_own = lax.optimization_barrier(
         (tokens.astype(jnp.float32) - b_pre.astype(jnp.float32)).astype(jnp.bfloat16)
     )
-    centered = lax.all_gather(centered_own, "feat", axis=0, tiled=True)
-    rebuilt_own = lax.psum_scatter(
-        jnp.dot(code_block, dict_rows, preferred_element_type=jnp.float32),
-        "feat",
-        scatter_dimension=0,
-        tiled=True,
+    centered = gathered(centered_own, "feat")
+    rebuilt_own = scattered_sum(
+        jnp.dot(code_block, dict_rows, preferred_element_type=jnp.float32), "feat"
     )
     scaled_own = (0.25 * (rebuilt_own - centered_own.astype(jnp.float32))).astype(jnp.bfloat16)
-    scaled = lax.all_gather(scaled_own, "feat", axis=0, tiled=True)
+    scaled = gathered(scaled_own, "feat")
     code_half = lax.dot_general(
         scaled, dict_rows, (((1,), (1,)), ((), ())), preferred_element_type=jnp.float32
     )

time: 128 us -> 46.7 us (0.36)
  blocking collectives: 62.9 us -> 0 us
  waiting for transfers between devices: 39.8 us -> 21.3 us
  between operations: 16.2 us -> 2.16 us
  starting transfers between devices: 0.04 us -> 14 us
  local copies, waits for them, and re-layouts: 0.73 us -> 2.34 us
    all_gather x2 -> x0, blocking collectives: 62.9 us -> none  [the longest x1 32.3 us: local(): centered = lax.all_gather(centered_own, 'feat', axis=0, tiled=True)]
    unnamed x2 -> x0, waiting for transfers between devices: 39.8 us -> none
    all_to_all x0 -> x3, waiting for transfers between devices: none -> 21.3 us  [exchanged(): return lax.all_to_all(blocks, axis, split_axis=0, concat_axis=0, tiled=True)]
    all_to_all x0 -> x3, starting transfers between devices: none -> 14 us  [exchanged(): return lax.all_to_all(blocks, axis, split_axis=0, concat_axis=0, tiled=True)]
    broadcast_in_dim x0 -> x2, local copies, waits for them, and re-layouts: none -> 1.45 us  [gathered(): copies = jnp.broadcast_to(own[None], (size,) + own.shape)]
  transfers between devices with their start and end apart: 2 -> 4, of which waited for: 1 -> 3; matrix products, arithmetic and copies ran while one was open for 2% -> 4% of each run, Pallas kernels for 0% -> 0%
where the time goes in v2:
time: 46.7 us; the launch traced here: 46.1 us
  waiting for transfers between devices  21.3 us (46%)
  starting transfers between devices  14 us (30%)
  matrix products  3.51 us (8%)
  other arithmetic  2.81 us (6%)
  local copies, waits for them, and re-layouts  2.34 us (5%)
  between operations  2.16 us (5%)
    all_to_all x3, waiting for transfers between devices, exchanged(): return lax.all_to_all(blocks, axis, split_axis=0, concat_axis=0, tiled=True)  21.3 us
    all_to_all x3, starting transfers between devices, exchanged(): return lax.all_to_all(blocks, axis, split_axis=0, concat_axis=0, tiled=True)  14 us
    dot_general x1, matrix products, local(): lax.dot_general(centered, pre_grad, (((0,), (0,)), ((), ())), preferred_e...  1.45 us
    broadcast_in_dim x2, local copies, waits for them, and re-layouts, gathered(): copies = jnp.broadcast_to(own[None], (size,) + own.shape)  1.45 us
    dot_general x1, matrix products, local(): lax.dot_general(code_block, scaled, (((0,), (0,)), ((), ())), preferred_e...  1.44 us
    reduce_sum x1, other arithmetic, slot_codes(): jnp.sum(jnp.where(matches, positive[:, :, None], jnp.zeros_like(positive)...  1.05 us
  transfers between devices with their start and end apart: 4, of which 3 were waited for; matrix products, arithmetic and copies ran while one was open for 4% of the time, Pallas kernels for 0%

profile of v2, /device:TPU:0, one launch (start us, length us, event | category | flops | bytes accessed | tf_op | source)
XLA Modules:
  0.0 46.1 jit_solution(6033954287758900107)
XLA Ops:
  0.6 0.0 copy-start
  0.6 0.0 copy-start.4
  0.7 0.0 copy-start.3
  2.1 0.7 %broadcast_maximum_fusion = f32[16,64]{1,0:T(8,128)S(1)} fusion(f32[16,64]{1,0:T(8,128)} %param.9), kind=kLoop, calls=%fused_computation.12 | loop fusion | flops 1024 | bytes 8192 | tf_op jit(solution)/shard_map/max | solution.py:29
  2.8 1.0 %select_reduce_fusion = bf16[16,128]{1,0:T(8,128)(2,1)S(1)} fusion(f32[16,64]{1,0:T(8,128)S(1)} %broadcast_maximum_fusion, s32[128]{0:T(128)S(1)} %iota_add_fusion, s32[16,64]{1,0:T(8,128)} %param.10, pred[128]{0:T(512)(128)(4,1)S(1)} %iota_compare_fusion), kind=kLoop, calls=%fused_computation.3 | loop fusion | flops 522240 | bytes 12928 | tf_op jit(solution)/shard_map/reduce_sum | solution.py:30
  3.8 0.0 copy-done
  3.8 0.2 convolution_convert_fusion.2
  4.1 0.0 copy-start.1
  4.1 0.0 copy-start.2
  4.1 0.8 %reshape.31 = bf16[8,2,4096]{2,1,0:T(2,128)(2,1)} reshape(bf16[16,4096]{1,0:T(8,128)(2,1)S(1)} %convolution_convert_fusion.2) | data formatting | bytes 262144 | tf_op jit(solution)/shard_map/reshape | solution.py:23
  4.8 7.3 %all-to-all-start = ((bf16[8,2,4096]{2,1,0:T(2,128)(2,1)}), bf16[8,2,4096]{2,1,0:T(2,128)(2,1)S(1)}, u32[]{:S(2)}, u32[]{:S(2)}) async-start(bf16[8,2,4096]{2,1,0:T(2,128)(2,1)} %reshape.31), calls=%async_computation | async-start | bytes 262144 | tf_op jit(solution)/shard_map/all_to_all | solution.py:12
  12.1 0.0 copy-done.4
  12.1 0.0 copy-done.3
  12.2 7.3 %all-to-all-done = bf16[8,2,4096]{2,1,0:T(2,128)(2,1)S(1)} async-done(((bf16[8,2,4096]{2,1,0:T(2,128)(2,1)}), bf16[8,2,4096]{2,1,0:T(2,128)(2,1)S(1)}, u32[]{:S(2)}, u32[]{:S(2)}) %all-to-all-start) | async-done | bytes 131104 | tf_op jit(solution)/shard_map/all_to_all | solution.py:12
  19.4 0.7 %broadcast_in_dim.25 = bf16[8,2,4096]{2,1,0:T(2,128)(2,1)} broadcast(bf16[2,4096]{1,0:T(2,128)(2,1)S(1)} %subtract_convert_fusion), dimensions={1,2} | broadcast | bytes 147456 | tf_op jit(solution)/shard_map/broadcast_in_dim | solution.py:17
  20.2 3.4 %all-to-all-start.2 = ((bf16[8,2,4096]{2,1,0:T(2,128)(2,1)}), bf16[8,2,4096]{2,1,0:T(2,128)(2,1)S(1)}, u32[]{:S(2)}, u32[]{:S(2)}) async-start(bf16[8,2,4096]{2,1,0:T(2,128)(2,1)} %broadcast_in_dim.25), calls=%async_computation.2 | async-start | bytes 262144 | tf_op jit(solution)/shard_map/all_to_all | solution.py:12
  23.6 0.1 convert_reduce_fusion
  23.7 7.1 %all-to-all-done.2 = bf16[8,2,4096]{2,1,0:T(2,128)(2,1)S(1)} async-done(((bf16[8,2,4096]{2,1,0:T(2,128)(2,1)}), bf16[8,2,4096]{2,1,0:T(2,128)(2,1)S(1)}, u32[]{:S(2)}, u32[]{:S(2)}) %all-to-all-start.2) | async-done | bytes 131104 | tf_op jit(solution)/shard_map/all_to_all | solution.py:12
  30.8 0.7 %broadcast_in_dim.24 = bf16[8,2,4096]{2,1,0:T(2,128)(2,1)} broadcast(bf16[2,4096]{1,0:T(2,128)(2,1)S(1)} %multiply_convert_fusion), dimensions={1,2} | broadcast | bytes 147456 | tf_op jit(solution)/shard_map/broadcast_in_dim | solution.py:17
  31.6 3.4 %all-to-all-start.1 = ((bf16[8,2,4096]{2,1,0:T(2,128)(2,1)}), bf16[8,2,4096]{2,1,0:T(2,128)(2,1)S(1)}, u32[]{:S(2)}, u32[]{:S(2)}) async-start(bf16[8,2,4096]{2,1,0:T(2,128)(2,1)} %broadcast_in_dim.24), calls=%async_computation.1 | async-start | bytes 262144 | tf_op jit(solution)/shard_map/all_to_all | solution.py:12
  34.9 0.0 copy-done.1
  35.0 0.0 copy-done.2
  35.0 0.4 and_reduce_fusion
  35.3 0.1 reshape.33
  35.4 6.8 %all-to-all-done.1 = bf16[8,2,4096]{2,1,0:T(2,128)(2,1)S(1)} async-done(((bf16[8,2,4096]{2,1,0:T(2,128)(2,1)}), bf16[8,2,4096]{2,1,0:T(2,128)(2,1)S(1)}, u32[]{:S(2)}, u32[]{:S(2)}) %all-to-all-start.1) | async-done | bytes 131104 | tf_op jit(solution)/shard_map/all_to_all | solution.py:12
  42.2 0.1 reshape.32
  42.3 0.4 fusion.2
  42.6 0.0 collective-permute-start
  42.7 1.4 %convolution_convert_fusion.1 = bf16[128,4096]{1,0:T(8,128)(2,1)} fusion(bf16[16,4096]{1,0:T(8,128)(2,1)S(1)} %reshape.32, bf16[16,128]{1,0:T(8,128)(2,1)S(1)} %select_reduce_fusion), kind=kOutput, calls=%fused_computation.1 | convolution fusion | flops 17301504 | bytes 1183744 | tf_op jit(solution)/shard_map/dot_general | solution.py:58
  44.1 0.0 collective-permute-done
  44.1 0.5 %convert_reduce_fusion.1 = (f32[128]{0:T(128)}, bf16[16,128]{1,0:T(8,128)(2,1)S(1)}) fusion(pred[16,128]{1,0:T(8,128)(4,1)S(1)} %and_reduce_fusion, f32[16,128]{1,0:T(8,128)S(1)} %fusion.2, f32[16,128]{1,0:T(8,128)S(1)} %collective-permute-done), kind=kLoop, calls=%fused_computation.9 | loop fusion | flops 10112 | bytes 23040 | tf_op jit(solution)/shard_map/reduce_sum | solution.py:64
  44.6 1.5 %convolution_convert_fusion = bf16[4096,128]{1,0:T(8,128)(2,1)} fusion(bf16[16,4096]{1,0:T(8,128)(2,1)S(1)} %reshape.33, bf16[16,128]{1,0:T(8,128)(2,1)S(1)} %get-tuple-element.4), kind=kOutput, calls=%fused_computation | convolution fusion | flops 17301504 | bytes 1183744 | tf_op jit(solution)/shard_map/dot_general | solution.py:61
  (6 shorter events, 0.1 us)
Async XLA Ops:
  0.6 3.2 %copy-start = (bf16[128,4096]{1,0:T(8,128)(2,1)S(1)}, bf16[128,4096]{1,0:T(8,128)(2,1)}, u32[]{:S(2)}) copy-start(bf16[128,4096]{1,0:T(8,128)(2,1)} %param.13) | copy-start | bytes 3145732
  0.6 11.5 %copy-start.4 = (bf16[4096]{0:T(1024)(128)(2,1)S(1)}, bf16[4096]{0:T(1024)(128)(2,1)}, u32[]{:S(2)}) copy-start(bf16[4096]{0:T(1024)(128)(2,1)} %param.8) | copy-start | bytes 24580
  0.7 11.5 %copy-start.3 = (bf16[2,4096]{1,0:T(2,128)(2,1)S(1)}, bf16[2,4096]{1,0:T(2,128)(2,1)}, u32[]{:S(2)}) copy-start(bf16[2,4096]{1,0:T(2,128)(2,1)} %param.7) | copy-start | bytes 49156
  4.1 30.9 %copy-start.1 = (f32[16,64]{1,0:T(8,128)S(1)}, f32[16,64]{1,0:T(8,128)}, u32[]{:S(2)}) copy-start(f32[16,64]{1,0:T(8,128)} %param.9) | copy-start | bytes 12292
  4.1 30.9 %copy-start.2 = (s32[16,64]{1,0:T(8,128)S(1)}, s32[16,64]{1,0:T(8,128)}, u32[]{:S(2)}) copy-start(s32[16,64]{1,0:T(8,128)} %param.10) | copy-start | bytes 12292
  4.8 14.6 %all-to-all-start = ((bf16[8,2,4096]{2,1,0:T(2,128)(2,1)}), bf16[8,2,4096]{2,1,0:T(2,128)(2,1)S(1)}, u32[]{:S(2)}, u32[]{:S(2)}) async-start(bf16[8,2,4096]{2,1,0:T(2,128)(2,1)} %reshape.31), calls=%async_computation | async-start | bytes 262144 | tf_op jit(solution)/shard_map/all_to_all | solution.py:12
  20.2 10.7 %all-to-all-start.2 = ((bf16[8,2,4096]{2,1,0:T(2,128)(2,1)}), bf16[8,2,4096]{2,1,0:T(2,128)(2,1)S(1)}, u32[]{:S(2)}, u32[]{:S(2)}) async-start(bf16[8,2,4096]{2,1,0:T(2,128)(2,1)} %broadcast_in_dim.25), calls=%async_computation.2 | async-start | bytes 262144 | tf_op jit(solution)/shard_map/all_to_all | solution.py:12
  31.6 10.7 %all-to-all-start.1 = ((bf16[8,2,4096]{2,1,0:T(2,128)(2,1)}), bf16[8,2,4096]{2,1,0:T(2,128)(2,1)S(1)}, u32[]{:S(2)}, u32[]{:S(2)}) async-start(bf16[8,2,4096]{2,1,0:T(2,128)(2,1)} %broadcast_in_dim.24), calls=%async_computation.1 | async-start | bytes 262144 | tf_op jit(solution)/shard_map/all_to_all | solution.py:12
  42.6 1.4 %collective-permute-start = (f32[16,128]{1,0:T(8,128)S(1)}, f32[16,128]{1,0:T(8,128)S(1)}, u32[]{:S(2)}, u32[]{:S(2)}) collective-permute-start(f32[16,128]{1,0:T(8,128)S(1)} %fusion.2), channel_id=1, source_target_pairs={{0,1},{1,0},{2,3},{3,2},{4,5},{5,4},{6,7},{7,6},{8,9},{9,8},{10,11... | collective-permute-start | bytes 24584 | tf_op jit(solution)/shard_map/ppermute | solution.py:8

commit v3 on v0

v3 whole, which is shorter than its diff:
```python
import functools

import jax
import jax.numpy as jnp
from jax import lax
from jax.experimental import pallas as pl
from jax.experimental.pallas import tpu as pltpu
from jax.sharding import PartitionSpec as P

VMEM = pl.BlockSpec(memory_space=pltpu.VMEM)


def swapped(shard, axis, distance):
    return lax.ppermute(shard, axis, [(i, i ^ distance) for i in range(lax.axis_size(axis))])


def halves(width):
    half = width // 2
    bit = lax.axis_index("feat") & 1
    return (
        pl.multiple_of(bit * half, half),
        pl.multiple_of((1 - bit) * half, half),
        half,
    )


def share(code, rows_ref, centered_ref, at, half):
    total = jnp.dot(code, rows_ref[:, pl.ds(at, half)], preferred_element_type=jnp.float32)
    rows = centered_ref.shape[0]
    centered = centered_ref[:, pl.ds(at, half)].astype(jnp.float32)
    token = lax.broadcasted_iota(jnp.int32, (total.shape[0], 1), 0)
    first = lax.axis_index("feat") * rows
    for i in range(rows):
        total -= jnp.where(token == first + i, centered[i : i + 1, :], 0.0)
    return total


def codes_kernel(
    top_ref, pre_ref, block_ref, count_ref, rows_ref, centered_ref, code_ref, raw_ref, send_ref
):
    tokens, latents = top_ref.shape
    slots, width = rows_ref.shape
    offsets = lax.broadcasted_iota(jnp.int32, (1, slots), 1)
    slot_ids = jnp.where(offsets < count_ref[...], block_ref[...] * slots + offsets, -1)
    top, pre = top_ref[...], pre_ref[...]
    raw = jnp.zeros((tokens, slots), jnp.float32)
    for k in range(latents):
        raw = jnp.where(top[:, k : k + 1] == slot_ids, pre[:, k : k + 1], raw)
    raw_ref[...] = raw
    code = jnp.maximum(raw, 0.0).astype(jnp.bfloat16)
    code_ref[...] = code
    _, other, half = halves(width)
    send_ref[...] = share(code, rows_ref, centered_ref, other, half).astype(jnp.bfloat16)


def codes(top_idx, pre_codes, blocks, counts, dict_rows, centered_own):
    tokens = top_idx.shape[0]
    slots, width = dict_rows.shape
    return pl.pallas_call(
        codes_kernel,
        out_shape=(
            jax.ShapeDtypeStruct((tokens, slots), jnp.bfloat16),
            jax.ShapeDtypeStruct((tokens, slots), jnp.float32),
            jax.ShapeDtypeStruct((tokens, width // 2), jnp.bfloat16),
        ),
        in_specs=[VMEM] * 6,
        out_specs=(VMEM,) * 3,
        cost_estimate=pl.CostEstimate(flops=10**6, bytes_accessed=2**20, transcendentals=0),
        name="codes",
    )(top_idx, pre_codes, blocks.reshape(1, 1), counts.reshape(1, 1), dict_rows, centered_own)


def own_kernel(code_ref, rows_ref, centered_ref, total_ref):
    own, _, half = halves(rows_ref.shape[1])
    total_ref[...] = share(code_ref[...], rows_ref, centered_ref, own, half)


def own_part(code, dict_rows, centered_own):
    half = dict_rows.shape[1] // 2
    return pl.pallas_call(
        own_kernel,
        out_shape=jax.ShapeDtypeStruct((code.shape[0], half), jnp.float32),
        in_specs=[VMEM] * 3,
        out_specs=VMEM,
        cost_estimate=pl.CostEstimate(flops=10**6, bytes_accessed=2**19, transcendentals=0),
        name="own_part",
    )(code, dict_rows, centered_own)


def code_half_kernel(own_ref, other_ref, rows_ref, half_ref, scaled_ref):
    own_at, other_at, half = halves(rows_ref.shape[1])
    total = jnp.zeros(half_ref.shape, jnp.float32)
    for ref, at in ((own_ref, own_at), (other_ref, other_at)):
        part = ref[...]
        scaled_ref[:, pl.ds(at, half)] = part
        total += lax.dot_general(
            part,
            rows_ref[:, pl.ds(at, half)],
            (((1,), (1,)), ((), ())),
            preferred_element_type=jnp.float32,
        )
    half_ref[...] = total


def code_half_of(scaled_own, scaled_other, dict_rows):
    tokens = scaled_own.shape[0]
    slots, width = dict_rows.shape
    return pl.pallas_call(
        code_half_kernel,
        out_shape=(
            jax.ShapeDtypeStruct((tokens, slots), jnp.float32),
            jax.ShapeDtypeStruct((tokens, width), jnp.bfloat16),
        ),
        in_specs=[VMEM] * 3,
        out_specs=(VMEM, VMEM),
        cost_estimate=pl.CostEstimate(flops=10**6, bytes_accessed=2**20, transcendentals=0),
        name="code_half",
    )(scaled_own, scaled_other, dict_rows)


def masked_kernel(rows, raw_ref, mine_ref, theirs_ref, grad_ref, benc_ref):
    tokens = raw_ref.shape[0]
    code_grad = mine_ref[...] + theirs_ref[...]
    pre_grad = jnp.where(raw_ref[...] > 0.0, code_grad, 0.0).astype(jnp.bfloat16)
    benc_ref[...] = jnp.sum(pre_grad.astype(jnp.float32), axis=0, keepdims=True)
    place = lax.broadcasted_iota(jnp.int32, (tokens, tokens), 0)
    token = lax.broadcasted_iota(jnp.int32, (tokens, tokens), 1)
    first = lax.axis_index("feat") * rows
    order = jnp.where(token == (place ^ first), 1.0, 0.0).astype(jnp.bfloat16)
    grad_ref[...] = jnp.dot(order, pre_grad, preferred_element_type=jnp.float32).astype(
        jnp.bfloat16
    )


def masked(raw, mine, theirs, rows):
    tokens, slots = raw.shape
    return pl.pallas_call(
        functools.partial(masked_kernel, rows),
        out_shape=(
            jax.ShapeDtypeStruct((tokens, slots), jnp.bfloat16),
            jax.ShapeDtypeStruct((1, slots), jnp.float32),
        ),
        in_specs=[VMEM] * 3,
        out_specs=(VMEM, VMEM),
        cost_estimate=pl.CostEstimate(flops=10**5, bytes_accessed=2**15, transcendentals=0),
        name="masked",
    )(raw, mine, theirs)


def local(tokens, b_pre, pre_codes, top_idx, blocks, counts, dict_rows):
    size = lax.axis_size("feat")
    rows, width = tokens.shape
    centered_own = lax.optimization_barrier(
        (tokens.astype(jnp.float32) - b_pre.astype(jnp.float32)).astype(jnp.bfloat16)
    )
    code, raw, send = codes(top_idx, pre_codes, blocks, counts, dict_rows, centered_own)

    arrived = swapped(send, "feat", 1)
    total = own_part(code, dict_rows, centered_own) + arrived.astype(jnp.float32)
    distance = 2
    while distance < size:
        total = total + swapped(total.astype(jnp.bfloat16), "feat", distance).astype(jnp.float32)
        distance *= 2
    scaled_own = (0.25 * total).astype(jnp.bfloat16)
    scaled_other = swapped(scaled_own, "feat", 1)

    centered = centered_own[None]
    distance = 1
    while distance < size:
        centered = jnp.concatenate([centered, swapped(centered, "feat", distance)], axis=0)
        distance *= 2
    centered = centered.reshape(size * rows, width)

    code_half, scaled = code_half_of(scaled_own, scaled_other, dict_rows)
    theirs = swapped(code_half, "tok", 1)
    grad_rows = lax.dot_general(
        code, scaled, (((0,), (0,)), ((), ())), preferred_element_type=jnp.float32
    ).astype(jnp.bfloat16)
    pre_grad, grad_benc = masked(raw, code_half, theirs, rows)
    grad_enc = lax.dot_general(
        centered, pre_grad, (((0,), (0,)), ((), ())), preferred_element_type=jnp.float32
    ).astype(jnp.bfloat16)
    return (grad_rows, grad_enc, grad_benc.reshape(-1))


def solution(mesh):
    return jax.shard_map(
        local,
        mesh=mesh,
        in_specs=(
            P(("grp", "feat"), "tok"),
            P(("grp", "tok")),
            P("grp", None),
            P("grp", None),
            P(("grp", "feat")),
            P(("grp", "feat")),
            P(("grp", "feat"), "tok"),
        ),
        out_specs=(P(("grp", "feat"), "tok"), P(("grp", "tok"), "feat"), P(("grp", "feat"))),
        check_vma=False,
    )
```

time: 128 us -> 40.5 us (0.32)
  blocking collectives: 62.9 us -> 0 us
  waiting for transfers between devices: 39.8 us -> 8.39 us
  between operations: 16.2 us -> 1.99 us
  starting transfers between devices: 0.04 us -> 10.3 us
  Pallas kernels: 0 us -> 8.34 us
  other arithmetic: 3.61 us -> 5.15 us
    all_gather x2 -> x0, blocking collectives: 62.9 us -> none  [the longest x1 32.3 us: local(): centered = lax.all_gather(centered_own, 'feat', axis=0, tiled=True)]
    unnamed x2 -> x0, waiting for transfers between devices: 39.8 us -> none
    ppermute x1 -> x8, starting transfers between devices: 0.01 us -> 10.3 us  [swapped(): lax.ppermute(shard, axis, [(i, i ^ distance) for i in range(lax.axis_size...]
    ppermute x1 -> x8, waiting for transfers between devices: 0.01 us -> 8.39 us  [swapped(): lax.ppermute(shard, axis, [(i, i ^ distance) for i in range(lax.axis_size...]
    pallas_call x0 -> x4, Pallas kernels: none -> 8.34 us  [the longest x1 2.52 us: codes(): pl.pallas_call(codes_kernel, out_shape=(jax.ShapeDtypeStruct((tokens, slo...]
    convert_element_type x0 -> x3, other arithmetic: none -> 2.79 us  [the longest x2 1.85 us: local(): total.astype(jnp.bfloat16)]
    reduce_sum x2 -> x0, other arithmetic: 1.58 us -> none  [the longest x1 1.05 us: slot_codes(): jnp.sum(jnp.where(matches, positive[:, :, None], jnp.zeros_like(positive)...]
    convert_element_type x1, other arithmetic: 0.02 us -> 1.33 us  [local(): (tokens.astype(jnp.float32) - b_pre.astype(jnp.float32)).astype(jnp.bfloa...]
  transfers between devices with their start and end apart: 2 -> 8, of which waited for: 1 -> 4; matrix products, arithmetic and copies ran while one was open for 2% -> 14% of each run, Pallas kernels for 0% -> 5%
where the time goes in v3:
time: 40.5 us; the launch traced here: 39.9 us
  starting transfers between devices  10.3 us (25%)
  waiting for transfers between devices  8.39 us (21%)
  Pallas kernels  8.34 us (21%)
  other arithmetic  5.15 us (13%)
  matrix products  4.47 us (11%)
  between operations  1.99 us (5%)
  local copies, waits for them, and re-layouts  1.29 us (3%)
    ppermute x8, starting transfers between devices, swapped(): lax.ppermute(shard, axis, [(i, i ^ distance) for i in range(lax.axis_size...  10.3 us
    ppermute x8, waiting for transfers between devices, swapped(): lax.ppermute(shard, axis, [(i, i ^ distance) for i in range(lax.axis_size...  8.39 us
    pallas_call x1, Pallas kernels, codes(): pl.pallas_call(codes_kernel, out_shape=(jax.ShapeDtypeStruct((tokens, slo...  2.52 us
    dot_general x1, matrix products, local(): lax.dot_general(code, scaled, (((0,), (0,)), ((), ())), preferred_element...  2.33 us
    pallas_call x1, Pallas kernels, code_half_of(): pl.pallas_call(code_half_kernel, out_shape=(jax.ShapeDtypeStruct((tokens,...  2.29 us
    dot_general x1, matrix products, local(): lax.dot_general(centered, pre_grad, (((0,), (0,)), ((), ())), preferred_e...  2.14 us
    pallas_call x1, Pallas kernels, own_part(): pl.pallas_call(own_kernel, out_shape=jax.ShapeDtypeStruct((code.shape[0],...  2.07 us
    convert_element_type x2, other arithmetic, local(): total.astype(jnp.bfloat16)  1.85 us
  transfers between devices with their start and end apart: 8, of which 4 were waited for; matrix products, arithmetic and copies ran while one was open for 14% of the time, Pallas kernels for 5%

profile of v3, /device:TPU:0, one launch (start us, length us, event | category | flops | bytes accessed | tf_op | source)
XLA Modules:
  0.0 39.9 jit_solution(2638765271164780740)
XLA Ops:
  1.9 0.7 %convert_element_type.34 = f32[4096]{0:T(1024)S(1)} convert(bf16[4096]{0:T(1024)(128)(2,1)} %param.8) | non-fusion elementwise | flops 4096 | bytes 24576 | tf_op jit(solution)/shard_map/convert_element_type | solution.py:154
  2.6 1.3 %subtract_convert_fusion.centered_ref = bf16[2,4096]{1,0:T(2,128)(2,1)} fusion(bf16[2,4096]{1,0:T(2,128)(2,1)} %param.7, f32[4096]{0:T(1024)S(1)} %convert_element_type.34), kind=kLoop, calls=%fused_computation.10 | loop fusion | flops 24576 | bytes 49152 | tf_op jit(solution)/shard_map/convert_element_type | solution.py:154
  4.0 0.0 copy-start
  4.0 0.0 copy-start.1
  4.0 2.5 %codes.1 = (bf16[16,128]{1,0:T(8,128)(2,1)}, f32[16,128]{1,0:T(8,128)}, bf16[16,2048]{1,0:T(8,128)(2,1)}) custom-call(s32[16,64]{1,0:T(8,128)} %top_ref.1, f32[16,64]{1,0:T(8,128)} %pre_ref.1, s32[1,1]{1,0:T(1,128)} %bitcast.8.block_ref, s32[1,1]{1,0:T(1,128)} %bitcast.9.count_ref, bf16[128,4096]{1,0:T(8,128)(2,1)} %rows_ref.5, ...), custom_call_target="tpu_custom_call" | custom-call | flops 1000000 | bytes 1048576 | tf_op jit(solution)/shard_map/codes/pallas_call | solution.py:59
  6.5 2.9 %collective-permute-start = (bf16[16,2048]{1,0:T(8,128)(2,1)}, bf16[16,2048]{1,0:T(8,128)(2,1)S(1)}, u32[]{:S(2)}, u32[]{:S(2)}) collective-permute-start(bf16[16,2048]{1,0:T(8,128)(2,1)} %get-tuple-element.11), channel_id=1, source_target_pairs={{0,2},{2,0},{4,6},{6,4},{8,10},{10,8},{12,14},{14,12},{1,3},{3,1},... | collective-permute-start | bytes 196616 | tf_op jit(solution)/shard_map/ppermute | solution.py:14
  9.4 0.0 copy-done
  9.4 0.1 collective-permute-start.4
  9.5 2.1 %own_part.1 = f32[16,2048]{1,0:T(8,128)} custom-call(bf16[16,128]{1,0:T(8,128)(2,1)} %get-tuple-element.10.code_ref, bf16[128,4096]{1,0:T(8,128)(2,1)} %rows_ref.5, bf16[2,4096]{1,0:T(2,128)(2,1)} %subtract_convert_fusion.centered_ref), custom_call_target="tpu_custom_call" | custom-call | flops 1000000 | bytes 524288 | tf_op jit(solution)/shard_map/own_part/pallas_call | solution.py:80
  11.6 0.5 %collective-permute-done = bf16[16,2048]{1,0:T(8,128)(2,1)S(1)} collective-permute-done((bf16[16,2048]{1,0:T(8,128)(2,1)}, bf16[16,2048]{1,0:T(8,128)(2,1)S(1)}, u32[]{:S(2)}, u32[]{:S(2)}) %collective-permute-start) | collective-permute-done | bytes 65568 | tf_op jit(solution)/shard_map/ppermute | solution.py:14
  12.1 0.9 %fusion = bf16[16,2048]{1,0:T(8,128)(2,1)S(1)} fusion(f32[16,2048]{1,0:T(8,128)} %own_part.1, bf16[16,2048]{1,0:T(8,128)(2,1)S(1)} %collective-permute-done), kind=kLoop, calls=%fused_computation.6 | loop fusion | flops 98304 | bytes 262144 | tf_op jit(solution)/shard_map/convert_element_type | solution.py:162
  13.0 2.0 %collective-permute-start.1 = (bf16[16,2048]{1,0:T(8,128)(2,1)S(1)}, bf16[16,2048]{1,0:T(8,128)(2,1)S(1)}, u32[]{:S(2)}, u32[]{:S(2)}) collective-permute-start(bf16[16,2048]{1,0:T(8,128)(2,1)S(1)} %fusion), channel_id=1, source_target_pairs={{0,4},{2,6},{4,0},{6,2},{8,12},{10,14},{12,8},{14,10},{1,5},{3,7},... | collective-permute-start | bytes 196616 | tf_op jit(solution)/shard_map/ppermute | solution.py:14
  15.0 0.0 collective-permute-done.4
  15.0 0.0 copy-done.1
  15.1 0.1 collective-permute-start.5
  15.2 2.2 %collective-permute-done.1 = bf16[16,2048]{1,0:T(8,128)(2,1)S(1)} collective-permute-done((bf16[16,2048]{1,0:T(8,128)(2,1)S(1)}, bf16[16,2048]{1,0:T(8,128)(2,1)S(1)}, u32[]{:S(2)}, u32[]{:S(2)}) %collective-permute-start.1) | collective-permute-done | bytes 65568 | tf_op jit(solution)/shard_map/ppermute | solution.py:14
  17.4 0.9 %fusion.1 = bf16[16,2048]{1,0:T(8,128)(2,1)S(1)} fusion(bf16[16,2048]{1,0:T(8,128)(2,1)S(1)} %collective-permute-done.1, f32[16,2048]{1,0:T(8,128)} %own_part.1, bf16[16,2048]{1,0:T(8,128)(2,1)S(1)} %collective-permute-done), kind=kLoop, calls=%fused_computation.8 | loop fusion | flops 163840 | bytes 327680 | tf_op jit(solution)/shard_map/convert_element_type | solution.py:162
  18.3 3.0 %collective-permute-start.2 = (bf16[16,2048]{1,0:T(8,128)(2,1)S(1)}, bf16[16,2048]{1,0:T(8,128)(2,1)S(1)}, u32[]{:S(2)}, u32[]{:S(2)}) collective-permute-start(bf16[16,2048]{1,0:T(8,128)(2,1)S(1)} %fusion.1), channel_id=1, source_target_pairs={{0,8},{2,10},{4,12},{6,14},{8,0},{10,2},{12,4},{14,6},{1,9},{3,11}... | collective-permute-start | bytes 196616 | tf_op jit(solution)/shard_map/ppermute | solution.py:14
  21.3 0.0 collective-permute-done.5
  21.3 0.1 pad_maximum_fusion.1
  21.4 0.0 copy-start.4
  21.4 0.6 %collective-permute-start.6 = (bf16[4,2,4096]{2,1,0:T(2,128)(2,1)S(1)}, bf16[4,2,4096]{2,1,0:T(2,128)(2,1)S(1)}, u32[]{:S(2)}, u32[]{:S(2)}) collective-permute-start(bf16[4,2,4096]{2,1,0:T(2,128)(2,1)S(1)} %pad_maximum_fusion.1), channel_id=1, source_target_pairs={{0,8},{2,10},{4,12},{6,14},{8,0},{10,2},{12,4},{14,6},{1,9},{3,11}... | collective-permute-start | bytes 196616 | tf_op jit(solution)/shard_map/ppermute | solution.py:14
  22.0 3.2 %collective-permute-done.2 = bf16[16,2048]{1,0:T(8,128)(2,1)S(1)} collective-permute-done((bf16[16,2048]{1,0:T(8,128)(2,1)S(1)}, bf16[16,2048]{1,0:T(8,128)(2,1)S(1)}, u32[]{:S(2)}, u32[]{:S(2)}) %collective-permute-start.2) | collective-permute-done | bytes 65568 | tf_op jit(solution)/shard_map/ppermute | solution.py:14
  25.2 0.9 %multiply_convert_fusion.own_ref = bf16[16,2048]{1,0:T(8,128)(2,1)S(1)} fusion(bf16[16,2048]{1,0:T(8,128)(2,1)S(1)} %collective-permute-done.2, bf16[16,2048]{1,0:T(8,128)(2,1)S(1)} %collective-permute-done.1, f32[16,2048]{1,0:T(8,128)} %own_part.1, bf16[16,2048]{1,0:T(8,128)(2,1)S(1)} %collective-permute-done), kind=kLoop, calls=%fused_computation.3 | loop fusion | flops 262144 | bytes 393216 | tf_op jit(solution)/shard_map/convert_element_type | solution.py:164
  26.1 0.0 copy-start.2
  26.2 1.6 %collective-permute-start.3 = (bf16[16,2048]{1,0:T(8,128)(2,1)S(1)}, bf16[16,2048]{1,0:T(8,128)(2,1)S(1)}, u32[]{:S(2)}, u32[]{:S(2)}) collective-permute-start(bf16[16,2048]{1,0:T(8,128)(2,1)S(1)} %multiply_convert_fusion.own_ref), channel_id=1, source_target_pairs={{0,2},{2,0},{4,6},{6,4},{8,10},{10,8},{12,14},{14,12},{1,3},{3,1},... | collective-permute-start | bytes 196616 | tf_op jit(solution)/shard_map/ppermute | solution.py:14
  27.7 0.0 collective-permute-done.6
  27.7 0.2 pad_maximum_fusion
  27.9 0.1 reshape.21
  28.0 2.5 %collective-permute-done.3.other_ref = bf16[16,2048]{1,0:T(8,128)(2,1)S(1)} collective-permute-done((bf16[16,2048]{1,0:T(8,128)(2,1)S(1)}, bf16[16,2048]{1,0:T(8,128)(2,1)S(1)}, u32[]{:S(2)}, u32[]{:S(2)}) %collective-permute-start.3) | collective-permute-done | bytes 65568 | tf_op jit(solution)/shard_map/ppermute | solution.py:14
  30.5 0.0 copy-done.2
  30.5 0.0 copy-start.3
  30.5 0.6 %copy-done.3 = bf16[16,2048]{1,0:T(8,128)(2,1)} copy-done((bf16[16,2048]{1,0:T(8,128)(2,1)}, bf16[16,2048]{1,0:T(8,128)(2,1)S(1)}, u32[]{:S(2)}) %copy-start.3) | copy-done | bytes 65560
  31.1 2.3 %code_half.1 = (f32[16,128]{1,0:T(8,128)}, bf16[16,4096]{1,0:T(8,128)(2,1)}) custom-call(bf16[16,2048]{1,0:T(8,128)(2,1)} %copy-done.2, bf16[16,2048]{1,0:T(8,128)(2,1)} %copy-done.3, bf16[128,4096]{1,0:T(8,128)(2,1)} %rows_ref.5), custom_call_target="tpu_custom_call" | custom-call | flops 1000000 | bytes 1048576 | tf_op jit(solution)/shard_map/code_half/pallas_call | solution.py:108
  33.4 0.0 collective-permute-start.7
  33.4 0.0 copy-done.4
  33.4 2.3 %convolution_convert_fusion.1 = bf16[128,4096]{1,0:T(8,128)(2,1)} fusion(bf16[16,128]{1,0:T(8,128)(2,1)S(1)} %copy-done.4, bf16[16,4096]{1,0:T(8,128)(2,1)} %get-tuple-element.12), kind=kOutput, calls=%fused_computation.1 | convolution fusion | flops 17301504 | bytes 1183744 | tf_op jit(solution)/shard_map/dot_general | solution.py:176
  35.7 0.0 collective-permute-done.7.theirs_ref
  35.7 0.0 copy-start.5
  35.7 0.6 %copy-done.5 = f32[16,128]{1,0:T(8,128)} copy-done((f32[16,128]{1,0:T(8,128)}, f32[16,128]{1,0:T(8,128)S(1)}, u32[]{:S(2)}) %copy-start.5) | copy-done | bytes 8216
  36.3 1.5 %masked.1 = (bf16[16,128]{1,0:T(8,128)(2,1)}, f32[1,128]{1,0:T(1,128)}) custom-call(f32[16,128]{1,0:T(8,128)} %get-tuple-element.13.raw_ref, f32[16,128]{1,0:T(8,128)} %get-tuple-element.14.mine_ref, f32[16,128]{1,0:T(8,128)} %copy-done.5), custom_call_target="tpu_custom_call" | custom-call | flops 100000 | bytes 32768 | tf_op jit(solution)/shard_map/masked/pallas_call | solution.py:137
  37.8 2.1 %convolution_convert_fusion = bf16[4096,128]{1,0:T(8,128)(2,1)} fusion(bf16[16,4096]{1,0:T(8,128)(2,1)S(1)} %reshape.21, bf16[16,128]{1,0:T(8,128)(2,1)} %get-tuple-element.15), kind=kOutput, calls=%fused_computation | convolution fusion | flops 17301504 | bytes 1183744 | tf_op jit(solution)/shard_map/dot_general | solution.py:180
  (1 shorter events, 0.0 us)
Async XLA Ops:
  4.0 5.5 %copy-start = (bf16[2,4096]{1,0:T(2,128)(2,1)S(1)}, bf16[2,4096]{1,0:T(2,128)(2,1)}, u32[]{:S(2)}) copy-start(bf16[2,4096]{1,0:T(2,128)(2,1)} %subtract_convert_fusion.centered_ref) | copy-start | bytes 49156
  4.0 11.1 %copy-start.1 = (bf16[2,4096]{1,0:T(2,128)(2,1)S(1)}, bf16[2,4096]{1,0:T(2,128)(2,1)}, u32[]{:S(2)}) copy-start(bf16[2,4096]{1,0:T(2,128)(2,1)} %subtract_convert_fusion.centered_ref) | copy-start | bytes 49156
  6.5 5.6 %collective-permute-start = (bf16[16,2048]{1,0:T(8,128)(2,1)}, bf16[16,2048]{1,0:T(8,128)(2,1)S(1)}, u32[]{:S(2)}, u32[]{:S(2)}) collective-permute-start(bf16[16,2048]{1,0:T(8,128)(2,1)} %get-tuple-element.11), channel_id=1, source_target_pairs={{0,2},{2,0},{4,6},{6,4},{8,10},{10,8},{12,14},{14,12},{1,3},{3,1},... | collective-permute-start | bytes 196616 | tf_op jit(solution)/shard_map/ppermute | solution.py:14
  9.4 5.6 %collective-permute-start.4 = (bf16[1,2,4096]{2,1,0:T(2,128)(2,1)S(1)}, bf16[1,2,4096]{2,1,0:T(2,128)(2,1)S(1)}, u32[]{:S(2)}, u32[]{:S(2)}) collective-permute-start(bf16[1,2,4096]{2,1,0:T(2,128)(2,1)S(1)} %bitcast.10), channel_id=1, source_target_pairs={{0,2},{2,0},{4,6},{6,4},{8,10},{10,8},{12,14},{14,12},{1,3},{3,1},... | collective-permute-start | bytes 49160 | tf_op jit(solution)/shard_map/ppermute | solution.py:14
  13.0 4.4 %collective-permute-start.1 = (bf16[16,2048]{1,0:T(8,128)(2,1)S(1)}, bf16[16,2048]{1,0:T(8,128)(2,1)S(1)}, u32[]{:S(2)}, u32[]{:S(2)}) collective-permute-start(bf16[16,2048]{1,0:T(8,128)(2,1)S(1)} %fusion), channel_id=1, source_target_pairs={{0,4},{2,6},{4,0},{6,2},{8,12},{10,14},{12,8},{14,10},{1,5},{3,7},... | collective-permute-start | bytes 196616 | tf_op jit(solution)/shard_map/ppermute | solution.py:14
  15.1 6.2 %collective-permute-start.5 = (bf16[2,2,4096]{2,1,0:T(2,128)(2,1)S(1)}, bf16[2,2,4096]{2,1,0:T(2,128)(2,1)S(1)}, u32[]{:S(2)}, u32[]{:S(2)}) collective-permute-start(bf16[2,2,4096]{2,1,0:T(2,128)(2,1)S(1)} %pad_maximum_fusion.2), channel_id=1, source_target_pairs={{0,4},{2,6},{4,0},{6,2},{8,12},{10,14},{12,8},{14,10},{1,5},{3,7},... | collective-permute-start | bytes 98312 | tf_op jit(solution)/shard_map/ppermute | solution.py:14
  18.3 6.9 %collective-permute-start.2 = (bf16[16,2048]{1,0:T(8,128)(2,1)S(1)}, bf16[16,2048]{1,0:T(8,128)(2,1)S(1)}, u32[]{:S(2)}, u32[]{:S(2)}) collective-permute-start(bf16[16,2048]{1,0:T(8,128)(2,1)S(1)} %fusion.1), channel_id=1, source_target_pairs={{0,8},{2,10},{4,12},{6,14},{8,0},{10,2},{12,4},{14,6},{1,9},{3,11}... | collective-permute-start | bytes 196616 | tf_op jit(solution)/shard_map/ppermute | solution.py:14
  21.4 12.0 %copy-start.4 = (bf16[16,128]{1,0:T(8,128)(2,1)S(1)}, bf16[16,128]{1,0:T(8,128)(2,1)}, u32[]{:S(2)}) copy-start(bf16[16,128]{1,0:T(8,128)(2,1)} %get-tuple-element.10.code_ref) | copy-start | bytes 12292
  21.4 6.3 %collective-permute-start.6 = (bf16[4,2,4096]{2,1,0:T(2,128)(2,1)S(1)}, bf16[4,2,4096]{2,1,0:T(2,128)(2,1)S(1)}, u32[]{:S(2)}, u32[]{:S(2)}) collective-permute-start(bf16[4,2,4096]{2,1,0:T(2,128)(2,1)S(1)} %pad_maximum_fusion.1), channel_id=1, source_target_pairs={{0,8},{2,10},{4,12},{6,14},{8,0},{10,2},{12,4},{14,6},{1,9},{3,11}... | collective-permute-start | bytes 196616 | tf_op jit(solution)/shard_map/ppermute | solution.py:14
  26.1 4.3 %copy-start.2 = (bf16[16,2048]{1,0:T(8,128)(2,1)}, bf16[16,2048]{1,0:T(8,128)(2,1)S(1)}, u32[]{:S(2)}) copy-start(bf16[16,2048]{1,0:T(8,128)(2,1)S(1)} %multiply_convert_fusion.own_ref) | copy-start | bytes 196612
  26.2 4.3 %collective-permute-start.3 = (bf16[16,2048]{1,0:T(8,128)(2,1)S(1)}, bf16[16,2048]{1,0:T(8,128)(2,1)S(1)}, u32[]{:S(2)}, u32[]{:S(2)}) collective-permute-start(bf16[16,2048]{1,0:T(8,128)(2,1)S(1)} %multiply_convert_fusion.own_ref), channel_id=1, source_target_pairs={{0,2},{2,0},{4,6},{6,4},{8,10},{10,8},{12,14},{14,12},{1,3},{3,1},... | collective-permute-start | bytes 196616 | tf_op jit(solution)/shard_map/ppermute | solution.py:14
  30.5 0.6 %copy-start.3 = (bf16[16,2048]{1,0:T(8,128)(2,1)}, bf16[16,2048]{1,0:T(8,128)(2,1)S(1)}, u32[]{:S(2)}) copy-start(bf16[16,2048]{1,0:T(8,128)(2,1)S(1)} %collective-permute-done.3.other_ref) | copy-start | bytes 196612
  33.4 2.3 %collective-permute-start.7 = (f32[16,128]{1,0:T(8,128)}, f32[16,128]{1,0:T(8,128)S(1)}, u32[]{:S(2)}, u32[]{:S(2)}) collective-permute-start(f32[16,128]{1,0:T(8,128)} %get-tuple-element.14.mine_ref), channel_id=1, source_target_pairs={{0,1},{1,0},{2,3},{3,2},{4,5},{5,4},{6,7},{7,6},{8,9},{9,8},{10,11... | collective-permute-start | bytes 24584 | tf_op jit(solution)/shard_map/ppermute | solution.py:14
  35.7 0.6 %copy-start.5 = (f32[16,128]{1,0:T(8,128)}, f32[16,128]{1,0:T(8,128)S(1)}, u32[]{:S(2)}) copy-start(f32[16,128]{1,0:T(8,128)S(1)} %collective-permute-done.7.theirs_ref) | copy-start | bytes 24580

commit v4 on v3

--- a/solution.py
+++ b/solution.py
@@ -8,6 +8,7 @@
 from jax.sharding import PartitionSpec as P
 
 VMEM = pl.BlockSpec(memory_space=pltpu.VMEM)
+PARAMS = pltpu.CompilerParams(vmem_limit_bytes=16 * 2**20)
 
 
 def swapped(shard, axis, distance):
@@ -65,6 +66,7 @@
         ),
         in_specs=[VMEM] * 6,
         out_specs=(VMEM,) * 3,
+        compiler_params=PARAMS,
         cost_estimate=pl.CostEstimate(flops=10**6, bytes_accessed=2**20, transcendentals=0),
         name="codes",
     )(top_idx, pre_codes, blocks.reshape(1, 1), counts.reshape(1, 1), dict_rows, centered_own)
@@ -82,6 +84,7 @@
         out_shape=jax.ShapeDtypeStruct((code.shape[0], half), jnp.float32),
         in_specs=[VMEM] * 3,
         out_specs=VMEM,
+        compiler_params=PARAMS,
         cost_estimate=pl.CostEstimate(flops=10**6, bytes_accessed=2**19, transcendentals=0),
         name="own_part",
     )(code, dict_rows, centered_own)
@@ -113,6 +116,7 @@
         ),
         in_specs=[VMEM] * 3,
         out_specs=(VMEM, VMEM),
+        compiler_params=PARAMS,
         cost_estimate=pl.CostEstimate(flops=10**6, bytes_accessed=2**20, transcendentals=0),
         name="code_half",
     )(scaled_own, scaled_other, dict_rows)
@@ -142,6 +146,7 @@
         ),
         in_specs=[VMEM] * 3,
         out_specs=(VMEM, VMEM),
+        compiler_params=PARAMS,
         cost_estimate=pl.CostEstimate(flops=10**5, bytes_accessed=2**15, transcendentals=0),
         name="masked",
     )(raw, mine, theirs)

time: 40.5 us -> 32 us (0.79)
  Pallas kernels: 8.34 us -> 1.68 us
  other arithmetic: 5.15 us -> 1.84 us
  starting transfers between devices: 10.3 us -> 12.1 us
  matrix products: 4.47 us -> 2.9 us
  local copies, waits for them, and re-layouts: 1.29 us -> 2.67 us
    pallas_call x1, Pallas kernels: 2.52 us -> 0.6 us  [codes(): pl.pallas_call(codes_kernel, out_shape=(jax.ShapeDtypeStruct((tokens, slo...]
    pallas_call x1, Pallas kernels: 2.29 us -> 0.37 us  [code_half_of(): pl.pallas_call(code_half_kernel, out_shape=(jax.ShapeDtypeStruct((tokens,...]
    pallas_call x1, Pallas kernels: 2.07 us -> 0.18 us  [own_part(): pl.pallas_call(own_kernel, out_shape=jax.ShapeDtypeStruct((code.shape[0],...]
    convert_element_type x2, other arithmetic: 1.85 us -> 0.04 us  [local(): total.astype(jnp.bfloat16)]
    ppermute x8, starting transfers between devices: 10.3 us -> 12.1 us  [swapped(): lax.ppermute(shard, axis, [(i, i ^ distance) for i in range(lax.axis_size...]
    unnamed x12 -> x8, local copies, waits for them, and re-layouts: 1.24 us -> 2.62 us
    pallas_call x1, Pallas kernels: 1.46 us -> 0.52 us  [masked(): pl.pallas_call(functools.partial(masked_kernel, rows), out_shape=(jax.Sha...]
    convert_element_type x1, other arithmetic: 0.94 us -> 0.04 us  [local(): scaled_own = (0.25 * total).astype(jnp.bfloat16)]
  transfers between devices with their start and end apart: 8 -> 8, of which waited for: 4 -> 5; matrix products, arithmetic and copies ran while one was open for 14% -> 6% of each run, Pallas kernels for 5% -> 1%
where the time goes in v4:
time: 32 us; the launch traced here: 31.5 us
  starting transfers between devices  12.1 us (38%)
  waiting for transfers between devices  8.4 us (26%)
  matrix products  2.9 us (9%)
  local copies, waits for them, and re-layouts  2.67 us (8%)
  between operations  1.98 us (6%)
  other arithmetic  1.84 us (6%)
  Pallas kernels  1.68 us (5%)
    ppermute x8, starting transfers between devices, swapped(): lax.ppermute(shard, axis, [(i, i ^ distance) for i in range(lax.axis_size...  12.1 us
    ppermute x8, waiting for transfers between devices, swapped(): lax.ppermute(shard, axis, [(i, i ^ distance) for i in range(lax.axis_size...  8.4 us
    unnamed x8, local copies, waits for them, and re-layouts  2.62 us
    dot_general x1, matrix products, local(): lax.dot_general(centered, pre_grad, (((0,), (0,)), ((), ())), preferred_e...  1.45 us
    dot_general x1, matrix products, local(): lax.dot_general(code, scaled, (((0,), (0,)), ((), ())), preferred_element...  1.45 us
    convert_element_type x1, other arithmetic, local(): (tokens.astype(jnp.float32) - b_pre.astype(jnp.float32)).astype(jnp.bfloa...  0.74 us
    convert_element_type x1, other arithmetic, local(): b_pre.astype(jnp.float32)  0.7 us
  transfers between devices with their start and end apart: 8, of which 5 were waited for; matrix products, arithmetic and copies ran while one was open for 6% of the time, Pallas kernels for 1%

profile of v4, /device:TPU:0, one launch (start us, length us, event | category | flops | bytes accessed | tf_op | source)
XLA Modules:
  0.0 31.5 jit_solution(5629810411362927533)
XLA Ops:
  1.9 0.7 %convert_element_type.34 = f32[4096]{0:T(1024)S(1)} convert(bf16[4096]{0:T(1024)(128)(2,1)} %param.8) | non-fusion elementwise | flops 4096 | bytes 24576 | tf_op jit(solution)/shard_map/convert_element_type | solution.py:159
  2.6 0.7 %subtract_convert_fusion.centered_ref = bf16[2,4096]{1,0:T(2,128)(2,1)S(1)} fusion(bf16[2,4096]{1,0:T(2,128)(2,1)} %param.7, f32[4096]{0:T(1024)S(1)} %convert_element_type.34), kind=kLoop, calls=%fused_computation.10 | loop fusion | flops 24576 | bytes 49152 | tf_op jit(solution)/shard_map/convert_element_type | solution.py:159
  3.4 0.0 copy-start
  3.4 1.2 %copy-done = bf16[128,4096]{1,0:T(8,128)(2,1)S(1)} copy-done((bf16[128,4096]{1,0:T(8,128)(2,1)S(1)}, bf16[128,4096]{1,0:T(8,128)(2,1)}, u32[]{:S(2)}) %copy-start) | copy-done | bytes 1048600
  4.6 0.0 copy-start.2
  4.6 0.7 %copy-done.2 = s32[16,64]{1,0:T(8,128)S(1)} copy-done((s32[16,64]{1,0:T(8,128)S(1)}, s32[16,64]{1,0:T(8,128)}, u32[]{:S(2)}) %copy-start.2) | copy-done | bytes 4120
  5.3 0.0 copy-start.3
  5.3 0.7 %copy-done.3 = f32[16,64]{1,0:T(8,128)S(1)} copy-done((f32[16,64]{1,0:T(8,128)S(1)}, f32[16,64]{1,0:T(8,128)}, u32[]{:S(2)}) %copy-start.3) | copy-done | bytes 4120
  6.0 0.0 copy-start.1
  6.0 0.6 %codes.1 = (bf16[16,128]{1,0:T(8,128)(2,1)S(1)}, f32[16,128]{1,0:T(8,128)S(1)}, bf16[16,2048]{1,0:T(8,128)(2,1)S(1)}) custom-call(s32[16,64]{1,0:T(8,128)S(1)} %copy-done.2, f32[16,64]{1,0:T(8,128)S(1)} %copy-done.3, s32[1,1]{1,0:T(1,128)} %bitcast.8.block_ref, s32[1,1]{1,0:T(1,128)} %bitcast.9.count_ref, bf16[128,4096]{1,0:T(8,128)(2,1)S(1)} %copy-done, ...), custom_call_target="tpu_custom_call" | custom-call | flops 1000000 | bytes 1048576 | tf_op jit(solution)/shard_map/codes/pallas_call | solution.py:60
  6.6 3.0 %collective-permute-start = (bf16[16,2048]{1,0:T(8,128)(2,1)S(1)}, bf16[16,2048]{1,0:T(8,128)(2,1)S(1)}, u32[]{:S(2)}, u32[]{:S(2)}) collective-permute-start(bf16[16,2048]{1,0:T(8,128)(2,1)S(1)} %get-tuple-element.11), channel_id=1, source_target_pairs={{0,2},{2,0},{4,6},{6,4},{8,10},{10,8},{12,14},{14,12},{1,3},{3,1},... | collective-permute-start | bytes 196616 | tf_op jit(solution)/shard_map/ppermute | solution.py:15
  9.6 0.1 collective-permute-start.4
  9.7 0.0 copy-done.1
  9.7 0.2 own_part.1
  9.9 2.1 %collective-permute-done = bf16[16,2048]{1,0:T(8,128)(2,1)S(1)} collective-permute-done((bf16[16,2048]{1,0:T(8,128)(2,1)S(1)}, bf16[16,2048]{1,0:T(8,128)(2,1)S(1)}, u32[]{:S(2)}, u32[]{:S(2)}) %collective-permute-start) | collective-permute-done | bytes 65568 | tf_op jit(solution)/shard_map/ppermute | solution.py:15
  12.0 2.2 %collective-permute-start.1 = (bf16[16,2048]{1,0:T(8,128)(2,1)S(1)}, bf16[16,2048]{1,0:T(8,128)(2,1)S(1)}, u32[]{:S(2)}, u32[]{:S(2)}) collective-permute-start(bf16[16,2048]{1,0:T(8,128)(2,1)S(1)} %fusion), channel_id=1, source_target_pairs={{0,4},{2,6},{4,0},{6,2},{8,12},{10,14},{12,8},{14,10},{1,5},{3,7},... | collective-permute-start | bytes 196616 | tf_op jit(solution)/shard_map/ppermute | solution.py:15
  14.2 0.0 collective-permute-done.4
  14.3 0.8 %collective-permute-start.5 = (bf16[2,2,4096]{2,1,0:T(2,128)(2,1)S(1)}, bf16[2,2,4096]{2,1,0:T(2,128)(2,1)S(1)}, u32[]{:S(2)}, u32[]{:S(2)}) collective-permute-start(bf16[2,2,4096]{2,1,0:T(2,128)(2,1)S(1)} %pad_maximum_fusion.2), channel_id=1, source_target_pairs={{0,4},{2,6},{4,0},{6,2},{8,12},{10,14},{12,8},{14,10},{1,5},{3,7},... | collective-permute-start | bytes 98312 | tf_op jit(solution)/shard_map/ppermute | solution.py:15
  15.0 1.4 %collective-permute-done.1 = bf16[16,2048]{1,0:T(8,128)(2,1)S(1)} collective-permute-done((bf16[16,2048]{1,0:T(8,128)(2,1)S(1)}, bf16[16,2048]{1,0:T(8,128)(2,1)S(1)}, u32[]{:S(2)}, u32[]{:S(2)}) %collective-permute-start.1) | collective-permute-done | bytes 65568 | tf_op jit(solution)/shard_map/ppermute | solution.py:15
  16.5 3.2 %collective-permute-start.2 = (bf16[16,2048]{1,0:T(8,128)(2,1)S(1)}, bf16[16,2048]{1,0:T(8,128)(2,1)S(1)}, u32[]{:S(2)}, u32[]{:S(2)}) collective-permute-start(bf16[16,2048]{1,0:T(8,128)(2,1)S(1)} %fusion.1), channel_id=1, source_target_pairs={{0,8},{2,10},{4,12},{6,14},{8,0},{10,2},{12,4},{14,6},{1,9},{3,11}... | collective-permute-start | bytes 196616 | tf_op jit(solution)/shard_map/ppermute | solution.py:15
  19.7 0.0 collective-permute-done.5
  19.7 0.1 pad_maximum_fusion.1
  19.8 1.2 %collective-permute-start.6 = (bf16[4,2,4096]{2,1,0:T(2,128)(2,1)S(1)}, bf16[4,2,4096]{2,1,0:T(2,128)(2,1)S(1)}, u32[]{:S(2)}, u32[]{:S(2)}) collective-permute-start(bf16[4,2,4096]{2,1,0:T(2,128)(2,1)S(1)} %pad_maximum_fusion.1), channel_id=1, source_target_pairs={{0,8},{2,10},{4,12},{6,14},{8,0},{10,2},{12,4},{14,6},{1,9},{3,11}... | collective-permute-start | bytes 196616 | tf_op jit(solution)/shard_map/ppermute | solution.py:15
  21.0 2.4 %collective-permute-done.2 = bf16[16,2048]{1,0:T(8,128)(2,1)S(1)} collective-permute-done((bf16[16,2048]{1,0:T(8,128)(2,1)S(1)}, bf16[16,2048]{1,0:T(8,128)(2,1)S(1)}, u32[]{:S(2)}, u32[]{:S(2)}) %collective-permute-start.2) | collective-permute-done | bytes 65568 | tf_op jit(solution)/shard_map/ppermute | solution.py:15
  23.4 1.6 %collective-permute-start.3 = (bf16[16,2048]{1,0:T(8,128)(2,1)S(1)}, bf16[16,2048]{1,0:T(8,128)(2,1)S(1)}, u32[]{:S(2)}, u32[]{:S(2)}) collective-permute-start(bf16[16,2048]{1,0:T(8,128)(2,1)S(1)} %multiply_convert_fusion.own_ref), channel_id=1, source_target_pairs={{0,2},{2,0},{4,6},{6,4},{8,10},{10,8},{12,14},{14,12},{1,3},{3,1},... | collective-permute-start | bytes 196616 | tf_op jit(solution)/shard_map/ppermute | solution.py:15
  25.0 0.1 collective-permute-done.6
  25.0 0.2 pad_maximum_fusion
  25.2 0.1 reshape.21
  25.3 2.4 %collective-permute-done.3.other_ref = bf16[16,2048]{1,0:T(8,128)(2,1)S(1)} collective-permute-done((bf16[16,2048]{1,0:T(8,128)(2,1)S(1)}, bf16[16,2048]{1,0:T(8,128)(2,1)S(1)}, u32[]{:S(2)}, u32[]{:S(2)}) %collective-permute-start.3) | collective-permute-done | bytes 65568 | tf_op jit(solution)/shard_map/ppermute | solution.py:15
  27.7 0.4 %code_half.1 = (f32[16,128]{1,0:T(8,128)S(1)}, bf16[16,4096]{1,0:T(8,128)(2,1)S(1)}) custom-call(bf16[16,2048]{1,0:T(8,128)(2,1)S(1)} %multiply_convert_fusion.own_ref, bf16[16,2048]{1,0:T(8,128)(2,1)S(1)} %collective-permute-done.3.other_ref, bf16[128,4096]{1,0:T(8,128)(2,1)S(1)} %copy-done.1), custom_call_target="tpu_custom_call" | custom-call | flops 1000000 | bytes 1048576 | tf_op jit(solution)/shard_map/code_half/pallas_call | solution.py:111
  28.1 0.0 collective-permute-start.7
  28.1 1.4 %convolution_convert_fusion.1 = bf16[128,4096]{1,0:T(8,128)(2,1)} fusion(bf16[16,128]{1,0:T(8,128)(2,1)S(1)} %get-tuple-element.10.code_ref, bf16[16,4096]{1,0:T(8,128)(2,1)S(1)} %get-tuple-element.12), kind=kOutput, calls=%fused_computation.1 | convolution fusion | flops 17301504 | bytes 1183744 | tf_op jit(solution)/shard_map/dot_general | solution.py:181
  29.5 0.0 collective-permute-done.7.theirs_ref
  29.5 0.5 %masked.1 = (bf16[16,128]{1,0:T(8,128)(2,1)S(1)}, f32[1,128]{1,0:T(1,128)}) custom-call(f32[16,128]{1,0:T(8,128)S(1)} %get-tuple-element.13.raw_ref, f32[16,128]{1,0:T(8,128)S(1)} %get-tuple-element.14.mine_ref, f32[16,128]{1,0:T(8,128)S(1)} %collective-permute-done.7.theirs_ref), custom_call_target="tpu_custom_call" | custom-call | flops 100000 | bytes 32768 | tf_op jit(solution)/shard_map/masked/pallas_call | solution.py:141
  30.1 1.5 %convolution_convert_fusion = bf16[4096,128]{1,0:T(8,128)(2,1)} fusion(bf16[16,4096]{1,0:T(8,128)(2,1)S(1)} %reshape.21, bf16[16,128]{1,0:T(8,128)(2,1)S(1)} %get-tuple-element.15), kind=kOutput, calls=%fused_computation | convolution fusion | flops 17301504 | bytes 1183744 | tf_op jit(solution)/shard_map/dot_general | solution.py:185
  (4 shorter events, 0.1 us)
Async XLA Ops:
  3.4 1.2 %copy-start = (bf16[128,4096]{1,0:T(8,128)(2,1)S(1)}, bf16[128,4096]{1,0:T(8,128)(2,1)}, u32[]{:S(2)}) copy-start(bf16[128,4096]{1,0:T(8,128)(2,1)} %rows_ref.5) | copy-start | bytes 3145732
  4.6 0.7 %copy-start.2 = (s32[16,64]{1,0:T(8,128)S(1)}, s32[16,64]{1,0:T(8,128)}, u32[]{:S(2)}) copy-start(s32[16,64]{1,0:T(8,128)} %top_ref.1) | copy-start | bytes 12292
  5.3 0.7 %copy-start.3 = (f32[16,64]{1,0:T(8,128)S(1)}, f32[16,64]{1,0:T(8,128)}, u32[]{:S(2)}) copy-start(f32[16,64]{1,0:T(8,128)} %pre_ref.1) | copy-start | bytes 12292
  6.0 3.7 %copy-start.1 = (bf16[128,4096]{1,0:T(8,128)(2,1)S(1)}, bf16[128,4096]{1,0:T(8,128)(2,1)}, u32[]{:S(2)}) copy-start(bf16[128,4096]{1,0:T(8,128)(2,1)} %rows_ref.5) | copy-start | bytes 3145732
  6.6 5.4 %collective-permute-start = (bf16[16,2048]{1,0:T(8,128)(2,1)S(1)}, bf16[16,2048]{1,0:T(8,128)(2,1)S(1)}, u32[]{:S(2)}, u32[]{:S(2)}) collective-permute-start(bf16[16,2048]{1,0:T(8,128)(2,1)S(1)} %get-tuple-element.11), channel_id=1, source_target_pairs={{0,2},{2,0},{4,6},{6,4},{8,10},{10,8},{12,14},{14,12},{1,3},{3,1},... | collective-permute-start | bytes 196616 | tf_op jit(solution)/shard_map/ppermute | solution.py:15
  9.6 4.6 %collective-permute-start.4 = (bf16[1,2,4096]{2,1,0:T(2,128)(2,1)S(1)}, bf16[1,2,4096]{2,1,0:T(2,128)(2,1)S(1)}, u32[]{:S(2)}, u32[]{:S(2)}) collective-permute-start(bf16[1,2,4096]{2,1,0:T(2,128)(2,1)S(1)} %bitcast.10), channel_id=1, source_target_pairs={{0,2},{2,0},{4,6},{6,4},{8,10},{10,8},{12,14},{14,12},{1,3},{3,1},... | collective-permute-start | bytes 49160 | tf_op jit(solution)/shard_map/ppermute | solution.py:15
  12.0 4.4 %collective-permute-start.1 = (bf16[16,2048]{1,0:T(8,128)(2,1)S(1)}, bf16[16,2048]{1,0:T(8,128)(2,1)S(1)}, u32[]{:S(2)}, u32[]{:S(2)}) collective-permute-start(bf16[16,2048]{1,0:T(8,128)(2,1)S(1)} %fusion), channel_id=1, source_target_pairs={{0,4},{2,6},{4,0},{6,2},{8,12},{10,14},{12,8},{14,10},{1,5},{3,7},... | collective-permute-start | bytes 196616 | tf_op jit(solution)/shard_map/ppermute | solution.py:15
  14.3 5.4 %collective-permute-start.5 = (bf16[2,2,4096]{2,1,0:T(2,128)(2,1)S(1)}, bf16[2,2,4096]{2,1,0:T(2,128)(2,1)S(1)}, u32[]{:S(2)}, u32[]{:S(2)}) collective-permute-start(bf16[2,2,4096]{2,1,0:T(2,128)(2,1)S(1)} %pad_maximum_fusion.2), channel_id=1, source_target_pairs={{0,4},{2,6},{4,0},{6,2},{8,12},{10,14},{12,8},{14,10},{1,5},{3,7},... | collective-permute-start | bytes 98312 | tf_op jit(solution)/shard_map/ppermute | solution.py:15
  16.5 6.9 %collective-permute-start.2 = (bf16[16,2048]{1,0:T(8,128)(2,1)S(1)}, bf16[16,2048]{1,0:T(8,128)(2,1)S(1)}, u32[]{:S(2)}, u32[]{:S(2)}) collective-permute-start(bf16[16,2048]{1,0:T(8,128)(2,1)S(1)} %fusion.1), channel_id=1, source_target_pairs={{0,8},{2,10},{4,12},{6,14},{8,0},{10,2},{12,4},{14,6},{1,9},{3,11}... | collective-permute-start | bytes 196616 | tf_op jit(solution)/shard_map/ppermute | solution.py:15
  19.8 5.2 %collective-permute-start.6 = (bf16[4,2,4096]{2,1,0:T(2,128)(2,1)S(1)}, bf16[4,2,4096]{2,1,0:T(2,128)(2,1)S(1)}, u32[]{:S(2)}, u32[]{:S(2)}) collective-permute-start(bf16[4,2,4096]{2,1,0:T(2,128)(2,1)S(1)} %pad_maximum_fusion.1), channel_id=1, source_target_pairs={{0,8},{2,10},{4,12},{6,14},{8,0},{10,2},{12,4},{14,6},{1,9},{3,11}... | collective-permute-start | bytes 196616 | tf_op jit(solution)/shard_map/ppermute | solution.py:15
  23.4 4.3 %collective-permute-start.3 = (bf16[16,2048]{1,0:T(8,128)(2,1)S(1)}, bf16[16,2048]{1,0:T(8,128)(2,1)S(1)}, u32[]{:S(2)}, u32[]{:S(2)}) collective-permute-start(bf16[16,2048]{1,0:T(8,128)(2,1)S(1)} %multiply_convert_fusion.own_ref), channel_id=1, source_target_pairs={{0,2},{2,0},{4,6},{6,4},{8,10},{10,8},{12,14},{14,12},{1,3},{3,1},... | collective-permute-start | bytes 196616 | tf_op jit(solution)/shard_map/ppermute | solution.py:15
  28.1 1.5 %collective-permute-start.7 = (f32[16,128]{1,0:T(8,128)S(1)}, f32[16,128]{1,0:T(8,128)S(1)}, u32[]{:S(2)}, u32[]{:S(2)}) collective-permute-start(f32[16,128]{1,0:T(8,128)S(1)} %get-tuple-element.14.mine_ref), channel_id=1, source_target_pairs={{0,1},{1,0},{2,3},{3,2},{4,5},{5,4},{6,7},{7,6},{8,9},{9,8},{10,11... | collective-permute-start | bytes 24584 | tf_op jit(solution)/shard_map/ppermute | solution.py:15

commit v5 on v4

--- a/solution.py
+++ b/solution.py
@@ -8,16 +8,36 @@
 from jax.sharding import PartitionSpec as P
 
 VMEM = pl.BlockSpec(memory_space=pltpu.VMEM)
+SMEM = pl.BlockSpec(memory_space=pltpu.SMEM)
+HBM = pl.BlockSpec(memory_space=pltpu.HBM)
 PARAMS = pltpu.CompilerParams(vmem_limit_bytes=16 * 2**20)
 
 
-def swapped(shard, axis, distance):
-    return lax.ppermute(shard, axis, [(i, i ^ distance) for i in range(lax.axis_size(axis))])
+def feat_bits():
+    return (lax.axis_size("feat") - 1).bit_length()
+
+
+def sum_bit(step, core):
+    return (step + core) % feat_bits()
+
+
+def token_bit(step, core):
+    return (feat_bits() - 1 - step + core) % feat_bits()
+
+
+def swapped(shard, bit_of):
+    cores = lax.axis_size("tok")
+    pairs = [
+        (f * cores + c, (f ^ 1 << bit_of(c)) * cores + c)
+        for f in range(lax.axis_size("feat"))
+        for c in range(cores)
+    ]
+    return lax.ppermute(shard, ("feat", "tok"), pairs)
 
 
 def halves(width):
     half = width // 2
-    bit = lax.axis_index("feat") & 1
+    bit = lax.axis_index("feat") >> (lax.axis_index("tok") % feat_bits()) & 1
     return (
         pl.multiple_of(bit * half, half),
         pl.multiple_of((1 - bit) * half, half),
@@ -25,10 +45,11 @@
     )
 
 
-def share(code, rows_ref, centered_ref, at, half):
+def share(code, rows_ref, tokens_ref, bias_ref, at, half):
     total = jnp.dot(code, rows_ref[:, pl.ds(at, half)], preferred_element_type=jnp.float32)
-    rows = centered_ref.shape[0]
-    centered = centered_ref[:, pl.ds(at, half)].astype(jnp.float32)
+    rows = tokens_ref.shape[0]
+    centered = tokens_ref[:, pl.ds(at, half)].astype(jnp.float32) - bias_ref[:, pl.ds(at, half)]
+    centered = centered.astype(jnp.bfloat16).astype(jnp.float32)
     token = lax.broadcasted_iota(jnp.int32, (total.shape[0], 1), 0)
     first = lax.axis_index("feat") * rows
     for i in range(rows):
@@ -36,13 +57,45 @@
     return total
 
 
-def codes_kernel(
-    top_ref, pre_ref, block_ref, count_ref, rows_ref, centered_ref, code_ref, raw_ref, send_ref
+def front_kernel(
+    tokens_hbm,
+    bias_hbm,
+    pre_hbm,
+    top_hbm,
+    rows_hbm,
+    block_ref,
+    count_ref,
+    code_ref,
+    raw_ref,
+    send_ref,
+    rows_ref,
+    bias_ref,
+    tokens_ref,
+    bias_flat,
+    pre_ref,
+    top_ref,
+    sems,
 ):
+    copies = [
+        pltpu.make_async_copy(source, target, sems.at[i])
+        for i, (source, target) in enumerate(
+            (
+                (top_hbm, top_ref),
+                (pre_hbm, pre_ref),
+                (rows_hbm, rows_ref),
+                (tokens_hbm, tokens_ref),
+                (bias_hbm, bias_flat),
+            )
+        )
+    ]
+    for copy in copies:
+        copy.start()
+    for copy in copies[:2]:
+        copy.wait()
     tokens, latents = top_ref.shape
     slots, width = rows_ref.shape
     offsets = lax.broadcasted_iota(jnp.int32, (1, slots), 1)
-    slot_ids = jnp.where(offsets < count_ref[...], block_ref[...] * slots + offsets, -1)
+    slot_ids = jnp.where(offsets < count_ref[0], block_ref[0] * slots + offsets, -1)
     top, pre = top_ref[...], pre_ref[...]
     raw = jnp.zeros((tokens, slots), jnp.float32)
     for k in range(latents):
@@ -50,44 +103,63 @@
     raw_ref[...] = raw
     code = jnp.maximum(raw, 0.0).astype(jnp.bfloat16)
     code_ref[...] = code
+    for copy in copies[2:]:
+        copy.wait()
+    bias_ref[...] = bias_flat[...].astype(jnp.float32).reshape(1, width)
     _, other, half = halves(width)
-    send_ref[...] = share(code, rows_ref, centered_ref, other, half).astype(jnp.bfloat16)
-
-
-def codes(top_idx, pre_codes, blocks, counts, dict_rows, centered_own):
-    tokens = top_idx.shape[0]
+    send_ref[...] = share(code, rows_ref, tokens_ref, bias_ref, other, half).astype(jnp.bfloat16)
+
+
+def front(tokens, b_pre, pre_codes, top_idx, blocks, counts, dict_rows):
+    count = top_idx.shape[0]
     slots, width = dict_rows.shape
     return pl.pallas_call(
-        codes_kernel,
+        front_kernel,
         out_shape=(
-            jax.ShapeDtypeStruct((tokens, slots), jnp.bfloat16),
-            jax.ShapeDtypeStruct((tokens, slots), jnp.float32),
-            jax.ShapeDtypeStruct((tokens, width // 2), jnp.bfloat16),
-        ),
-        in_specs=[VMEM] * 6,
-        out_specs=(VMEM,) * 3,
+            jax.ShapeDtypeStruct((count, slots), jnp.bfloat16),
+            jax.ShapeDtypeStruct((count, slots), jnp.float32),
+            jax.ShapeDtypeStruct((count, width // 2), jnp.bfloat16),
+            jax.ShapeDtypeStruct(dict_rows.shape, jnp.bfloat16),
+            jax.ShapeDtypeStruct((1, width), jnp.float32),
+        ),
+        in_specs=[HBM] * 5 + [SMEM] * 2,
+        out_specs=(VMEM,) * 5,
+        scratch_shapes=[
+            pltpu.VMEM(tokens.shape, tokens.dtype),
+            pltpu.VMEM(b_pre.shape, b_pre.dtype),
+            pltpu.VMEM(pre_codes.shape, pre_codes.dtype),
+            pltpu.VMEM(top_idx.shape, top_idx.dtype),
+            pltpu.SemaphoreType.DMA((5,)),
+        ],
         compiler_params=PARAMS,
         cost_estimate=pl.CostEstimate(flops=10**6, bytes_accessed=2**20, transcendentals=0),
-        name="codes",
-    )(top_idx, pre_codes, blocks.reshape(1, 1), counts.reshape(1, 1), dict_rows, centered_own)
-
-
-def own_kernel(code_ref, rows_ref, centered_ref, total_ref):
+        name="front",
+    )(
+        *(
+            pltpu.with_memory_space_constraint(array, pltpu.HBM)
+            for array in (tokens, b_pre, pre_codes, top_idx, dict_rows)
+        ),
+        blocks,
+        counts,
+    )
+
+
+def own_kernel(code_ref, rows_ref, tokens_ref, bias_ref, total_ref):
     own, _, half = halves(rows_ref.shape[1])
-    total_ref[...] = share(code_ref[...], rows_ref, centered_ref, own, half)
-
-
-def own_part(code, dict_rows, centered_own):
+    total_ref[...] = share(code_ref[...], rows_ref, tokens_ref, bias_ref, own, half)
+
+
+def own_part(code, dict_rows, tokens, bias):
     half = dict_rows.shape[1] // 2
     return pl.pallas_call(
         own_kernel,
         out_shape=jax.ShapeDtypeStruct((code.shape[0], half), jnp.float32),
-        in_specs=[VMEM] * 3,
+        in_specs=[VMEM] * 4,
         out_specs=VMEM,
         compiler_params=PARAMS,
         cost_estimate=pl.CostEstimate(flops=10**6, bytes_accessed=2**19, transcendentals=0),
         name="own_part",
-    )(code, dict_rows, centered_own)
+    )(code, dict_rows, tokens, bias)
 
 
 def code_half_kernel(own_ref, other_ref, rows_ref, half_ref, scaled_ref):
@@ -129,8 +201,13 @@
     benc_ref[...] = jnp.sum(pre_grad.astype(jnp.float32), axis=0, keepdims=True)
     place = lax.broadcasted_iota(jnp.int32, (tokens, tokens), 0)
     token = lax.broadcasted_iota(jnp.int32, (tokens, tokens), 1)
-    first = lax.axis_index("feat") * rows
-    order = jnp.where(token == (place ^ first), 1.0, 0.0).astype(jnp.bfloat16)
+    core = lax.axis_index("tok")
+    block = place // rows
+    distance = jnp.zeros_like(place)
+    for step in range(feat_bits()):
+        distance |= (block >> step & 1) << token_bit(step, core)
+    source = (lax.axis_index("feat") ^ distance) * rows + place % rows
+    order = jnp.where(token == source, 1.0, 0.0).astype(jnp.bfloat16)
     grad_ref[...] = jnp.dot(order, pre_grad, preferred_element_type=jnp.float32).astype(
         jnp.bfloat16
     )
@@ -153,31 +230,28 @@
 
 
 def local(tokens, b_pre, pre_codes, top_idx, blocks, counts, dict_rows):
-    size = lax.axis_size("feat")
     rows, width = tokens.shape
-    centered_own = lax.optimization_barrier(
-        (tokens.astype(jnp.float32) - b_pre.astype(jnp.float32)).astype(jnp.bfloat16)
-    )
-    code, raw, send = codes(top_idx, pre_codes, blocks, counts, dict_rows, centered_own)
-
-    arrived = swapped(send, "feat", 1)
-    total = own_part(code, dict_rows, centered_own) + arrived.astype(jnp.float32)
-    distance = 2
-    while distance < size:
-        total = total + swapped(total.astype(jnp.bfloat16), "feat", distance).astype(jnp.float32)
-        distance *= 2
+    gathered = tokens[None]
+    for step in range(feat_bits()):
+        arrived = swapped(gathered, functools.partial(token_bit, step))
+        gathered = jnp.concatenate([gathered, arrived], axis=0)
+
+    code, raw, send, dict_rows, bias = front(
+        tokens, b_pre, pre_codes, top_idx, blocks, counts, dict_rows
+    )
+    arrived = swapped(send, functools.partial(sum_bit, 0))
+    total = own_part(code, dict_rows, tokens, bias) + arrived.astype(jnp.float32)
+    for step in range(1, feat_bits()):
+        arrived = swapped(total.astype(jnp.bfloat16), functools.partial(sum_bit, step))
+        total = total + arrived.astype(jnp.float32)
     scaled_own = (0.25 * total).astype(jnp.bfloat16)
-    scaled_other = swapped(scaled_own, "feat", 1)
-
-    centered = centered_own[None]
-    distance = 1
-    while distance < size:
-        centered = jnp.concatenate([centered, swapped(centered, "feat", distance)], axis=0)
-        distance *= 2
-    centered = centered.reshape(size * rows, width)
+    scaled_other = swapped(scaled_own, functools.partial(sum_bit, 0))
+
+    centered = gathered.reshape(-1, width).astype(jnp.float32) - bias
+    centered = lax.optimization_barrier(centered.astype(jnp.bfloat16))
 
     code_half, scaled = code_half_of(scaled_own, scaled_other, dict_rows)
-    theirs = swapped(code_half, "tok", 1)
+    theirs = lax.ppermute(code_half, "tok", [(i, 1 - i) for i in range(2)])
     grad_rows = lax.dot_general(
         code, scaled, (((0,), (0,)), ((), ())), preferred_element_type=jnp.float32
     ).astype(jnp.bfloat16)

time: 32 us -> 30 us (0.938)
  local copies, waits for them, and re-layouts: 2.67 us -> 0.19 us
  other arithmetic: 1.84 us -> 0.42 us
  Pallas kernels: 1.68 us -> 2.61 us
  starting transfers between devices: 12.1 us -> 12.7 us
  waiting for transfers between devices: 8.4 us -> 8.89 us
    unnamed x8 -> x2, local copies, waits for them, and re-layouts: 2.62 us -> 0.01 us
    convert_element_type x2, other arithmetic: 1.44 us -> 0.18 us  [the longest x1 0.16 us: local(): centered = gathered.reshape(-1, width).astype(jnp.float32) - bias]
    pallas_call x1, Pallas kernels: 0.6 us -> 1.52 us  [front(): pl.pallas_call(front_kernel, out_shape=(jax.ShapeDtypeStruct((count, slot...]
    ppermute x8, starting transfers between devices: 12.1 us -> 12.7 us  [the longest x7 12.7 us: swapped(): return lax.ppermute(shard, ('feat', 'tok'), pairs)]
    ppermute x8, waiting for transfers between devices: 8.4 us -> 8.89 us  [the longest x7 8.89 us: swapped(): return lax.ppermute(shard, ('feat', 'tok'), pairs)]
  transfers between devices with their start and end apart: 8 -> 8, of which waited for: 5 -> 5; matrix products, arithmetic and copies ran while one was open for 6% -> 7% of each run, Pallas kernels for 1% -> 6%
where the time goes in v5:
time: 30 us; the launch traced here: 29.7 us
  starting transfers between devices  12.7 us (42%)
  waiting for transfers between devices  8.89 us (30%)
  matrix products  2.9 us (10%)
  Pallas kernels  2.61 us (9%)
  between operations  1.99 us (7%)
  other arithmetic  0.42 us (1%)
    ppermute x7, starting transfers between devices, swapped(): return lax.ppermute(shard, ('feat', 'tok'), pairs)  12.7 us
    ppermute x7, waiting for transfers between devices, swapped(): return lax.ppermute(shard, ('feat', 'tok'), pairs)  8.89 us
    pallas_call x1, Pallas kernels, front(): pl.pallas_call(front_kernel, out_shape=(jax.ShapeDtypeStruct((count, slot...  1.52 us
    dot_general x1, matrix products, local(): lax.dot_general(centered, pre_grad, (((0,), (0,)), ((), ())), preferred_e...  1.45 us
    dot_general x1, matrix products, local(): lax.dot_general(code, scaled, (((0,), (0,)), ((), ())), preferred_element...  1.45 us
  transfers between devices with their start and end apart: 8, of which 5 were waited for; matrix products, arithmetic and copies ran while one was open for 7% of the time, Pallas kernels for 6%

profile of v5, /device:TPU:0, one launch (start us, length us, event | category | flops | bytes accessed | tf_op | source)
XLA Modules:
  0.0 29.7 jit_solution(2942811669272518736)
XLA Ops:
  0.6 0.0 copy-start
  0.6 4.1 %collective-permute-start.4 = (bf16[1,2,4096]{2,1,0:T(2,128)(2,1)}, bf16[1,2,4096]{2,1,0:T(2,128)(2,1)S(1)}, u32[]{:S(2)}, u32[]{:S(2)}) collective-permute-start(bf16[1,2,4096]{2,1,0:T(2,128)(2,1)} %bitcast.7), channel_id=1, source_target_pairs={{0,8},{1,3},{2,10},{3,1},{4,12},{5,7},{6,14},{7,5},{8,0},{9,11},{1... | collective-permute-start | bytes 49160 | tf_op jit(solution)/shard_map/ppermute | solution.py:35
  6.0 1.5 %front.1 = (bf16[16,128]{1,0:T(8,128)(2,1)S(1)}, f32[16,128]{1,0:T(8,128)S(1)}, bf16[16,2048]{1,0:T(8,128)(2,1)S(1)}, bf16[128,4096]{1,0:T(8,128)(2,1)S(1)}, f32[1,4096]{1,0:T(1,128)S(1)}) custom-call(bf16[2,4096]{1,0:T(2,128)(2,1)} %tokens_ref.1, bf16[4096]{0:T(1024)(128)(2,1)} %bias_hbm.1, f32[16,64]{1,0:T(8,128)} %pre_hbm.1, s32[16,64]{1,0:T(8,128)} %top_hbm.1, ...), custom_call_target="tpu_custom_call" | custom-call | flops 1000000 | bytes 1048576 | tf_op jit(solution)/shard_map/front/pallas_call | solution.py:116
  7.6 1.6 %collective-permute-start = (bf16[16,2048]{1,0:T(8,128)(2,1)S(1)}, bf16[16,2048]{1,0:T(8,128)(2,1)S(1)}, u32[]{:S(2)}, u32[]{:S(2)}) collective-permute-start(bf16[16,2048]{1,0:T(8,128)(2,1)S(1)} %get-tuple-element.15), channel_id=1, source_target_pairs={{0,2},{1,5},{2,0},{3,7},{4,6},{5,1},{6,4},{7,3},{8,10},{9,13},{10,... | collective-permute-start | bytes 196616 | tf_op jit(solution)/shard_map/ppermute | solution.py:35
  9.1 0.0 copy-done
  9.1 0.2 own_part.1
  9.3 0.0 collective-permute-done.4
  9.4 1.6 %collective-permute-start.5 = (bf16[2,2,4096]{2,1,0:T(2,128)(2,1)S(1)}, bf16[2,2,4096]{2,1,0:T(2,128)(2,1)S(1)}, u32[]{:S(2)}, u32[]{:S(2)}) collective-permute-start(bf16[2,2,4096]{2,1,0:T(2,128)(2,1)S(1)} %pad_maximum_fusion.1), channel_id=1, source_target_pairs={{0,4},{1,9},{2,6},{3,11},{4,0},{5,13},{6,2},{7,15},{8,12},{9,1},{1... | collective-permute-start | bytes 98312 | tf_op jit(solution)/shard_map/ppermute | solution.py:35
  11.0 0.9 %collective-permute-done = bf16[16,2048]{1,0:T(8,128)(2,1)S(1)} collective-permute-done((bf16[16,2048]{1,0:T(8,128)(2,1)S(1)}, bf16[16,2048]{1,0:T(8,128)(2,1)S(1)}, u32[]{:S(2)}, u32[]{:S(2)}) %collective-permute-start) | collective-permute-done | bytes 65568 | tf_op jit(solution)/shard_map/ppermute | solution.py:35
  11.9 1.6 %collective-permute-start.1 = (bf16[16,2048]{1,0:T(8,128)(2,1)S(1)}, bf16[16,2048]{1,0:T(8,128)(2,1)S(1)}, u32[]{:S(2)}, u32[]{:S(2)}) collective-permute-start(bf16[16,2048]{1,0:T(8,128)(2,1)S(1)} %fusion), channel_id=1, source_target_pairs={{0,4},{1,9},{2,6},{3,11},{4,0},{5,13},{6,2},{7,15},{8,12},{9,1},{1... | collective-permute-start | bytes 196616 | tf_op jit(solution)/shard_map/ppermute | solution.py:35
  13.6 0.0 collective-permute-done.5
  13.6 0.1 pad_maximum_fusion
  13.7 1.6 %collective-permute-start.6 = (bf16[4,2,4096]{2,1,0:T(2,128)(2,1)S(1)}, bf16[4,2,4096]{2,1,0:T(2,128)(2,1)S(1)}, u32[]{:S(2)}, u32[]{:S(2)}) collective-permute-start(bf16[4,2,4096]{2,1,0:T(2,128)(2,1)S(1)} %pad_maximum_fusion), channel_id=1, source_target_pairs={{0,2},{1,5},{2,0},{3,7},{4,6},{5,1},{6,4},{7,3},{8,10},{9,13},{10,... | collective-permute-start | bytes 196616 | tf_op jit(solution)/shard_map/ppermute | solution.py:35
  15.2 1.0 %collective-permute-done.1 = bf16[16,2048]{1,0:T(8,128)(2,1)S(1)} collective-permute-done((bf16[16,2048]{1,0:T(8,128)(2,1)S(1)}, bf16[16,2048]{1,0:T(8,128)(2,1)S(1)}, u32[]{:S(2)}, u32[]{:S(2)}) %collective-permute-start.1) | collective-permute-done | bytes 65568 | tf_op jit(solution)/shard_map/ppermute | solution.py:35
  16.3 0.6 %collective-permute-start.2 = (bf16[16,2048]{1,0:T(8,128)(2,1)S(1)}, bf16[16,2048]{1,0:T(8,128)(2,1)S(1)}, u32[]{:S(2)}, u32[]{:S(2)}) collective-permute-start(bf16[16,2048]{1,0:T(8,128)(2,1)S(1)} %fusion.1), channel_id=1, source_target_pairs={{0,8},{1,3},{2,10},{3,1},{4,12},{5,7},{6,14},{7,5},{8,0},{9,11},{1... | collective-permute-start | bytes 196616 | tf_op jit(solution)/shard_map/ppermute | solution.py:35
  16.9 1.5 %collective-permute-done.6 = bf16[4,2,4096]{2,1,0:T(2,128)(2,1)S(1)} collective-permute-done((bf16[4,2,4096]{2,1,0:T(2,128)(2,1)S(1)}, bf16[4,2,4096]{2,1,0:T(2,128)(2,1)S(1)}, u32[]{:S(2)}, u32[]{:S(2)}) %collective-permute-start.6) | collective-permute-done | bytes 65568 | tf_op jit(solution)/shard_map/ppermute | solution.py:35
  18.4 0.2 maximum_convert_fusion
  18.5 0.2 reshape.13
  18.7 2.8 %collective-permute-done.2 = bf16[16,2048]{1,0:T(8,128)(2,1)S(1)} collective-permute-done((bf16[16,2048]{1,0:T(8,128)(2,1)S(1)}, bf16[16,2048]{1,0:T(8,128)(2,1)S(1)}, u32[]{:S(2)}, u32[]{:S(2)}) %collective-permute-start.2) | collective-permute-done | bytes 65568 | tf_op jit(solution)/shard_map/ppermute | solution.py:35
  21.6 1.6 %collective-permute-start.3 = (bf16[16,2048]{1,0:T(8,128)(2,1)S(1)}, bf16[16,2048]{1,0:T(8,128)(2,1)S(1)}, u32[]{:S(2)}, u32[]{:S(2)}) collective-permute-start(bf16[16,2048]{1,0:T(8,128)(2,1)S(1)} %multiply_convert_fusion.own_ref), channel_id=1, source_target_pairs={{0,2},{1,5},{2,0},{3,7},{4,6},{5,1},{6,4},{7,3},{8,10},{9,13},{10,... | collective-permute-start | bytes 196616 | tf_op jit(solution)/shard_map/ppermute | solution.py:35
  23.2 2.7 %collective-permute-done.3.other_ref = bf16[16,2048]{1,0:T(8,128)(2,1)S(1)} collective-permute-done((bf16[16,2048]{1,0:T(8,128)(2,1)S(1)}, bf16[16,2048]{1,0:T(8,128)(2,1)S(1)}, u32[]{:S(2)}, u32[]{:S(2)}) %collective-permute-start.3) | collective-permute-done | bytes 65568 | tf_op jit(solution)/shard_map/ppermute | solution.py:35
  25.9 0.4 %code_half.1 = (f32[16,128]{1,0:T(8,128)S(1)}, bf16[16,4096]{1,0:T(8,128)(2,1)S(1)}) custom-call(bf16[16,2048]{1,0:T(8,128)(2,1)S(1)} %multiply_convert_fusion.own_ref, bf16[16,2048]{1,0:T(8,128)(2,1)S(1)} %collective-permute-done.3.other_ref, bf16[128,4096]{1,0:T(8,128)(2,1)S(1)} %get-tuple-element.13.rows_ref), custom_call_target="tpu_custom_call" | custom-call | flops 1000000 | bytes 1048576 | tf_op jit(solution)/shard_map/code_half/pallas_call | solution.py:183
  26.3 0.0 collective-permute-start.7
  26.3 1.4 %convolution_convert_fusion.1 = bf16[128,4096]{1,0:T(8,128)(2,1)} fusion(bf16[16,128]{1,0:T(8,128)(2,1)S(1)} %get-tuple-element.12.code_ref, bf16[16,4096]{1,0:T(8,128)(2,1)S(1)} %get-tuple-element.16), kind=kOutput, calls=%fused_computation.1 | convolution fusion | flops 17301504 | bytes 1183744 | tf_op jit(solution)/shard_map/dot_general | solution.py:255
  27.7 0.0 collective-permute-done.7.theirs_ref
  27.8 0.5 %masked.1 = (bf16[16,128]{1,0:T(8,128)(2,1)S(1)}, f32[1,128]{1,0:T(1,128)}) custom-call(f32[16,128]{1,0:T(8,128)S(1)} %get-tuple-element.17.raw_ref, f32[16,128]{1,0:T(8,128)S(1)} %get-tuple-element.18.mine_ref, f32[16,128]{1,0:T(8,128)S(1)} %collective-permute-done.7.theirs_ref), custom_call_target="tpu_custom_call" | custom-call | flops 100000 | bytes 32768 | tf_op jit(solution)/shard_map/masked/pallas_call | solution.py:218
  28.3 1.5 %convolution_convert_fusion = bf16[4096,128]{1,0:T(8,128)(2,1)} fusion(bf16[16,4096]{1,0:T(8,128)(2,1)S(1)} %subtract_convert_fusion, bf16[16,128]{1,0:T(8,128)(2,1)S(1)} %get-tuple-element.19), kind=kOutput, calls=%fused_computation | convolution fusion | flops 17301504 | bytes 1183744 | tf_op jit(solution)/shard_map/dot_general | solution.py:259
  (5 shorter events, 0.2 us)
Async XLA Ops:
  0.6 8.5 %copy-start = (bf16[2,4096]{1,0:T(2,128)(2,1)S(1)}, bf16[2,4096]{1,0:T(2,128)(2,1)}, u32[]{:S(2)}) copy-start(bf16[2,4096]{1,0:T(2,128)(2,1)} %tokens_ref.1) | copy-start | bytes 49156
  0.6 8.7 %collective-permute-start.4 = (bf16[1,2,4096]{2,1,0:T(2,128)(2,1)}, bf16[1,2,4096]{2,1,0:T(2,128)(2,1)S(1)}, u32[]{:S(2)}, u32[]{:S(2)}) collective-permute-start(bf16[1,2,4096]{2,1,0:T(2,128)(2,1)} %bitcast.7), channel_id=1, source_target_pairs={{0,8},{1,3},{2,10},{3,1},{4,12},{5,7},{6,14},{7,5},{8,0},{9,11},{1... | collective-permute-start | bytes 49160 | tf_op jit(solution)/shard_map/ppermute | solution.py:35
  7.6 4.3 %collective-permute-start = (bf16[16,2048]{1,0:T(8,128)(2,1)S(1)}, bf16[16,2048]{1,0:T(8,128)(2,1)S(1)}, u32[]{:S(2)}, u32[]{:S(2)}) collective-permute-start(bf16[16,2048]{1,0:T(8,128)(2,1)S(1)} %get-tuple-element.15), channel_id=1, source_target_pairs={{0,2},{1,5},{2,0},{3,7},{4,6},{5,1},{6,4},{7,3},{8,10},{9,13},{10,... | collective-permute-start | bytes 196616 | tf_op jit(solution)/shard_map/ppermute | solution.py:35
  9.4 4.2 %collective-permute-start.5 = (bf16[2,2,4096]{2,1,0:T(2,128)(2,1)S(1)}, bf16[2,2,4096]{2,1,0:T(2,128)(2,1)S(1)}, u32[]{:S(2)}, u32[]{:S(2)}) collective-permute-start(bf16[2,2,4096]{2,1,0:T(2,128)(2,1)S(1)} %pad_maximum_fusion.1), channel_id=1, source_target_pairs={{0,4},{1,9},{2,6},{3,11},{4,0},{5,13},{6,2},{7,15},{8,12},{9,1},{1... | collective-permute-start | bytes 98312 | tf_op jit(solution)/shard_map/ppermute | solution.py:35
  11.9 4.3 %collective-permute-start.1 = (bf16[16,2048]{1,0:T(8,128)(2,1)S(1)}, bf16[16,2048]{1,0:T(8,128)(2,1)S(1)}, u32[]{:S(2)}, u32[]{:S(2)}) collective-permute-start(bf16[16,2048]{1,0:T(8,128)(2,1)S(1)} %fusion), channel_id=1, source_target_pairs={{0,4},{1,9},{2,6},{3,11},{4,0},{5,13},{6,2},{7,15},{8,12},{9,1},{1... | collective-permute-start | bytes 196616 | tf_op jit(solution)/shard_map/ppermute | solution.py:35
  13.7 4.7 %collective-permute-start.6 = (bf16[4,2,4096]{2,1,0:T(2,128)(2,1)S(1)}, bf16[4,2,4096]{2,1,0:T(2,128)(2,1)S(1)}, u32[]{:S(2)}, u32[]{:S(2)}) collective-permute-start(bf16[4,2,4096]{2,1,0:T(2,128)(2,1)S(1)} %pad_maximum_fusion), channel_id=1, source_target_pairs={{0,2},{1,5},{2,0},{3,7},{4,6},{5,1},{6,4},{7,3},{8,10},{9,13},{10,... | collective-permute-start | bytes 196616 | tf_op jit(solution)/shard_map/ppermute | solution.py:35
  16.3 5.3 %collective-permute-start.2 = (bf16[16,2048]{1,0:T(8,128)(2,1)S(1)}, bf16[16,2048]{1,0:T(8,128)(2,1)S(1)}, u32[]{:S(2)}, u32[]{:S(2)}) collective-permute-start(bf16[16,2048]{1,0:T(8,128)(2,1)S(1)} %fusion.1), channel_id=1, source_target_pairs={{0,8},{1,3},{2,10},{3,1},{4,12},{5,7},{6,14},{7,5},{8,0},{9,11},{1... | collective-permute-start | bytes 196616 | tf_op jit(solution)/shard_map/ppermute | solution.py:35
  21.6 4.3 %collective-permute-start.3 = (bf16[16,2048]{1,0:T(8,128)(2,1)S(1)}, bf16[16,2048]{1,0:T(8,128)(2,1)S(1)}, u32[]{:S(2)}, u32[]{:S(2)}) collective-permute-start(bf16[16,2048]{1,0:T(8,128)(2,1)S(1)} %multiply_convert_fusion.own_ref), channel_id=1, source_target_pairs={{0,2},{1,5},{2,0},{3,7},{4,6},{5,1},{6,4},{7,3},{8,10},{9,13},{10,... | collective-permute-start | bytes 196616 | tf_op jit(solution)/shard_map/ppermute | solution.py:35
  26.3 1.5 %collective-permute-start.7 = (f32[16,128]{1,0:T(8,128)S(1)}, f32[16,128]{1,0:T(8,128)S(1)}, u32[]{:S(2)}, u32[]{:S(2)}) collective-permute-start(f32[16,128]{1,0:T(8,128)S(1)} %get-tuple-element.18.mine_ref), channel_id=1, source_target_pairs={{0,1},{1,0},{2,3},{3,2},{4,5},{5,4},{6,7},{7,6},{8,9},{9,8},{10,11... | collective-permute-start | bytes 24584 | tf_op jit(solution)/shard_map/ppermute | solution.py:254

commit v6 on v5

--- a/solution.py
+++ b/solution.py
@@ -19,10 +19,6 @@
 
 def sum_bit(step, core):
     return (step + core) % feat_bits()
-
-
-def token_bit(step, core):
-    return (feat_bits() - 1 - step + core) % feat_bits()
 
 
 def swapped(shard, bit_of):
@@ -35,20 +31,10 @@
     return lax.ppermute(shard, ("feat", "tok"), pairs)
 
 
-def halves(width):
-    half = width // 2
-    bit = lax.axis_index("feat") >> (lax.axis_index("tok") % feat_bits()) & 1
-    return (
-        pl.multiple_of(bit * half, half),
-        pl.multiple_of((1 - bit) * half, half),
-        half,
-    )
-
-
-def share(code, rows_ref, tokens_ref, bias_ref, at, half):
-    total = jnp.dot(code, rows_ref[:, pl.ds(at, half)], preferred_element_type=jnp.float32)
+def share(code, rows_ref, tokens_ref, bias_ref):
+    total = jnp.dot(code, rows_ref[...], preferred_element_type=jnp.float32)
     rows = tokens_ref.shape[0]
-    centered = tokens_ref[:, pl.ds(at, half)].astype(jnp.float32) - bias_ref[:, pl.ds(at, half)]
+    centered = tokens_ref[...].astype(jnp.float32) - bias_ref[...]
     centered = centered.astype(jnp.bfloat16).astype(jnp.float32)
     token = lax.broadcasted_iota(jnp.int32, (total.shape[0], 1), 0)
     first = lax.axis_index("feat") * rows
@@ -67,7 +53,7 @@
     count_ref,
     code_ref,
     raw_ref,
-    send_ref,
+    total_ref,
     rows_ref,
     bias_ref,
     tokens_ref,
@@ -106,8 +92,7 @@
     for copy in copies[2:]:
         copy.wait()
     bias_ref[...] = bias_flat[...].astype(jnp.float32).reshape(1, width)
-    _, other, half = halves(width)
-    send_ref[...] = share(code, rows_ref, tokens_ref, bias_ref, other, half).astype(jnp.bfloat16)
+    total_ref[...] = share(code, rows_ref, tokens_ref, bias_ref)
 
 
 def front(tokens, b_pre, pre_codes, top_idx, blocks, counts, dict_rows):
@@ -118,7 +103,7 @@
         out_shape=(
             jax.ShapeDtypeStruct((count, slots), jnp.bfloat16),
             jax.ShapeDtypeStruct((count, slots), jnp.float32),
-            jax.ShapeDtypeStruct((count, width // 2), jnp.bfloat16),
+            jax.ShapeDtypeStruct((count, width), jnp.float32),
             jax.ShapeDtypeStruct(dict_rows.shape, jnp.bfloat16),
             jax.ShapeDtypeStruct((1, width), jnp.float32),
         ),
@@ -144,54 +129,43 @@
     )
 
 
-def own_kernel(code_ref, rows_ref, tokens_ref, bias_ref, total_ref):
-    own, _, half = halves(rows_ref.shape[1])
-    total_ref[...] = share(code_ref[...], rows_ref, tokens_ref, bias_ref, own, half)
-
-
-def own_part(code, dict_rows, tokens, bias):
-    half = dict_rows.shape[1] // 2
-    return pl.pallas_call(
-        own_kernel,
-        out_shape=jax.ShapeDtypeStruct((code.shape[0], half), jnp.float32),
-        in_specs=[VMEM] * 4,
+def joined_kernel(first_ref, second_ref, after_ref, out_ref):
+    count = first_ref.shape[0]
+    out_ref[:count] = first_ref[...]
+    out_ref[count:] = second_ref[...]
+
+
+def joined(first, second, after):
+    return pl.pallas_call(
+        joined_kernel,
+        out_shape=jax.ShapeDtypeStruct((2 * first.shape[0],) + first.shape[1:], first.dtype),
+        in_specs=[VMEM, VMEM, pl.BlockSpec(memory_space=pl.ANY)],
         out_specs=VMEM,
         compiler_params=PARAMS,
-        cost_estimate=pl.CostEstimate(flops=10**6, bytes_accessed=2**19, transcendentals=0),
-        name="own_part",
-    )(code, dict_rows, tokens, bias)
-
-
-def code_half_kernel(own_ref, other_ref, rows_ref, half_ref, scaled_ref):
-    own_at, other_at, half = halves(rows_ref.shape[1])
-    total = jnp.zeros(half_ref.shape, jnp.float32)
-    for ref, at in ((own_ref, own_at), (other_ref, other_at)):
-        part = ref[...]
-        scaled_ref[:, pl.ds(at, half)] = part
-        total += lax.dot_general(
-            part,
-            rows_ref[:, pl.ds(at, half)],
-            (((1,), (1,)), ((), ())),
-            preferred_element_type=jnp.float32,
-        )
-    half_ref[...] = total
-
-
-def code_half_of(scaled_own, scaled_other, dict_rows):
-    tokens = scaled_own.shape[0]
-    slots, width = dict_rows.shape
+        cost_estimate=pl.CostEstimate(flops=10**6, bytes_accessed=2**20, transcendentals=0),
+        name="joined",
+    )(first, second, after)
+
+
+def code_half_kernel(scaled_ref, rows_ref, half_ref):
+    half_ref[...] = lax.dot_general(
+        scaled_ref[...],
+        rows_ref[...],
+        (((1,), (1,)), ((), ())),
+        preferred_element_type=jnp.float32,
+    )
+
+
+def code_half_of(scaled, dict_rows):
     return pl.pallas_call(
         code_half_kernel,
-        out_shape=(
-            jax.ShapeDtypeStruct((tokens, slots), jnp.float32),
-            jax.ShapeDtypeStruct((tokens, width), jnp.bfloat16),
-        ),
-        in_specs=[VMEM] * 3,
-        out_specs=(VMEM, VMEM),
+        out_shape=jax.ShapeDtypeStruct((scaled.shape[0], dict_rows.shape[0]), jnp.float32),
+        in_specs=[VMEM] * 2,
+        out_specs=VMEM,
         compiler_params=PARAMS,
         cost_estimate=pl.CostEstimate(flops=10**6, bytes_accessed=2**20, transcendentals=0),
         name="code_half",
-    )(scaled_own, scaled_other, dict_rows)
+    )(scaled, dict_rows)
 
 
 def masked_kernel(rows, raw_ref, mine_ref, theirs_ref, grad_ref, benc_ref):
@@ -205,7 +179,7 @@
     block = place // rows
     distance = jnp.zeros_like(place)
     for step in range(feat_bits()):
-        distance |= (block >> step & 1) << token_bit(step, core)
+        distance |= (block >> step & 1) << sum_bit(step, core)
     source = (lax.axis_index("feat") ^ distance) * rows + place % rows
     order = jnp.where(token == source, 1.0, 0.0).astype(jnp.bfloat16)
     grad_ref[...] = jnp.dot(order, pre_grad, preferred_element_type=jnp.float32).astype(
@@ -231,26 +205,26 @@
 
 def local(tokens, b_pre, pre_codes, top_idx, blocks, counts, dict_rows):
     rows, width = tokens.shape
-    gathered = tokens[None]
+    gathered = [tokens[None], swapped(tokens[None], functools.partial(sum_bit, 0))]
+    code, raw, total, dict_rows, bias = front(
+        tokens, b_pre, pre_codes, top_idx, blocks, counts, dict_rows
+    )
     for step in range(feat_bits()):
-        arrived = swapped(gathered, functools.partial(token_bit, step))
-        gathered = jnp.concatenate([gathered, arrived], axis=0)
-
-    code, raw, send, dict_rows, bias = front(
-        tokens, b_pre, pre_codes, top_idx, blocks, counts, dict_rows
-    )
-    arrived = swapped(send, functools.partial(sum_bit, 0))
-    total = own_part(code, dict_rows, tokens, bias) + arrived.astype(jnp.float32)
-    for step in range(1, feat_bits()):
-        arrived = swapped(total.astype(jnp.bfloat16), functools.partial(sum_bit, step))
+        bit_of = functools.partial(sum_bit, step)
+        total, gathered = lax.optimization_barrier((total, gathered))
+        sent = total.astype(jnp.bfloat16)
+        arrived = swapped(sent, bit_of)
+        if step > 0:
+            block = joined(*gathered, sent)
+            gathered = [block, swapped(block, bit_of)]
         total = total + arrived.astype(jnp.float32)
-    scaled_own = (0.25 * total).astype(jnp.bfloat16)
-    scaled_other = swapped(scaled_own, functools.partial(sum_bit, 0))
-
-    centered = gathered.reshape(-1, width).astype(jnp.float32) - bias
+    scaled = (0.25 * total).astype(jnp.bfloat16)
+    code_half = code_half_of(scaled, dict_rows)
+
+    gathered = joined(*gathered, code_half).reshape(-1, width)
+    centered = gathered.astype(jnp.float32) - bias
     centered = lax.optimization_barrier(centered.astype(jnp.bfloat16))
 
-    code_half, scaled = code_half_of(scaled_own, scaled_other, dict_rows)
     theirs = lax.ppermute(code_half, "tok", [(i, 1 - i) for i in range(2)])
     grad_rows = lax.dot_general(
         code, scaled, (((0,), (0,)), ((), ())), preferred_element_type=jnp.float32

time: 30 us -> 30.9 us (1.030)
  waiting for transfers between devices: 8.89 us -> 13.9 us
  starting transfers between devices: 12.7 us -> 9.21 us
    ppermute x7 -> x6, waiting for transfers between devices: 8.89 us -> 13.9 us  [swapped(): return lax.ppermute(shard, ('feat', 'tok'), pairs)]
    ppermute x7 -> x6, starting transfers between devices: 12.7 us -> 9.2 us  [swapped(): return lax.ppermute(shard, ('feat', 'tok'), pairs)]
  transfers between devices with their start and end apart: 8 -> 7, of which waited for: 5 -> 5; matrix products, arithmetic and copies ran while one was open for 7% -> 5% of each run, Pallas kernels for 6% -> 6%
where the time goes in v6:
time: 30.9 us; the launch traced here: 30.7 us
  waiting for transfers between devices  13.9 us (45%)
  starting transfers between devices  9.21 us (30%)
  matrix products  2.88 us (9%)
  Pallas kernels  2.48 us (8%)
  between operations  2.01 us (7%)
    ppermute x6, waiting for transfers between devices, swapped(): return lax.ppermute(shard, ('feat', 'tok'), pairs)  13.9 us
    ppermute x6, starting transfers between devices, swapped(): return lax.ppermute(shard, ('feat', 'tok'), pairs)  9.2 us
    pallas_call x1, Pallas kernels, front(): pl.pallas_call(front_kernel, out_shape=(jax.ShapeDtypeStruct((count, slot...  1.57 us
    dot_general x1, matrix products, local(): lax.dot_general(centered, pre_grad, (((0,), (0,)), ((), ())), preferred_e...  1.45 us
    dot_general x1, matrix products, local(): lax.dot_general(code, scaled, (((0,), (0,)), ((), ())), preferred_element...  1.43 us
  transfers between devices with their start and end apart: 7, of which 5 were waited for; matrix products, arithmetic and copies ran while one was open for 5% of the time, Pallas kernels for 6%

profile of v6, /device:TPU:0, one launch (start us, length us, event | category | flops | bytes accessed | tf_op | source)
XLA Modules:
  0.0 30.7 jit_solution(9076029882999218586)
XLA Ops:
  0.6 3.0 %collective-permute-start = (bf16[1,2,4096]{2,1,0:T(2,128)(2,1)}, bf16[1,2,4096]{2,1,0:T(2,128)(2,1)S(1)}, u32[]{:S(2)}, u32[]{:S(2)}) collective-permute-start(bf16[1,2,4096]{2,1,0:T(2,128)(2,1)} %bitcast.7), channel_id=1, source_target_pairs={{0,2},{1,5},{2,0},{3,7},{4,6},{5,1},{6,4},{7,3},{8,10},{9,13},{10,... | collective-permute-start | bytes 49160 | tf_op jit(solution)/shard_map/ppermute | solution.py:31
  4.9 0.0 copy-start
  4.9 1.6 %front.1 = (bf16[16,128]{1,0:T(8,128)(2,1)S(1)}, f32[16,128]{1,0:T(8,128)S(1)}, f32[16,4096]{1,0:T(8,128)S(1)}, bf16[128,4096]{1,0:T(8,128)(2,1)S(1)}, f32[1,4096]{1,0:T(1,128)S(1)}) custom-call(bf16[2,4096]{1,0:T(2,128)(2,1)} %tokens_hbm.1, bf16[4096]{0:T(1024)(128)(2,1)} %bias_hbm.1, f32[16,64]{1,0:T(8,128)} %pre_hbm.1, s32[16,64]{1,0:T(8,128)} %top_hbm.1, ...), custom_call_target="tpu_custom_call" | custom-call | flops 1000000 | bytes 1048576 | tf_op jit(solution)/shard_map/front/pallas_call | solution.py:101
  6.5 0.0 collective-permute-done.second_ref
  6.6 1.1 %collective-permute-start.1 = (bf16[16,4096]{1,0:T(8,128)(2,1)S(1)}, bf16[16,4096]{1,0:T(8,128)(2,1)S(1)}, u32[]{:S(2)}, u32[]{:S(2)}) collective-permute-start(bf16[16,4096]{1,0:T(8,128)(2,1)S(1)} %convert_element_type.36), channel_id=1, source_target_pairs={{0,2},{1,5},{2,0},{3,7},{4,6},{5,1},{6,4},{7,3},{8,10},{9,13},{10,... | collective-permute-start | bytes 393224 | tf_op jit(solution)/shard_map/ppermute | solution.py:31
  7.7 3.9 %collective-permute-done.1 = bf16[16,4096]{1,0:T(8,128)(2,1)S(1)} collective-permute-done((bf16[16,4096]{1,0:T(8,128)(2,1)S(1)}, bf16[16,4096]{1,0:T(8,128)(2,1)S(1)}, u32[]{:S(2)}, u32[]{:S(2)}) %collective-permute-start.1) | collective-permute-done | bytes 131104 | tf_op jit(solution)/shard_map/ppermute | solution.py:31
  11.6 1.6 %collective-permute-start.2 = (bf16[16,4096]{1,0:T(8,128)(2,1)S(1)}, bf16[16,4096]{1,0:T(8,128)(2,1)S(1)}, u32[]{:S(2)}, u32[]{:S(2)}) collective-permute-start(bf16[16,4096]{1,0:T(8,128)(2,1)S(1)} %convert_element_type.38.after_ref), channel_id=1, source_target_pairs={{0,4},{1,9},{2,6},{3,11},{4,0},{5,13},{6,2},{7,15},{8,12},{9,1},{1... | collective-permute-start | bytes 393224 | tf_op jit(solution)/shard_map/ppermute | solution.py:31
  13.3 0.0 copy-done
  13.3 0.4 %collective-permute-start.3 = (bf16[2,2,4096]{2,1,0:T(2,128)(2,1)S(1)}, bf16[2,2,4096]{2,1,0:T(2,128)(2,1)S(1)}, u32[]{:S(2)}, u32[]{:S(2)}) collective-permute-start(bf16[2,2,4096]{2,1,0:T(2,128)(2,1)S(1)} %joined.3.first_ref), channel_id=1, source_target_pairs={{0,4},{1,9},{2,6},{3,11},{4,0},{5,13},{6,2},{7,15},{8,12},{9,1},{1... | collective-permute-start | bytes 98312 | tf_op jit(solution)/shard_map/ppermute | solution.py:31
  13.7 4.3 %collective-permute-done.2 = bf16[16,4096]{1,0:T(8,128)(2,1)S(1)} collective-permute-done((bf16[16,4096]{1,0:T(8,128)(2,1)S(1)}, bf16[16,4096]{1,0:T(8,128)(2,1)S(1)}, u32[]{:S(2)}, u32[]{:S(2)}) %collective-permute-start.2) | collective-permute-done | bytes 131104 | tf_op jit(solution)/shard_map/ppermute | solution.py:31
  18.1 0.3 %collective-permute-done.3.second_ref = bf16[2,2,4096]{2,1,0:T(2,128)(2,1)S(1)} collective-permute-done((bf16[2,2,4096]{2,1,0:T(2,128)(2,1)S(1)}, bf16[2,2,4096]{2,1,0:T(2,128)(2,1)S(1)}, u32[]{:S(2)}, u32[]{:S(2)}) %collective-permute-start.3) | collective-permute-done | bytes 32800 | tf_op jit(solution)/shard_map/ppermute | solution.py:31
  18.5 1.4 %collective-permute-start.4 = (bf16[16,4096]{1,0:T(8,128)(2,1)S(1)}, bf16[16,4096]{1,0:T(8,128)(2,1)S(1)}, u32[]{:S(2)}, u32[]{:S(2)}) collective-permute-start(bf16[16,4096]{1,0:T(8,128)(2,1)S(1)} %convert_element_type.40.after_ref), channel_id=1, source_target_pairs={{0,8},{1,3},{2,10},{3,1},{4,12},{5,7},{6,14},{7,5},{8,0},{9,11},{1... | collective-permute-start | bytes 393224 | tf_op jit(solution)/shard_map/ppermute | solution.py:31
  19.9 1.6 %collective-permute-start.5 = (bf16[4,2,4096]{2,1,0:T(2,128)(2,1)S(1)}, bf16[4,2,4096]{2,1,0:T(2,128)(2,1)S(1)}, u32[]{:S(2)}, u32[]{:S(2)}) collective-permute-start(bf16[4,2,4096]{2,1,0:T(2,128)(2,1)S(1)} %joined.4.first_ref), channel_id=1, source_target_pairs={{0,8},{1,3},{2,10},{3,1},{4,12},{5,7},{6,14},{7,5},{8,0},{9,11},{1... | collective-permute-start | bytes 196616 | tf_op jit(solution)/shard_map/ppermute | solution.py:31
  21.5 5.0 %collective-permute-done.4 = bf16[16,4096]{1,0:T(8,128)(2,1)S(1)} collective-permute-done((bf16[16,4096]{1,0:T(8,128)(2,1)S(1)}, bf16[16,4096]{1,0:T(8,128)(2,1)S(1)}, u32[]{:S(2)}, u32[]{:S(2)}) %collective-permute-start.4) | collective-permute-done | bytes 131104 | tf_op jit(solution)/shard_map/ppermute | solution.py:31
  26.5 0.4 %code_half.1.after_ref.mine_ref = f32[16,128]{1,0:T(8,128)S(1)} custom-call(bf16[16,4096]{1,0:T(8,128)(2,1)S(1)} %multiply_convert_fusion.scaled_ref, bf16[128,4096]{1,0:T(8,128)(2,1)S(1)} %get-tuple-element.30.rows_ref), custom_call_target="tpu_custom_call" | custom-call | flops 1000000 | bytes 1048576 | tf_op jit(solution)/shard_map/code_half/pallas_call | solution.py:160
  26.9 0.0 collective-permute-start.6
  26.9 0.3 collective-permute-done.5.second_ref
  27.3 1.4 %convolution_convert_fusion.1 = bf16[128,4096]{1,0:T(8,128)(2,1)} fusion(bf16[16,128]{1,0:T(8,128)(2,1)S(1)} %get-tuple-element.19, bf16[16,4096]{1,0:T(8,128)(2,1)S(1)} %multiply_convert_fusion.scaled_ref), kind=kOutput, calls=%fused_computation.1 | convolution fusion | flops 17301504 | bytes 1183744 | tf_op jit(solution)/shard_map/dot_general | solution.py:229
  28.7 0.0 collective-permute-done.6.theirs_ref
  28.7 0.5 %masked.1 = (bf16[16,128]{1,0:T(8,128)(2,1)S(1)}, f32[1,128]{1,0:T(1,128)}) custom-call(f32[16,128]{1,0:T(8,128)S(1)} %get-tuple-element.32.raw_ref, f32[16,128]{1,0:T(8,128)S(1)} %code_half.1.after_ref.mine_ref, f32[16,128]{1,0:T(8,128)S(1)} %collective-permute-done.6.theirs_ref), custom_call_target="tpu_custom_call" | custom-call | flops 100000 | bytes 32768 | tf_op jit(solution)/shard_map/masked/pallas_call | solution.py:192
  29.2 1.5 %convolution_convert_fusion = bf16[4096,128]{1,0:T(8,128)(2,1)} fusion(bf16[16,4096]{1,0:T(8,128)(2,1)S(1)} %subtract_convert_fusion, bf16[16,128]{1,0:T(8,128)(2,1)S(1)} %get-tuple-element.33), kind=kOutput, calls=%fused_computation | convolution fusion | flops 17301504 | bytes 1183744 | tf_op jit(solution)/shard_map/dot_general | solution.py:233
  (11 shorter events, 0.2 us)
Async XLA Ops:
  0.6 5.9 %collective-permute-start = (bf16[1,2,4096]{2,1,0:T(2,128)(2,1)}, bf16[1,2,4096]{2,1,0:T(2,128)(2,1)S(1)}, u32[]{:S(2)}, u32[]{:S(2)}) collective-permute-start(bf16[1,2,4096]{2,1,0:T(2,128)(2,1)} %bitcast.7), channel_id=1, source_target_pairs={{0,2},{1,5},{2,0},{3,7},{4,6},{5,1},{6,4},{7,3},{8,10},{9,13},{10,... | collective-permute-start | bytes 49160 | tf_op jit(solution)/shard_map/ppermute | solution.py:31
  4.9 8.4 %copy-start = (bf16[2,4096]{1,0:T(2,128)(2,1)S(1)}, bf16[2,4096]{1,0:T(2,128)(2,1)}, u32[]{:S(2)}) copy-start(bf16[2,4096]{1,0:T(2,128)(2,1)} %tokens_hbm.1) | copy-start | bytes 49156
  6.6 5.0 %collective-permute-start.1 = (bf16[16,4096]{1,0:T(8,128)(2,1)S(1)}, bf16[16,4096]{1,0:T(8,128)(2,1)S(1)}, u32[]{:S(2)}, u32[]{:S(2)}) collective-permute-start(bf16[16,4096]{1,0:T(8,128)(2,1)S(1)} %convert_element_type.36), channel_id=1, source_target_pairs={{0,2},{1,5},{2,0},{3,7},{4,6},{5,1},{6,4},{7,3},{8,10},{9,13},{10,... | collective-permute-start | bytes 393224 | tf_op jit(solution)/shard_map/ppermute | solution.py:31
  11.6 6.4 %collective-permute-start.2 = (bf16[16,4096]{1,0:T(8,128)(2,1)S(1)}, bf16[16,4096]{1,0:T(8,128)(2,1)S(1)}, u32[]{:S(2)}, u32[]{:S(2)}) collective-permute-start(bf16[16,4096]{1,0:T(8,128)(2,1)S(1)} %convert_element_type.38.after_ref), channel_id=1, source_target_pairs={{0,4},{1,9},{2,6},{3,11},{4,0},{5,13},{6,2},{7,15},{8,12},{9,1},{1... | collective-permute-start | bytes 393224 | tf_op jit(solution)/shard_map/ppermute | solution.py:31
  13.3 5.2 %collective-permute-start.3 = (bf16[2,2,4096]{2,1,0:T(2,128)(2,1)S(1)}, bf16[2,2,4096]{2,1,0:T(2,128)(2,1)S(1)}, u32[]{:S(2)}, u32[]{:S(2)}) collective-permute-start(bf16[2,2,4096]{2,1,0:T(2,128)(2,1)S(1)} %joined.3.first_ref), channel_id=1, source_target_pairs={{0,4},{1,9},{2,6},{3,11},{4,0},{5,13},{6,2},{7,15},{8,12},{9,1},{1... | collective-permute-start | bytes 98312 | tf_op jit(solution)/shard_map/ppermute | solution.py:31
  18.5 8.0 %collective-permute-start.4 = (bf16[16,4096]{1,0:T(8,128)(2,1)S(1)}, bf16[16,4096]{1,0:T(8,128)(2,1)S(1)}, u32[]{:S(2)}, u32[]{:S(2)}) collective-permute-start(bf16[16,4096]{1,0:T(8,128)(2,1)S(1)} %convert_element_type.40.after_ref), channel_id=1, source_target_pairs={{0,8},{1,3},{2,10},{3,1},{4,12},{5,7},{6,14},{7,5},{8,0},{9,11},{1... | collective-permute-start | bytes 393224 | tf_op jit(solution)/shard_map/ppermute | solution.py:31
  19.9 7.3 %collective-permute-start.5 = (bf16[4,2,4096]{2,1,0:T(2,128)(2,1)S(1)}, bf16[4,2,4096]{2,1,0:T(2,128)(2,1)S(1)}, u32[]{:S(2)}, u32[]{:S(2)}) collective-permute-start(bf16[4,2,4096]{2,1,0:T(2,128)(2,1)S(1)} %joined.4.first_ref), channel_id=1, source_target_pairs={{0,8},{1,3},{2,10},{3,1},{4,12},{5,7},{6,14},{7,5},{8,0},{9,11},{1... | collective-permute-start | bytes 196616 | tf_op jit(solution)/shard_map/ppermute | solution.py:31
  26.9 1.8 %collective-permute-start.6 = (f32[16,128]{1,0:T(8,128)S(1)}, f32[16,128]{1,0:T(8,128)S(1)}, u32[]{:S(2)}, u32[]{:S(2)}) collective-permute-start(f32[16,128]{1,0:T(8,128)S(1)} %code_half.1.after_ref.mine_ref), channel_id=1, source_target_pairs={{0,1},{1,0},{2,3},{3,2},{4,5},{5,4},{6,7},{7,6},{8,9},{9,8},{10,11... | collective-permute-start | bytes 24584 | tf_op jit(solution)/shard_map/ppermute | solution.py:228

commit v7 on v5

--- a/solution.py
+++ b/solution.py
@@ -19,10 +19,6 @@
 
 def sum_bit(step, core):
     return (step + core) % feat_bits()
-
-
-def token_bit(step, core):
-    return (feat_bits() - 1 - step + core) % feat_bits()
 
 
 def swapped(shard, bit_of):
@@ -69,8 +65,8 @@
     raw_ref,
     send_ref,
     rows_ref,
+    tokens_ref,
     bias_ref,
-    tokens_ref,
     bias_flat,
     pre_ref,
     top_ref,
@@ -120,12 +116,12 @@
             jax.ShapeDtypeStruct((count, slots), jnp.float32),
             jax.ShapeDtypeStruct((count, width // 2), jnp.bfloat16),
             jax.ShapeDtypeStruct(dict_rows.shape, jnp.bfloat16),
+            jax.ShapeDtypeStruct(tokens.shape, tokens.dtype),
             jax.ShapeDtypeStruct((1, width), jnp.float32),
         ),
         in_specs=[HBM] * 5 + [SMEM] * 2,
-        out_specs=(VMEM,) * 5,
+        out_specs=(VMEM,) * 6,
         scratch_shapes=[
-            pltpu.VMEM(tokens.shape, tokens.dtype),
             pltpu.VMEM(b_pre.shape, b_pre.dtype),
             pltpu.VMEM(pre_codes.shape, pre_codes.dtype),
             pltpu.VMEM(top_idx.shape, top_idx.dtype),
@@ -162,22 +158,75 @@
     )(code, dict_rows, tokens, bias)
 
 
-def code_half_kernel(own_ref, other_ref, rows_ref, half_ref, scaled_ref):
-    own_at, other_at, half = halves(rows_ref.shape[1])
-    total = jnp.zeros(half_ref.shape, jnp.float32)
-    for ref, at in ((own_ref, own_at), (other_ref, other_at)):
-        part = ref[...]
-        scaled_ref[:, pl.ds(at, half)] = part
-        total += lax.dot_general(
-            part,
-            rows_ref[:, pl.ds(at, half)],
-            (((1,), (1,)), ((), ())),
-            preferred_element_type=jnp.float32,
-        )
-    half_ref[...] = total
-
-
-def code_half_of(scaled_own, scaled_other, dict_rows):
+def joined_kernel(first_ref, second_ref, after_ref, out_ref):
+    count = first_ref.shape[0]
+    out_ref[:count] = first_ref[...]
+    out_ref[count:] = second_ref[...]
+
+
+def copied_kernel(block_ref, after_ref, out_ref):
+    out_ref[...] = block_ref[...]
+
+
+def copied(block, after):
+    return pl.pallas_call(
+        copied_kernel,
+        out_shape=jax.ShapeDtypeStruct(block.shape, block.dtype),
+        in_specs=[VMEM, pl.BlockSpec(memory_space=pl.ANY)],
+        out_specs=VMEM,
+        compiler_params=PARAMS,
+        cost_estimate=pl.CostEstimate(flops=10**6, bytes_accessed=2**20, transcendentals=0),
+        name="copied",
+    )(block, after)
+
+
+def joined(first, second, after):
+    return pl.pallas_call(
+        joined_kernel,
+        out_shape=jax.ShapeDtypeStruct((2 * first.shape[0],) + first.shape[1:], first.dtype),
+        in_specs=[VMEM, VMEM, pl.BlockSpec(memory_space=pl.ANY)],
+        out_specs=VMEM,
+        compiler_params=PARAMS,
+        cost_estimate=pl.CostEstimate(flops=10**6, bytes_accessed=2**20, transcendentals=0),
+        name="joined",
+    )(first, second, after)
+
+
+def product(part_ref, rows_ref, at, half):
+    return lax.dot_general(
+        part_ref[...],
+        rows_ref[:, pl.ds(at, half)],
+        (((1,), (1,)), ((), ())),
+        preferred_element_type=jnp.float32,
+    )
+
+
+def first_product_kernel(own_ref, rows_ref, half_ref):
+    own, _, half = halves(rows_ref.shape[1])
+    half_ref[...] = product(own_ref, rows_ref, own, half)
+
+
+def code_half_kernel(own_ref, other_ref, first_ref, rows_ref, half_ref, scaled_ref):
+    own, other, half = halves(rows_ref.shape[1])
+    half_ref[...] = first_ref[...] + product(other_ref, rows_ref, other, half)
+    scaled_ref[:, pl.ds(own, half)] = own_ref[...]
+    scaled_ref[:, pl.ds(other, half)] = other_ref[...]
+
+
+def first_product(scaled_own, dict_rows):
+    tokens = scaled_own.shape[0]
+    return pl.pallas_call(
+        first_product_kernel,
+        out_shape=jax.ShapeDtypeStruct((tokens, dict_rows.shape[0]), jnp.float32),
+        in_specs=[VMEM] * 2,
+        out_specs=VMEM,
+        compiler_params=PARAMS,
+        cost_estimate=pl.CostEstimate(flops=10**6, bytes_accessed=2**20, transcendentals=0),
+        name="first_product",
+    )(scaled_own, dict_rows)
+
+
+def code_half_of(scaled_own, scaled_other, first, dict_rows):
     tokens = scaled_own.shape[0]
     slots, width = dict_rows.shape
     return pl.pallas_call(
@@ -186,12 +235,12 @@
             jax.ShapeDtypeStruct((tokens, slots), jnp.float32),
             jax.ShapeDtypeStruct((tokens, width), jnp.bfloat16),
         ),
-        in_specs=[VMEM] * 3,
+        in_specs=[VMEM] * 4,
         out_specs=(VMEM, VMEM),
         compiler_params=PARAMS,
         cost_estimate=pl.CostEstimate(flops=10**6, bytes_accessed=2**20, transcendentals=0),
         name="code_half",
-    )(scaled_own, scaled_other, dict_rows)
+    )(scaled_own, scaled_other, first, dict_rows)
 
 
 def masked_kernel(rows, raw_ref, mine_ref, theirs_ref, grad_ref, benc_ref):
@@ -205,7 +254,7 @@
     block = place // rows
     distance = jnp.zeros_like(place)
     for step in range(feat_bits()):
-        distance |= (block >> step & 1) << token_bit(step, core)
+        distance |= (block >> step & 1) << sum_bit(step, core)
     source = (lax.axis_index("feat") ^ distance) * rows + place % rows
     order = jnp.where(token == source, 1.0, 0.0).astype(jnp.bfloat16)
     grad_ref[...] = jnp.dot(order, pre_grad, preferred_element_type=jnp.float32).astype(
@@ -231,26 +280,32 @@
 
 def local(tokens, b_pre, pre_codes, top_idx, blocks, counts, dict_rows):
     rows, width = tokens.shape
+    code, raw, sent, dict_rows, tokens, bias = front(
+        tokens, b_pre, pre_codes, top_idx, blocks, counts, dict_rows
+    )
     gathered = tokens[None]
     for step in range(feat_bits()):
-        arrived = swapped(gathered, functools.partial(token_bit, step))
-        gathered = jnp.concatenate([gathered, arrived], axis=0)
-
-    code, raw, send, dict_rows, bias = front(
-        tokens, b_pre, pre_codes, top_idx, blocks, counts, dict_rows
-    )
-    arrived = swapped(send, functools.partial(sum_bit, 0))
-    total = own_part(code, dict_rows, tokens, bias) + arrived.astype(jnp.float32)
-    for step in range(1, feat_bits()):
-        arrived = swapped(total.astype(jnp.bfloat16), functools.partial(sum_bit, step))
+        bit_of = functools.partial(sum_bit, step)
+        arrived = swapped(sent, bit_of)
+        if step == 0:
+            total = own_part(code, dict_rows, tokens, bias)
+            block = copied(gathered, sent)
+        else:
+            block = joined(*gathered, sent)
+        gathered = [block, swapped(block, bit_of)]
         total = total + arrived.astype(jnp.float32)
+        if step < feat_bits() - 1:
+            total, gathered = lax.optimization_barrier((total, gathered))
+            sent = total.astype(jnp.bfloat16)
     scaled_own = (0.25 * total).astype(jnp.bfloat16)
     scaled_other = swapped(scaled_own, functools.partial(sum_bit, 0))
 
-    centered = gathered.reshape(-1, width).astype(jnp.float32) - bias
+    first = first_product(scaled_own, dict_rows)
+    gathered = joined(*gathered, scaled_own).reshape(-1, width)
+    centered = gathered.astype(jnp.float32) - bias
     centered = lax.optimization_barrier(centered.astype(jnp.bfloat16))
 
-    code_half, scaled = code_half_of(scaled_own, scaled_other, dict_rows)
+    code_half, scaled = code_half_of(scaled_own, scaled_other, first, dict_rows)
     theirs = lax.ppermute(code_half, "tok", [(i, 1 - i) for i in range(2)])
     grad_rows = lax.dot_general(
         code, scaled, (((0,), (0,)), ((), ())), preferred_element_type=jnp.float32

time: 30 us -> 30.2 us (level)
  waiting for transfers between devices: 8.89 us -> 13.2 us
  starting transfers between devices: 12.7 us -> 9 us
  other arithmetic: 0.42 us -> 0.09 us
    ppermute x7, waiting for transfers between devices: 8.89 us -> 13.2 us  [swapped(): return lax.ppermute(shard, ('feat', 'tok'), pairs)]
    ppermute x7, starting transfers between devices: 12.7 us -> 8.97 us  [swapped(): return lax.ppermute(shard, ('feat', 'tok'), pairs)]
  transfers between devices with their start and end apart: 8 -> 8, of which waited for: 5 -> 7; matrix products, arithmetic and copies ran while one was open for 7% -> 5% of each run, Pallas kernels for 6% -> 2%
where the time goes in v7:
time: 30.2 us; the launch traced here: 29.9 us
  waiting for transfers between devices  13.2 us (44%)
  starting transfers between devices  9 us (30%)
  matrix products  2.88 us (10%)
  Pallas kernels  2.74 us (9%)
  between operations  1.99 us (7%)
    ppermute x7, waiting for transfers between devices, swapped(): return lax.ppermute(shard, ('feat', 'tok'), pairs)  13.2 us
    ppermute x7, starting transfers between devices, swapped(): return lax.ppermute(shard, ('feat', 'tok'), pairs)  8.97 us
    pallas_call x1, Pallas kernels, front(): pl.pallas_call(front_kernel, out_shape=(jax.ShapeDtypeStruct((count, slot...  1.52 us
    dot_general x1, matrix products, local(): lax.dot_general(centered, pre_grad, (((0,), (0,)), ((), ())), preferred_e...  1.45 us
    dot_general x1, matrix products, local(): lax.dot_general(code, scaled, (((0,), (0,)), ((), ())), preferred_element...  1.43 us
  transfers between devices with their start and end apart: 8, of which 7 were waited for; matrix products, arithmetic and copies ran while one was open for 5% of the time, Pallas kernels for 2%

profile of v7, /device:TPU:0, one launch (start us, length us, event | category | flops | bytes accessed | tf_op | source)
XLA Modules:
  0.0 29.9 jit_solution(6380309442878715846)
XLA Ops:
  1.9 1.5 %front.1 = (bf16[16,128]{1,0:T(8,128)(2,1)S(1)}, f32[16,128]{1,0:T(8,128)S(1)}, bf16[16,2048]{1,0:T(8,128)(2,1)S(1)}, bf16[128,4096]{1,0:T(8,128)(2,1)S(1)}, bf1...) custom-call(bf16[2,4096]{1,0:T(2,128)(2,1)} %tokens_hbm.1, bf16[4096]{0:T(1024)(128)(2,1)} %bias_hbm.1, f32[16,64]{1,0:T(8,128)} %pre_hbm.1, ...), custom_call_target="tpu_custom_call" | custom-call | flops 1000000 | bytes 1048576 | tf_op jit(solution)/shard_map/front/pallas_call | solution.py:112
  3.5 3.0 %collective-permute-start = (bf16[16,2048]{1,0:T(8,128)(2,1)S(1)}, bf16[16,2048]{1,0:T(8,128)(2,1)S(1)}, u32[]{:S(2)}, u32[]{:S(2)}) collective-permute-start(bf16[16,2048]{1,0:T(8,128)(2,1)S(1)} %get-tuple-element.23.after_ref), channel_id=1, source_target_pairs={{0,2},{1,5},{2,0},{3,7},{4,6},{5,1},{6,4},{7,3},{8,10},{9,13},{10,... | collective-permute-start | bytes 196616 | tf_op jit(solution)/shard_map/ppermute | solution.py:31
  6.5 0.1 collective-permute-start.1
  6.5 0.2 own_part.1
  6.7 2.0 %collective-permute-done = bf16[16,2048]{1,0:T(8,128)(2,1)S(1)} collective-permute-done((bf16[16,2048]{1,0:T(8,128)(2,1)S(1)}, bf16[16,2048]{1,0:T(8,128)(2,1)S(1)}, u32[]{:S(2)}, u32[]{:S(2)}) %collective-permute-start) | collective-permute-done | bytes 65568 | tf_op jit(solution)/shard_map/ppermute | solution.py:31
  8.7 1.5 %collective-permute-done.1.second_ref = bf16[1,2,4096]{2,1,0:T(2,128)(2,1)S(1)} collective-permute-done((bf16[1,2,4096]{2,1,0:T(2,128)(2,1)S(1)}, bf16[1,2,4096]{2,1,0:T(2,128)(2,1)S(1)}, u32[]{:S(2)}, u32[]{:S(2)}) %collective-permute-start.1) | collective-permute-done | bytes 16416 | tf_op jit(solution)/shard_map/ppermute | solution.py:31
  10.2 1.6 %collective-permute-start.2 = (bf16[16,2048]{1,0:T(8,128)(2,1)S(1)}, bf16[16,2048]{1,0:T(8,128)(2,1)S(1)}, u32[]{:S(2)}, u32[]{:S(2)}) collective-permute-start(bf16[16,2048]{1,0:T(8,128)(2,1)S(1)} %convert_element_type.34.after_ref), channel_id=1, source_target_pairs={{0,4},{1,9},{2,6},{3,11},{4,0},{5,13},{6,2},{7,15},{8,12},{9,1},{1... | collective-permute-start | bytes 196616 | tf_op jit(solution)/shard_map/ppermute | solution.py:31
  11.9 0.4 %collective-permute-start.3 = (bf16[2,2,4096]{2,1,0:T(2,128)(2,1)S(1)}, bf16[2,2,4096]{2,1,0:T(2,128)(2,1)S(1)}, u32[]{:S(2)}, u32[]{:S(2)}) collective-permute-start(bf16[2,2,4096]{2,1,0:T(2,128)(2,1)S(1)} %joined.3.first_ref), channel_id=1, source_target_pairs={{0,4},{1,9},{2,6},{3,11},{4,0},{5,13},{6,2},{7,15},{8,12},{9,1},{1... | collective-permute-start | bytes 98312 | tf_op jit(solution)/shard_map/ppermute | solution.py:31
  12.3 2.3 %collective-permute-done.2 = bf16[16,2048]{1,0:T(8,128)(2,1)S(1)} collective-permute-done((bf16[16,2048]{1,0:T(8,128)(2,1)S(1)}, bf16[16,2048]{1,0:T(8,128)(2,1)S(1)}, u32[]{:S(2)}, u32[]{:S(2)}) %collective-permute-start.2) | collective-permute-done | bytes 65568 | tf_op jit(solution)/shard_map/ppermute | solution.py:31
  14.6 1.3 %collective-permute-done.3.second_ref = bf16[2,2,4096]{2,1,0:T(2,128)(2,1)S(1)} collective-permute-done((bf16[2,2,4096]{2,1,0:T(2,128)(2,1)S(1)}, bf16[2,2,4096]{2,1,0:T(2,128)(2,1)S(1)}, u32[]{:S(2)}, u32[]{:S(2)}) %collective-permute-start.3) | collective-permute-done | bytes 32800 | tf_op jit(solution)/shard_map/ppermute | solution.py:31
  15.9 2.5 %collective-permute-start.4 = (bf16[16,2048]{1,0:T(8,128)(2,1)S(1)}, bf16[16,2048]{1,0:T(8,128)(2,1)S(1)}, u32[]{:S(2)}, u32[]{:S(2)}) collective-permute-start(bf16[16,2048]{1,0:T(8,128)(2,1)S(1)} %convert_element_type.36.after_ref), channel_id=1, source_target_pairs={{0,8},{1,3},{2,10},{3,1},{4,12},{5,7},{6,14},{7,5},{8,0},{9,11},{1... | collective-permute-start | bytes 196616 | tf_op jit(solution)/shard_map/ppermute | solution.py:31
  18.4 0.5 %collective-permute-start.6 = (bf16[4,2,4096]{2,1,0:T(2,128)(2,1)S(1)}, bf16[4,2,4096]{2,1,0:T(2,128)(2,1)S(1)}, u32[]{:S(2)}, u32[]{:S(2)}) collective-permute-start(bf16[4,2,4096]{2,1,0:T(2,128)(2,1)S(1)} %joined.4.first_ref), channel_id=1, source_target_pairs={{0,8},{1,3},{2,10},{3,1},{4,12},{5,7},{6,14},{7,5},{8,0},{9,11},{1... | collective-permute-start | bytes 196616 | tf_op jit(solution)/shard_map/ppermute | solution.py:31
  18.9 3.0 %collective-permute-done.4 = bf16[16,2048]{1,0:T(8,128)(2,1)S(1)} collective-permute-done((bf16[16,2048]{1,0:T(8,128)(2,1)S(1)}, bf16[16,2048]{1,0:T(8,128)(2,1)S(1)}, u32[]{:S(2)}, u32[]{:S(2)}) %collective-permute-start.4) | collective-permute-done | bytes 65568 | tf_op jit(solution)/shard_map/ppermute | solution.py:31
  21.9 0.8 %collective-permute-start.5 = (bf16[16,2048]{1,0:T(8,128)(2,1)S(1)}, bf16[16,2048]{1,0:T(8,128)(2,1)S(1)}, u32[]{:S(2)}, u32[]{:S(2)}) collective-permute-start(bf16[16,2048]{1,0:T(8,128)(2,1)S(1)} %multiply_convert_fusion.own_ref.after_ref), channel_id=1, source_target_pairs={{0,2},{1,5},{2,0},{3,7},{4,6},{5,1},{6,4},{7,3},{8,10},{9,13},{10,... | collective-permute-start | bytes 196616 | tf_op jit(solution)/shard_map/ppermute | solution.py:31
  22.7 1.6 %collective-permute-done.6.second_ref = bf16[4,2,4096]{2,1,0:T(2,128)(2,1)S(1)} collective-permute-done((bf16[4,2,4096]{2,1,0:T(2,128)(2,1)S(1)}, bf16[4,2,4096]{2,1,0:T(2,128)(2,1)S(1)}, u32[]{:S(2)}, u32[]{:S(2)}) %collective-permute-start.6) | collective-permute-done | bytes 65568 | tf_op jit(solution)/shard_map/ppermute | solution.py:31
  24.4 0.3 first_product.1.first_ref
  24.7 1.6 %collective-permute-done.5.other_ref = bf16[16,2048]{1,0:T(8,128)(2,1)S(1)} collective-permute-done((bf16[16,2048]{1,0:T(8,128)(2,1)S(1)}, bf16[16,2048]{1,0:T(8,128)(2,1)S(1)}, u32[]{:S(2)}, u32[]{:S(2)}) %collective-permute-start.5) | collective-permute-done | bytes 65568 | tf_op jit(solution)/shard_map/ppermute | solution.py:31
  26.2 0.2 code_half.1
  26.5 0.0 collective-permute-start.7
  26.5 1.4 %convolution_convert_fusion.1 = bf16[128,4096]{1,0:T(8,128)(2,1)} fusion(bf16[16,128]{1,0:T(8,128)(2,1)S(1)} %get-tuple-element.19.code_ref, bf16[16,4096]{1,0:T(8,128)(2,1)S(1)} %get-tuple-element.28), kind=kOutput, calls=%fused_computation.1 | convolution fusion | flops 17301504 | bytes 1183744 | tf_op jit(solution)/shard_map/dot_general | solution.py:310
  27.9 0.0 collective-permute-done.7.theirs_ref
  27.9 0.5 %masked.1 = (bf16[16,128]{1,0:T(8,128)(2,1)S(1)}, f32[1,128]{1,0:T(1,128)}) custom-call(f32[16,128]{1,0:T(8,128)S(1)} %get-tuple-element.31.raw_ref, f32[16,128]{1,0:T(8,128)S(1)} %get-tuple-element.32.mine_ref, f32[16,128]{1,0:T(8,128)S(1)} %collective-permute-done.7.theirs_ref), custom_call_target="tpu_custom_call" | custom-call | flops 100000 | bytes 32768 | tf_op jit(solution)/shard_map/masked/pallas_call | solution.py:267
  28.5 1.5 %convolution_convert_fusion = bf16[4096,128]{1,0:T(8,128)(2,1)} fusion(bf16[16,4096]{1,0:T(8,128)(2,1)S(1)} %subtract_convert_fusion, bf16[16,128]{1,0:T(8,128)(2,1)S(1)} %get-tuple-element.33), kind=kOutput, calls=%fused_computation | convolution fusion | flops 17301504 | bytes 1183744 | tf_op jit(solution)/shard_map/dot_general | solution.py:314
  (11 shorter events, 0.1 us)
Async XLA Ops:
  3.5 5.2 %collective-permute-start = (bf16[16,2048]{1,0:T(8,128)(2,1)S(1)}, bf16[16,2048]{1,0:T(8,128)(2,1)S(1)}, u32[]{:S(2)}, u32[]{:S(2)}) collective-permute-start(bf16[16,2048]{1,0:T(8,128)(2,1)S(1)} %get-tuple-element.23.after_ref), channel_id=1, source_target_pairs={{0,2},{1,5},{2,0},{3,7},{4,6},{5,1},{6,4},{7,3},{8,10},{9,13},{10,... | collective-permute-start | bytes 196616 | tf_op jit(solution)/shard_map/ppermute | solution.py:31
  6.5 3.7 %collective-permute-start.1 = (bf16[1,2,4096]{2,1,0:T(2,128)(2,1)S(1)}, bf16[1,2,4096]{2,1,0:T(2,128)(2,1)S(1)}, u32[]{:S(2)}, u32[]{:S(2)}) collective-permute-start(bf16[1,2,4096]{2,1,0:T(2,128)(2,1)S(1)} %copied.1.first_ref), channel_id=1, source_target_pairs={{0,2},{1,5},{2,0},{3,7},{4,6},{5,1},{6,4},{7,3},{8,10},{9,13},{10,... | collective-permute-start | bytes 49160 | tf_op jit(solution)/shard_map/ppermute | solution.py:31
  10.2 4.4 %collective-permute-start.2 = (bf16[16,2048]{1,0:T(8,128)(2,1)S(1)}, bf16[16,2048]{1,0:T(8,128)(2,1)S(1)}, u32[]{:S(2)}, u32[]{:S(2)}) collective-permute-start(bf16[16,2048]{1,0:T(8,128)(2,1)S(1)} %convert_element_type.34.after_ref), channel_id=1, source_target_pairs={{0,4},{1,9},{2,6},{3,11},{4,0},{5,13},{6,2},{7,15},{8,12},{9,1},{1... | collective-permute-start | bytes 196616 | tf_op jit(solution)/shard_map/ppermute | solution.py:31
  11.9 4.0 %collective-permute-start.3 = (bf16[2,2,4096]{2,1,0:T(2,128)(2,1)S(1)}, bf16[2,2,4096]{2,1,0:T(2,128)(2,1)S(1)}, u32[]{:S(2)}, u32[]{:S(2)}) collective-permute-start(bf16[2,2,4096]{2,1,0:T(2,128)(2,1)S(1)} %joined.3.first_ref), channel_id=1, source_target_pairs={{0,4},{1,9},{2,6},{3,11},{4,0},{5,13},{6,2},{7,15},{8,12},{9,1},{1... | collective-permute-start | bytes 98312 | tf_op jit(solution)/shard_map/ppermute | solution.py:31
  15.9 6.0 %collective-permute-start.4 = (bf16[16,2048]{1,0:T(8,128)(2,1)S(1)}, bf16[16,2048]{1,0:T(8,128)(2,1)S(1)}, u32[]{:S(2)}, u32[]{:S(2)}) collective-permute-start(bf16[16,2048]{1,0:T(8,128)(2,1)S(1)} %convert_element_type.36.after_ref), channel_id=1, source_target_pairs={{0,8},{1,3},{2,10},{3,1},{4,12},{5,7},{6,14},{7,5},{8,0},{9,11},{1... | collective-permute-start | bytes 196616 | tf_op jit(solution)/shard_map/ppermute | solution.py:31
  18.4 5.9 %collective-permute-start.6 = (bf16[4,2,4096]{2,1,0:T(2,128)(2,1)S(1)}, bf16[4,2,4096]{2,1,0:T(2,128)(2,1)S(1)}, u32[]{:S(2)}, u32[]{:S(2)}) collective-permute-start(bf16[4,2,4096]{2,1,0:T(2,128)(2,1)S(1)} %joined.4.first_ref), channel_id=1, source_target_pairs={{0,8},{1,3},{2,10},{3,1},{4,12},{5,7},{6,14},{7,5},{8,0},{9,11},{1... | collective-permute-start | bytes 196616 | tf_op jit(solution)/shard_map/ppermute | solution.py:31
  21.9 4.3 %collective-permute-start.5 = (bf16[16,2048]{1,0:T(8,128)(2,1)S(1)}, bf16[16,2048]{1,0:T(8,128)(2,1)S(1)}, u32[]{:S(2)}, u32[]{:S(2)}) collective-permute-start(bf16[16,2048]{1,0:T(8,128)(2,1)S(1)} %multiply_convert_fusion.own_ref.after_ref), channel_id=1, source_target_pairs={{0,2},{1,5},{2,0},{3,7},{4,6},{5,1},{6,4},{7,3},{8,10},{9,13},{10,... | collective-permute-start | bytes 196616 | tf_op jit(solution)/shard_map/ppermute | solution.py:31
  26.5 1.5 %collective-permute-start.7 = (f32[16,128]{1,0:T(8,128)S(1)}, f32[16,128]{1,0:T(8,128)S(1)}, u32[]{:S(2)}, u32[]{:S(2)}) collective-permute-start(f32[16,128]{1,0:T(8,128)S(1)} %get-tuple-element.32.mine_ref), channel_id=1, source_target_pairs={{0,1},{1,0},{2,3},{3,2},{4,5},{5,4},{6,7},{7,6},{8,9},{9,8},{10,11... | collective-permute-start | bytes 24584 | tf_op jit(solution)/shard_map/ppermute | solution.py:309

commit v8 on v6

v8 whole, which is shorter than its diff:
```python
import functools

import jax
import jax.numpy as jnp
from jax import lax
from jax.experimental import pallas as pl
from jax.experimental.pallas import tpu as pltpu
from jax.sharding import PartitionSpec as P

VMEM = pl.BlockSpec(memory_space=pltpu.VMEM)
SMEM = pl.BlockSpec(memory_space=pltpu.SMEM)
HBM = pl.BlockSpec(memory_space=pltpu.HBM)
ANY = pl.BlockSpec(memory_space=pl.ANY)
ROWS = 16
MERGED = 2


def kernel_call(kernel, out_shape, in_specs, out_specs, tokens, scratch_shapes=()):
    limit = (16 if tokens <= ROWS else 40) * 2**20
    return pl.pallas_call(
        kernel,
        out_shape=out_shape,
        in_specs=in_specs,
        out_specs=out_specs,
        scratch_shapes=scratch_shapes,
        compiler_params=pltpu.CompilerParams(vmem_limit_bytes=limit),
        cost_estimate=pl.CostEstimate(flops=10**6, bytes_accessed=2**20, transcendentals=0),
    )


def shape(*sizes, dtype=jnp.bfloat16):
    return jax.ShapeDtypeStruct(sizes, dtype)


def feat_bits():
    return (lax.axis_size("feat") - 1).bit_length()


def sum_bit(step, core):
    return (step + core) % feat_bits()


def swapped(shard, step):
    cores = lax.axis_size("tok")
    pairs = [
        (f * cores + c, (f ^ 1 << sum_bit(step, c)) * cores + c)
        for f in range(lax.axis_size("feat"))
        for c in range(cores)
    ]
    return lax.ppermute(shard, ("feat", "tok"), pairs)


def halves(width):
    half = width // 2
    bit = lax.axis_index("feat") >> (lax.axis_index("tok") % feat_bits()) & 1
    return (
        pl.multiple_of(bit * half, half),
        pl.multiple_of((1 - bit) * half, half),
        half,
    )


def stacked(rows, pieces):
    width = rows.shape[1] // pieces
    return jnp.concatenate(
        [
            rows[i : i + 1, c * width : (c + 1) * width]
            for i in range(rows.shape[0])
            for c in range(pieces)
        ],
        axis=0,
    )


def share(code, rows_ref, centered_ref, at, half):
    total = jnp.dot(code, rows_ref[:, pl.ds(at, half)], preferred_element_type=jnp.float32)
    rows = centered_ref.shape[0]
    centered = centered_ref[:, pl.ds(at, half)]
    token = lax.broadcasted_iota(jnp.int32, (total.shape[0], 1), 0)
    first = lax.axis_index("feat") * rows
    for i in range(rows):
        total -= jnp.where(token == first + i, centered[i : i + 1, :], 0.0)
    return total


def front_kernel(
    tokens_hbm,
    bias_hbm,
    pre_hbm,
    top_hbm,
    rows_hbm,
    block_ref,
    count_ref,
    code_ref,
    raw_ref,
    sent_ref,
    tokens_block_ref,
    rows_ref,
    centered_ref,
    bias_ref,
    tokens_ref,
    bias_flat,
    pre_ref,
    top_ref,
    sems,
):
    copies = [
        pltpu.make_async_copy(source, target, sems.at[i])
        for i, (source, target) in enumerate(
            (
                (top_hbm, top_ref),
                (pre_hbm, pre_ref),
                (tokens_hbm, tokens_ref),
                (bias_hbm, bias_flat),
                (rows_hbm, rows_ref),
            )
        )
    ]
    for copy in copies:
        copy.start()
    for copy in copies[:2]:
        copy.wait()
    count, latents = top_ref.shape
    slots, width = rows_ref.shape
    offsets = lax.broadcasted_iota(jnp.int32, (1, slots), 1)
    slot_ids = jnp.where(offsets < count_ref[0], block_ref[0] * slots + offsets, -1)
    top, pre = top_ref[...], pre_ref[...]
    raw = jnp.zeros((count, slots), jnp.float32)
    for k in range(latents):
        raw = jnp.where(top[:, k : k + 1] == slot_ids, pre[:, k : k + 1], raw)
    raw_ref[...] = raw
    code = jnp.maximum(raw, 0.0).astype(jnp.bfloat16)
    code_ref[...] = code

    for copy in copies[2:4]:
        copy.wait()
    tokens = tokens_ref[...].astype(jnp.float32)
    pieces = ROWS // tokens.shape[0]
    bias = bias_flat[...].astype(jnp.float32).reshape(1, width)
    bias_ref[...] = stacked(bias, pieces)
    centered_ref[...] = (tokens - bias).astype(jnp.bfloat16).astype(jnp.float32)
    tokens_block = stacked(tokens, pieces).astype(jnp.bfloat16)
    tokens_block_ref[...] = tokens_block

    copies[4].wait()
    _, other, half = halves(width)
    sent_ref[:, :half] = share(code, rows_ref, centered_ref, other, half).astype(jnp.bfloat16)
    if sent_ref.shape[1] > half:
        sent_ref[:, half:] = tokens_block


def front(tokens, b_pre, pre_codes, top_idx, blocks, counts, dict_rows, merged):
    count = top_idx.shape[0]
    slots, width = dict_rows.shape
    pieces = ROWS // tokens.shape[0]
    block = width // pieces
    return kernel_call(
        front_kernel,
        (
            shape(count, slots),
            shape(count, slots, dtype=jnp.float32),
            shape(count, width // 2 + merged * block),
            shape(ROWS, block),
            shape(slots, width),
            shape(*tokens.shape, dtype=jnp.float32),
            shape(pieces, block, dtype=jnp.float32),
        ),
        [HBM] * 5 + [SMEM] * 2,
        (VMEM,) * 7,
        count,
        [
            pltpu.VMEM(tokens.shape, tokens.dtype),
            pltpu.VMEM(b_pre.shape, b_pre.dtype),
            pltpu.VMEM(pre_codes.shape, pre_codes.dtype),
            pltpu.VMEM(top_idx.shape, top_idx.dtype),
            pltpu.SemaphoreType.DMA((5,)),
        ],
    )(
        *(
            pltpu.with_memory_space_constraint(array, pltpu.HBM)
            for array in (tokens, b_pre, pre_codes, top_idx, dict_rows)
        ),
        blocks,
        counts,
    )


def own_kernel(code_ref, rows_ref, centered_ref, total_ref):
    own, _, half = halves(rows_ref.shape[1])
    total_ref[...] = share(code_ref[...], rows_ref, centered_ref, own, half)


def own_part(code, dict_rows, centered):
    count, half = code.shape[0], dict_rows.shape[1] // 2
    return kernel_call(
        own_kernel, shape(count, half, dtype=jnp.float32), [VMEM] * 3, VMEM, count
    )(code, dict_rows, centered)


def added_kernel(total_ref, own_ref, arrived_ref, sum_ref, sent_ref):
    half = total_ref.shape[1]
    total = total_ref[...] + arrived_ref[:, :half].astype(jnp.float32)
    sum_ref[...] = total
    sent_ref[:, :half] = total.astype(jnp.bfloat16)
    if sent_ref.shape[1] > half:
        block = own_ref.shape[1] - half
        sent_ref[:, half : half + block] = own_ref[:, half:]
        sent_ref[:, half + block :] = arrived_ref[:, half:]


def added(total, own, arrived, merged):
    count, half = total.shape
    block = own.shape[1] - half
    return kernel_call(
        added_kernel,
        (
            shape(count, half, dtype=jnp.float32),
            shape(count, half + (2 * block if merged else 0)),
        ),
        [VMEM] * 3,
        (VMEM, VMEM),
        count,
    )(total, own, arrived)


def joined_kernel(skip, first_ref, second_ref, after_ref, out_ref):
    width = first_ref.shape[1] - skip
    out_ref[:, :width] = first_ref[:, skip:]
    out_ref[:, width:] = second_ref[:, skip:]


def joined(first, second, skip, after):
    return kernel_call(
        functools.partial(joined_kernel, skip),
        shape(first.shape[0], 2 * (first.shape[1] - skip)),
        [VMEM, VMEM, ANY],
        VMEM,
        first.shape[0],
    )(first, second, after)


def turned_kernel(own_ref, arrived_ref, bias_ref, after_ref, out_ref):
    pieces, width = bias_ref.shape
    bias = jnp.concatenate([bias_ref[...]] * (ROWS // pieces), axis=0)
    blocks = [
        (ref[:, at : at + width].astype(jnp.float32) - bias).astype(jnp.bfloat16)
        for ref in (own_ref, arrived_ref)
        for at in range(0, ref.shape[1], width)
    ]
    out_ref[...] = jnp.concatenate(blocks, axis=0).astype(jnp.float32).T.astype(jnp.bfloat16)


def turned(own, arrived, bias, after, count):
    blocks = 2 * own.shape[1] // bias.shape[1]
    return kernel_call(
        turned_kernel,
        shape(bias.shape[1], blocks * ROWS),
        [VMEM, VMEM, VMEM, ANY],
        VMEM,
        count,
    )(own, arrived, bias, after)


def product(part_ref, rows_ref, at, half):
    return lax.dot_general(
        part_ref[...],
        rows_ref[:, pl.ds(at, half)],
        (((1,), (1,)), ((), ())),
        preferred_element_type=jnp.float32,
    )


def first_product_kernel(own_ref, rows_ref, half_ref):
    own, _, half = halves(rows_ref.shape[1])
    half_ref[...] = product(own_ref, rows_ref, own, half)


def first_product(scaled_own, dict_rows):
    count = scaled_own.shape[0]
    return kernel_call(
        first_product_kernel,
        shape(count, dict_rows.shape[0], dtype=jnp.float32),
        [VMEM] * 2,
        VMEM,
        count,
    )(scaled_own, dict_rows)


def code_half_kernel(own_ref, other_ref, first_ref, rows_ref, half_ref, scaled_ref):
    own, other, half = halves(rows_ref.shape[1])
    half_ref[...] = first_ref[...] + product(other_ref, rows_ref, other, half)
    scaled_ref[:, pl.ds(own, half)] = own_ref[...]
    scaled_ref[:, pl.ds(other, half)] = other_ref[...]


def code_half_of(scaled_own, scaled_other, first, dict_rows):
    count = scaled_own.shape[0]
    slots, width = dict_rows.shape
    return kernel_call(
        code_half_kernel,
        (shape(count, slots, dtype=jnp.float32), shape(count, width)),
        [VMEM] * 4,
        (VMEM, VMEM),
        count,
    )(scaled_own, scaled_other, first, dict_rows)


def final_kernel(
    rows, raw_ref, mine_ref, theirs_ref, turned_ref, enc_hbm, benc_ref, enc_ref, sems
):
    count, slots = raw_ref.shape
    width, depth = turned_ref.shape
    pieces = ROWS // rows
    code_grad = mine_ref[...] + theirs_ref[...]
    pre_grad = jnp.where(raw_ref[...] > 0.0, code_grad, 0.0).astype(jnp.bfloat16)
    place = lax.broadcasted_iota(jnp.int32, (depth, count), 0)
    token = lax.broadcasted_iota(jnp.int32, (depth, count), 1)
    core = lax.axis_index("tok")
    block = place // ROWS
    distance = jnp.zeros_like(place)
    for step in range(feat_bits()):
        distance |= (block >> step & 1) << sum_bit(step, core)
    source = (lax.axis_index("feat") ^ distance) * rows + place % ROWS // pieces
    order = jnp.where(token == source, 1.0, 0.0).astype(jnp.bfloat16)
    spread = jnp.dot(order, pre_grad, preferred_element_type=jnp.float32)
    piece = lax.broadcasted_iota(jnp.int32, (depth, slots), 0) % pieces
    copies = []
    for c in range(0, pieces, 2):
        pair = [jnp.where(piece == c + i, spread, 0.0).astype(jnp.bfloat16) for i in range(2)]
        out = jnp.dot(
            turned_ref[...],
            jnp.concatenate(pair, axis=1),
            preferred_element_type=jnp.float32,
        ).astype(jnp.bfloat16)
        for i in range(2):
            enc_ref[(c + i) * width : (c + i + 1) * width, :] = out[:, i * slots : (i + 1) * slots]
        part = pl.ds(c * width, 2 * width)
        copies.append(pltpu.make_async_copy(enc_ref.at[part], enc_hbm.at[part], sems.at[c // 2]))
        copies[-1].start()
    benc_ref[...] = jnp.sum(pre_grad.astype(jnp.float32), axis=0, keepdims=True)
    for copy in copies:
        copy.wait()


def final(raw, mine, theirs, turned_tokens, rows):
    count, slots = raw.shape
    pieces = ROWS // rows
    width = turned_tokens.shape[0] * pieces
    return kernel_call(
        functools.partial(final_kernel, rows),
        (shape(width, slots), shape(1, slots, dtype=jnp.float32)),
        [VMEM] * 4,
        (HBM, VMEM),
        count,
        [pltpu.VMEM((width, slots), jnp.bfloat16), pltpu.SemaphoreType.DMA((pieces // 2,))],
    )(raw, mine, theirs, turned_tokens)


def local(tokens, b_pre, pre_codes, top_idx, blocks, counts, dict_rows):
    rows, count = tokens.shape[0], top_idx.shape[0]
    half = dict_rows.shape[1] // 2
    steps = feat_bits()
    merged = min(MERGED, steps - 1) if count == ROWS else 0

    code, raw, sent, block, dict_rows, centered, bias = front(
        tokens, b_pre, pre_codes, top_idx, blocks, counts, dict_rows, merged > 0
    )
    for step in range(steps):
        arrived = swapped(sent, step)
        if step == 0:
            total = own_part(code, dict_rows, centered)
        if step >= merged:
            if step == merged > 0:
                block = joined(own, previous, half, sent)
            elif step > 0:
                block = joined(block, arrived_block, 0, sent)
            arrived_block = swapped(block, step)
        if step < steps - 1:
            own, previous = sent, arrived
            total, sent = added(total, own, arrived, step + 1 < merged)
    total = total + arrived.astype(jnp.float32)
    scaled_own = (0.25 * total).astype(jnp.bfloat16)
    scaled_other = swapped(scaled_own, 0)

    first = first_product(scaled_own, dict_rows)
    turned_tokens = turned(block, arrived_block, bias, scaled_own, count)

    code_half, scaled = code_half_of(scaled_own, scaled_other, first, dict_rows)
    theirs = lax.ppermute(code_half, "tok", [(i, 1 - i) for i in range(2)])
    grad_rows = lax.dot_general(
        code, scaled, (((0,), (0,)), ((), ())), preferred_element_type=jnp.float32
    ).astype(jnp.bfloat16)
    grad_enc, grad_benc = final(raw, code_half, theirs, turned_tokens, rows)
    return (grad_rows, grad_enc, grad_benc.reshape(-1))


def solution(mesh):
    return jax.shard_map(
        local,
        mesh=mesh,
        in_specs=(
            P(("grp", "feat"), "tok"),
            P(("grp", "tok")),
            P("grp", None),
            P("grp", None),
            P(("grp", "feat")),
            P(("grp", "feat")),
            P(("grp", "feat"), "tok"),
        ),
        out_specs=(P(("grp", "feat"), "tok"), P(("grp", "tok"), "feat"), P(("grp", "feat"))),
        check_vma=False,
    )
```

time: 30.9 us -> 28.9 us (0.935)
  the two profiles are of different devices: /device:TPU:0 before, /device:TPU:31 now
where the time goes in v8:
time: 28.9 us; the launch traced here: 28.6 us
  waiting for transfers between devices  13.3 us (46%)
  starting transfers between devices  7.16 us (25%)
  Pallas kernels  4.72 us (16%)
  between operations  1.97 us (7%)
  matrix products  1.43 us (5%)
    ppermute x5, waiting for transfers between devices, swapped(): return lax.ppermute(shard, ('feat', 'tok'), pairs)  13.3 us
    ppermute x1, starting transfers between devices, local(): theirs = lax.ppermute(code_half, 'tok', [(i, 1 - i) for i in range(2)])  5.2 us
    ppermute x5, starting transfers between devices, swapped(): return lax.ppermute(shard, ('feat', 'tok'), pairs)  1.96 us
    pallas_call x1, Pallas kernels, front(): kernel_call(front_kernel, (shape(count, slots), shape(count, slots, dtype...  1.96 us
    pallas_call x1, Pallas kernels, final(): kernel_call(functools.partial(final_kernel, rows), (shape(width, slots),...  1.94 us
    dot_general x1, matrix products, local(): lax.dot_general(code, scaled, (((0,), (0,)), ((), ())), preferred_element...  1.43 us
  transfers between devices with their start and end apart: 6, of which 5 were waited for; matrix products, arithmetic and copies ran while one was open for 5% of the time, Pallas kernels for 2%

profile of v8, /device:TPU:31, one launch (start us, length us, event | category | flops | bytes accessed | tf_op | source)
XLA Modules:
  0.0 28.6 jit_solution(18128040003253328658)
XLA Ops:
  1.9 2.0 %shard_map.94 = (bf16[16,128]{1,0:T(8,128)(2,1)S(1)}, f32[16,128]{1,0:T(8,128)S(1)}, bf16[16,2560]{1,0:T(8,128)(2,1)S(1)}, bf16[16,512]{1,0:T(8,128)(2,1)}, bf16...) custom-call(bf16[2,4096]{1,0:T(2,128)(2,1)} %tokens_hbm.1, bf16[4096]{0:T(1024)(128)(2,1)} %bias_hbm.1, ...), custom_call_target="tpu_custom_call" | custom-call | flops 1000000 | bytes 1048576 | tf_op jit(solution)/shard_map/pallas_call | solution.py:157
  3.9 0.2 collective-permute-start
  4.1 0.2 shard_map.95.total_ref
  4.3 2.9 %collective-permute-done.arrived_ref = bf16[16,2560]{1,0:T(8,128)(2,1)S(1)} collective-permute-done((bf16[16,2560]{1,0:T(8,128)(2,1)S(1)}, bf16[16,2560]{1,0:T(8,128)(2,1)S(1)}, u32[]{:S(2)}, u32[]{:S(2)}) %collective-permute-start) | collective-permute-done | bytes 81952 | tf_op jit(solution)/shard_map/ppermute | solution.py:50
  7.3 0.1 collective-permute-start.1
  7.4 5.3 %collective-permute-done.1.arrived_ref.second_ref = bf16[16,3072]{1,0:T(8,128)(2,1)S(1)} collective-permute-done((bf16[16,3072]{1,0:T(8,128)(2,1)S(1)}, bf16[16,3072]{1,0:T(8,128)(2,1)S(1)}, u32[]{:S(2)}, u32[]{:S(2)}) %collective-permute-start.1) | collective-permute-done | bytes 98336 | tf_op jit(solution)/shard_map/ppermute | solution.py:50
  12.7 0.3 %collective-permute-start.2 = (bf16[16,2048]{1,0:T(8,128)(2,1)S(1)}, bf16[16,2048]{1,0:T(8,128)(2,1)S(1)}, u32[]{:S(2)}, u32[]{:S(2)}) collective-permute-start(bf16[16,2048]{1,0:T(8,128)(2,1)S(1)} %get-tuple-element.24.after_ref), channel_id=1, source_target_pairs={{0,8},{1,3},{2,10},{3,1},{4,12},{5,7},{6,14},{7,5},{8,0},{9,11},{1... | collective-permute-start | bytes 196616 | tf_op jit(solution)/shard_map/ppermute | solution.py:50
  13.1 1.2 %collective-permute-start.5 = (bf16[16,2048]{1,0:T(8,128)(2,1)S(1)}, bf16[16,2048]{1,0:T(8,128)(2,1)S(1)}, u32[]{:S(2)}, u32[]{:S(2)}) collective-permute-start(bf16[16,2048]{1,0:T(8,128)(2,1)S(1)} %shard_map.100.own_ref), channel_id=1, source_target_pairs={{0,8},{1,3},{2,10},{3,1},{4,12},{5,7},{6,14},{7,5},{8,0},{9,11},{1... | collective-permute-start | bytes 196616 | tf_op jit(solution)/shard_map/ppermute | solution.py:50
  14.3 1.6 %collective-permute-done.2 = bf16[16,2048]{1,0:T(8,128)(2,1)S(1)} collective-permute-done((bf16[16,2048]{1,0:T(8,128)(2,1)S(1)}, bf16[16,2048]{1,0:T(8,128)(2,1)S(1)}, u32[]{:S(2)}, u32[]{:S(2)}) %collective-permute-start.2) | collective-permute-done | bytes 65568 | tf_op jit(solution)/shard_map/ppermute | solution.py:50
  15.9 0.1 collective-permute-start.3
  16.0 0.3 shard_map.98.first_ref
  16.3 0.3 %collective-permute-done.5.arrived_ref = bf16[16,2048]{1,0:T(8,128)(2,1)S(1)} collective-permute-done((bf16[16,2048]{1,0:T(8,128)(2,1)S(1)}, bf16[16,2048]{1,0:T(8,128)(2,1)S(1)}, u32[]{:S(2)}, u32[]{:S(2)}) %collective-permute-start.5) | collective-permute-done | bytes 65568 | tf_op jit(solution)/shard_map/ppermute | solution.py:50
  16.6 0.1 shard_map.101.turned_ref
  16.7 3.1 %collective-permute-done.3.other_ref = bf16[16,2048]{1,0:T(8,128)(2,1)S(1)} collective-permute-done((bf16[16,2048]{1,0:T(8,128)(2,1)S(1)}, bf16[16,2048]{1,0:T(8,128)(2,1)S(1)}, u32[]{:S(2)}, u32[]{:S(2)}) %collective-permute-start.3) | collective-permute-done | bytes 65568 | tf_op jit(solution)/shard_map/ppermute | solution.py:50
  19.8 0.2 shard_map.99
  20.1 5.2 %collective-permute-start.4 = (f32[16,128]{1,0:T(8,128)S(1)}, f32[16,128]{1,0:T(8,128)S(1)}, u32[]{:S(2)}, u32[]{:S(2)}) collective-permute-start(f32[16,128]{1,0:T(8,128)S(1)} %get-tuple-element.27.mine_ref), channel_id=1, source_target_pairs={{0,1},{1,0},{2,3},{3,2},{4,5},{5,4},{6,7},{7,6},{8,9},{9,8},{10,11... | collective-permute-start | bytes 24584 | tf_op jit(solution)/shard_map/ppermute | solution.py:389
  25.3 1.4 %convolution_convert_fusion = bf16[128,4096]{1,0:T(8,128)(2,1)} fusion(bf16[16,128]{1,0:T(8,128)(2,1)S(1)} %get-tuple-element.17.code_ref, bf16[16,4096]{1,0:T(8,128)(2,1)S(1)} %get-tuple-element.25), kind=kOutput, calls=%fused_computation | convolution fusion | flops 17301504 | bytes 1183744 | tf_op jit(solution)/shard_map/dot_general | solution.py:390
  26.7 0.0 collective-permute-done.4.theirs_ref
  26.7 1.9 %shard_map.102 = (bf16[4096,128]{1,0:T(8,128)(2,1)}, f32[1,128]{1,0:T(1,128)}) custom-call(f32[16,128]{1,0:T(8,128)S(1)} %get-tuple-element.26.raw_ref, f32[16,128]{1,0:T(8,128)S(1)} %get-tuple-element.27.mine_ref, f32[16,128]{1,0:T(8,128)S(1)} %collective-permute-done.4.theirs_ref, bf16[512,128]{1,0:T(8,128)(2,1)S(1)} %shard_map.101.turned_ref), custom_call_target="tpu_custom_call" | custom-call | flops 1000000 | bytes 1048576 | tf_op jit(solution)/shard_map/pallas_call | solution.py:349
  (4 shorter events, 0.1 us)
Async XLA Ops:
  3.9 3.4 %collective-permute-start = (bf16[16,2560]{1,0:T(8,128)(2,1)S(1)}, bf16[16,2560]{1,0:T(8,128)(2,1)S(1)}, u32[]{:S(2)}, u32[]{:S(2)}) collective-permute-start(bf16[16,2560]{1,0:T(8,128)(2,1)S(1)} %get-tuple-element.20.own_ref), channel_id=1, source_target_pairs={{0,2},{1,5},{2,0},{3,7},{4,6},{5,1},{6,4},{7,3},{8,10},{9,13},{10,... | collective-permute-start | bytes 245768 | tf_op jit(solution)/shard_map/ppermute | solution.py:50
  7.3 5.4 %collective-permute-start.1 = (bf16[16,3072]{1,0:T(8,128)(2,1)S(1)}, bf16[16,3072]{1,0:T(8,128)(2,1)S(1)}, u32[]{:S(2)}, u32[]{:S(2)}) collective-permute-start(bf16[16,3072]{1,0:T(8,128)(2,1)S(1)} %get-tuple-element.22.own_ref.first_ref), channel_id=1, source_target_pairs={{0,4},{1,9},{2,6},{3,11},{4,0},{5,13},{6,2},{7,15},{8,12},{9,1},{1... | collective-permute-start | bytes 294920 | tf_op jit(solution)/shard_map/ppermute | solution.py:50
  12.7 3.2 %collective-permute-start.2 = (bf16[16,2048]{1,0:T(8,128)(2,1)S(1)}, bf16[16,2048]{1,0:T(8,128)(2,1)S(1)}, u32[]{:S(2)}, u32[]{:S(2)}) collective-permute-start(bf16[16,2048]{1,0:T(8,128)(2,1)S(1)} %get-tuple-element.24.after_ref), channel_id=1, source_target_pairs={{0,8},{1,3},{2,10},{3,1},{4,12},{5,7},{6,14},{7,5},{8,0},{9,11},{1... | collective-permute-start | bytes 196616 | tf_op jit(solution)/shard_map/ppermute | solution.py:50
  13.1 3.6 %collective-permute-start.5 = (bf16[16,2048]{1,0:T(8,128)(2,1)S(1)}, bf16[16,2048]{1,0:T(8,128)(2,1)S(1)}, u32[]{:S(2)}, u32[]{:S(2)}) collective-permute-start(bf16[16,2048]{1,0:T(8,128)(2,1)S(1)} %shard_map.100.own_ref), channel_id=1, source_target_pairs={{0,8},{1,3},{2,10},{3,1},{4,12},{5,7},{6,14},{7,5},{8,0},{9,11},{1... | collective-permute-start | bytes 196616 | tf_op jit(solution)/shard_map/ppermute | solution.py:50
  15.9 3.9 %collective-permute-start.3 = (bf16[16,2048]{1,0:T(8,128)(2,1)S(1)}, bf16[16,2048]{1,0:T(8,128)(2,1)S(1)}, u32[]{:S(2)}, u32[]{:S(2)}) collective-permute-start(bf16[16,2048]{1,0:T(8,128)(2,1)S(1)} %multiply_convert_fusion.own_ref.after_ref), channel_id=1, source_target_pairs={{0,2},{1,5},{2,0},{3,7},{4,6},{5,1},{6,4},{7,3},{8,10},{9,13},{10,... | collective-permute-start | bytes 196616 | tf_op jit(solution)/shard_map/ppermute | solution.py:50
  20.1 6.6 %collective-permute-start.4 = (f32[16,128]{1,0:T(8,128)S(1)}, f32[16,128]{1,0:T(8,128)S(1)}, u32[]{:S(2)}, u32[]{:S(2)}) collective-permute-start(f32[16,128]{1,0:T(8,128)S(1)} %get-tuple-element.27.mine_ref), channel_id=1, source_target_pairs={{0,1},{1,0},{2,3},{3,2},{4,5},{5,4},{6,7},{7,6},{8,9},{9,8},{10,11... | collective-permute-start | bytes 24584 | tf_op jit(solution)/shard_map/ppermute | solution.py:389

commit v9 on v8

--- a/solution.py
+++ b/solution.py
@@ -10,9 +10,7 @@
 VMEM = pl.BlockSpec(memory_space=pltpu.VMEM)
 SMEM = pl.BlockSpec(memory_space=pltpu.SMEM)
 HBM = pl.BlockSpec(memory_space=pltpu.HBM)
-ANY = pl.BlockSpec(memory_space=pl.ANY)
 ROWS = 16
-MERGED = 2
 
 
 def kernel_call(kernel, out_shape, in_specs, out_specs, tokens, scratch_shapes=()):
@@ -40,10 +38,17 @@
     return (step + core) % feat_bits()
 
 
-def swapped(shard, step):
+def token_bit(step, core):
+    last = feat_bits() - 1
+    order = [sum_bit(at, core) for at in range(last + 1)]
+    order.remove(last)
+    return ([last] + order)[step]
+
+
+def swapped(shard, bit_of, step):
     cores = lax.axis_size("tok")
     pairs = [
-        (f * cores + c, (f ^ 1 << sum_bit(step, c)) * cores + c)
+        (f * cores + c, (f ^ 1 << bit_of(step, c)) * cores + c)
         for f in range(lax.axis_size("feat"))
         for c in range(cores)
     ]
@@ -94,11 +99,10 @@
     code_ref,
     raw_ref,
     sent_ref,
-    tokens_block_ref,
     rows_ref,
     centered_ref,
+    tokens_ref,
     bias_ref,
-    tokens_ref,
     bias_flat,
     pre_ref,
     top_ref,
@@ -135,41 +139,33 @@
     for copy in copies[2:4]:
         copy.wait()
     tokens = tokens_ref[...].astype(jnp.float32)
-    pieces = ROWS // tokens.shape[0]
     bias = bias_flat[...].astype(jnp.float32).reshape(1, width)
-    bias_ref[...] = stacked(bias, pieces)
+    bias_ref[...] = bias
     centered_ref[...] = (tokens - bias).astype(jnp.bfloat16).astype(jnp.float32)
-    tokens_block = stacked(tokens, pieces).astype(jnp.bfloat16)
-    tokens_block_ref[...] = tokens_block
 
     copies[4].wait()
     _, other, half = halves(width)
-    sent_ref[:, :half] = share(code, rows_ref, centered_ref, other, half).astype(jnp.bfloat16)
-    if sent_ref.shape[1] > half:
-        sent_ref[:, half:] = tokens_block
-
-
-def front(tokens, b_pre, pre_codes, top_idx, blocks, counts, dict_rows, merged):
+    sent_ref[...] = share(code, rows_ref, centered_ref, other, half).astype(jnp.bfloat16)
+
+
+def front(tokens, b_pre, pre_codes, top_idx, blocks, counts, dict_rows):
     count = top_idx.shape[0]
     slots, width = dict_rows.shape
-    pieces = ROWS // tokens.shape[0]
-    block = width // pieces
     return kernel_call(
         front_kernel,
         (
             shape(count, slots),
             shape(count, slots, dtype=jnp.float32),
-            shape(count, width // 2 + merged * block),
-            shape(ROWS, block),
+            shape(count, width // 2),
             shape(slots, width),
             shape(*tokens.shape, dtype=jnp.float32),
-            shape(pieces, block, dtype=jnp.float32),
+            shape(*tokens.shape),
+            shape(1, width, dtype=jnp.float32),
         ),
         [HBM] * 5 + [SMEM] * 2,
         (VMEM,) * 7,
         count,
         [
-            pltpu.VMEM(tokens.shape, tokens.dtype),
             pltpu.VMEM(b_pre.shape, b_pre.dtype),
             pltpu.VMEM(pre_codes.shape, pre_codes.dtype),
             pltpu.VMEM(top_idx.shape, top_idx.dtype),
@@ -197,49 +193,28 @@
     )(code, dict_rows, centered)
 
 
-def added_kernel(total_ref, own_ref, arrived_ref, sum_ref, sent_ref):
-    half = total_ref.shape[1]
-    total = total_ref[...] + arrived_ref[:, :half].astype(jnp.float32)
-    sum_ref[...] = total
-    sent_ref[:, :half] = total.astype(jnp.bfloat16)
-    if sent_ref.shape[1] > half:
-        block = own_ref.shape[1] - half
-        sent_ref[:, half : half + block] = own_ref[:, half:]
-        sent_ref[:, half + block :] = arrived_ref[:, half:]
-
-
-def added(total, own, arrived, merged):
-    count, half = total.shape
-    block = own.shape[1] - half
-    return kernel_call(
-        added_kernel,
-        (
-            shape(count, half, dtype=jnp.float32),
-            shape(count, half + (2 * block if merged else 0)),
-        ),
+def pieces_kernel(own_ref, arrived_ref, bias_ref, block_ref, pieces_ref):
+    pieces, width = pieces_ref.shape
+    for i, ref in enumerate((own_ref, arrived_ref)):
+        block_ref[:, i * width : (i + 1) * width] = stacked(
+            ref[...].astype(jnp.float32), pieces
+        ).astype(jnp.bfloat16)
+    pieces_ref[...] = stacked(bias_ref[...], pieces)
+
+
+def in_pieces(own, arrived, bias, count):
+    pieces = ROWS // own.shape[0]
+    width = own.shape[1] // pieces
+    return kernel_call(
+        pieces_kernel,
+        (shape(ROWS, 2 * width), shape(pieces, width, dtype=jnp.float32)),
         [VMEM] * 3,
         (VMEM, VMEM),
         count,
-    )(total, own, arrived)
-
-
-def joined_kernel(skip, first_ref, second_ref, after_ref, out_ref):
-    width = first_ref.shape[1] - skip
-    out_ref[:, :width] = first_ref[:, skip:]
-    out_ref[:, width:] = second_ref[:, skip:]
-
-
-def joined(first, second, skip, after):
-    return kernel_call(
-        functools.partial(joined_kernel, skip),
-        shape(first.shape[0], 2 * (first.shape[1] - skip)),
-        [VMEM, VMEM, ANY],
-        VMEM,
-        first.shape[0],
-    )(first, second, after)
-
-
-def turned_kernel(own_ref, arrived_ref, bias_ref, after_ref, out_ref):
+    )(own, arrived, bias)
+
+
+def turned_kernel(own_ref, arrived_ref, bias_ref, out_ref):
     pieces, width = bias_ref.shape
     bias = jnp.concatenate([bias_ref[...]] * (ROWS // pieces), axis=0)
     blocks = [
@@ -250,15 +225,15 @@
     out_ref[...] = jnp.concatenate(blocks, axis=0).astype(jnp.float32).T.astype(jnp.bfloat16)
 
 
-def turned(own, arrived, bias, after, count):
+def turned(own, arrived, bias, count):
     blocks = 2 * own.shape[1] // bias.shape[1]
     return kernel_call(
         turned_kernel,
         shape(bias.shape[1], blocks * ROWS),
-        [VMEM, VMEM, VMEM, ANY],
+        [VMEM] * 3,
         VMEM,
         count,
-    )(own, arrived, bias, after)
+    )(own, arrived, bias)
 
 
 def product(part_ref, rows_ref, at, half):
@@ -319,7 +294,10 @@
     block = place // ROWS
     distance = jnp.zeros_like(place)
     for step in range(feat_bits()):
-        distance |= (block >> step & 1) << sum_bit(step, core)
+        bit = sum(
+            jnp.where(core == c, token_bit(step, c), 0) for c in range(lax.axis_size("tok"))
+        )
+        distance |= (block >> step & 1) << bit
     source = (lax.axis_index("feat") ^ distance) * rows + place % ROWS // pieces
     order = jnp.where(token == source, 1.0, 0.0).astype(jnp.bfloat16)
     spread = jnp.dot(order, pre_grad, preferred_element_type=jnp.float32)
@@ -358,32 +336,28 @@
 
 def local(tokens, b_pre, pre_codes, top_idx, blocks, counts, dict_rows):
     rows, count = tokens.shape[0], top_idx.shape[0]
-    half = dict_rows.shape[1] // 2
-    steps = feat_bits()
-    merged = min(MERGED, steps - 1) if count == ROWS else 0
-
-    code, raw, sent, block, dict_rows, centered, bias = front(
-        tokens, b_pre, pre_codes, top_idx, blocks, counts, dict_rows, merged > 0
-    )
-    for step in range(steps):
-        arrived = swapped(sent, step)
+    last = feat_bits() - 1
+    arrived_tokens = swapped(tokens, token_bit, 0)
+    code, raw, sent, dict_rows, centered, tokens, bias = front(
+        tokens, b_pre, pre_codes, top_idx, blocks, counts, dict_rows
+    )
+    sent, arrived_tokens = lax.optimization_barrier((sent, arrived_tokens))
+    for step in range(last + 1):
+        arrived = swapped(sent, sum_bit, step)
         if step == 0:
             total = own_part(code, dict_rows, centered)
-        if step >= merged:
-            if step == merged > 0:
-                block = joined(own, previous, half, sent)
-            elif step > 0:
-                block = joined(block, arrived_block, 0, sent)
-            arrived_block = swapped(block, step)
-        if step < steps - 1:
-            own, previous = sent, arrived
-            total, sent = added(total, own, arrived, step + 1 < merged)
-    total = total + arrived.astype(jnp.float32)
+            block, bias = in_pieces(tokens, arrived_tokens, bias, count)
+        elif step < last:
+            block = jnp.concatenate([block, arrived_block], axis=1)
+        if step < last:
+            arrived_block = swapped(block, token_bit, step + 1)
+        total = total + arrived.astype(jnp.float32)
+        sent = total.astype(jnp.bfloat16)
     scaled_own = (0.25 * total).astype(jnp.bfloat16)
-    scaled_other = swapped(scaled_own, 0)
+    scaled_other = swapped(scaled_own, sum_bit, 0)
 
     first = first_product(scaled_own, dict_rows)
-    turned_tokens = turned(block, arrived_block, bias, scaled_own, count)
+    turned_tokens = turned(block, arrived_block, bias, count)
 
     code_half, scaled = code_half_of(scaled_own, scaled_other, first, dict_rows)
     theirs = lax.ppermute(code_half, "tok", [(i, 1 - i) for i in range(2)])

time: 28.9 us -> 29.9 us (1.035)
  the two profiles are of different devices: /device:TPU:31 before, /device:TPU:0 now
where the time goes in v9:
time: 29.9 us; the launch traced here: 29.6 us
  starting transfers between devices  13.1 us (44%)
  waiting for transfers between devices  8.72 us (29%)
  Pallas kernels  4.29 us (14%)
  between operations  1.99 us (7%)
  matrix products  1.42 us (5%)
    ppermute x7, starting transfers between devices, swapped(): return lax.ppermute(shard, ('feat', 'tok'), pairs)  13.1 us
    ppermute x7, waiting for transfers between devices, swapped(): return lax.ppermute(shard, ('feat', 'tok'), pairs)  8.72 us
    pallas_call x1, Pallas kernels, final(): kernel_call(functools.partial(final_kernel, rows), (shape(width, slots),...  1.94 us
    pallas_call x1, Pallas kernels, front(): kernel_call(front_kernel, (shape(count, slots), shape(count, slots, dtype...  1.53 us
    dot_general x1, matrix products, local(): lax.dot_general(code, scaled, (((0,), (0,)), ((), ())), preferred_element...  1.42 us
  transfers between devices with their start and end apart: 8, of which 4 were waited for; matrix products, arithmetic and copies ran while one was open for 5% of the time, Pallas kernels for 7%

profile of v9, /device:TPU:0, one launch (start us, length us, event | category | flops | bytes accessed | tf_op | source)
XLA Modules:
  0.0 29.6 jit_solution(9303545335614297582)
XLA Ops:
  0.6 4.1 %collective-permute-start = (bf16[2,4096]{1,0:T(2,128)(2,1)}, bf16[2,4096]{1,0:T(2,128)(2,1)S(1)}, u32[]{:S(2)}, u32[]{:S(2)}) collective-permute-start(bf16[2,4096]{1,0:T(2,128)(2,1)} %tokens_hbm.1), channel_id=1, source_target_pairs={{0,8},{1,9},{2,10},{3,11},{4,12},{5,13},{6,14},{7,15},{8,0},{9,1},... | collective-permute-start | bytes 49160 | tf_op jit(solution)/shard_map/ppermute | solution.py:55
  6.0 1.5 %shard_map.94 = (bf16[16,128]{1,0:T(8,128)(2,1)S(1)}, f32[16,128]{1,0:T(8,128)S(1)}, bf16[16,2048]{1,0:T(8,128)(2,1)S(1)}, bf16[128,4096]{1,0:T(8,128)(2,1)S(1)}...) custom-call(bf16[2,4096]{1,0:T(2,128)(2,1)} %tokens_hbm.1, bf16[4096]{0:T(1024)(128)(2,1)} %bias_hbm.1, ...), custom_call_target="tpu_custom_call" | custom-call | flops 1000000 | bytes 1048576 | tf_op jit(solution)/shard_map/pallas_call | solution.py:154
  7.6 0.0 collective-permute-done.arrived_ref
  7.6 1.6 %collective-permute-start.1 = (bf16[16,2048]{1,0:T(8,128)(2,1)S(1)}, bf16[16,2048]{1,0:T(8,128)(2,1)S(1)}, u32[]{:S(2)}, u32[]{:S(2)}) collective-permute-start(bf16[16,2048]{1,0:T(8,128)(2,1)S(1)} %get-tuple-element.22), channel_id=1, source_target_pairs={{0,2},{1,5},{2,0},{3,7},{4,6},{5,1},{6,4},{7,3},{8,10},{9,13},{10,... | collective-permute-start | bytes 196616 | tf_op jit(solution)/shard_map/ppermute | solution.py:55
  9.1 0.2 shard_map.95
  9.4 0.6 %collective-permute-start.6 = (bf16[16,1024]{1,0:T(8,128)(2,1)S(1)}, bf16[16,1024]{1,0:T(8,128)(2,1)S(1)}, u32[]{:S(2)}, u32[]{:S(2)}) collective-permute-start(bf16[16,1024]{1,0:T(8,128)(2,1)S(1)} %get-tuple-element.29), channel_id=1, source_target_pairs={{0,2},{1,5},{2,0},{3,7},{4,6},{5,1},{6,4},{7,3},{8,10},{9,13},{10,... | collective-permute-start | bytes 98312 | tf_op jit(solution)/shard_map/ppermute | solution.py:55
  10.0 1.9 %collective-permute-done.1 = bf16[16,2048]{1,0:T(8,128)(2,1)S(1)} collective-permute-done((bf16[16,2048]{1,0:T(8,128)(2,1)S(1)}, bf16[16,2048]{1,0:T(8,128)(2,1)S(1)}, u32[]{:S(2)}, u32[]{:S(2)}) %collective-permute-start.1) | collective-permute-done | bytes 65568 | tf_op jit(solution)/shard_map/ppermute | solution.py:55
  11.9 1.6 %collective-permute-start.2 = (bf16[16,2048]{1,0:T(8,128)(2,1)S(1)}, bf16[16,2048]{1,0:T(8,128)(2,1)S(1)}, u32[]{:S(2)}, u32[]{:S(2)}) collective-permute-start(bf16[16,2048]{1,0:T(8,128)(2,1)S(1)} %fusion), channel_id=1, source_target_pairs={{0,4},{1,9},{2,6},{3,11},{4,0},{5,13},{6,2},{7,15},{8,12},{9,1},{1... | collective-permute-start | bytes 196616 | tf_op jit(solution)/shard_map/ppermute | solution.py:55
  13.6 2.7 %collective-permute-done.2 = bf16[16,2048]{1,0:T(8,128)(2,1)S(1)} collective-permute-done((bf16[16,2048]{1,0:T(8,128)(2,1)S(1)}, bf16[16,2048]{1,0:T(8,128)(2,1)S(1)}, u32[]{:S(2)}, u32[]{:S(2)}) %collective-permute-start.2) | collective-permute-done | bytes 65568 | tf_op jit(solution)/shard_map/ppermute | solution.py:55
  16.3 2.0 %collective-permute-start.3 = (bf16[16,2048]{1,0:T(8,128)(2,1)S(1)}, bf16[16,2048]{1,0:T(8,128)(2,1)S(1)}, u32[]{:S(2)}, u32[]{:S(2)}) collective-permute-start(bf16[16,2048]{1,0:T(8,128)(2,1)S(1)} %fusion.1), channel_id=1, source_target_pairs={{0,8},{1,3},{2,10},{3,1},{4,12},{5,7},{6,14},{7,5},{8,0},{9,11},{1... | collective-permute-start | bytes 196616 | tf_op jit(solution)/shard_map/ppermute | solution.py:55
  18.3 0.0 collective-permute-done.6
  18.3 1.6 %collective-permute-start.7 = (bf16[16,2048]{1,0:T(8,128)(2,1)S(1)}, bf16[16,2048]{1,0:T(8,128)(2,1)S(1)}, u32[]{:S(2)}, u32[]{:S(2)}) collective-permute-start(bf16[16,2048]{1,0:T(8,128)(2,1)S(1)} %constant_dynamic-update-slice_fusion.own_ref), channel_id=1, source_target_pairs={{0,4},{1,3},{2,6},{3,1},{4,0},{5,7},{6,2},{7,5},{8,12},{9,11},{10,... | collective-permute-start | bytes 196616 | tf_op jit(solution)/shard_map/ppermute | solution.py:55
  19.9 1.7 %collective-permute-done.3 = bf16[16,2048]{1,0:T(8,128)(2,1)S(1)} collective-permute-done((bf16[16,2048]{1,0:T(8,128)(2,1)S(1)}, bf16[16,2048]{1,0:T(8,128)(2,1)S(1)}, u32[]{:S(2)}, u32[]{:S(2)}) %collective-permute-start.3) | collective-permute-done | bytes 65568 | tf_op jit(solution)/shard_map/ppermute | solution.py:55
  21.7 1.6 %collective-permute-start.4 = (bf16[16,2048]{1,0:T(8,128)(2,1)S(1)}, bf16[16,2048]{1,0:T(8,128)(2,1)S(1)}, u32[]{:S(2)}, u32[]{:S(2)}) collective-permute-start(bf16[16,2048]{1,0:T(8,128)(2,1)S(1)} %multiply_convert_fusion.own_ref), channel_id=1, source_target_pairs={{0,2},{1,5},{2,0},{3,7},{4,6},{5,1},{6,4},{7,3},{8,10},{9,13},{10,... | collective-permute-start | bytes 196616 | tf_op jit(solution)/shard_map/ppermute | solution.py:55
  23.2 0.0 collective-permute-done.7.arrived_ref
  23.2 0.1 shard_map.99.turned_ref
  23.3 0.3 shard_map.96.first_ref
  23.6 2.4 %collective-permute-done.4.other_ref = bf16[16,2048]{1,0:T(8,128)(2,1)S(1)} collective-permute-done((bf16[16,2048]{1,0:T(8,128)(2,1)S(1)}, bf16[16,2048]{1,0:T(8,128)(2,1)S(1)}, u32[]{:S(2)}, u32[]{:S(2)}) %collective-permute-start.4) | collective-permute-done | bytes 65568 | tf_op jit(solution)/shard_map/ppermute | solution.py:55
  26.0 0.2 shard_map.97
  26.2 0.0 collective-permute-start.5
  26.3 1.4 %convolution_convert_fusion = bf16[128,4096]{1,0:T(8,128)(2,1)} fusion(bf16[16,128]{1,0:T(8,128)(2,1)S(1)} %get-tuple-element.18.code_ref, bf16[16,4096]{1,0:T(8,128)(2,1)S(1)} %get-tuple-element.23), kind=kOutput, calls=%fused_computation | convolution fusion | flops 17301504 | bytes 1183744 | tf_op jit(solution)/shard_map/dot_general | solution.py:364
  27.7 0.0 collective-permute-done.5.theirs_ref
  27.7 1.9 %shard_map.100 = (bf16[4096,128]{1,0:T(8,128)(2,1)}, f32[1,128]{1,0:T(1,128)}) custom-call(f32[16,128]{1,0:T(8,128)S(1)} %get-tuple-element.24.raw_ref, f32[16,128]{1,0:T(8,128)S(1)} %get-tuple-element.25.mine_ref, f32[16,128]{1,0:T(8,128)S(1)} %collective-permute-done.5.theirs_ref, bf16[512,128]{1,0:T(8,128)(2,1)S(1)} %shard_map.99.turned_ref), custom_call_target="tpu_custom_call" | custom-call | flops 1000000 | bytes 1048576 | tf_op jit(solution)/shard_map/pallas_call | solution.py:327
  (6 shorter events, 0.1 us)
Async XLA Ops:
  0.6 6.9 %collective-permute-start = (bf16[2,4096]{1,0:T(2,128)(2,1)}, bf16[2,4096]{1,0:T(2,128)(2,1)S(1)}, u32[]{:S(2)}, u32[]{:S(2)}) collective-permute-start(bf16[2,4096]{1,0:T(2,128)(2,1)} %tokens_hbm.1), channel_id=1, source_target_pairs={{0,8},{1,9},{2,10},{3,11},{4,12},{5,13},{6,14},{7,15},{8,0},{9,1},... | collective-permute-start | bytes 49160 | tf_op jit(solution)/shard_map/ppermute | solution.py:55
  7.6 4.3 %collective-permute-start.1 = (bf16[16,2048]{1,0:T(8,128)(2,1)S(1)}, bf16[16,2048]{1,0:T(8,128)(2,1)S(1)}, u32[]{:S(2)}, u32[]{:S(2)}) collective-permute-start(bf16[16,2048]{1,0:T(8,128)(2,1)S(1)} %get-tuple-element.22), channel_id=1, source_target_pairs={{0,2},{1,5},{2,0},{3,7},{4,6},{5,1},{6,4},{7,3},{8,10},{9,13},{10,... | collective-permute-start | bytes 196616 | tf_op jit(solution)/shard_map/ppermute | solution.py:55
  9.4 8.9 %collective-permute-start.6 = (bf16[16,1024]{1,0:T(8,128)(2,1)S(1)}, bf16[16,1024]{1,0:T(8,128)(2,1)S(1)}, u32[]{:S(2)}, u32[]{:S(2)}) collective-permute-start(bf16[16,1024]{1,0:T(8,128)(2,1)S(1)} %get-tuple-element.29), channel_id=1, source_target_pairs={{0,2},{1,5},{2,0},{3,7},{4,6},{5,1},{6,4},{7,3},{8,10},{9,13},{10,... | collective-permute-start | bytes 98312 | tf_op jit(solution)/shard_map/ppermute | solution.py:55
  11.9 4.3 %collective-permute-start.2 = (bf16[16,2048]{1,0:T(8,128)(2,1)S(1)}, bf16[16,2048]{1,0:T(8,128)(2,1)S(1)}, u32[]{:S(2)}, u32[]{:S(2)}) collective-permute-start(bf16[16,2048]{1,0:T(8,128)(2,1)S(1)} %fusion), channel_id=1, source_target_pairs={{0,4},{1,9},{2,6},{3,11},{4,0},{5,13},{6,2},{7,15},{8,12},{9,1},{1... | collective-permute-start | bytes 196616 | tf_op jit(solution)/shard_map/ppermute | solution.py:55
  16.3 5.3 %collective-permute-start.3 = (bf16[16,2048]{1,0:T(8,128)(2,1)S(1)}, bf16[16,2048]{1,0:T(8,128)(2,1)S(1)}, u32[]{:S(2)}, u32[]{:S(2)}) collective-permute-start(bf16[16,2048]{1,0:T(8,128)(2,1)S(1)} %fusion.1), channel_id=1, source_target_pairs={{0,8},{1,3},{2,10},{3,1},{4,12},{5,7},{6,14},{7,5},{8,0},{9,11},{1... | collective-permute-start | bytes 196616 | tf_op jit(solution)/shard_map/ppermute | solution.py:55
  18.3 4.9 %collective-permute-start.7 = (bf16[16,2048]{1,0:T(8,128)(2,1)S(1)}, bf16[16,2048]{1,0:T(8,128)(2,1)S(1)}, u32[]{:S(2)}, u32[]{:S(2)}) collective-permute-start(bf16[16,2048]{1,0:T(8,128)(2,1)S(1)} %constant_dynamic-update-slice_fusion.own_ref), channel_id=1, source_target_pairs={{0,4},{1,3},{2,6},{3,1},{4,0},{5,7},{6,2},{7,5},{8,12},{9,11},{10,... | collective-permute-start | bytes 196616 | tf_op jit(solution)/shard_map/ppermute | solution.py:55
  21.7 4.3 %collective-permute-start.4 = (bf16[16,2048]{1,0:T(8,128)(2,1)S(1)}, bf16[16,2048]{1,0:T(8,128)(2,1)S(1)}, u32[]{:S(2)}, u32[]{:S(2)}) collective-permute-start(bf16[16,2048]{1,0:T(8,128)(2,1)S(1)} %multiply_convert_fusion.own_ref), channel_id=1, source_target_pairs={{0,2},{1,5},{2,0},{3,7},{4,6},{5,1},{6,4},{7,3},{8,10},{9,13},{10,... | collective-permute-start | bytes 196616 | tf_op jit(solution)/shard_map/ppermute | solution.py:55
  26.2 1.5 %collective-permute-start.5 = (f32[16,128]{1,0:T(8,128)S(1)}, f32[16,128]{1,0:T(8,128)S(1)}, u32[]{:S(2)}, u32[]{:S(2)}) collective-permute-start(f32[16,128]{1,0:T(8,128)S(1)} %get-tuple-element.25.mine_ref), channel_id=1, source_target_pairs={{0,1},{1,0},{2,3},{3,2},{4,5},{5,4},{6,7},{7,6},{8,9},{9,8},{10,11... | collective-permute-start | bytes 24584 | tf_op jit(solution)/shard_map/ppermute | solution.py:363

commit v10 on v8

--- a/solution.py
+++ b/solution.py
@@ -11,8 +11,8 @@
 SMEM = pl.BlockSpec(memory_space=pltpu.SMEM)
 HBM = pl.BlockSpec(memory_space=pltpu.HBM)
 ANY = pl.BlockSpec(memory_space=pl.ANY)
+MERGED = 2
 ROWS = 16
-MERGED = 2
 
 
 def kernel_call(kernel, out_shape, in_specs, out_specs, tokens, scratch_shapes=()):
@@ -36,28 +36,20 @@
     return (lax.axis_size("feat") - 1).bit_length()
 
 
-def sum_bit(step, core):
-    return (step + core) % feat_bits()
+def bit_of(step, core):
+    last = feat_bits() - 1
+    ends = [0, last] if core == 0 else [last, 0]
+    return (ends + list(range(1, last)))[step] if last else 0
 
 
 def swapped(shard, step):
     cores = lax.axis_size("tok")
     pairs = [
-        (f * cores + c, (f ^ 1 << sum_bit(step, c)) * cores + c)
+        (f * cores + c, (f ^ 1 << bit_of(step, c)) * cores + c)
         for f in range(lax.axis_size("feat"))
         for c in range(cores)
     ]
     return lax.ppermute(shard, ("feat", "tok"), pairs)
-
-
-def halves(width):
-    half = width // 2
-    bit = lax.axis_index("feat") >> (lax.axis_index("tok") % feat_bits()) & 1
-    return (
-        pl.multiple_of(bit * half, half),
-        pl.multiple_of((1 - bit) * half, half),
-        half,
-    )
 
 
 def stacked(rows, pieces):
@@ -73,9 +65,10 @@
 
 
 def share(code, rows_ref, centered_ref, at, half):
-    total = jnp.dot(code, rows_ref[:, pl.ds(at, half)], preferred_element_type=jnp.float32)
+    part = pl.ds(at, half)
+    total = jnp.dot(code, rows_ref[:, part], preferred_element_type=jnp.float32)
     rows = centered_ref.shape[0]
-    centered = centered_ref[:, pl.ds(at, half)]
+    centered = centered_ref[:, part]
     token = lax.broadcasted_iota(jnp.int32, (total.shape[0], 1), 0)
     first = lax.axis_index("feat") * rows
     for i in range(rows):
@@ -93,12 +86,12 @@
     count_ref,
     code_ref,
     raw_ref,
+    total_ref,
     sent_ref,
-    tokens_block_ref,
     rows_ref,
     centered_ref,
+    tokens_ref,
     bias_ref,
-    tokens_ref,
     bias_flat,
     pre_ref,
     top_ref,
@@ -135,41 +128,35 @@
     for copy in copies[2:4]:
         copy.wait()
     tokens = tokens_ref[...].astype(jnp.float32)
-    pieces = ROWS // tokens.shape[0]
     bias = bias_flat[...].astype(jnp.float32).reshape(1, width)
-    bias_ref[...] = stacked(bias, pieces)
+    bias_ref[...] = bias
     centered_ref[...] = (tokens - bias).astype(jnp.bfloat16).astype(jnp.float32)
-    tokens_block = stacked(tokens, pieces).astype(jnp.bfloat16)
-    tokens_block_ref[...] = tokens_block
 
     copies[4].wait()
-    _, other, half = halves(width)
-    sent_ref[:, :half] = share(code, rows_ref, centered_ref, other, half).astype(jnp.bfloat16)
-    if sent_ref.shape[1] > half:
-        sent_ref[:, half:] = tokens_block
-
-
-def front(tokens, b_pre, pre_codes, top_idx, blocks, counts, dict_rows, merged):
+    total = share(code, rows_ref, centered_ref, 0, width // 2)
+    total_ref[...] = total
+    sent_ref[...] = total.astype(jnp.bfloat16)
+
+
+def front(tokens, b_pre, pre_codes, top_idx, blocks, counts, dict_rows):
     count = top_idx.shape[0]
     slots, width = dict_rows.shape
-    pieces = ROWS // tokens.shape[0]
-    block = width // pieces
     return kernel_call(
         front_kernel,
         (
             shape(count, slots),
             shape(count, slots, dtype=jnp.float32),
-            shape(count, width // 2 + merged * block),
-            shape(ROWS, block),
+            shape(count, width // 2, dtype=jnp.float32),
+            shape(count, width // 2),
             shape(slots, width),
             shape(*tokens.shape, dtype=jnp.float32),
-            shape(pieces, block, dtype=jnp.float32),
+            shape(*tokens.shape),
+            shape(1, width, dtype=jnp.float32),
         ),
         [HBM] * 5 + [SMEM] * 2,
-        (VMEM,) * 7,
+        (VMEM,) * 8,
         count,
         [
-            pltpu.VMEM(tokens.shape, tokens.dtype),
             pltpu.VMEM(b_pre.shape, b_pre.dtype),
             pltpu.VMEM(pre_codes.shape, pre_codes.dtype),
             pltpu.VMEM(top_idx.shape, top_idx.dtype),
@@ -185,19 +172,40 @@
     )
 
 
-def own_kernel(code_ref, rows_ref, centered_ref, total_ref):
-    own, _, half = halves(rows_ref.shape[1])
-    total_ref[...] = share(code_ref[...], rows_ref, centered_ref, own, half)
-
-
-def own_part(code, dict_rows, centered):
+def second_kernel(
+    code_ref, rows_ref, centered_ref, tokens_ref, bias_ref, total_ref, sent_ref, block_ref, pieces_ref
+):
+    half = total_ref.shape[1]
+    total = share(code_ref[...], rows_ref, centered_ref, half, half)
+    total_ref[...] = total
+    sent_ref[:, :half] = total.astype(jnp.bfloat16)
+    pieces = pieces_ref.shape[0]
+    block = stacked(tokens_ref[...].astype(jnp.float32), pieces).astype(jnp.bfloat16)
+    block_ref[...] = block
+    if sent_ref.shape[1] > half:
+        sent_ref[:, half:] = block
+    pieces_ref[...] = stacked(bias_ref[...], pieces)
+
+
+def second(code, dict_rows, centered, tokens, bias, merged):
     count, half = code.shape[0], dict_rows.shape[1] // 2
-    return kernel_call(
-        own_kernel, shape(count, half, dtype=jnp.float32), [VMEM] * 3, VMEM, count
-    )(code, dict_rows, centered)
-
-
-def added_kernel(total_ref, own_ref, arrived_ref, sum_ref, sent_ref):
+    pieces = ROWS // tokens.shape[0]
+    width = tokens.shape[1] // pieces
+    return kernel_call(
+        second_kernel,
+        (
+            shape(count, half, dtype=jnp.float32),
+            shape(count, half + (width if merged else 0)),
+            shape(ROWS, width),
+            shape(pieces, width, dtype=jnp.float32),
+        ),
+        [VMEM] * 5,
+        (VMEM,) * 4,
+        count,
+    )(code, dict_rows, centered, tokens, bias)
+
+
+def added_kernel(total_ref, own_ref, arrived_ref, after_ref, sum_ref, sent_ref):
     half = total_ref.shape[1]
     total = total_ref[...] + arrived_ref[:, :half].astype(jnp.float32)
     sum_ref[...] = total
@@ -208,7 +216,7 @@
         sent_ref[:, half + block :] = arrived_ref[:, half:]
 
 
-def added(total, own, arrived, merged):
+def added(total, own, arrived, after, merged):
     count, half = total.shape
     block = own.shape[1] - half
     return kernel_call(
@@ -217,10 +225,10 @@
             shape(count, half, dtype=jnp.float32),
             shape(count, half + (2 * block if merged else 0)),
         ),
-        [VMEM] * 3,
+        [VMEM] * 3 + [ANY],
         (VMEM, VMEM),
         count,
-    )(total, own, arrived)
+    )(total, own, arrived, after)
 
 
 def joined_kernel(skip, first_ref, second_ref, after_ref, out_ref):
@@ -255,7 +263,7 @@
     return kernel_call(
         turned_kernel,
         shape(bias.shape[1], blocks * ROWS),
-        [VMEM, VMEM, VMEM, ANY],
+        [VMEM] * 3 + [ANY],
         VMEM,
         count,
     )(own, arrived, bias, after)
@@ -270,31 +278,30 @@
     )
 
 
-def first_product_kernel(own_ref, rows_ref, half_ref):
-    own, _, half = halves(rows_ref.shape[1])
-    half_ref[...] = product(own_ref, rows_ref, own, half)
-
-
-def first_product(scaled_own, dict_rows):
-    count = scaled_own.shape[0]
+def first_product_kernel(first_ref, rows_ref, half_ref):
+    half_ref[...] = product(first_ref, rows_ref, 0, first_ref.shape[1])
+
+
+def first_product(scaled_first, dict_rows):
+    count = scaled_first.shape[0]
     return kernel_call(
         first_product_kernel,
         shape(count, dict_rows.shape[0], dtype=jnp.float32),
         [VMEM] * 2,
         VMEM,
         count,
-    )(scaled_own, dict_rows)
-
-
-def code_half_kernel(own_ref, other_ref, first_ref, rows_ref, half_ref, scaled_ref):
-    own, other, half = halves(rows_ref.shape[1])
-    half_ref[...] = first_ref[...] + product(other_ref, rows_ref, other, half)
-    scaled_ref[:, pl.ds(own, half)] = own_ref[...]
-    scaled_ref[:, pl.ds(other, half)] = other_ref[...]
-
-
-def code_half_of(scaled_own, scaled_other, first, dict_rows):
-    count = scaled_own.shape[0]
+    )(scaled_first, dict_rows)
+
+
+def code_half_kernel(first_ref, second_ref, product_ref, rows_ref, half_ref, scaled_ref):
+    half = first_ref.shape[1]
+    half_ref[...] = product_ref[...] + product(second_ref, rows_ref, half, half)
+    scaled_ref[:, :half] = first_ref[...]
+    scaled_ref[:, half:] = second_ref[...]
+
+
+def code_half_of(scaled_first, scaled_second, first, dict_rows):
+    count = scaled_first.shape[0]
     slots, width = dict_rows.shape
     return kernel_call(
         code_half_kernel,
@@ -302,7 +309,7 @@
         [VMEM] * 4,
         (VMEM, VMEM),
         count,
-    )(scaled_own, scaled_other, first, dict_rows)
+    )(scaled_first, scaled_second, first, dict_rows)
 
 
 def final_kernel(
@@ -319,7 +326,10 @@
     block = place // ROWS
     distance = jnp.zeros_like(place)
     for step in range(feat_bits()):
-        distance |= (block >> step & 1) << sum_bit(step, core)
+        bit = sum(
+            jnp.where(core == c, bit_of(step, c), 0) for c in range(lax.axis_size("tok"))
+        )
+        distance |= (block >> step & 1) << bit
     source = (lax.axis_index("feat") ^ distance) * rows + place % ROWS // pieces
     order = jnp.where(token == source, 1.0, 0.0).astype(jnp.bfloat16)
     spread = jnp.dot(order, pre_grad, preferred_element_type=jnp.float32)
@@ -358,34 +368,40 @@
 
 def local(tokens, b_pre, pre_codes, top_idx, blocks, counts, dict_rows):
     rows, count = tokens.shape[0], top_idx.shape[0]
+    steps = feat_bits()
     half = dict_rows.shape[1] // 2
-    steps = feat_bits()
     merged = min(MERGED, steps - 1) if count == ROWS else 0
 
-    code, raw, sent, block, dict_rows, centered, bias = front(
-        tokens, b_pre, pre_codes, top_idx, blocks, counts, dict_rows, merged > 0
+    code, raw, total, sent, dict_rows, centered, tokens, bias = front(
+        tokens, b_pre, pre_codes, top_idx, blocks, counts, dict_rows
     )
     for step in range(steps):
         arrived = swapped(sent, step)
         if step == 0:
-            total = own_part(code, dict_rows, centered)
+            total_second, sent_second, block, bias = second(
+                code, dict_rows, centered, tokens, bias, merged > 0
+            )
+        else:
+            own, previous = sent_second, arrived_second
+            total_second, sent_second = added(
+                total_second, own, previous, sent, step < merged
+            )
+        arrived_second = swapped(sent_second, step)
         if step >= merged:
             if step == merged > 0:
-                block = joined(own, previous, half, sent)
+                block = joined(own, previous, half, sent_second)
             elif step > 0:
-                block = joined(block, arrived_block, 0, sent)
+                block = joined(block, arrived_block, 0, sent_second)
             arrived_block = swapped(block, step)
-        if step < steps - 1:
-            own, previous = sent, arrived
-            total, sent = added(total, own, arrived, step + 1 < merged)
-    total = total + arrived.astype(jnp.float32)
-    scaled_own = (0.25 * total).astype(jnp.bfloat16)
-    scaled_other = swapped(scaled_own, 0)
-
-    first = first_product(scaled_own, dict_rows)
-    turned_tokens = turned(block, arrived_block, bias, scaled_own, count)
-
-    code_half, scaled = code_half_of(scaled_own, scaled_other, first, dict_rows)
+        total = total + arrived.astype(jnp.float32)
+        sent = total.astype(jnp.bfloat16)
+    scaled_first = (0.25 * total).astype(jnp.bfloat16)
+    scaled_second = (0.25 * (total_second + arrived_second.astype(jnp.float32))).astype(
+        jnp.bfloat16
+    )
+    first = first_product(scaled_first, dict_rows)
+    code_half, scaled = code_half_of(scaled_first, scaled_second, first, dict_rows)
+    turned_tokens = turned(block, arrived_block, bias, code_half, count)
     theirs = lax.ppermute(code_half, "tok", [(i, 1 - i) for i in range(2)])
     grad_rows = lax.dot_general(
         code, scaled, (((0,), (0,)), ((), ())), preferred_element_type=jnp.float32

time: 28.9 us -> 26.3 us (0.910)
  the two profiles are of different devices: /device:TPU:31 before, /device:TPU:0 now
where the time goes in v10:
time: 26.3 us; the launch traced here: 26.1 us
  starting transfers between devices  12.6 us (48%)
  waiting for transfers between devices  5.14 us (20%)
  Pallas kernels  4.84 us (18%)
  between operations  1.99 us (8%)
  matrix products  1.42 us (5%)
    ppermute x7, starting transfers between devices, swapped(): return lax.ppermute(shard, ('feat', 'tok'), pairs)  12.6 us
    ppermute x7, waiting for transfers between devices, swapped(): return lax.ppermute(shard, ('feat', 'tok'), pairs)  5.14 us
    pallas_call x1, Pallas kernels, final(): kernel_call(functools.partial(final_kernel, rows), (shape(width, slots),...  1.95 us
    pallas_call x1, Pallas kernels, front(): kernel_call(front_kernel, (shape(count, slots), shape(count, slots, dtype...  1.53 us
    dot_general x1, matrix products, local(): lax.dot_general(code, scaled, (((0,), (0,)), ((), ())), preferred_element...  1.42 us
    pallas_call x1, Pallas kernels, second(): kernel_call(second_kernel, (shape(count, half, dtype=jnp.float32), shape(...  0.75 us
  transfers between devices with their start and end apart: 8, of which 4 were waited for; matrix products, arithmetic and copies ran while one was open for 6% of the time, Pallas kernels for 5%

profile of v10, /device:TPU:0, one launch (start us, length us, event | category | flops | bytes accessed | tf_op | source)
XLA Modules:
  0.0 26.1 jit_solution(15495139232191914981)
XLA Ops:
  1.9 1.5 %shard_map.94 = (bf16[16,128]{1,0:T(8,128)(2,1)S(1)}, f32[16,128]{1,0:T(8,128)S(1)}, f32[16,2048]{1,0:T(8,128)S(1)}, bf16[16,2048]{1,0:T(8,128)(2,1)S(1)}, bf16[...) custom-call(bf16[2,4096]{1,0:T(2,128)(2,1)} %tokens_hbm.1, ...), custom_call_target="tpu_custom_call" | custom-call | flops 1000000 | bytes 1048576 | tf_op jit(solution)/shard_map/pallas_call | solution.py:144
  3.5 3.0 %collective-permute-start = (bf16[16,2048]{1,0:T(8,128)(2,1)S(1)}, bf16[16,2048]{1,0:T(8,128)(2,1)S(1)}, u32[]{:S(2)}, u32[]{:S(2)}) collective-permute-start(bf16[16,2048]{1,0:T(8,128)(2,1)S(1)} %get-tuple-element.24), channel_id=1, source_target_pairs={{0,2},{1,9},{2,0},{3,11},{4,6},{5,13},{6,4},{7,15},{8,10},{9,1},{1... | collective-permute-start | bytes 196616 | tf_op jit(solution)/shard_map/ppermute | solution.py:52
  6.5 0.8 %shard_map.95 = (f32[16,2048]{1,0:T(8,128)S(1)}, bf16[16,2560]{1,0:T(8,128)(2,1)S(1)}, bf16[16,512]{1,0:T(8,128)(2,1)}, f32[8,512]{1,0:T(8,128)S(1)}) custom-call(bf16[16,128]{1,0:T(8,128)(2,1)S(1)} %get-tuple-element.22.code_ref, bf16[128,4096]{1,0:T(8,128)(2,1)S(1)} %get-tuple-element.25.rows_ref, f32[2,4096]{1,0:T(2,128)S(1)} %get-tuple-element.26.centered_ref, ...), custom_call_target="tpu_custom_call" | custom-call | flops 1000000 | bytes 1048576 | tf_op jit(solution)/shard_map/pallas_call | solution.py:194
  7.2 0.0 collective-permute-start.3
  7.2 1.5 %collective-permute-done = bf16[16,2048]{1,0:T(8,128)(2,1)S(1)} collective-permute-done((bf16[16,2048]{1,0:T(8,128)(2,1)S(1)}, bf16[16,2048]{1,0:T(8,128)(2,1)S(1)}, u32[]{:S(2)}, u32[]{:S(2)}) %collective-permute-start) | collective-permute-done | bytes 65568 | tf_op jit(solution)/shard_map/ppermute | solution.py:52
  8.7 3.2 %collective-permute-start.1 = (bf16[16,2048]{1,0:T(8,128)(2,1)S(1)}, bf16[16,2048]{1,0:T(8,128)(2,1)S(1)}, u32[]{:S(2)}, u32[]{:S(2)}) collective-permute-start(bf16[16,2048]{1,0:T(8,128)(2,1)S(1)} %fusion.after_ref), channel_id=1, source_target_pairs={{0,8},{1,3},{2,10},{3,1},{4,12},{5,7},{6,14},{7,5},{8,0},{9,11},{1... | collective-permute-start | bytes 196616 | tf_op jit(solution)/shard_map/ppermute | solution.py:52
  11.9 0.0 collective-permute-done.3.arrived_ref
  11.9 2.5 %collective-permute-start.4 = (bf16[16,3072]{1,0:T(8,128)(2,1)S(1)}, bf16[16,3072]{1,0:T(8,128)(2,1)S(1)}, u32[]{:S(2)}, u32[]{:S(2)}) collective-permute-start(bf16[16,3072]{1,0:T(8,128)(2,1)S(1)} %get-tuple-element.32.own_ref.first_ref), channel_id=1, source_target_pairs={{0,8},{1,3},{2,10},{3,1},{4,12},{5,7},{6,14},{7,5},{8,0},{9,11},{1... | collective-permute-start | bytes 294920 | tf_op jit(solution)/shard_map/ppermute | solution.py:52
  14.5 0.0 collective-permute-done.1
  14.5 1.7 %collective-permute-start.2 = (bf16[16,2048]{1,0:T(8,128)(2,1)S(1)}, bf16[16,2048]{1,0:T(8,128)(2,1)S(1)}, u32[]{:S(2)}, u32[]{:S(2)}) collective-permute-start(bf16[16,2048]{1,0:T(8,128)(2,1)S(1)} %fusion.1.after_ref), channel_id=1, source_target_pairs={{0,4},{1,5},{2,6},{3,7},{4,0},{5,1},{6,2},{7,3},{8,12},{9,13},{10,... | collective-permute-start | bytes 196616 | tf_op jit(solution)/shard_map/ppermute | solution.py:52
  16.2 1.5 %collective-permute-done.4.arrived_ref.second_ref = bf16[16,3072]{1,0:T(8,128)(2,1)S(1)} collective-permute-done((bf16[16,3072]{1,0:T(8,128)(2,1)S(1)}, bf16[16,3072]{1,0:T(8,128)(2,1)S(1)}, u32[]{:S(2)}, u32[]{:S(2)}) %collective-permute-start.4) | collective-permute-done | bytes 98336 | tf_op jit(solution)/shard_map/ppermute | solution.py:52
  17.7 2.1 %collective-permute-start.5 = (bf16[16,2048]{1,0:T(8,128)(2,1)S(1)}, bf16[16,2048]{1,0:T(8,128)(2,1)S(1)}, u32[]{:S(2)}, u32[]{:S(2)}) collective-permute-start(bf16[16,2048]{1,0:T(8,128)(2,1)S(1)} %get-tuple-element.34.after_ref), channel_id=1, source_target_pairs={{0,4},{1,5},{2,6},{3,7},{4,0},{5,1},{6,2},{7,3},{8,12},{9,13},{10,... | collective-permute-start | bytes 196616 | tf_op jit(solution)/shard_map/ppermute | solution.py:52
  19.7 0.1 collective-permute-start.7
  19.8 0.0 collective-permute-done.2
  19.9 0.2 shard_map.98.product_ref
  20.1 1.9 %collective-permute-done.5 = bf16[16,2048]{1,0:T(8,128)(2,1)S(1)} collective-permute-done((bf16[16,2048]{1,0:T(8,128)(2,1)S(1)}, bf16[16,2048]{1,0:T(8,128)(2,1)S(1)}, u32[]{:S(2)}, u32[]{:S(2)}) %collective-permute-start.5) | collective-permute-done | bytes 65568 | tf_op jit(solution)/shard_map/ppermute | solution.py:52
  22.0 0.2 shard_map.99
  22.2 0.0 collective-permute-start.6
  22.3 1.4 %convolution_convert_fusion = bf16[128,4096]{1,0:T(8,128)(2,1)} fusion(bf16[16,128]{1,0:T(8,128)(2,1)S(1)} %get-tuple-element.22.code_ref, bf16[16,4096]{1,0:T(8,128)(2,1)S(1)} %get-tuple-element.35), kind=kOutput, calls=%fused_computation | convolution fusion | flops 17301504 | bytes 1183744 | tf_op jit(solution)/shard_map/dot_general | solution.py:406
  23.7 0.3 %collective-permute-done.7.arrived_ref = bf16[16,2048]{1,0:T(8,128)(2,1)S(1)} collective-permute-done((bf16[16,2048]{1,0:T(8,128)(2,1)S(1)}, bf16[16,2048]{1,0:T(8,128)(2,1)S(1)}, u32[]{:S(2)}, u32[]{:S(2)}) %collective-permute-start.7) | collective-permute-done | bytes 65568 | tf_op jit(solution)/shard_map/ppermute | solution.py:52
  24.0 0.1 shard_map.101.turned_ref
  24.1 0.0 collective-permute-done.6.theirs_ref
  24.1 1.9 %shard_map.102 = (bf16[4096,128]{1,0:T(8,128)(2,1)}, f32[1,128]{1,0:T(1,128)}) custom-call(f32[16,128]{1,0:T(8,128)S(1)} %get-tuple-element.36.raw_ref, f32[16,128]{1,0:T(8,128)S(1)} %get-tuple-element.37.after_ref.mine_ref, f32[16,128]{1,0:T(8,128)S(1)} %collective-permute-done.6.theirs_ref, bf16[512,128]{1,0:T(8,128)(2,1)S(1)} %shard_map.101.turned_ref), custom_call_target="tpu_custom_call" | custom-call | flops 1000000 | bytes 1048576 | tf_op jit(solution)/shard_map/pallas_call | solution.py:359
  (7 shorter events, 0.1 us)
Async XLA Ops:
  3.5 5.2 %collective-permute-start = (bf16[16,2048]{1,0:T(8,128)(2,1)S(1)}, bf16[16,2048]{1,0:T(8,128)(2,1)S(1)}, u32[]{:S(2)}, u32[]{:S(2)}) collective-permute-start(bf16[16,2048]{1,0:T(8,128)(2,1)S(1)} %get-tuple-element.24), channel_id=1, source_target_pairs={{0,2},{1,9},{2,0},{3,11},{4,6},{5,13},{6,4},{7,15},{8,10},{9,1},{1... | collective-permute-start | bytes 196616 | tf_op jit(solution)/shard_map/ppermute | solution.py:52
  7.2 4.7 %collective-permute-start.3 = (bf16[16,2560]{1,0:T(8,128)(2,1)S(1)}, bf16[16,2560]{1,0:T(8,128)(2,1)S(1)}, u32[]{:S(2)}, u32[]{:S(2)}) collective-permute-start(bf16[16,2560]{1,0:T(8,128)(2,1)S(1)} %get-tuple-element.30.own_ref), channel_id=1, source_target_pairs={{0,2},{1,9},{2,0},{3,11},{4,6},{5,13},{6,4},{7,15},{8,10},{9,1},{1... | collective-permute-start | bytes 245768 | tf_op jit(solution)/shard_map/ppermute | solution.py:52
  8.7 5.7 %collective-permute-start.1 = (bf16[16,2048]{1,0:T(8,128)(2,1)S(1)}, bf16[16,2048]{1,0:T(8,128)(2,1)S(1)}, u32[]{:S(2)}, u32[]{:S(2)}) collective-permute-start(bf16[16,2048]{1,0:T(8,128)(2,1)S(1)} %fusion.after_ref), channel_id=1, source_target_pairs={{0,8},{1,3},{2,10},{3,1},{4,12},{5,7},{6,14},{7,5},{8,0},{9,11},{1... | collective-permute-start | bytes 196616 | tf_op jit(solution)/shard_map/ppermute | solution.py:52
  11.9 5.7 %collective-permute-start.4 = (bf16[16,3072]{1,0:T(8,128)(2,1)S(1)}, bf16[16,3072]{1,0:T(8,128)(2,1)S(1)}, u32[]{:S(2)}, u32[]{:S(2)}) collective-permute-start(bf16[16,3072]{1,0:T(8,128)(2,1)S(1)} %get-tuple-element.32.own_ref.first_ref), channel_id=1, source_target_pairs={{0,8},{1,3},{2,10},{3,1},{4,12},{5,7},{6,14},{7,5},{8,0},{9,11},{1... | collective-permute-start | bytes 294920 | tf_op jit(solution)/shard_map/ppermute | solution.py:52
  14.5 5.3 %collective-permute-start.2 = (bf16[16,2048]{1,0:T(8,128)(2,1)S(1)}, bf16[16,2048]{1,0:T(8,128)(2,1)S(1)}, u32[]{:S(2)}, u32[]{:S(2)}) collective-permute-start(bf16[16,2048]{1,0:T(8,128)(2,1)S(1)} %fusion.1.after_ref), channel_id=1, source_target_pairs={{0,4},{1,5},{2,6},{3,7},{4,0},{5,1},{6,2},{7,3},{8,12},{9,13},{10,... | collective-permute-start | bytes 196616 | tf_op jit(solution)/shard_map/ppermute | solution.py:52
  17.7 4.3 %collective-permute-start.5 = (bf16[16,2048]{1,0:T(8,128)(2,1)S(1)}, bf16[16,2048]{1,0:T(8,128)(2,1)S(1)}, u32[]{:S(2)}, u32[]{:S(2)}) collective-permute-start(bf16[16,2048]{1,0:T(8,128)(2,1)S(1)} %get-tuple-element.34.after_ref), channel_id=1, source_target_pairs={{0,4},{1,5},{2,6},{3,7},{4,0},{5,1},{6,2},{7,3},{8,12},{9,13},{10,... | collective-permute-start | bytes 196616 | tf_op jit(solution)/shard_map/ppermute | solution.py:52
  19.7 4.3 %collective-permute-start.7 = (bf16[16,2048]{1,0:T(8,128)(2,1)S(1)}, bf16[16,2048]{1,0:T(8,128)(2,1)S(1)}, u32[]{:S(2)}, u32[]{:S(2)}) collective-permute-start(bf16[16,2048]{1,0:T(8,128)(2,1)S(1)} %shard_map.100.own_ref), channel_id=1, source_target_pairs={{0,4},{1,5},{2,6},{3,7},{4,0},{5,1},{6,2},{7,3},{8,12},{9,13},{10,... | collective-permute-start | bytes 196616 | tf_op jit(solution)/shard_map/ppermute | solution.py:52
  22.2 1.9 %collective-permute-start.6 = (f32[16,128]{1,0:T(8,128)S(1)}, f32[16,128]{1,0:T(8,128)S(1)}, u32[]{:S(2)}, u32[]{:S(2)}) collective-permute-start(f32[16,128]{1,0:T(8,128)S(1)} %get-tuple-element.37.after_ref.mine_ref), channel_id=1, source_target_pairs={{0,1},{1,0},{2,3},{3,2},{4,5},{5,4},{6,7},{7,6},{8,9},{9,8},{10,11... | collective-permute-start | bytes 24584 | tf_op jit(solution)/shard_map/ppermute | solution.py:405

commit v11 on v10

--- a/solution.py
+++ b/solution.py
@@ -32,14 +32,18 @@
     return jax.ShapeDtypeStruct(sizes, dtype)
 
 
+def first_width(width):
+    return width // 2
+
+
 def feat_bits():
     return (lax.axis_size("feat") - 1).bit_length()
 
 
 def bit_of(step, core):
     last = feat_bits() - 1
-    ends = [0, last] if core == 0 else [last, 0]
-    return (ends + list(range(1, last)))[step] if last else 0
+    middle = list(range(1, last))
+    return ([0, last] + middle if core == 0 else [last] + middle + [0])[step] if last else 0
 
 
 def swapped(shard, step):
@@ -55,17 +59,12 @@
 def stacked(rows, pieces):
     width = rows.shape[1] // pieces
     return jnp.concatenate(
-        [
-            rows[i : i + 1, c * width : (c + 1) * width]
-            for i in range(rows.shape[0])
-            for c in range(pieces)
-        ],
-        axis=0,
-    )
-
-
-def share(code, rows_ref, centered_ref, at, half):
-    part = pl.ds(at, half)
+        [rows[:, c * width : (c + 1) * width] for c in range(pieces)], axis=0
+    )
+
+
+def share(code, rows_ref, centered_ref, at, width):
+    part = pl.ds(at, width)
     total = jnp.dot(code, rows_ref[:, part], preferred_element_type=jnp.float32)
     rows = centered_ref.shape[0]
     centered = centered_ref[:, part]
@@ -133,7 +132,7 @@
     centered_ref[...] = (tokens - bias).astype(jnp.bfloat16).astype(jnp.float32)
 
     copies[4].wait()
-    total = share(code, rows_ref, centered_ref, 0, width // 2)
+    total = share(code, rows_ref, centered_ref, 0, total_ref.shape[1])
     total_ref[...] = total
     sent_ref[...] = total.astype(jnp.bfloat16)
 
@@ -146,8 +145,8 @@
         (
             shape(count, slots),
             shape(count, slots, dtype=jnp.float32),
-            shape(count, width // 2, dtype=jnp.float32),
-            shape(count, width // 2),
+            shape(count, first_width(width), dtype=jnp.float32),
+            shape(count, first_width(width)),
             shape(slots, width),
             shape(*tokens.shape, dtype=jnp.float32),
             shape(*tokens.shape),
@@ -172,37 +171,33 @@
     )
 
 
-def second_kernel(
-    code_ref, rows_ref, centered_ref, tokens_ref, bias_ref, total_ref, sent_ref, block_ref, pieces_ref
-):
-    half = total_ref.shape[1]
-    total = share(code_ref[...], rows_ref, centered_ref, half, half)
+def second_kernel(code_ref, rows_ref, centered_ref, tokens_ref, total_ref, sent_ref, block_ref):
+    width = total_ref.shape[1]
+    total = share(code_ref[...], rows_ref, centered_ref, rows_ref.shape[1] - width, width)
     total_ref[...] = total
-    sent_ref[:, :half] = total.astype(jnp.bfloat16)
-    pieces = pieces_ref.shape[0]
+    sent_ref[:, :width] = total.astype(jnp.bfloat16)
+    pieces = ROWS // tokens_ref.shape[0]
     block = stacked(tokens_ref[...].astype(jnp.float32), pieces).astype(jnp.bfloat16)
     block_ref[...] = block
-    if sent_ref.shape[1] > half:
-        sent_ref[:, half:] = block
-    pieces_ref[...] = stacked(bias_ref[...], pieces)
-
-
-def second(code, dict_rows, centered, tokens, bias, merged):
-    count, half = code.shape[0], dict_rows.shape[1] // 2
-    pieces = ROWS // tokens.shape[0]
-    width = tokens.shape[1] // pieces
+    if sent_ref.shape[1] > width:
+        sent_ref[:, width:] = block
+
+
+def second(code, dict_rows, centered, tokens, merged):
+    count, width = code.shape[0], dict_rows.shape[1]
+    chunk = width - first_width(width)
+    block = tokens.shape[0] * width // ROWS
     return kernel_call(
         second_kernel,
         (
-            shape(count, half, dtype=jnp.float32),
-            shape(count, half + (width if merged else 0)),
-            shape(ROWS, width),
-            shape(pieces, width, dtype=jnp.float32),
+            shape(count, chunk, dtype=jnp.float32),
+            shape(count, chunk + (block if merged else 0)),
+            shape(ROWS, block),
         ),
-        [VMEM] * 5,
-        (VMEM,) * 4,
-        count,
-    )(code, dict_rows, centered, tokens, bias)
+        [VMEM] * 4,
+        (VMEM,) * 3,
+        count,
+    )(code, dict_rows, centered, tokens)
 
 
 def added_kernel(total_ref, own_ref, arrived_ref, after_ref, sum_ref, sent_ref):
@@ -247,9 +242,10 @@
     )(first, second, after)
 
 
-def turned_kernel(own_ref, arrived_ref, bias_ref, after_ref, out_ref):
-    pieces, width = bias_ref.shape
-    bias = jnp.concatenate([bias_ref[...]] * (ROWS // pieces), axis=0)
+def turned_kernel(rows, own_ref, arrived_ref, bias_ref, after_ref, out_ref):
+    bias = jnp.concatenate([bias_ref[...]] * rows, axis=0)
+    bias = stacked(bias, ROWS // rows)
+    width = bias.shape[1]
     blocks = [
         (ref[:, at : at + width].astype(jnp.float32) - bias).astype(jnp.bfloat16)
         for ref in (own_ref, arrived_ref)
@@ -258,58 +254,96 @@
     out_ref[...] = jnp.concatenate(blocks, axis=0).astype(jnp.float32).T.astype(jnp.bfloat16)
 
 
-def turned(own, arrived, bias, after, count):
-    blocks = 2 * own.shape[1] // bias.shape[1]
-    return kernel_call(
-        turned_kernel,
-        shape(bias.shape[1], blocks * ROWS),
+def turned(own, arrived, bias, after, rows, count):
+    width = bias.shape[1] * rows // ROWS
+    return kernel_call(
+        functools.partial(turned_kernel, rows),
+        shape(width, 2 * own.shape[1] // width * ROWS),
         [VMEM] * 3 + [ANY],
         VMEM,
         count,
     )(own, arrived, bias, after)
 
 
-def product(part_ref, rows_ref, at, half):
+def scaled_of(total_ref, arrived_ref):
+    total = total_ref[...] + arrived_ref[:, : total_ref.shape[1]].astype(jnp.float32)
+    return (0.25 * total).astype(jnp.bfloat16)
+
+
+def product(part, rows_ref, at):
     return lax.dot_general(
-        part_ref[...],
-        rows_ref[:, pl.ds(at, half)],
+        part,
+        rows_ref[:, at : at + part.shape[1]],
         (((1,), (1,)), ((), ())),
         preferred_element_type=jnp.float32,
     )
 
 
-def first_product_kernel(first_ref, rows_ref, half_ref):
-    half_ref[...] = product(first_ref, rows_ref, 0, first_ref.shape[1])
-
-
-def first_product(scaled_first, dict_rows):
-    count = scaled_first.shape[0]
-    return kernel_call(
-        first_product_kernel,
-        shape(count, dict_rows.shape[0], dtype=jnp.float32),
-        [VMEM] * 2,
-        VMEM,
-        count,
-    )(scaled_first, dict_rows)
-
-
-def code_half_kernel(first_ref, second_ref, product_ref, rows_ref, half_ref, scaled_ref):
-    half = first_ref.shape[1]
-    half_ref[...] = product_ref[...] + product(second_ref, rows_ref, half, half)
-    scaled_ref[:, :half] = first_ref[...]
-    scaled_ref[:, half:] = second_ref[...]
-
-
-def code_half_of(scaled_first, scaled_second, first, dict_rows):
-    count = scaled_first.shape[0]
-    slots, width = dict_rows.shape
-    return kernel_call(
-        code_half_kernel,
-        (shape(count, slots, dtype=jnp.float32), shape(count, width)),
-        [VMEM] * 4,
+def first_product_kernel(total_ref, arrived_ref, rows_ref, scaled_ref, half_ref):
+    scaled = scaled_of(total_ref, arrived_ref)
+    scaled_ref[...] = scaled
+    half_ref[...] = product(scaled, rows_ref, 0)
+
+
+def second_product_kernel(
+    total_ref, arrived_ref, rows_ref, first_ref, after_ref, scaled_ref, half_ref
+):
+    scaled = scaled_of(total_ref, arrived_ref)
+    scaled_ref[...] = scaled
+    half_ref[...] = first_ref[...] + product(scaled, rows_ref, rows_ref.shape[1] - scaled.shape[1])
+
+
+def products(total, arrived, dict_rows, *first):
+    count, width = total.shape
+    return kernel_call(
+        second_product_kernel if first else first_product_kernel,
+        (shape(count, width), shape(count, dict_rows.shape[0], dtype=jnp.float32)),
+        [VMEM] * 3 + ([VMEM, ANY] if first else []),
         (VMEM, VMEM),
         count,
-    )(scaled_first, scaled_second, first, dict_rows)
+    )(total, arrived, dict_rows, *first)
+
+
+def grad_rows_kernel(at, code_ref, scaled_ref, *refs):
+    out_hbm, mark_ref, out_ref, sems = refs[-4:]
+    mark_ref[...] = jnp.zeros_like(mark_ref)
+    slots, width = out_ref.shape
+    code = code_ref[...].astype(jnp.float32).T.astype(jnp.bfloat16)
+    step = width // sems.shape[0]
+    copies = []
+    for i in range(sems.shape[0]):
+        part = pl.ds(i * step, step)
+        out_ref[:, part] = jnp.dot(
+            code, scaled_ref[:, part], preferred_element_type=jnp.float32
+        ).astype(jnp.bfloat16)
+        copies.append(
+            pltpu.make_async_copy(
+                out_ref.at[:, part], out_hbm.at[:, pl.ds(at + i * step, step)], sems.at[i]
+            )
+        )
+        copies[-1].start()
+    for copy in copies:
+        copy.wait()
+
+
+def grad_rows_part(code, scaled, width, written=None):
+    count, slots = code.shape
+    chunk = scaled.shape[1]
+    at = 0 if written is None else width - chunk
+    limit = (16 if count <= ROWS else 40) * 2**20
+    return pl.pallas_call(
+        functools.partial(grad_rows_kernel, at),
+        out_shape=(shape(slots, width), shape(1, slots, dtype=jnp.float32)),
+        in_specs=[VMEM] * 2 + ([] if written is None else [HBM]),
+        out_specs=(HBM, VMEM),
+        scratch_shapes=[
+            pltpu.VMEM((slots, chunk), jnp.bfloat16),
+            pltpu.SemaphoreType.DMA((2,)),
+        ],
+        input_output_aliases={} if written is None else {2: 0},
+        compiler_params=pltpu.CompilerParams(vmem_limit_bytes=limit),
+        cost_estimate=pl.CostEstimate(flops=10**6, bytes_accessed=2**20, transcendentals=0),
+    )(code, scaled, *(() if written is None else (written,)))
 
 
 def final_kernel(
@@ -330,10 +364,10 @@
             jnp.where(core == c, bit_of(step, c), 0) for c in range(lax.axis_size("tok"))
         )
         distance |= (block >> step & 1) << bit
-    source = (lax.axis_index("feat") ^ distance) * rows + place % ROWS // pieces
+    source = (lax.axis_index("feat") ^ distance) * rows + place % rows
     order = jnp.where(token == source, 1.0, 0.0).astype(jnp.bfloat16)
     spread = jnp.dot(order, pre_grad, preferred_element_type=jnp.float32)
-    piece = lax.broadcasted_iota(jnp.int32, (depth, slots), 0) % pieces
+    piece = lax.broadcasted_iota(jnp.int32, (depth, slots), 0) % ROWS // rows
     copies = []
     for c in range(0, pieces, 2):
         pair = [jnp.where(piece == c + i, spread, 0.0).astype(jnp.bfloat16) for i in range(2)]
@@ -369,7 +403,7 @@
 def local(tokens, b_pre, pre_codes, top_idx, blocks, counts, dict_rows):
     rows, count = tokens.shape[0], top_idx.shape[0]
     steps = feat_bits()
-    half = dict_rows.shape[1] // 2
+    width = dict_rows.shape[1]
     merged = min(MERGED, steps - 1) if count == ROWS else 0
 
     code, raw, total, sent, dict_rows, centered, tokens, bias = front(
@@ -378,8 +412,8 @@
     for step in range(steps):
         arrived = swapped(sent, step)
         if step == 0:
-            total_second, sent_second, block, bias = second(
-                code, dict_rows, centered, tokens, bias, merged > 0
+            total_second, sent_second, block = second(
+                code, dict_rows, centered, tokens, merged > 0
             )
         else:
             own, previous = sent_second, arrived_second
@@ -389,23 +423,21 @@
         arrived_second = swapped(sent_second, step)
         if step >= merged:
             if step == merged > 0:
-                block = joined(own, previous, half, sent_second)
+                block = joined(own, previous, total_second.shape[1], sent_second)
             elif step > 0:
                 block = joined(block, arrived_block, 0, sent_second)
             arrived_block = swapped(block, step)
-        total = total + arrived.astype(jnp.float32)
-        sent = total.astype(jnp.bfloat16)
-    scaled_first = (0.25 * total).astype(jnp.bfloat16)
-    scaled_second = (0.25 * (total_second + arrived_second.astype(jnp.float32))).astype(
-        jnp.bfloat16
-    )
-    first = first_product(scaled_first, dict_rows)
-    code_half, scaled = code_half_of(scaled_first, scaled_second, first, dict_rows)
-    turned_tokens = turned(block, arrived_block, bias, code_half, count)
+        if step < steps - 1:
+            total = total + arrived.astype(jnp.float32)
+            sent = total.astype(jnp.bfloat16)
+    scaled, product_first = products(total, arrived, dict_rows)
+    grad_rows, mark = grad_rows_part(code, scaled, width)
+    scaled, code_half = products(
+        total_second, arrived_second, dict_rows, product_first, mark
+    )
     theirs = lax.ppermute(code_half, "tok", [(i, 1 - i) for i in range(2)])
-    grad_rows = lax.dot_general(
-        code, scaled, (((0,), (0,)), ((), ())), preferred_element_type=jnp.float32
-    ).astype(jnp.bfloat16)
+    grad_rows, _ = grad_rows_part(code, scaled, width, grad_rows)
+    turned_tokens = turned(block, arrived_block, bias, code_half, rows, count)
     grad_enc, grad_benc = final(raw, code_half, theirs, turned_tokens, rows)
     return (grad_rows, grad_enc, grad_benc.reshape(-1))
 

time: 26.3 us -> 26.1 us (level)
  Pallas kernels: 4.84 us -> 7.45 us
  waiting for transfers between devices: 5.14 us -> 3.15 us
  matrix products: 1.42 us -> 0 us
  starting transfers between devices: 12.6 us -> 13.2 us
    pallas_call x4 -> x6, Pallas kernels: 1.32 us -> 3.95 us  [the longest x2 2.68 us: grad_rows_part(): pl.pallas_call(functools.partial(grad_rows_kernel, at), out_shape=(shape(...]
    ppermute x7, waiting for transfers between devices: 5.14 us -> 3.15 us  [swapped(): return lax.ppermute(shard, ('feat', 'tok'), pairs)]
    dot_general x1 -> x0, matrix products: 1.42 us -> none  [local(): lax.dot_general(code, scaled, (((0,), (0,)), ((), ())), preferred_element...]
    ppermute x7, starting transfers between devices: 12.6 us -> 13.1 us  [swapped(): return lax.ppermute(shard, ('feat', 'tok'), pairs)]
  transfers between devices with their start and end apart: 8 -> 8, of which waited for: 4 -> 3; matrix products, arithmetic and copies ran while one was open for 6% -> 0% of each run, Pallas kernels for 5% -> 15%
where the time goes in v11:
time: 26.1 us; the launch traced here: 25.8 us
  starting transfers between devices  13.2 us (51%)
  Pallas kernels  7.45 us (29%)
  waiting for transfers between devices  3.15 us (12%)
  between operations  2 us (8%)
    ppermute x7, starting transfers between devices, swapped(): return lax.ppermute(shard, ('feat', 'tok'), pairs)  13.1 us
    ppermute x7, waiting for transfers between devices, swapped(): return lax.ppermute(shard, ('feat', 'tok'), pairs)  3.15 us
    pallas_call x2, Pallas kernels, grad_rows_part(): pl.pallas_call(functools.partial(grad_rows_kernel, at), out_shape=(shape(...  2.68 us
    pallas_call x1, Pallas kernels, final(): kernel_call(functools.partial(final_kernel, rows), (shape(width, slots),...  1.94 us
    pallas_call x1, Pallas kernels, front(): kernel_call(front_kernel, (shape(count, slots), shape(count, slots, dtype...  1.53 us
    pallas_call x1, Pallas kernels, second(): kernel_call(second_kernel, (shape(count, chunk, dtype=jnp.float32), shape...  0.68 us
  transfers between devices with their start and end apart: 8, of which 3 were waited for; matrix products, arithmetic and copies ran while one was open for 0% of the time, Pallas kernels for 15%

profile of v11, /device:TPU:0, one launch (start us, length us, event | category | flops | bytes accessed | tf_op | source)
XLA Modules:
  0.0 25.8 jit_solution(7980660913124160046)
XLA Ops:
  1.9 1.5 %shard_map.94 = (bf16[16,128]{1,0:T(8,128)(2,1)S(1)}, f32[16,128]{1,0:T(8,128)S(1)}, f32[16,2048]{1,0:T(8,128)S(1)}, bf16[16,2048]{1,0:T(8,128)(2,1)S(1)}, bf16[...) custom-call(bf16[2,4096]{1,0:T(2,128)(2,1)} %tokens_hbm.1, ...), custom_call_target="tpu_custom_call" | custom-call | flops 1000000 | bytes 1048576 | tf_op jit(solution)/shard_map/pallas_call | solution.py:143
  3.5 3.0 %collective-permute-start.1 = (bf16[16,2048]{1,0:T(8,128)(2,1)S(1)}, bf16[16,2048]{1,0:T(8,128)(2,1)S(1)}, u32[]{:S(2)}, u32[]{:S(2)}) collective-permute-start(bf16[16,2048]{1,0:T(8,128)(2,1)S(1)} %get-tuple-element.33), channel_id=1, source_target_pairs={{0,2},{1,9},{2,0},{3,11},{4,6},{5,13},{6,4},{7,15},{8,10},{9,1},{1... | collective-permute-start | bytes 196616 | tf_op jit(solution)/shard_map/ppermute | solution.py:56
  6.5 0.7 %shard_map.95 = (f32[16,2048]{1,0:T(8,128)S(1)}, bf16[16,2560]{1,0:T(8,128)(2,1)S(1)}, bf16[16,512]{1,0:T(8,128)(2,1)}) custom-call(bf16[16,128]{1,0:T(8,128)(2,1)S(1)} %get-tuple-element.26.code_ref, bf16[128,4096]{1,0:T(8,128)(2,1)S(1)} %get-tuple-element.27.rows_ref, f32[2,4096]{1,0:T(2,128)S(1)} %get-tuple-element.28.centered_ref, ...), custom_call_target="tpu_custom_call" | custom-call | flops 1000000 | bytes 1048576 | tf_op jit(solution)/shard_map/pallas_call | solution.py:190
  7.1 0.0 collective-permute-start
  7.2 1.5 %collective-permute-done.1 = bf16[16,2048]{1,0:T(8,128)(2,1)S(1)} collective-permute-done((bf16[16,2048]{1,0:T(8,128)(2,1)S(1)}, bf16[16,2048]{1,0:T(8,128)(2,1)S(1)}, u32[]{:S(2)}, u32[]{:S(2)}) %collective-permute-start.1) | collective-permute-done | bytes 65568 | tf_op jit(solution)/shard_map/ppermute | solution.py:56
  8.7 3.2 %collective-permute-start.3 = (bf16[16,2048]{1,0:T(8,128)(2,1)S(1)}, bf16[16,2048]{1,0:T(8,128)(2,1)S(1)}, u32[]{:S(2)}, u32[]{:S(2)}) collective-permute-start(bf16[16,2048]{1,0:T(8,128)(2,1)S(1)} %fusion.after_ref), channel_id=1, source_target_pairs={{0,8},{1,5},{2,10},{3,7},{4,12},{5,1},{6,14},{7,3},{8,0},{9,13},{1... | collective-permute-start | bytes 196616 | tf_op jit(solution)/shard_map/ppermute | solution.py:56
  11.9 0.0 collective-permute-done.arrived_ref
  11.9 2.3 %collective-permute-start.2 = (bf16[16,3072]{1,0:T(8,128)(2,1)S(1)}, bf16[16,3072]{1,0:T(8,128)(2,1)S(1)}, u32[]{:S(2)}, u32[]{:S(2)}) collective-permute-start(bf16[16,3072]{1,0:T(8,128)(2,1)S(1)} %get-tuple-element.35.own_ref.first_ref), channel_id=1, source_target_pairs={{0,8},{1,5},{2,10},{3,7},{4,12},{5,1},{6,14},{7,3},{8,0},{9,13},{1... | collective-permute-start | bytes 294920 | tf_op jit(solution)/shard_map/ppermute | solution.py:56
  14.3 0.0 collective-permute-done.3
  14.3 2.5 %collective-permute-start.5 = (bf16[16,2048]{1,0:T(8,128)(2,1)S(1)}, bf16[16,2048]{1,0:T(8,128)(2,1)S(1)}, u32[]{:S(2)}, u32[]{:S(2)}) collective-permute-start(bf16[16,2048]{1,0:T(8,128)(2,1)S(1)} %get-tuple-element.49.after_ref), channel_id=1, source_target_pairs={{0,4},{1,3},{2,6},{3,1},{4,0},{5,7},{6,2},{7,5},{8,12},{9,11},{10,... | collective-permute-start | bytes 196616 | tf_op jit(solution)/shard_map/ppermute | solution.py:56
  16.8 0.7 %collective-permute-done.2.arrived_ref.second_ref = bf16[16,3072]{1,0:T(8,128)(2,1)S(1)} collective-permute-done((bf16[16,3072]{1,0:T(8,128)(2,1)S(1)}, bf16[16,3072]{1,0:T(8,128)(2,1)S(1)}, u32[]{:S(2)}, u32[]{:S(2)}) %collective-permute-start.2) | collective-permute-done | bytes 98336 | tf_op jit(solution)/shard_map/ppermute | solution.py:56
  17.5 1.7 %collective-permute-start.4 = (bf16[16,2048]{1,0:T(8,128)(2,1)S(1)}, bf16[16,2048]{1,0:T(8,128)(2,1)S(1)}, u32[]{:S(2)}, u32[]{:S(2)}) collective-permute-start(bf16[16,2048]{1,0:T(8,128)(2,1)S(1)} %get-tuple-element.37.after_ref), channel_id=1, source_target_pairs={{0,4},{1,3},{2,6},{3,1},{4,0},{5,7},{6,2},{7,5},{8,12},{9,11},{10,... | collective-permute-start | bytes 196616 | tf_op jit(solution)/shard_map/ppermute | solution.py:56
  19.2 0.4 %collective-permute-start.7 = (bf16[16,2048]{1,0:T(8,128)(2,1)S(1)}, bf16[16,2048]{1,0:T(8,128)(2,1)S(1)}, u32[]{:S(2)}, u32[]{:S(2)}) collective-permute-start(bf16[16,2048]{1,0:T(8,128)(2,1)S(1)} %shard_map.102.own_ref), channel_id=1, source_target_pairs={{0,4},{1,3},{2,6},{3,1},{4,0},{5,7},{6,2},{7,5},{8,12},{9,11},{10,... | collective-permute-start | bytes 196616 | tf_op jit(solution)/shard_map/ppermute | solution.py:56
  19.6 0.0 collective-permute-done.5.arrived_ref
  19.6 0.2 shard_map.98
  19.9 1.1 %shard_map.99 = (bf16[128,4096]{1,0:T(8,128)(2,1)}, f32[1,128]{1,0:T(1,128)S(1)}) custom-call(bf16[16,128]{1,0:T(8,128)(2,1)S(1)} %get-tuple-element.26.code_ref, bf16[16,2048]{1,0:T(8,128)(2,1)S(1)} %get-tuple-element.39.scaled_ref), custom_call_target="tpu_custom_call" | custom-call | flops 1000000 | bytes 1048576 | tf_op jit(solution)/shard_map/pallas_call | solution.py:334
  21.0 0.9 %collective-permute-done.4.arrived_ref = bf16[16,2048]{1,0:T(8,128)(2,1)S(1)} collective-permute-done((bf16[16,2048]{1,0:T(8,128)(2,1)S(1)}, bf16[16,2048]{1,0:T(8,128)(2,1)S(1)}, u32[]{:S(2)}, u32[]{:S(2)}) %collective-permute-start.4) | collective-permute-done | bytes 65568 | tf_op jit(solution)/shard_map/ppermute | solution.py:56
  21.9 0.2 shard_map.100
  22.1 0.0 collective-permute-start.6
  22.1 1.6 %shard_map.101 = (bf16[128,4096]{1,0:T(8,128)(2,1)}, f32[1,128]{1,0:T(1,128)}) custom-call(bf16[16,128]{1,0:T(8,128)(2,1)S(1)} %get-tuple-element.26.code_ref, bf16[16,2048]{1,0:T(8,128)(2,1)S(1)} %get-tuple-element.41.scaled_ref, bf16[128,4096]{1,0:T(8,128)(2,1)} %get-tuple-element.42.refs_0_), custom_call_target="tpu_custom_call", output_to_operand_aliasing={{0}: (2, {})} | custom-call | flops 1000000 | bytes 1048576 | tf_op jit(solution)/shard_map/pallas_call | solution.py:334
  23.7 0.0 collective-permute-done.7.arrived_ref
  23.7 0.1 shard_map.103.turned_ref
  23.9 0.0 collective-permute-done.6.theirs_ref
  23.9 1.9 %shard_map.104 = (bf16[4096,128]{1,0:T(8,128)(2,1)}, f32[1,128]{1,0:T(1,128)}) custom-call(f32[16,128]{1,0:T(8,128)S(1)} %get-tuple-element.44.raw_ref, f32[16,128]{1,0:T(8,128)S(1)} %get-tuple-element.45.after_ref.mine_ref, f32[16,128]{1,0:T(8,128)S(1)} %collective-permute-done.6.theirs_ref, bf16[512,128]{1,0:T(8,128)(2,1)S(1)} %shard_map.103.turned_ref), custom_call_target="tpu_custom_call" | custom-call | flops 1000000 | bytes 1048576 | tf_op jit(solution)/shard_map/pallas_call | solution.py:393
  (5 shorter events, 0.1 us)
Async XLA Ops:
  3.5 5.2 %collective-permute-start.1 = (bf16[16,2048]{1,0:T(8,128)(2,1)S(1)}, bf16[16,2048]{1,0:T(8,128)(2,1)S(1)}, u32[]{:S(2)}, u32[]{:S(2)}) collective-permute-start(bf16[16,2048]{1,0:T(8,128)(2,1)S(1)} %get-tuple-element.33), channel_id=1, source_target_pairs={{0,2},{1,9},{2,0},{3,11},{4,6},{5,13},{6,4},{7,15},{8,10},{9,1},{1... | collective-permute-start | bytes 196616 | tf_op jit(solution)/shard_map/ppermute | solution.py:56
  7.1 4.8 %collective-permute-start = (bf16[16,2560]{1,0:T(8,128)(2,1)S(1)}, bf16[16,2560]{1,0:T(8,128)(2,1)S(1)}, u32[]{:S(2)}, u32[]{:S(2)}) collective-permute-start(bf16[16,2560]{1,0:T(8,128)(2,1)S(1)} %get-tuple-element.31.own_ref), channel_id=1, source_target_pairs={{0,2},{1,9},{2,0},{3,11},{4,6},{5,13},{6,4},{7,15},{8,10},{9,1},{1... | collective-permute-start | bytes 245768 | tf_op jit(solution)/shard_map/ppermute | solution.py:56
  8.7 5.5 %collective-permute-start.3 = (bf16[16,2048]{1,0:T(8,128)(2,1)S(1)}, bf16[16,2048]{1,0:T(8,128)(2,1)S(1)}, u32[]{:S(2)}, u32[]{:S(2)}) collective-permute-start(bf16[16,2048]{1,0:T(8,128)(2,1)S(1)} %fusion.after_ref), channel_id=1, source_target_pairs={{0,8},{1,5},{2,10},{3,7},{4,12},{5,1},{6,14},{7,3},{8,0},{9,13},{1... | collective-permute-start | bytes 196616 | tf_op jit(solution)/shard_map/ppermute | solution.py:56
  11.9 5.6 %collective-permute-start.2 = (bf16[16,3072]{1,0:T(8,128)(2,1)S(1)}, bf16[16,3072]{1,0:T(8,128)(2,1)S(1)}, u32[]{:S(2)}, u32[]{:S(2)}) collective-permute-start(bf16[16,3072]{1,0:T(8,128)(2,1)S(1)} %get-tuple-element.35.own_ref.first_ref), channel_id=1, source_target_pairs={{0,8},{1,5},{2,10},{3,7},{4,12},{5,1},{6,14},{7,3},{8,0},{9,13},{1... | collective-permute-start | bytes 294920 | tf_op jit(solution)/shard_map/ppermute | solution.py:56
  14.3 5.4 %collective-permute-start.5 = (bf16[16,2048]{1,0:T(8,128)(2,1)S(1)}, bf16[16,2048]{1,0:T(8,128)(2,1)S(1)}, u32[]{:S(2)}, u32[]{:S(2)}) collective-permute-start(bf16[16,2048]{1,0:T(8,128)(2,1)S(1)} %get-tuple-element.49.after_ref), channel_id=1, source_target_pairs={{0,4},{1,3},{2,6},{3,1},{4,0},{5,7},{6,2},{7,5},{8,12},{9,11},{10,... | collective-permute-start | bytes 196616 | tf_op jit(solution)/shard_map/ppermute | solution.py:56
  17.5 4.3 %collective-permute-start.4 = (bf16[16,2048]{1,0:T(8,128)(2,1)S(1)}, bf16[16,2048]{1,0:T(8,128)(2,1)S(1)}, u32[]{:S(2)}, u32[]{:S(2)}) collective-permute-start(bf16[16,2048]{1,0:T(8,128)(2,1)S(1)} %get-tuple-element.37.after_ref), channel_id=1, source_target_pairs={{0,4},{1,3},{2,6},{3,1},{4,0},{5,7},{6,2},{7,5},{8,12},{9,11},{10,... | collective-permute-start | bytes 196616 | tf_op jit(solution)/shard_map/ppermute | solution.py:56
  19.2 4.5 %collective-permute-start.7 = (bf16[16,2048]{1,0:T(8,128)(2,1)S(1)}, bf16[16,2048]{1,0:T(8,128)(2,1)S(1)}, u32[]{:S(2)}, u32[]{:S(2)}) collective-permute-start(bf16[16,2048]{1,0:T(8,128)(2,1)S(1)} %shard_map.102.own_ref), channel_id=1, source_target_pairs={{0,4},{1,3},{2,6},{3,1},{4,0},{5,7},{6,2},{7,5},{8,12},{9,11},{10,... | collective-permute-start | bytes 196616 | tf_op jit(solution)/shard_map/ppermute | solution.py:56
  22.1 1.8 %collective-permute-start.6 = (f32[16,128]{1,0:T(8,128)S(1)}, f32[16,128]{1,0:T(8,128)S(1)}, u32[]{:S(2)}, u32[]{:S(2)}) collective-permute-start(f32[16,128]{1,0:T(8,128)S(1)} %get-tuple-element.45.after_ref.mine_ref), channel_id=1, source_target_pairs={{0,1},{1,0},{2,3},{3,2},{4,5},{5,4},{6,7},{7,6},{8,9},{9,8},{10,11... | collective-permute-start | bytes 24584 | tf_op jit(solution)/shard_map/ppermute | solution.py:438

commit v12 on v11

--- a/solution.py
+++ b/solution.py
@@ -171,16 +171,19 @@
     )
 
 
-def second_kernel(code_ref, rows_ref, centered_ref, tokens_ref, total_ref, sent_ref, block_ref):
+def second_kernel(
+    code_ref, rows_ref, centered_ref, tokens_ref, total_ref, sent_ref, block_ref=None
+):
     width = total_ref.shape[1]
     total = share(code_ref[...], rows_ref, centered_ref, rows_ref.shape[1] - width, width)
     total_ref[...] = total
     sent_ref[:, :width] = total.astype(jnp.bfloat16)
     pieces = ROWS // tokens_ref.shape[0]
     block = stacked(tokens_ref[...].astype(jnp.float32), pieces).astype(jnp.bfloat16)
-    block_ref[...] = block
-    if sent_ref.shape[1] > width:
+    if block_ref is None:
         sent_ref[:, width:] = block
+    else:
+        block_ref[...] = block
 
 
 def second(code, dict_rows, centered, tokens, merged):
@@ -192,10 +195,10 @@
         (
             shape(count, chunk, dtype=jnp.float32),
             shape(count, chunk + (block if merged else 0)),
-            shape(ROWS, block),
+            *([] if merged else [shape(ROWS, block)]),
         ),
         [VMEM] * 4,
-        (VMEM,) * 3,
+        (VMEM,) * (2 if merged else 3),
         count,
     )(code, dict_rows, centered, tokens)
 
@@ -304,9 +307,8 @@
     )(total, arrived, dict_rows, *first)
 
 
-def grad_rows_kernel(at, code_ref, scaled_ref, *refs):
-    out_hbm, mark_ref, out_ref, sems = refs[-4:]
-    mark_ref[...] = jnp.zeros_like(mark_ref)
+def grad_rows_kernel(at, code_ref, scaled_ref, other_ref, out_hbm, *refs):
+    out_ref, sems = refs[-2:]
     slots, width = out_ref.shape
     code = code_ref[...].astype(jnp.float32).T.astype(jnp.bfloat16)
     step = width // sems.shape[0]
@@ -326,34 +328,43 @@
         copy.wait()
 
 
+def first_rows_kernel(code_ref, scaled_ref, out_hbm, mark_ref, out_ref, sems):
+    mark_ref[...] = jnp.zeros_like(mark_ref)
+    grad_rows_kernel(0, code_ref, scaled_ref, None, out_hbm, out_ref, sems)
+
+
 def grad_rows_part(code, scaled, width, written=None):
     count, slots = code.shape
     chunk = scaled.shape[1]
-    at = 0 if written is None else width - chunk
     limit = (16 if count <= ROWS else 40) * 2**20
+    first = written is None
+    mark = shape(1, slots, dtype=jnp.float32)
     return pl.pallas_call(
-        functools.partial(grad_rows_kernel, at),
-        out_shape=(shape(slots, width), shape(1, slots, dtype=jnp.float32)),
-        in_specs=[VMEM] * 2 + ([] if written is None else [HBM]),
-        out_specs=(HBM, VMEM),
+        first_rows_kernel if first else functools.partial(grad_rows_kernel, width - chunk),
+        out_shape=(shape(slots, width), mark) if first else shape(slots, width),
+        in_specs=[VMEM] * 2 + ([] if first else [HBM]),
+        out_specs=(HBM, VMEM) if first else HBM,
         scratch_shapes=[
             pltpu.VMEM((slots, chunk), jnp.bfloat16),
             pltpu.SemaphoreType.DMA((2,)),
         ],
-        input_output_aliases={} if written is None else {2: 0},
+        input_output_aliases={} if first else {2: 0},
         compiler_params=pltpu.CompilerParams(vmem_limit_bytes=limit),
         cost_estimate=pl.CostEstimate(flops=10**6, bytes_accessed=2**20, transcendentals=0),
-    )(code, scaled, *(() if written is None else (written,)))
+    )(code, scaled, *(() if first else (written,)))
 
 
 def final_kernel(
-    rows, raw_ref, mine_ref, theirs_ref, turned_ref, enc_hbm, benc_ref, enc_ref, sems
+    rows, raw_ref, mine_ref, theirs_ref, turned_ref, enc_hbm, benc_hbm, enc_ref, benc_ref, sems
 ):
     count, slots = raw_ref.shape
     width, depth = turned_ref.shape
     pieces = ROWS // rows
     code_grad = mine_ref[...] + theirs_ref[...]
     pre_grad = jnp.where(raw_ref[...] > 0.0, code_grad, 0.0).astype(jnp.bfloat16)
+    benc_ref[...] = jnp.sum(pre_grad.astype(jnp.float32), axis=0, keepdims=True)
+    copies = [pltpu.make_async_copy(benc_ref, benc_hbm, sems.at[pieces // 2])]
+    copies[0].start()
     place = lax.broadcasted_iota(jnp.int32, (depth, count), 0)
     token = lax.broadcasted_iota(jnp.int32, (depth, count), 1)
     core = lax.axis_index("tok")
@@ -368,7 +379,6 @@
     order = jnp.where(token == source, 1.0, 0.0).astype(jnp.bfloat16)
     spread = jnp.dot(order, pre_grad, preferred_element_type=jnp.float32)
     piece = lax.broadcasted_iota(jnp.int32, (depth, slots), 0) % ROWS // rows
-    copies = []
     for c in range(0, pieces, 2):
         pair = [jnp.where(piece == c + i, spread, 0.0).astype(jnp.bfloat16) for i in range(2)]
         out = jnp.dot(
@@ -381,7 +391,6 @@
         part = pl.ds(c * width, 2 * width)
         copies.append(pltpu.make_async_copy(enc_ref.at[part], enc_hbm.at[part], sems.at[c // 2]))
         copies[-1].start()
-    benc_ref[...] = jnp.sum(pre_grad.astype(jnp.float32), axis=0, keepdims=True)
     for copy in copies:
         copy.wait()
 
@@ -394,9 +403,13 @@
         functools.partial(final_kernel, rows),
         (shape(width, slots), shape(1, slots, dtype=jnp.float32)),
         [VMEM] * 4,
-        (HBM, VMEM),
-        count,
-        [pltpu.VMEM((width, slots), jnp.bfloat16), pltpu.SemaphoreType.DMA((pieces // 2,))],
+        (HBM, HBM),
+        count,
+        [
+            pltpu.VMEM((width, slots), jnp.bfloat16),
+            pltpu.VMEM((1, slots), jnp.float32),
+            pltpu.SemaphoreType.DMA((pieces // 2 + 1,)),
+        ],
     )(raw, mine, theirs, turned_tokens)
 
 
@@ -412,7 +425,7 @@
     for step in range(steps):
         arrived = swapped(sent, step)
         if step == 0:
-            total_second, sent_second, block = second(
+            total_second, sent_second, *block = second(
                 code, dict_rows, centered, tokens, merged > 0
             )
         else:
@@ -424,7 +437,9 @@
         if step >= merged:
             if step == merged > 0:
                 block = joined(own, previous, total_second.shape[1], sent_second)
-            elif step > 0:
+            elif step == 0:
+                (block,) = block
+            else:
                 block = joined(block, arrived_block, 0, sent_second)
             arrived_block = swapped(block, step)
         if step < steps - 1:
@@ -436,7 +451,7 @@
         total_second, arrived_second, dict_rows, product_first, mark
     )
     theirs = lax.ppermute(code_half, "tok", [(i, 1 - i) for i in range(2)])
-    grad_rows, _ = grad_rows_part(code, scaled, width, grad_rows)
+    grad_rows = grad_rows_part(code, scaled, width, grad_rows)
     turned_tokens = turned(block, arrived_block, bias, code_half, rows, count)
     grad_enc, grad_benc = final(raw, code_half, theirs, turned_tokens, rows)
     return (grad_rows, grad_enc, grad_benc.reshape(-1))

time: 26.1 us -> 25.3 us (0.969)
  Pallas kernels: 7.45 us -> 5.94 us
  waiting for transfers between devices: 3.15 us -> 4.17 us
  starting transfers between devices: 13.2 us -> 12.9 us
    ppermute x7, waiting for transfers between devices: 3.15 us -> 4.17 us  [swapped(): return lax.ppermute(shard, ('feat', 'tok'), pairs)]
    pallas_call x2, Pallas kernels: 2.68 us -> 2.17 us  [grad_rows_part(): pl.pallas_call(first_rows_kernel if first else functools.partial(grad_row...]
    pallas_call x1, Pallas kernels: 1.94 us -> 1.44 us  [final(): kernel_call(functools.partial(final_kernel, rows), (shape(width, slots),...]
    pallas_call x1, Pallas kernels: 0.68 us -> 0.19 us  [second(): kernel_call(second_kernel, (shape(count, chunk, dtype=jnp.float32), shape...]
    ppermute x7, starting transfers between devices: 13.1 us -> 12.9 us  [swapped(): return lax.ppermute(shard, ('feat', 'tok'), pairs)]
  transfers between devices with their start and end apart: 8 -> 8, of which waited for: 3 -> 5; matrix products, arithmetic and copies ran while one was open for 0% -> 0% of each run, Pallas kernels for 15% -> 12%
where the time goes in v12:
time: 25.3 us; the launch traced here: 25.1 us
  starting transfers between devices  12.9 us (51%)
  Pallas kernels  5.94 us (23%)
  waiting for transfers between devices  4.17 us (16%)
  between operations  1.99 us (8%)
    ppermute x7, starting transfers between devices, swapped(): return lax.ppermute(shard, ('feat', 'tok'), pairs)  12.9 us
    ppermute x7, waiting for transfers between devices, swapped(): return lax.ppermute(shard, ('feat', 'tok'), pairs)  4.17 us
    pallas_call x2, Pallas kernels, grad_rows_part(): pl.pallas_call(first_rows_kernel if first else functools.partial(grad_row...  2.17 us
    pallas_call x1, Pallas kernels, front(): kernel_call(front_kernel, (shape(count, slots), shape(count, slots, dtype...  1.53 us
    pallas_call x1, Pallas kernels, final(): kernel_call(functools.partial(final_kernel, rows), (shape(width, slots),...  1.44 us
  transfers between devices with their start and end apart: 8, of which 5 were waited for; matrix products, arithmetic and copies ran while one was open for 0% of the time, Pallas kernels for 12%

profile of v12, /device:TPU:0, one launch (start us, length us, event | category | flops | bytes accessed | tf_op | source)
XLA Modules:
  0.0 25.1 jit_solution(7580852798516230112)
XLA Ops:
  1.9 1.5 %shard_map.94 = (bf16[16,128]{1,0:T(8,128)(2,1)S(1)}, f32[16,128]{1,0:T(8,128)S(1)}, f32[16,2048]{1,0:T(8,128)S(1)}, bf16[16,2048]{1,0:T(8,128)(2,1)S(1)}, bf16[...) custom-call(bf16[2,4096]{1,0:T(2,128)(2,1)} %tokens_hbm.1, ...), custom_call_target="tpu_custom_call" | custom-call | flops 1000000 | bytes 1048576 | tf_op jit(solution)/shard_map/pallas_call | solution.py:143
  3.5 3.0 %collective-permute-start.1 = (bf16[16,2048]{1,0:T(8,128)(2,1)S(1)}, bf16[16,2048]{1,0:T(8,128)(2,1)S(1)}, u32[]{:S(2)}, u32[]{:S(2)}) collective-permute-start(bf16[16,2048]{1,0:T(8,128)(2,1)S(1)} %get-tuple-element.32), channel_id=1, source_target_pairs={{0,2},{1,9},{2,0},{3,11},{4,6},{5,13},{6,4},{7,15},{8,10},{9,1},{1... | collective-permute-start | bytes 196616 | tf_op jit(solution)/shard_map/ppermute | solution.py:56
  6.5 0.2 shard_map.95
  6.6 0.1 collective-permute-start
  6.7 2.0 %collective-permute-done.1 = bf16[16,2048]{1,0:T(8,128)(2,1)S(1)} collective-permute-done((bf16[16,2048]{1,0:T(8,128)(2,1)S(1)}, bf16[16,2048]{1,0:T(8,128)(2,1)S(1)}, u32[]{:S(2)}, u32[]{:S(2)}) %collective-permute-start.1) | collective-permute-done | bytes 65568 | tf_op jit(solution)/shard_map/ppermute | solution.py:56
  8.7 3.2 %collective-permute-start.3 = (bf16[16,2048]{1,0:T(8,128)(2,1)S(1)}, bf16[16,2048]{1,0:T(8,128)(2,1)S(1)}, u32[]{:S(2)}, u32[]{:S(2)}) collective-permute-start(bf16[16,2048]{1,0:T(8,128)(2,1)S(1)} %fusion.after_ref), channel_id=1, source_target_pairs={{0,8},{1,5},{2,10},{3,7},{4,12},{5,1},{6,14},{7,3},{8,0},{9,13},{1... | collective-permute-start | bytes 196616 | tf_op jit(solution)/shard_map/ppermute | solution.py:56
  11.9 0.0 collective-permute-done.arrived_ref
  11.9 1.9 %collective-permute-start.2 = (bf16[16,3072]{1,0:T(8,128)(2,1)S(1)}, bf16[16,3072]{1,0:T(8,128)(2,1)S(1)}, u32[]{:S(2)}, u32[]{:S(2)}) collective-permute-start(bf16[16,3072]{1,0:T(8,128)(2,1)S(1)} %get-tuple-element.34.own_ref.first_ref), channel_id=1, source_target_pairs={{0,8},{1,5},{2,10},{3,7},{4,12},{5,1},{6,14},{7,3},{8,0},{9,13},{1... | collective-permute-start | bytes 294920 | tf_op jit(solution)/shard_map/ppermute | solution.py:56
  13.8 0.3 %collective-permute-done.3 = bf16[16,2048]{1,0:T(8,128)(2,1)S(1)} collective-permute-done((bf16[16,2048]{1,0:T(8,128)(2,1)S(1)}, bf16[16,2048]{1,0:T(8,128)(2,1)S(1)}, u32[]{:S(2)}, u32[]{:S(2)}) %collective-permute-start.3) | collective-permute-done | bytes 65568 | tf_op jit(solution)/shard_map/ppermute | solution.py:56
  14.2 2.6 %collective-permute-start.5 = (bf16[16,2048]{1,0:T(8,128)(2,1)S(1)}, bf16[16,2048]{1,0:T(8,128)(2,1)S(1)}, u32[]{:S(2)}, u32[]{:S(2)}) collective-permute-start(bf16[16,2048]{1,0:T(8,128)(2,1)S(1)} %get-tuple-element.47.after_ref), channel_id=1, source_target_pairs={{0,4},{1,3},{2,6},{3,1},{4,0},{5,7},{6,2},{7,5},{8,12},{9,11},{10,... | collective-permute-start | bytes 196616 | tf_op jit(solution)/shard_map/ppermute | solution.py:56
  16.8 0.7 %collective-permute-done.2.arrived_ref.second_ref = bf16[16,3072]{1,0:T(8,128)(2,1)S(1)} collective-permute-done((bf16[16,3072]{1,0:T(8,128)(2,1)S(1)}, bf16[16,3072]{1,0:T(8,128)(2,1)S(1)}, u32[]{:S(2)}, u32[]{:S(2)}) %collective-permute-start.2) | collective-permute-done | bytes 98336 | tf_op jit(solution)/shard_map/ppermute | solution.py:56
  17.5 1.7 %collective-permute-start.4 = (bf16[16,2048]{1,0:T(8,128)(2,1)S(1)}, bf16[16,2048]{1,0:T(8,128)(2,1)S(1)}, u32[]{:S(2)}, u32[]{:S(2)}) collective-permute-start(bf16[16,2048]{1,0:T(8,128)(2,1)S(1)} %get-tuple-element.36.after_ref), channel_id=1, source_target_pairs={{0,4},{1,3},{2,6},{3,1},{4,0},{5,7},{6,2},{7,5},{8,12},{9,11},{10,... | collective-permute-start | bytes 196616 | tf_op jit(solution)/shard_map/ppermute | solution.py:56
  19.2 0.4 %collective-permute-start.7 = (bf16[16,2048]{1,0:T(8,128)(2,1)S(1)}, bf16[16,2048]{1,0:T(8,128)(2,1)S(1)}, u32[]{:S(2)}, u32[]{:S(2)}) collective-permute-start(bf16[16,2048]{1,0:T(8,128)(2,1)S(1)} %shard_map.102.own_ref), channel_id=1, source_target_pairs={{0,4},{1,3},{2,6},{3,1},{4,0},{5,7},{6,2},{7,5},{8,12},{9,11},{10,... | collective-permute-start | bytes 196616 | tf_op jit(solution)/shard_map/ppermute | solution.py:56
  19.6 0.0 collective-permute-done.5.arrived_ref
  19.6 0.2 shard_map.98
  19.9 1.1 %shard_map.99 = (bf16[128,4096]{1,0:T(8,128)(2,1)}, f32[1,128]{1,0:T(1,128)S(1)}) custom-call(bf16[16,128]{1,0:T(8,128)(2,1)S(1)} %get-tuple-element.25.code_ref, bf16[16,2048]{1,0:T(8,128)(2,1)S(1)} %get-tuple-element.38.scaled_ref), custom_call_target="tpu_custom_call" | custom-call | flops 1000000 | bytes 1048576 | tf_op jit(solution)/shard_map/pallas_call | solution.py:342
  21.0 0.9 %collective-permute-done.4.arrived_ref = bf16[16,2048]{1,0:T(8,128)(2,1)S(1)} collective-permute-done((bf16[16,2048]{1,0:T(8,128)(2,1)S(1)}, bf16[16,2048]{1,0:T(8,128)(2,1)S(1)}, u32[]{:S(2)}, u32[]{:S(2)}) %collective-permute-start.4) | collective-permute-done | bytes 65568 | tf_op jit(solution)/shard_map/ppermute | solution.py:56
  21.9 0.2 shard_map.100
  22.1 0.0 collective-permute-start.6
  22.1 1.1 %shard_map.101 = bf16[128,4096]{1,0:T(8,128)(2,1)} custom-call(bf16[16,128]{1,0:T(8,128)(2,1)S(1)} %get-tuple-element.25.code_ref, bf16[16,2048]{1,0:T(8,128)(2,1)S(1)} %get-tuple-element.40.scaled_ref, bf16[128,4096]{1,0:T(8,128)(2,1)} %get-tuple-element.41.other_ref), custom_call_target="tpu_custom_call", output_to_operand_aliasing={{}: (2, {})} | custom-call | flops 1000000 | bytes 1048576 | tf_op jit(solution)/shard_map/pallas_call | solution.py:342
  23.2 0.3 %collective-permute-done.7.arrived_ref = bf16[16,2048]{1,0:T(8,128)(2,1)S(1)} collective-permute-done((bf16[16,2048]{1,0:T(8,128)(2,1)S(1)}, bf16[16,2048]{1,0:T(8,128)(2,1)S(1)}, u32[]{:S(2)}, u32[]{:S(2)}) %collective-permute-start.7) | collective-permute-done | bytes 65568 | tf_op jit(solution)/shard_map/ppermute | solution.py:56
  23.5 0.1 shard_map.103.turned_ref
  23.6 0.0 collective-permute-done.6.theirs_ref
  23.6 1.4 %shard_map.104 = (bf16[4096,128]{1,0:T(8,128)(2,1)}, f32[1,128]{1,0:T(1,128)}) custom-call(f32[16,128]{1,0:T(8,128)S(1)} %get-tuple-element.42.raw_ref, f32[16,128]{1,0:T(8,128)S(1)} %get-tuple-element.43.after_ref.mine_ref, f32[16,128]{1,0:T(8,128)S(1)} %collective-permute-done.6.theirs_ref, bf16[512,128]{1,0:T(8,128)(2,1)S(1)} %shard_map.103.turned_ref), custom_call_target="tpu_custom_call" | custom-call | flops 1000000 | bytes 1048576 | tf_op jit(solution)/shard_map/pallas_call | solution.py:402
  (5 shorter events, 0.1 us)
Async XLA Ops:
  3.5 5.2 %collective-permute-start.1 = (bf16[16,2048]{1,0:T(8,128)(2,1)S(1)}, bf16[16,2048]{1,0:T(8,128)(2,1)S(1)}, u32[]{:S(2)}, u32[]{:S(2)}) collective-permute-start(bf16[16,2048]{1,0:T(8,128)(2,1)S(1)} %get-tuple-element.32), channel_id=1, source_target_pairs={{0,2},{1,9},{2,0},{3,11},{4,6},{5,13},{6,4},{7,15},{8,10},{9,1},{1... | collective-permute-start | bytes 196616 | tf_op jit(solution)/shard_map/ppermute | solution.py:56
  6.6 5.3 %collective-permute-start = (bf16[16,2560]{1,0:T(8,128)(2,1)S(1)}, bf16[16,2560]{1,0:T(8,128)(2,1)S(1)}, u32[]{:S(2)}, u32[]{:S(2)}) collective-permute-start(bf16[16,2560]{1,0:T(8,128)(2,1)S(1)} %get-tuple-element.30.own_ref), channel_id=1, source_target_pairs={{0,2},{1,9},{2,0},{3,11},{4,6},{5,13},{6,4},{7,15},{8,10},{9,1},{1... | collective-permute-start | bytes 245768 | tf_op jit(solution)/shard_map/ppermute | solution.py:56
  8.7 5.4 %collective-permute-start.3 = (bf16[16,2048]{1,0:T(8,128)(2,1)S(1)}, bf16[16,2048]{1,0:T(8,128)(2,1)S(1)}, u32[]{:S(2)}, u32[]{:S(2)}) collective-permute-start(bf16[16,2048]{1,0:T(8,128)(2,1)S(1)} %fusion.after_ref), channel_id=1, source_target_pairs={{0,8},{1,5},{2,10},{3,7},{4,12},{5,1},{6,14},{7,3},{8,0},{9,13},{1... | collective-permute-start | bytes 196616 | tf_op jit(solution)/shard_map/ppermute | solution.py:56
  11.9 5.6 %collective-permute-start.2 = (bf16[16,3072]{1,0:T(8,128)(2,1)S(1)}, bf16[16,3072]{1,0:T(8,128)(2,1)S(1)}, u32[]{:S(2)}, u32[]{:S(2)}) collective-permute-start(bf16[16,3072]{1,0:T(8,128)(2,1)S(1)} %get-tuple-element.34.own_ref.first_ref), channel_id=1, source_target_pairs={{0,8},{1,5},{2,10},{3,7},{4,12},{5,1},{6,14},{7,3},{8,0},{9,13},{1... | collective-permute-start | bytes 294920 | tf_op jit(solution)/shard_map/ppermute | solution.py:56
  14.2 5.5 %collective-permute-start.5 = (bf16[16,2048]{1,0:T(8,128)(2,1)S(1)}, bf16[16,2048]{1,0:T(8,128)(2,1)S(1)}, u32[]{:S(2)}, u32[]{:S(2)}) collective-permute-start(bf16[16,2048]{1,0:T(8,128)(2,1)S(1)} %get-tuple-element.47.after_ref), channel_id=1, source_target_pairs={{0,4},{1,3},{2,6},{3,1},{4,0},{5,7},{6,2},{7,5},{8,12},{9,11},{10,... | collective-permute-start | bytes 196616 | tf_op jit(solution)/shard_map/ppermute | solution.py:56
  17.5 4.3 %collective-permute-start.4 = (bf16[16,2048]{1,0:T(8,128)(2,1)S(1)}, bf16[16,2048]{1,0:T(8,128)(2,1)S(1)}, u32[]{:S(2)}, u32[]{:S(2)}) collective-permute-start(bf16[16,2048]{1,0:T(8,128)(2,1)S(1)} %get-tuple-element.36.after_ref), channel_id=1, source_target_pairs={{0,4},{1,3},{2,6},{3,1},{4,0},{5,7},{6,2},{7,5},{8,12},{9,11},{10,... | collective-permute-start | bytes 196616 | tf_op jit(solution)/shard_map/ppermute | solution.py:56
  19.2 4.3 %collective-permute-start.7 = (bf16[16,2048]{1,0:T(8,128)(2,1)S(1)}, bf16[16,2048]{1,0:T(8,128)(2,1)S(1)}, u32[]{:S(2)}, u32[]{:S(2)}) collective-permute-start(bf16[16,2048]{1,0:T(8,128)(2,1)S(1)} %shard_map.102.own_ref), channel_id=1, source_target_pairs={{0,4},{1,3},{2,6},{3,1},{4,0},{5,7},{6,2},{7,5},{8,12},{9,11},{10,... | collective-permute-start | bytes 196616 | tf_op jit(solution)/shard_map/ppermute | solution.py:56
  22.1 1.5 %collective-permute-start.6 = (f32[16,128]{1,0:T(8,128)S(1)}, f32[16,128]{1,0:T(8,128)S(1)}, u32[]{:S(2)}, u32[]{:S(2)}) collective-permute-start(f32[16,128]{1,0:T(8,128)S(1)} %get-tuple-element.43.after_ref.mine_ref), channel_id=1, source_target_pairs={{0,1},{1,0},{2,3},{3,2},{4,5},{5,4},{6,7},{7,6},{8,9},{9,8},{10,11... | collective-permute-start | bytes 24584 | tf_op jit(solution)/shard_map/ppermute | solution.py:453

commit v13 on v12

--- a/solution.py
+++ b/solution.py
@@ -76,26 +76,10 @@
 
 
 def front_kernel(
-    tokens_hbm,
-    bias_hbm,
-    pre_hbm,
-    top_hbm,
-    rows_hbm,
-    block_ref,
-    count_ref,
-    code_ref,
-    raw_ref,
-    total_ref,
-    sent_ref,
-    rows_ref,
-    centered_ref,
-    tokens_ref,
-    bias_ref,
-    bias_flat,
-    pre_ref,
-    top_ref,
-    sems,
+    tokens_hbm, bias_hbm, pre_hbm, top_hbm, rows_hbm, block_ref, count_ref, *refs
 ):
+    code_ref, raw_ref, total_ref, sent_ref, rows_ref, centered_ref, bias_ref, *cut = refs[:-5]
+    tokens_ref, bias_flat, pre_ref, top_ref, sems = refs[-5:]
     copies = [
         pltpu.make_async_copy(source, target, sems.at[i])
         for i, (source, target) in enumerate(
@@ -134,28 +118,36 @@
     copies[4].wait()
     total = share(code, rows_ref, centered_ref, 0, total_ref.shape[1])
     total_ref[...] = total
-    sent_ref[...] = total.astype(jnp.bfloat16)
-
-
-def front(tokens, b_pre, pre_codes, top_idx, blocks, counts, dict_rows):
+    width = total.shape[1]
+    sent_ref[:, :width] = total.astype(jnp.bfloat16)
+    block = stacked(tokens, ROWS // tokens.shape[0]).astype(jnp.bfloat16)
+    if cut:
+        cut[0][...] = block
+    else:
+        sent_ref[:, width:] = block
+
+
+def front(tokens, b_pre, pre_codes, top_idx, blocks, counts, dict_rows, merged):
     count = top_idx.shape[0]
     slots, width = dict_rows.shape
+    chunk, block = first_width(width), tokens.shape[0] * width // ROWS
     return kernel_call(
         front_kernel,
         (
             shape(count, slots),
             shape(count, slots, dtype=jnp.float32),
-            shape(count, first_width(width), dtype=jnp.float32),
-            shape(count, first_width(width)),
+            shape(count, chunk, dtype=jnp.float32),
+            shape(count, chunk + (block if merged else 0)),
             shape(slots, width),
             shape(*tokens.shape, dtype=jnp.float32),
-            shape(*tokens.shape),
             shape(1, width, dtype=jnp.float32),
+            *([] if merged else [shape(ROWS, block)]),
         ),
         [HBM] * 5 + [SMEM] * 2,
-        (VMEM,) * 8,
+        (VMEM,) * (7 if merged else 8),
         count,
         [
+            pltpu.VMEM(tokens.shape, tokens.dtype),
             pltpu.VMEM(b_pre.shape, b_pre.dtype),
             pltpu.VMEM(pre_codes.shape, pre_codes.dtype),
             pltpu.VMEM(top_idx.shape, top_idx.dtype),
@@ -171,36 +163,23 @@
     )
 
 
-def second_kernel(
-    code_ref, rows_ref, centered_ref, tokens_ref, total_ref, sent_ref, block_ref=None
-):
+def second_kernel(code_ref, rows_ref, centered_ref, total_ref, sent_ref):
     width = total_ref.shape[1]
     total = share(code_ref[...], rows_ref, centered_ref, rows_ref.shape[1] - width, width)
     total_ref[...] = total
-    sent_ref[:, :width] = total.astype(jnp.bfloat16)
-    pieces = ROWS // tokens_ref.shape[0]
-    block = stacked(tokens_ref[...].astype(jnp.float32), pieces).astype(jnp.bfloat16)
-    if block_ref is None:
-        sent_ref[:, width:] = block
-    else:
-        block_ref[...] = block
-
-
-def second(code, dict_rows, centered, tokens, merged):
+    sent_ref[...] = total.astype(jnp.bfloat16)
+
+
+def second(code, dict_rows, centered):
     count, width = code.shape[0], dict_rows.shape[1]
     chunk = width - first_width(width)
-    block = tokens.shape[0] * width // ROWS
     return kernel_call(
         second_kernel,
-        (
-            shape(count, chunk, dtype=jnp.float32),
-            shape(count, chunk + (block if merged else 0)),
-            *([] if merged else [shape(ROWS, block)]),
-        ),
-        [VMEM] * 4,
-        (VMEM,) * (2 if merged else 3),
-        count,
-    )(code, dict_rows, centered, tokens)
+        (shape(count, chunk, dtype=jnp.float32), shape(count, chunk)),
+        [VMEM] * 3,
+        (VMEM, VMEM),
+        count,
+    )(code, dict_rows, centered)
 
 
 def added_kernel(total_ref, own_ref, arrived_ref, after_ref, sum_ref, sent_ref):
@@ -419,32 +398,29 @@
     width = dict_rows.shape[1]
     merged = min(MERGED, steps - 1) if count == ROWS else 0
 
-    code, raw, total, sent, dict_rows, centered, tokens, bias = front(
-        tokens, b_pre, pre_codes, top_idx, blocks, counts, dict_rows
+    code, raw, total, sent, dict_rows, centered, bias, *block = front(
+        tokens, b_pre, pre_codes, top_idx, blocks, counts, dict_rows, merged > 0
     )
     for step in range(steps):
         arrived = swapped(sent, step)
         if step == 0:
-            total_second, sent_second, *block = second(
-                code, dict_rows, centered, tokens, merged > 0
-            )
+            total_second, sent_second = second(code, dict_rows, centered)
         else:
-            own, previous = sent_second, arrived_second
             total_second, sent_second = added(
-                total_second, own, previous, sent, step < merged
+                total_second, sent_second, arrived_second, sent, False
             )
         arrived_second = swapped(sent_second, step)
         if step >= merged:
             if step == merged > 0:
-                block = joined(own, previous, total_second.shape[1], sent_second)
+                block = joined(own, previous, total.shape[1], sent_second)
             elif step == 0:
                 (block,) = block
             else:
                 block = joined(block, arrived_block, 0, sent_second)
             arrived_block = swapped(block, step)
         if step < steps - 1:
-            total = total + arrived.astype(jnp.float32)
-            sent = total.astype(jnp.bfloat16)
+            own, previous = sent, arrived
+            total, sent = added(total, own, previous, sent_second, step + 1 < merged)
     scaled, product_first = products(total, arrived, dict_rows)
     grad_rows, mark = grad_rows_part(code, scaled, width)
     scaled, code_half = products(

time: 25.3 us -> 25.3 us (level)
  transfers between devices with their start and end apart: 8 -> 8, of which waited for: 5 -> 4; matrix products, arithmetic and copies ran while one was open for 0% -> 0% of each run, Pallas kernels for 12% -> 12%
where the time goes in v13:
time: 25.3 us; the launch traced here: 25 us
  starting transfers between devices  12.7 us (50%)
  Pallas kernels  5.99 us (24%)
  waiting for transfers between devices  4.32 us (17%)
  between operations  2 us (8%)
    ppermute x7, starting transfers between devices, swapped(): return lax.ppermute(shard, ('feat', 'tok'), pairs)  12.7 us
    ppermute x7, waiting for transfers between devices, swapped(): return lax.ppermute(shard, ('feat', 'tok'), pairs)  4.31 us
    pallas_call x2, Pallas kernels, grad_rows_part(): pl.pallas_call(first_rows_kernel if first else functools.partial(grad_row...  2.17 us
    pallas_call x1, Pallas kernels, front(): kernel_call(front_kernel, (shape(count, slots), shape(count, slots, dtype...  1.53 us
    pallas_call x1, Pallas kernels, final(): kernel_call(functools.partial(final_kernel, rows), (shape(width, slots),...  1.44 us
  transfers between devices with their start and end apart: 8, of which 4 were waited for; matrix products, arithmetic and copies ran while one was open for 0% of the time, Pallas kernels for 12%

profile of v13, /device:TPU:0, one launch (start us, length us, event | category | flops | bytes accessed | tf_op | source)
XLA Modules:
  0.0 25.0 jit_solution(9476218398101545507)
XLA Ops:
  1.9 1.5 %shard_map.94 = (bf16[16,128]{1,0:T(8,128)(2,1)S(1)}, f32[16,128]{1,0:T(8,128)S(1)}, f32[16,2048]{1,0:T(8,128)S(1)}, bf16[16,2560]{1,0:T(8,128)(2,1)S(1)}, bf16[...) custom-call(bf16[2,4096]{1,0:T(2,128)(2,1)} %tokens_hbm.1, bf16[4096]{0:T(1024)(128)(2,1)} %bias_hbm.1, ...), custom_call_target="tpu_custom_call" | custom-call | flops 1000000 | bytes 1048576 | tf_op jit(solution)/shard_map/pallas_call | solution.py:134
  3.5 3.0 %collective-permute-start.1 = (bf16[16,2560]{1,0:T(8,128)(2,1)S(1)}, bf16[16,2560]{1,0:T(8,128)(2,1)S(1)}, u32[]{:S(2)}, u32[]{:S(2)}) collective-permute-start(bf16[16,2560]{1,0:T(8,128)(2,1)S(1)} %get-tuple-element.34.own_ref), channel_id=1, source_target_pairs={{0,2},{1,9},{2,0},{3,11},{4,6},{5,13},{6,4},{7,15},{8,10},{9,1},{1... | collective-permute-start | bytes 245768 | tf_op jit(solution)/shard_map/ppermute | solution.py:56
  6.5 0.2 shard_map.95
  6.7 0.1 collective-permute-start
  6.7 2.2 %collective-permute-done.1.arrived_ref = bf16[16,2560]{1,0:T(8,128)(2,1)S(1)} collective-permute-done((bf16[16,2560]{1,0:T(8,128)(2,1)S(1)}, bf16[16,2560]{1,0:T(8,128)(2,1)S(1)}, u32[]{:S(2)}, u32[]{:S(2)}) %collective-permute-start.1) | collective-permute-done | bytes 81952 | tf_op jit(solution)/shard_map/ppermute | solution.py:56
  8.9 3.2 %collective-permute-start.3 = (bf16[16,3072]{1,0:T(8,128)(2,1)S(1)}, bf16[16,3072]{1,0:T(8,128)(2,1)S(1)}, u32[]{:S(2)}, u32[]{:S(2)}) collective-permute-start(bf16[16,3072]{1,0:T(8,128)(2,1)S(1)} %get-tuple-element.35.after_ref.own_ref.first_ref), channel_id=1, source_target_pairs={{0,8},{1,5},{2,10},{3,7},{4,12},{5,1},{6,14},{7,3},{8,0},{9,13},{1... | collective-permute-start | bytes 294920 | tf_op jit(solution)/shard_map/ppermute | solution.py:56
  12.1 0.0 collective-permute-done.arrived_ref
  12.1 1.5 %collective-permute-start.2 = (bf16[16,2048]{1,0:T(8,128)(2,1)S(1)}, bf16[16,2048]{1,0:T(8,128)(2,1)S(1)}, u32[]{:S(2)}, u32[]{:S(2)}) collective-permute-start(bf16[16,2048]{1,0:T(8,128)(2,1)S(1)} %get-tuple-element.37.after_ref.own_ref), channel_id=1, source_target_pairs={{0,8},{1,5},{2,10},{3,7},{4,12},{5,1},{6,14},{7,3},{8,0},{9,13},{1... | collective-permute-start | bytes 196616 | tf_op jit(solution)/shard_map/ppermute | solution.py:56
  13.7 1.3 %collective-permute-done.3.arrived_ref.second_ref = bf16[16,3072]{1,0:T(8,128)(2,1)S(1)} collective-permute-done((bf16[16,3072]{1,0:T(8,128)(2,1)S(1)}, bf16[16,3072]{1,0:T(8,128)(2,1)S(1)}, u32[]{:S(2)}, u32[]{:S(2)}) %collective-permute-start.3) | collective-permute-done | bytes 98336 | tf_op jit(solution)/shard_map/ppermute | solution.py:56
  14.9 2.8 %collective-permute-start.5 = (bf16[16,2048]{1,0:T(8,128)(2,1)S(1)}, bf16[16,2048]{1,0:T(8,128)(2,1)S(1)}, u32[]{:S(2)}, u32[]{:S(2)}) collective-permute-start(bf16[16,2048]{1,0:T(8,128)(2,1)S(1)} %get-tuple-element.39.after_ref), channel_id=1, source_target_pairs={{0,4},{1,3},{2,6},{3,1},{4,0},{5,7},{6,2},{7,5},{8,12},{9,11},{10,... | collective-permute-start | bytes 196616 | tf_op jit(solution)/shard_map/ppermute | solution.py:56
  17.7 0.0 collective-permute-done.2.arrived_ref
  17.7 1.4 %collective-permute-start.4 = (bf16[16,2048]{1,0:T(8,128)(2,1)S(1)}, bf16[16,2048]{1,0:T(8,128)(2,1)S(1)}, u32[]{:S(2)}, u32[]{:S(2)}) collective-permute-start(bf16[16,2048]{1,0:T(8,128)(2,1)S(1)} %get-tuple-element.41.after_ref), channel_id=1, source_target_pairs={{0,4},{1,3},{2,6},{3,1},{4,0},{5,7},{6,2},{7,5},{8,12},{9,11},{10,... | collective-permute-start | bytes 196616 | tf_op jit(solution)/shard_map/ppermute | solution.py:56
  19.1 0.7 %collective-permute-start.7 = (bf16[16,2048]{1,0:T(8,128)(2,1)S(1)}, bf16[16,2048]{1,0:T(8,128)(2,1)S(1)}, u32[]{:S(2)}, u32[]{:S(2)}) collective-permute-start(bf16[16,2048]{1,0:T(8,128)(2,1)S(1)} %shard_map.104.own_ref), channel_id=1, source_target_pairs={{0,4},{1,3},{2,6},{3,1},{4,0},{5,7},{6,2},{7,5},{8,12},{9,11},{10,... | collective-permute-start | bytes 196616 | tf_op jit(solution)/shard_map/ppermute | solution.py:56
  19.8 0.1 collective-permute-done.5.arrived_ref
  20.0 0.2 shard_map.100
  20.2 1.1 %shard_map.101 = (bf16[128,4096]{1,0:T(8,128)(2,1)}, f32[1,128]{1,0:T(1,128)S(1)}) custom-call(bf16[16,128]{1,0:T(8,128)(2,1)S(1)} %get-tuple-element.28.code_ref, bf16[16,2048]{1,0:T(8,128)(2,1)S(1)} %get-tuple-element.44.scaled_ref), custom_call_target="tpu_custom_call" | custom-call | flops 1000000 | bytes 1048576 | tf_op jit(solution)/shard_map/pallas_call | solution.py:321
  21.3 0.8 %collective-permute-done.4.arrived_ref = bf16[16,2048]{1,0:T(8,128)(2,1)S(1)} collective-permute-done((bf16[16,2048]{1,0:T(8,128)(2,1)S(1)}, bf16[16,2048]{1,0:T(8,128)(2,1)S(1)}, u32[]{:S(2)}, u32[]{:S(2)}) %collective-permute-start.4) | collective-permute-done | bytes 65568 | tf_op jit(solution)/shard_map/ppermute | solution.py:56
  22.1 0.2 shard_map.102
  22.3 0.0 collective-permute-start.6
  22.3 1.1 %shard_map.103 = bf16[128,4096]{1,0:T(8,128)(2,1)} custom-call(bf16[16,128]{1,0:T(8,128)(2,1)S(1)} %get-tuple-element.28.code_ref, bf16[16,2048]{1,0:T(8,128)(2,1)S(1)} %get-tuple-element.46.scaled_ref, bf16[128,4096]{1,0:T(8,128)(2,1)} %get-tuple-element.47.other_ref), custom_call_target="tpu_custom_call", output_to_operand_aliasing={{}: (2, {})} | custom-call | flops 1000000 | bytes 1048576 | tf_op jit(solution)/shard_map/pallas_call | solution.py:321
  23.4 0.0 collective-permute-done.7.arrived_ref
  23.4 0.1 shard_map.105.turned_ref
  23.5 0.0 collective-permute-done.6.theirs_ref
  23.6 1.4 %shard_map.106 = (bf16[4096,128]{1,0:T(8,128)(2,1)}, f32[1,128]{1,0:T(1,128)}) custom-call(f32[16,128]{1,0:T(8,128)S(1)} %get-tuple-element.48.raw_ref, f32[16,128]{1,0:T(8,128)S(1)} %get-tuple-element.49.after_ref.mine_ref, f32[16,128]{1,0:T(8,128)S(1)} %collective-permute-done.6.theirs_ref, bf16[512,128]{1,0:T(8,128)(2,1)S(1)} %shard_map.105.turned_ref), custom_call_target="tpu_custom_call" | custom-call | flops 1000000 | bytes 1048576 | tf_op jit(solution)/shard_map/pallas_call | solution.py:381
  (5 shorter events, 0.1 us)
Async XLA Ops:
  3.5 5.4 %collective-permute-start.1 = (bf16[16,2560]{1,0:T(8,128)(2,1)S(1)}, bf16[16,2560]{1,0:T(8,128)(2,1)S(1)}, u32[]{:S(2)}, u32[]{:S(2)}) collective-permute-start(bf16[16,2560]{1,0:T(8,128)(2,1)S(1)} %get-tuple-element.34.own_ref), channel_id=1, source_target_pairs={{0,2},{1,9},{2,0},{3,11},{4,6},{5,13},{6,4},{7,15},{8,10},{9,1},{1... | collective-permute-start | bytes 245768 | tf_op jit(solution)/shard_map/ppermute | solution.py:56
  6.7 5.4 %collective-permute-start = (bf16[16,2048]{1,0:T(8,128)(2,1)S(1)}, bf16[16,2048]{1,0:T(8,128)(2,1)S(1)}, u32[]{:S(2)}, u32[]{:S(2)}) collective-permute-start(bf16[16,2048]{1,0:T(8,128)(2,1)S(1)} %get-tuple-element.32.after_ref.own_ref), channel_id=1, source_target_pairs={{0,2},{1,9},{2,0},{3,11},{4,6},{5,13},{6,4},{7,15},{8,10},{9,1},{1... | collective-permute-start | bytes 196616 | tf_op jit(solution)/shard_map/ppermute | solution.py:56
  8.9 6.0 %collective-permute-start.3 = (bf16[16,3072]{1,0:T(8,128)(2,1)S(1)}, bf16[16,3072]{1,0:T(8,128)(2,1)S(1)}, u32[]{:S(2)}, u32[]{:S(2)}) collective-permute-start(bf16[16,3072]{1,0:T(8,128)(2,1)S(1)} %get-tuple-element.35.after_ref.own_ref.first_ref), channel_id=1, source_target_pairs={{0,8},{1,5},{2,10},{3,7},{4,12},{5,1},{6,14},{7,3},{8,0},{9,13},{1... | collective-permute-start | bytes 294920 | tf_op jit(solution)/shard_map/ppermute | solution.py:56
  12.1 5.6 %collective-permute-start.2 = (bf16[16,2048]{1,0:T(8,128)(2,1)S(1)}, bf16[16,2048]{1,0:T(8,128)(2,1)S(1)}, u32[]{:S(2)}, u32[]{:S(2)}) collective-permute-start(bf16[16,2048]{1,0:T(8,128)(2,1)S(1)} %get-tuple-element.37.after_ref.own_ref), channel_id=1, source_target_pairs={{0,8},{1,5},{2,10},{3,7},{4,12},{5,1},{6,14},{7,3},{8,0},{9,13},{1... | collective-permute-start | bytes 196616 | tf_op jit(solution)/shard_map/ppermute | solution.py:56
  14.9 5.0 %collective-permute-start.5 = (bf16[16,2048]{1,0:T(8,128)(2,1)S(1)}, bf16[16,2048]{1,0:T(8,128)(2,1)S(1)}, u32[]{:S(2)}, u32[]{:S(2)}) collective-permute-start(bf16[16,2048]{1,0:T(8,128)(2,1)S(1)} %get-tuple-element.39.after_ref), channel_id=1, source_target_pairs={{0,4},{1,3},{2,6},{3,1},{4,0},{5,7},{6,2},{7,5},{8,12},{9,11},{10,... | collective-permute-start | bytes 196616 | tf_op jit(solution)/shard_map/ppermute | solution.py:56
  17.7 4.3 %collective-permute-start.4 = (bf16[16,2048]{1,0:T(8,128)(2,1)S(1)}, bf16[16,2048]{1,0:T(8,128)(2,1)S(1)}, u32[]{:S(2)}, u32[]{:S(2)}) collective-permute-start(bf16[16,2048]{1,0:T(8,128)(2,1)S(1)} %get-tuple-element.41.after_ref), channel_id=1, source_target_pairs={{0,4},{1,3},{2,6},{3,1},{4,0},{5,7},{6,2},{7,5},{8,12},{9,11},{10,... | collective-permute-start | bytes 196616 | tf_op jit(solution)/shard_map/ppermute | solution.py:56
  19.1 4.3 %collective-permute-start.7 = (bf16[16,2048]{1,0:T(8,128)(2,1)S(1)}, bf16[16,2048]{1,0:T(8,128)(2,1)S(1)}, u32[]{:S(2)}, u32[]{:S(2)}) collective-permute-start(bf16[16,2048]{1,0:T(8,128)(2,1)S(1)} %shard_map.104.own_ref), channel_id=1, source_target_pairs={{0,4},{1,3},{2,6},{3,1},{4,0},{5,7},{6,2},{7,5},{8,12},{9,11},{10,... | collective-permute-start | bytes 196616 | tf_op jit(solution)/shard_map/ppermute | solution.py:56
  22.3 1.3 %collective-permute-start.6 = (f32[16,128]{1,0:T(8,128)S(1)}, f32[16,128]{1,0:T(8,128)S(1)}, u32[]{:S(2)}, u32[]{:S(2)}) collective-permute-start(f32[16,128]{1,0:T(8,128)S(1)} %get-tuple-element.49.after_ref.mine_ref), channel_id=1, source_target_pairs={{0,1},{1,0},{2,3},{3,2},{4,5},{5,4},{6,7},{7,6},{8,9},{9,8},{10,11... | collective-permute-start | bytes 24584 | tf_op jit(solution)/shard_map/ppermute | solution.py:429

commit v14 on v13

--- a/solution.py
+++ b/solution.py
@@ -15,7 +15,7 @@
 ROWS = 16
 
 
-def kernel_call(kernel, out_shape, in_specs, out_specs, tokens, scratch_shapes=()):
+def kernel_call(kernel, out_shape, in_specs, out_specs, tokens, scratch_shapes=(), aliases={}):
     limit = (16 if tokens <= ROWS else 40) * 2**20
     return pl.pallas_call(
         kernel,
@@ -23,6 +23,7 @@
         in_specs=in_specs,
         out_specs=out_specs,
         scratch_shapes=scratch_shapes,
+        input_output_aliases=aliases,
         compiler_params=pltpu.CompilerParams(vmem_limit_bytes=limit),
         cost_estimate=pl.CostEstimate(flops=10**6, bytes_accessed=2**20, transcendentals=0),
     )
@@ -41,9 +42,8 @@
 
 
 def bit_of(step, core):
-    last = feat_bits() - 1
-    middle = list(range(1, last))
-    return ([0, last] + middle if core == 0 else [last] + middle + [0])[step] if last else 0
+    bits = list(range(feat_bits()))
+    return (bits[-1:] + bits[:-1] if core == 0 else bits)[step]
 
 
 def swapped(shard, step):
@@ -286,64 +286,79 @@
     )(total, arrived, dict_rows, *first)
 
 
-def grad_rows_kernel(at, code_ref, scaled_ref, other_ref, out_hbm, *refs):
-    out_ref, sems = refs[-2:]
-    slots, width = out_ref.shape
+def outer(code_ref, scaled):
     code = code_ref[...].astype(jnp.float32).T.astype(jnp.bfloat16)
-    step = width // sems.shape[0]
+    return jnp.dot(code, scaled, preferred_element_type=jnp.float32).astype(jnp.bfloat16)
+
+
+def first_rows_kernel(code_ref, scaled_ref, out_hbm, mark_ref, out_ref, sems):
+    mark_ref[...] = jnp.zeros_like(mark_ref)
+    step = out_ref.shape[1] // sems.shape[0]
     copies = []
     for i in range(sems.shape[0]):
         part = pl.ds(i * step, step)
-        out_ref[:, part] = jnp.dot(
-            code, scaled_ref[:, part], preferred_element_type=jnp.float32
-        ).astype(jnp.bfloat16)
+        out_ref[:, part] = outer(code_ref, scaled_ref[:, part])
         copies.append(
-            pltpu.make_async_copy(
-                out_ref.at[:, part], out_hbm.at[:, pl.ds(at + i * step, step)], sems.at[i]
-            )
+            pltpu.make_async_copy(out_ref.at[:, part], out_hbm.at[:, part], sems.at[i])
         )
         copies[-1].start()
     for copy in copies:
         copy.wait()
 
 
-def first_rows_kernel(code_ref, scaled_ref, out_hbm, mark_ref, out_ref, sems):
-    mark_ref[...] = jnp.zeros_like(mark_ref)
-    grad_rows_kernel(0, code_ref, scaled_ref, None, out_hbm, out_ref, sems)
-
-
-def grad_rows_part(code, scaled, width, written=None):
+def first_rows(code, scaled, width):
     count, slots = code.shape
     chunk = scaled.shape[1]
-    limit = (16 if count <= ROWS else 40) * 2**20
-    first = written is None
-    mark = shape(1, slots, dtype=jnp.float32)
-    return pl.pallas_call(
-        first_rows_kernel if first else functools.partial(grad_rows_kernel, width - chunk),
-        out_shape=(shape(slots, width), mark) if first else shape(slots, width),
-        in_specs=[VMEM] * 2 + ([] if first else [HBM]),
-        out_specs=(HBM, VMEM) if first else HBM,
-        scratch_shapes=[
-            pltpu.VMEM((slots, chunk), jnp.bfloat16),
-            pltpu.SemaphoreType.DMA((2,)),
-        ],
-        input_output_aliases={} if first else {2: 0},
-        compiler_params=pltpu.CompilerParams(vmem_limit_bytes=limit),
-        cost_estimate=pl.CostEstimate(flops=10**6, bytes_accessed=2**20, transcendentals=0),
-    )(code, scaled, *(() if first else (written,)))
+    return kernel_call(
+        first_rows_kernel,
+        (shape(slots, width), shape(1, slots, dtype=jnp.float32)),
+        [VMEM] * 2,
+        (HBM, VMEM),
+        count,
+        [pltpu.VMEM((slots, chunk), jnp.bfloat16), pltpu.SemaphoreType.DMA((2,))],
+    )(code, scaled)
+
+
+def second_rows_kernel(code_ref, scaled_ref, out_ref):
+    out_ref[...] = outer(code_ref, scaled_ref[...])
+
+
+def second_rows(code, scaled):
+    count, slots = code.shape
+    return kernel_call(
+        second_rows_kernel, shape(slots, scaled.shape[1]), [VMEM] * 2, VMEM, count
+    )(code, scaled)
 
 
 def final_kernel(
-    rows, raw_ref, mine_ref, theirs_ref, turned_ref, enc_hbm, benc_hbm, enc_ref, benc_ref, sems
+    rows,
+    raw_ref,
+    mine_ref,
+    theirs_ref,
+    turned_ref,
+    last_rows_ref,
+    written_hbm,
+    rows_hbm,
+    enc_hbm,
+    benc_hbm,
+    enc_ref,
+    benc_ref,
+    sems,
 ):
+    chunk = last_rows_ref.shape[1]
+    last = rows_hbm.shape[1] - chunk
+    copies = [
+        pltpu.make_async_copy(last_rows_ref, rows_hbm.at[:, pl.ds(last, chunk)], sems.at[0])
+    ]
+    copies[0].start()
     count, slots = raw_ref.shape
     width, depth = turned_ref.shape
     pieces = ROWS // rows
     code_grad = mine_ref[...] + theirs_ref[...]
     pre_grad = jnp.where(raw_ref[...] > 0.0, code_grad, 0.0).astype(jnp.bfloat16)
     benc_ref[...] = jnp.sum(pre_grad.astype(jnp.float32), axis=0, keepdims=True)
-    copies = [pltpu.make_async_copy(benc_ref, benc_hbm, sems.at[pieces // 2])]
-    copies[0].start()
+    copies.append(pltpu.make_async_copy(benc_ref, benc_hbm, sems.at[1]))
+    copies[1].start()
     place = lax.broadcasted_iota(jnp.int32, (depth, count), 0)
     token = lax.broadcasted_iota(jnp.int32, (depth, count), 1)
     core = lax.axis_index("tok")
@@ -368,28 +383,29 @@
         for i in range(2):
             enc_ref[(c + i) * width : (c + i + 1) * width, :] = out[:, i * slots : (i + 1) * slots]
         part = pl.ds(c * width, 2 * width)
-        copies.append(pltpu.make_async_copy(enc_ref.at[part], enc_hbm.at[part], sems.at[c // 2]))
+        copies.append(pltpu.make_async_copy(enc_ref.at[part], enc_hbm.at[part], sems.at[c // 2 + 2]))
         copies[-1].start()
     for copy in copies:
         copy.wait()
 
 
-def final(raw, mine, theirs, turned_tokens, rows):
+def final(raw, mine, theirs, turned_tokens, last_rows, written, rows):
     count, slots = raw.shape
     pieces = ROWS // rows
     width = turned_tokens.shape[0] * pieces
     return kernel_call(
         functools.partial(final_kernel, rows),
-        (shape(width, slots), shape(1, slots, dtype=jnp.float32)),
-        [VMEM] * 4,
-        (HBM, HBM),
+        (shape(slots, width), shape(width, slots), shape(1, slots, dtype=jnp.float32)),
+        [VMEM] * 5 + [HBM],
+        (HBM, HBM, HBM),
         count,
         [
             pltpu.VMEM((width, slots), jnp.bfloat16),
             pltpu.VMEM((1, slots), jnp.float32),
-            pltpu.SemaphoreType.DMA((pieces // 2 + 1,)),
+            pltpu.SemaphoreType.DMA((pieces // 2 + 2,)),
         ],
-    )(raw, mine, theirs, turned_tokens)
+        {5: 0},
+    )(raw, mine, theirs, turned_tokens, last_rows, written)
 
 
 def local(tokens, b_pre, pre_codes, top_idx, blocks, counts, dict_rows):
@@ -422,14 +438,16 @@
             own, previous = sent, arrived
             total, sent = added(total, own, previous, sent_second, step + 1 < merged)
     scaled, product_first = products(total, arrived, dict_rows)
-    grad_rows, mark = grad_rows_part(code, scaled, width)
+    written, mark = first_rows(code, scaled, width)
     scaled, code_half = products(
         total_second, arrived_second, dict_rows, product_first, mark
     )
     theirs = lax.ppermute(code_half, "tok", [(i, 1 - i) for i in range(2)])
-    grad_rows = grad_rows_part(code, scaled, width, grad_rows)
+    last_rows = second_rows(code, scaled)
     turned_tokens = turned(block, arrived_block, bias, code_half, rows, count)
-    grad_enc, grad_benc = final(raw, code_half, theirs, turned_tokens, rows)
+    grad_rows, grad_enc, grad_benc = final(
+        raw, code_half, theirs, turned_tokens, last_rows, written, rows
+    )
     return (grad_rows, grad_enc, grad_benc.reshape(-1))
 
 

time: 25.3 us -> 25.7 us (1.016)
  waiting for transfers between devices: 4.32 us -> 5.56 us
  Pallas kernels: 5.99 us -> 5.25 us
    ppermute x7, waiting for transfers between devices: 4.31 us -> 5.56 us  [swapped(): return lax.ppermute(shard, ('feat', 'tok'), pairs)]
    pallas_call x3, Pallas kernels: 3.61 us -> 2.87 us  [the longest x1 1.45 us: final(): kernel_call(functools.partial(final_kernel, rows), (shape(slots, width),...]
  transfers between devices with their start and end apart: 8 -> 8, of which waited for: 4 -> 4; matrix products, arithmetic and copies ran while one was open for 0% -> 0% of each run, Pallas kernels for 12% -> 9%
where the time goes in v14:
time: 25.7 us; the launch traced here: 25.5 us
  starting transfers between devices  12.7 us (49%)
  waiting for transfers between devices  5.56 us (22%)
  Pallas kernels  5.25 us (20%)
  between operations  2 us (8%)
    ppermute x7, starting transfers between devices, swapped(): return lax.ppermute(shard, ('feat', 'tok'), pairs)  12.6 us
    ppermute x7, waiting for transfers between devices, swapped(): return lax.ppermute(shard, ('feat', 'tok'), pairs)  5.56 us
    pallas_call x1, Pallas kernels, front(): kernel_call(front_kernel, (shape(count, slots), shape(count, slots, dtype...  1.53 us
    pallas_call x1, Pallas kernels, final(): kernel_call(functools.partial(final_kernel, rows), (shape(slots, width),...  1.45 us
    pallas_call x1, Pallas kernels, first_rows(): kernel_call(first_rows_kernel, (shape(slots, width), shape(1, slots, dtyp...  1.09 us
  transfers between devices with their start and end apart: 8, of which 4 were waited for; matrix products, arithmetic and copies ran while one was open for 0% of the time, Pallas kernels for 9%

profile of v14, /device:TPU:0, one launch (start us, length us, event | category | flops | bytes accessed | tf_op | source)
XLA Modules:
  0.0 25.5 jit_solution(9475173866283915336)
XLA Ops:
  1.9 1.5 %shard_map.94 = (bf16[16,128]{1,0:T(8,128)(2,1)S(1)}, f32[16,128]{1,0:T(8,128)S(1)}, f32[16,2048]{1,0:T(8,128)S(1)}, bf16[16,2560]{1,0:T(8,128)(2,1)S(1)}, bf16[...) custom-call(bf16[2,4096]{1,0:T(2,128)(2,1)} %tokens_hbm.1, bf16[4096]{0:T(1024)(128)(2,1)} %bias_hbm.1, ...), custom_call_target="tpu_custom_call" | custom-call | flops 1000000 | bytes 1048576 | tf_op jit(solution)/shard_map/pallas_call | solution.py:134
  3.5 4.1 %collective-permute-start.1 = (bf16[16,2560]{1,0:T(8,128)(2,1)S(1)}, bf16[16,2560]{1,0:T(8,128)(2,1)S(1)}, u32[]{:S(2)}, u32[]{:S(2)}) collective-permute-start(bf16[16,2560]{1,0:T(8,128)(2,1)S(1)} %get-tuple-element.36.own_ref), channel_id=1, source_target_pairs={{0,8},{1,3},{2,10},{3,1},{4,12},{5,7},{6,14},{7,5},{8,0},{9,11},{1... | collective-permute-start | bytes 245768 | tf_op jit(solution)/shard_map/ppermute | solution.py:56
  7.6 0.2 shard_map.95
  7.7 0.1 collective-permute-start
  7.8 2.2 %collective-permute-done.1.arrived_ref = bf16[16,2560]{1,0:T(8,128)(2,1)S(1)} collective-permute-done((bf16[16,2560]{1,0:T(8,128)(2,1)S(1)}, bf16[16,2560]{1,0:T(8,128)(2,1)S(1)}, u32[]{:S(2)}, u32[]{:S(2)}) %collective-permute-start.1) | collective-permute-done | bytes 81952 | tf_op jit(solution)/shard_map/ppermute | solution.py:56
  10.0 1.9 %collective-permute-start.3 = (bf16[16,3072]{1,0:T(8,128)(2,1)S(1)}, bf16[16,3072]{1,0:T(8,128)(2,1)S(1)}, u32[]{:S(2)}, u32[]{:S(2)}) collective-permute-start(bf16[16,3072]{1,0:T(8,128)(2,1)S(1)} %get-tuple-element.37.after_ref.own_ref.first_ref), channel_id=1, source_target_pairs={{0,2},{1,5},{2,0},{3,7},{4,6},{5,1},{6,4},{7,3},{8,10},{9,13},{10,... | collective-permute-start | bytes 294920 | tf_op jit(solution)/shard_map/ppermute | solution.py:56
  11.9 1.1 %collective-permute-done.arrived_ref = bf16[16,2048]{1,0:T(8,128)(2,1)S(1)} collective-permute-done((bf16[16,2048]{1,0:T(8,128)(2,1)S(1)}, bf16[16,2048]{1,0:T(8,128)(2,1)S(1)}, u32[]{:S(2)}, u32[]{:S(2)}) %collective-permute-start) | collective-permute-done | bytes 65568 | tf_op jit(solution)/shard_map/ppermute | solution.py:56
  13.1 1.6 %collective-permute-start.2 = (bf16[16,2048]{1,0:T(8,128)(2,1)S(1)}, bf16[16,2048]{1,0:T(8,128)(2,1)S(1)}, u32[]{:S(2)}, u32[]{:S(2)}) collective-permute-start(bf16[16,2048]{1,0:T(8,128)(2,1)S(1)} %get-tuple-element.39.after_ref.own_ref), channel_id=1, source_target_pairs={{0,2},{1,5},{2,0},{3,7},{4,6},{5,1},{6,4},{7,3},{8,10},{9,13},{10,... | collective-permute-start | bytes 196616 | tf_op jit(solution)/shard_map/ppermute | solution.py:56
  14.7 0.0 collective-permute-done.3.arrived_ref.second_ref
  14.7 2.7 %collective-permute-start.5 = (bf16[16,2048]{1,0:T(8,128)(2,1)S(1)}, bf16[16,2048]{1,0:T(8,128)(2,1)S(1)}, u32[]{:S(2)}, u32[]{:S(2)}) collective-permute-start(bf16[16,2048]{1,0:T(8,128)(2,1)S(1)} %get-tuple-element.41.after_ref), channel_id=1, source_target_pairs={{0,4},{1,9},{2,6},{3,11},{4,0},{5,13},{6,2},{7,15},{8,12},{9,1},{1... | collective-permute-start | bytes 196616 | tf_op jit(solution)/shard_map/ppermute | solution.py:56
  17.4 0.0 collective-permute-done.2.arrived_ref
  17.4 2.2 %collective-permute-start.4 = (bf16[16,2048]{1,0:T(8,128)(2,1)S(1)}, bf16[16,2048]{1,0:T(8,128)(2,1)S(1)}, u32[]{:S(2)}, u32[]{:S(2)}) collective-permute-start(bf16[16,2048]{1,0:T(8,128)(2,1)S(1)} %get-tuple-element.43.after_ref), channel_id=1, source_target_pairs={{0,4},{1,9},{2,6},{3,11},{4,0},{5,13},{6,2},{7,15},{8,12},{9,1},{1... | collective-permute-start | bytes 196616 | tf_op jit(solution)/shard_map/ppermute | solution.py:56
  19.6 0.1 collective-permute-start.7
  19.7 0.9 %collective-permute-done.5.arrived_ref = bf16[16,2048]{1,0:T(8,128)(2,1)S(1)} collective-permute-done((bf16[16,2048]{1,0:T(8,128)(2,1)S(1)}, bf16[16,2048]{1,0:T(8,128)(2,1)S(1)}, u32[]{:S(2)}, u32[]{:S(2)}) %collective-permute-start.5) | collective-permute-done | bytes 65568 | tf_op jit(solution)/shard_map/ppermute | solution.py:56
  20.6 0.2 shard_map.100
  20.9 1.1 %shard_map.101 = (bf16[128,4096]{1,0:T(8,128)(2,1)}, f32[1,128]{1,0:T(1,128)S(1)}) custom-call(bf16[16,128]{1,0:T(8,128)(2,1)S(1)} %get-tuple-element.30.code_ref, bf16[16,2048]{1,0:T(8,128)(2,1)S(1)} %get-tuple-element.46.scaled_ref), custom_call_target="tpu_custom_call" | custom-call | flops 1000000 | bytes 1048576 | tf_op jit(solution)/shard_map/pallas_call | solution.py:312
  22.0 0.0 collective-permute-done.4.arrived_ref
  22.0 0.2 shard_map.102
  22.2 0.0 collective-permute-start.6
  22.2 0.3 %shard_map.105.last_rows_ref = bf16[128,2048]{1,0:T(8,128)(2,1)S(1)} custom-call(bf16[16,128]{1,0:T(8,128)(2,1)S(1)} %get-tuple-element.30.code_ref, bf16[16,2048]{1,0:T(8,128)(2,1)S(1)} %get-tuple-element.50.scaled_ref), custom_call_target="tpu_custom_call" | custom-call | flops 1000000 | bytes 1048576 | tf_op jit(solution)/shard_map/pallas_call | solution.py:328
  22.6 1.3 %collective-permute-done.7.arrived_ref = bf16[16,2048]{1,0:T(8,128)(2,1)S(1)} collective-permute-done((bf16[16,2048]{1,0:T(8,128)(2,1)S(1)}, bf16[16,2048]{1,0:T(8,128)(2,1)S(1)}, u32[]{:S(2)}, u32[]{:S(2)}) %collective-permute-start.7) | collective-permute-done | bytes 65568 | tf_op jit(solution)/shard_map/ppermute | solution.py:56
  23.9 0.1 shard_map.104.turned_ref
  24.0 0.0 collective-permute-done.6.theirs_ref
  24.0 1.4 %shard_map.106 = (bf16[128,4096]{1,0:T(8,128)(2,1)}, bf16[4096,128]{1,0:T(8,128)(2,1)}, f32[1,128]{1,0:T(1,128)}) custom-call(f32[16,128]{1,0:T(8,128)S(1)} %get-tuple-element.29.raw_ref, f32[16,128]{1,0:T(8,128)S(1)} %get-tuple-element.48.after_ref.mine_ref, f32[16,128]{1,0:T(8,128)S(1)} %collective-permute-done.6.theirs_ref, ...), custom_call_target="tpu_custom_call", output_to_operand_aliasing={{0}: (5, {})} | custom-call | flops 1000000 | bytes 1048576 | tf_op jit(solution)/shard_map/pallas_call | solution.py:396
  (5 shorter events, 0.1 us)
Async XLA Ops:
  3.5 6.5 %collective-permute-start.1 = (bf16[16,2560]{1,0:T(8,128)(2,1)S(1)}, bf16[16,2560]{1,0:T(8,128)(2,1)S(1)}, u32[]{:S(2)}, u32[]{:S(2)}) collective-permute-start(bf16[16,2560]{1,0:T(8,128)(2,1)S(1)} %get-tuple-element.36.own_ref), channel_id=1, source_target_pairs={{0,8},{1,3},{2,10},{3,1},{4,12},{5,7},{6,14},{7,5},{8,0},{9,11},{1... | collective-permute-start | bytes 245768 | tf_op jit(solution)/shard_map/ppermute | solution.py:56
  7.7 5.3 %collective-permute-start = (bf16[16,2048]{1,0:T(8,128)(2,1)S(1)}, bf16[16,2048]{1,0:T(8,128)(2,1)S(1)}, u32[]{:S(2)}, u32[]{:S(2)}) collective-permute-start(bf16[16,2048]{1,0:T(8,128)(2,1)S(1)} %get-tuple-element.34.after_ref.own_ref), channel_id=1, source_target_pairs={{0,8},{1,3},{2,10},{3,1},{4,12},{5,7},{6,14},{7,5},{8,0},{9,11},{1... | collective-permute-start | bytes 196616 | tf_op jit(solution)/shard_map/ppermute | solution.py:56
  10.0 4.7 %collective-permute-start.3 = (bf16[16,3072]{1,0:T(8,128)(2,1)S(1)}, bf16[16,3072]{1,0:T(8,128)(2,1)S(1)}, u32[]{:S(2)}, u32[]{:S(2)}) collective-permute-start(bf16[16,3072]{1,0:T(8,128)(2,1)S(1)} %get-tuple-element.37.after_ref.own_ref.first_ref), channel_id=1, source_target_pairs={{0,2},{1,5},{2,0},{3,7},{4,6},{5,1},{6,4},{7,3},{8,10},{9,13},{10,... | collective-permute-start | bytes 294920 | tf_op jit(solution)/shard_map/ppermute | solution.py:56
  13.1 4.3 %collective-permute-start.2 = (bf16[16,2048]{1,0:T(8,128)(2,1)S(1)}, bf16[16,2048]{1,0:T(8,128)(2,1)S(1)}, u32[]{:S(2)}, u32[]{:S(2)}) collective-permute-start(bf16[16,2048]{1,0:T(8,128)(2,1)S(1)} %get-tuple-element.39.after_ref.own_ref), channel_id=1, source_target_pairs={{0,2},{1,5},{2,0},{3,7},{4,6},{5,1},{6,4},{7,3},{8,10},{9,13},{10,... | collective-permute-start | bytes 196616 | tf_op jit(solution)/shard_map/ppermute | solution.py:56
  14.7 5.9 %collective-permute-start.5 = (bf16[16,2048]{1,0:T(8,128)(2,1)S(1)}, bf16[16,2048]{1,0:T(8,128)(2,1)S(1)}, u32[]{:S(2)}, u32[]{:S(2)}) collective-permute-start(bf16[16,2048]{1,0:T(8,128)(2,1)S(1)} %get-tuple-element.41.after_ref), channel_id=1, source_target_pairs={{0,4},{1,9},{2,6},{3,11},{4,0},{5,13},{6,2},{7,15},{8,12},{9,1},{1... | collective-permute-start | bytes 196616 | tf_op jit(solution)/shard_map/ppermute | solution.py:56
  17.4 4.5 %collective-permute-start.4 = (bf16[16,2048]{1,0:T(8,128)(2,1)S(1)}, bf16[16,2048]{1,0:T(8,128)(2,1)S(1)}, u32[]{:S(2)}, u32[]{:S(2)}) collective-permute-start(bf16[16,2048]{1,0:T(8,128)(2,1)S(1)} %get-tuple-element.43.after_ref), channel_id=1, source_target_pairs={{0,4},{1,9},{2,6},{3,11},{4,0},{5,13},{6,2},{7,15},{8,12},{9,1},{1... | collective-permute-start | bytes 196616 | tf_op jit(solution)/shard_map/ppermute | solution.py:56
  19.6 4.3 %collective-permute-start.7 = (bf16[16,2048]{1,0:T(8,128)(2,1)S(1)}, bf16[16,2048]{1,0:T(8,128)(2,1)S(1)}, u32[]{:S(2)}, u32[]{:S(2)}) collective-permute-start(bf16[16,2048]{1,0:T(8,128)(2,1)S(1)} %shard_map.103.own_ref), channel_id=1, source_target_pairs={{0,4},{1,9},{2,6},{3,11},{4,0},{5,13},{6,2},{7,15},{8,12},{9,1},{1... | collective-permute-start | bytes 196616 | tf_op jit(solution)/shard_map/ppermute | solution.py:56
  22.2 1.8 %collective-permute-start.6 = (f32[16,128]{1,0:T(8,128)S(1)}, f32[16,128]{1,0:T(8,128)S(1)}, u32[]{:S(2)}, u32[]{:S(2)}) collective-permute-start(f32[16,128]{1,0:T(8,128)S(1)} %get-tuple-element.48.after_ref.mine_ref), channel_id=1, source_target_pairs={{0,1},{1,0},{2,3},{3,2},{4,5},{5,4},{6,7},{7,6},{8,9},{9,8},{10,11... | collective-permute-start | bytes 24584 | tf_op jit(solution)/shard_map/ppermute | solution.py:445

commit v15 on v14

--- a/solution.py
+++ b/solution.py
@@ -11,11 +11,11 @@
 SMEM = pl.BlockSpec(memory_space=pltpu.SMEM)
 HBM = pl.BlockSpec(memory_space=pltpu.HBM)
 ANY = pl.BlockSpec(memory_space=pl.ANY)
-MERGED = 2
+EARLY = 10**9
 ROWS = 16
 
 
-def kernel_call(kernel, out_shape, in_specs, out_specs, tokens, scratch_shapes=(), aliases={}):
+def kernel_call(kernel, out_shape, in_specs, out_specs, tokens, scratch_shapes=(), flops=10**6):
     limit = (16 if tokens <= ROWS else 40) * 2**20
     return pl.pallas_call(
         kernel,
@@ -23,9 +23,8 @@
         in_specs=in_specs,
         out_specs=out_specs,
         scratch_shapes=scratch_shapes,
-        input_output_aliases=aliases,
         compiler_params=pltpu.CompilerParams(vmem_limit_bytes=limit),
-        cost_estimate=pl.CostEstimate(flops=10**6, bytes_accessed=2**20, transcendentals=0),
+        cost_estimate=pl.CostEstimate(flops=flops, bytes_accessed=2**20, transcendentals=0),
     )
 
 
@@ -193,7 +192,7 @@
         sent_ref[:, half + block :] = arrived_ref[:, half:]
 
 
-def added(total, own, arrived, after, merged):
+def added(total, own, arrived, after, merged, flops=10**6):
     count, half = total.shape
     block = own.shape[1] - half
     return kernel_call(
@@ -205,46 +204,47 @@
         [VMEM] * 3 + [ANY],
         (VMEM, VMEM),
         count,
+        flops=flops,
     )(total, own, arrived, after)
 
 
-def joined_kernel(skip, first_ref, second_ref, after_ref, out_ref):
-    width = first_ref.shape[1] - skip
-    out_ref[:, :width] = first_ref[:, skip:]
-    out_ref[:, width:] = second_ref[:, skip:]
-
-
-def joined(first, second, skip, after):
-    return kernel_call(
-        functools.partial(joined_kernel, skip),
-        shape(first.shape[0], 2 * (first.shape[1] - skip)),
+def joined_kernel(first_ref, second_ref, after_ref, out_ref):
+    width = first_ref.shape[1]
+    out_ref[:, :width] = first_ref[...]
+    out_ref[:, width:] = second_ref[...]
+
+
+def joined(first, second, after):
+    return kernel_call(
+        joined_kernel,
+        shape(first.shape[0], 2 * first.shape[1]),
         [VMEM, VMEM, ANY],
         VMEM,
         first.shape[0],
     )(first, second, after)
 
 
-def turned_kernel(rows, own_ref, arrived_ref, bias_ref, after_ref, out_ref):
+def turned_kernel(skip, rows, own_ref, arrived_ref, bias_ref, out_ref):
     bias = jnp.concatenate([bias_ref[...]] * rows, axis=0)
     bias = stacked(bias, ROWS // rows)
     width = bias.shape[1]
     blocks = [
         (ref[:, at : at + width].astype(jnp.float32) - bias).astype(jnp.bfloat16)
         for ref in (own_ref, arrived_ref)
-        for at in range(0, ref.shape[1], width)
+        for at in range(skip, ref.shape[1], width)
     ]
     out_ref[...] = jnp.concatenate(blocks, axis=0).astype(jnp.float32).T.astype(jnp.bfloat16)
 
 
-def turned(own, arrived, bias, after, rows, count):
+def turned(own, arrived, skip, bias, rows, count):
     width = bias.shape[1] * rows // ROWS
     return kernel_call(
-        functools.partial(turned_kernel, rows),
-        shape(width, 2 * own.shape[1] // width * ROWS),
-        [VMEM] * 3 + [ANY],
+        functools.partial(turned_kernel, skip, rows),
+        shape(width, 2 * (own.shape[1] - skip) // width * ROWS),
+        [VMEM] * 3,
         VMEM,
         count,
-    )(own, arrived, bias, after)
+    )(own, arrived, bias)
 
 
 def scaled_of(total_ref, arrived_ref):
@@ -267,9 +267,7 @@
     half_ref[...] = product(scaled, rows_ref, 0)
 
 
-def second_product_kernel(
-    total_ref, arrived_ref, rows_ref, first_ref, after_ref, scaled_ref, half_ref
-):
+def second_product_kernel(total_ref, arrived_ref, rows_ref, first_ref, scaled_ref, half_ref):
     scaled = scaled_of(total_ref, arrived_ref)
     scaled_ref[...] = scaled
     half_ref[...] = first_ref[...] + product(scaled, rows_ref, rows_ref.shape[1] - scaled.shape[1])
@@ -280,7 +278,7 @@
     return kernel_call(
         second_product_kernel if first else first_product_kernel,
         (shape(count, width), shape(count, dict_rows.shape[0], dtype=jnp.float32)),
-        [VMEM] * 3 + ([VMEM, ANY] if first else []),
+        [VMEM] * (3 + len(first)),
         (VMEM, VMEM),
         count,
     )(total, arrived, dict_rows, *first)
@@ -291,43 +289,21 @@
     return jnp.dot(code, scaled, preferred_element_type=jnp.float32).astype(jnp.bfloat16)
 
 
-def first_rows_kernel(code_ref, scaled_ref, out_hbm, mark_ref, out_ref, sems):
-    mark_ref[...] = jnp.zeros_like(mark_ref)
-    step = out_ref.shape[1] // sems.shape[0]
-    copies = []
-    for i in range(sems.shape[0]):
-        part = pl.ds(i * step, step)
-        out_ref[:, part] = outer(code_ref, scaled_ref[:, part])
-        copies.append(
-            pltpu.make_async_copy(out_ref.at[:, part], out_hbm.at[:, part], sems.at[i])
-        )
-        copies[-1].start()
-    for copy in copies:
-        copy.wait()
-
-
-def first_rows(code, scaled, width):
+def grad_rows_kernel(code_ref, first_ref, second_ref, out_ref):
+    chunk = first_ref.shape[1]
+    out_ref[:, :chunk] = outer(code_ref, first_ref[...])
+    out_ref[:, chunk:] = outer(code_ref, second_ref[...])
+
+
+def grad_rows_of(code, first, second):
     count, slots = code.shape
-    chunk = scaled.shape[1]
-    return kernel_call(
-        first_rows_kernel,
-        (shape(slots, width), shape(1, slots, dtype=jnp.float32)),
-        [VMEM] * 2,
-        (HBM, VMEM),
-        count,
-        [pltpu.VMEM((slots, chunk), jnp.bfloat16), pltpu.SemaphoreType.DMA((2,))],
-    )(code, scaled)
-
-
-def second_rows_kernel(code_ref, scaled_ref, out_ref):
-    out_ref[...] = outer(code_ref, scaled_ref[...])
-
-
-def second_rows(code, scaled):
-    count, slots = code.shape
-    return kernel_call(
-        second_rows_kernel, shape(slots, scaled.shape[1]), [VMEM] * 2, VMEM, count
-    )(code, scaled)
+    return kernel_call(
+        grad_rows_kernel,
+        shape(slots, first.shape[1] + second.shape[1]),
+        [VMEM] * 3,
+        VMEM,
+        count,
+    )(code, first, second)
 
 
 def final_kernel(
@@ -336,8 +312,7 @@
     mine_ref,
     theirs_ref,
     turned_ref,
-    last_rows_ref,
-    written_hbm,
+    rows_ref,
     rows_hbm,
     enc_hbm,
     benc_hbm,
@@ -345,11 +320,7 @@
     benc_ref,
     sems,
 ):
-    chunk = last_rows_ref.shape[1]
-    last = rows_hbm.shape[1] - chunk
-    copies = [
-        pltpu.make_async_copy(last_rows_ref, rows_hbm.at[:, pl.ds(last, chunk)], sems.at[0])
-    ]
+    copies = [pltpu.make_async_copy(rows_ref, rows_hbm, sems.at[0])]
     copies[0].start()
     count, slots = raw_ref.shape
     width, depth = turned_ref.shape
@@ -389,14 +360,14 @@
         copy.wait()
 
 
-def final(raw, mine, theirs, turned_tokens, last_rows, written, rows):
+def final(raw, mine, theirs, turned_tokens, grad_rows, rows):
     count, slots = raw.shape
     pieces = ROWS // rows
     width = turned_tokens.shape[0] * pieces
     return kernel_call(
         functools.partial(final_kernel, rows),
-        (shape(slots, width), shape(width, slots), shape(1, slots, dtype=jnp.float32)),
-        [VMEM] * 5 + [HBM],
+        (shape(*grad_rows.shape), shape(width, slots), shape(1, slots, dtype=jnp.float32)),
+        [VMEM] * 5,
         (HBM, HBM, HBM),
         count,
         [
@@ -404,18 +375,16 @@
             pltpu.VMEM((1, slots), jnp.float32),
             pltpu.SemaphoreType.DMA((pieces // 2 + 2,)),
         ],
-        {5: 0},
-    )(raw, mine, theirs, turned_tokens, last_rows, written)
+    )(raw, mine, theirs, turned_tokens, grad_rows)
 
 
 def local(tokens, b_pre, pre_codes, top_idx, blocks, counts, dict_rows):
     rows, count = tokens.shape[0], top_idx.shape[0]
     steps = feat_bits()
-    width = dict_rows.shape[1]
-    merged = min(MERGED, steps - 1) if count == ROWS else 0
+    merged = count == ROWS
 
     code, raw, total, sent, dict_rows, centered, bias, *block = front(
-        tokens, b_pre, pre_codes, top_idx, blocks, counts, dict_rows, merged > 0
+        tokens, b_pre, pre_codes, top_idx, blocks, counts, dict_rows, merged
     )
     for step in range(steps):
         arrived = swapped(sent, step)
@@ -423,30 +392,27 @@
             total_second, sent_second = second(code, dict_rows, centered)
         else:
             total_second, sent_second = added(
-                total_second, sent_second, arrived_second, sent, False
+                total_second, sent_second, arrived_second, sent, False, EARLY
             )
         arrived_second = swapped(sent_second, step)
-        if step >= merged:
-            if step == merged > 0:
-                block = joined(own, previous, total.shape[1], sent_second)
-            elif step == 0:
-                (block,) = block
-            else:
-                block = joined(block, arrived_block, 0, sent_second)
-            arrived_block = swapped(block, step)
+        if not merged:
+            own_block = joined(own_block, arrived_block, sent_second) if step else block[0]
+            arrived_block = swapped(own_block, step)
         if step < steps - 1:
-            own, previous = sent, arrived
-            total, sent = added(total, own, previous, sent_second, step + 1 < merged)
+            total, sent = added(total, sent, arrived, sent_second, merged)
+    skip = 0
+    if merged:
+        own_block, arrived_block, skip = sent, arrived, total.shape[1]
+
     scaled, product_first = products(total, arrived, dict_rows)
-    written, mark = first_rows(code, scaled, width)
-    scaled, code_half = products(
-        total_second, arrived_second, dict_rows, product_first, mark
+    turned_tokens = turned(own_block, arrived_block, skip, bias, rows, count)
+    scaled_second, code_half = products(
+        total_second, arrived_second, dict_rows, product_first
     )
     theirs = lax.ppermute(code_half, "tok", [(i, 1 - i) for i in range(2)])
-    last_rows = second_rows(code, scaled)
-    turned_tokens = turned(block, arrived_block, bias, code_half, rows, count)
+    grad_rows = grad_rows_of(code, scaled, scaled_second)
     grad_rows, grad_enc, grad_benc = final(
-        raw, code_half, theirs, turned_tokens, last_rows, written, rows
+        raw, code_half, theirs, turned_tokens, grad_rows, rows
     )
     return (grad_rows, grad_enc, grad_benc.reshape(-1))
 

time: 25.7 us -> 25 us (0.973)
  Pallas kernels: 5.25 us -> 4.29 us
  waiting for transfers between devices: 5.56 us -> 5.91 us
    pallas_call x5 -> x3, Pallas kernels: 2.99 us -> 2.02 us  [the longest x1 1.44 us: final(): kernel_call(functools.partial(final_kernel, rows), (shape(*grad_rows.shap...]
    ppermute x1, waiting for transfers between devices: 0.01 us -> 0.58 us  [local(): theirs = lax.ppermute(code_half, 'tok', [(i, 1 - i) for i in range(2)])]
    ppermute x7 -> x6, waiting for transfers between devices: 5.56 us -> 5.34 us  [swapped(): return lax.ppermute(shard, ('feat', 'tok'), pairs)]
    ppermute x7 -> x6, starting transfers between devices: 12.6 us -> 12.5 us  [swapped(): return lax.ppermute(shard, ('feat', 'tok'), pairs)]
  transfers between devices with their start and end apart: 8 -> 7, of which waited for: 4 -> 5; matrix products, arithmetic and copies ran while one was open for 0% -> 0% of each run, Pallas kernels for 9% -> 4%
where the time goes in v15:
time: 25 us; the launch traced here: 24.7 us
  starting transfers between devices  12.6 us (50%)
  waiting for transfers between devices  5.91 us (24%)
  Pallas kernels  4.29 us (17%)
  between operations  1.97 us (8%)
    ppermute x6, starting transfers between devices, swapped(): return lax.ppermute(shard, ('feat', 'tok'), pairs)  12.5 us
    ppermute x6, waiting for transfers between devices, swapped(): return lax.ppermute(shard, ('feat', 'tok'), pairs)  5.34 us
    pallas_call x1, Pallas kernels, front(): kernel_call(front_kernel, (shape(count, slots), shape(count, slots, dtype...  1.53 us
    pallas_call x1, Pallas kernels, final(): kernel_call(functools.partial(final_kernel, rows), (shape(*grad_rows.shap...  1.44 us
    ppermute x1, waiting for transfers between devices, local(): theirs = lax.ppermute(code_half, 'tok', [(i, 1 - i) for i in range(2)])  0.58 us
  transfers between devices with their start and end apart: 7, of which 5 were waited for; matrix products, arithmetic and copies ran while one was open for 0% of the time, Pallas kernels for 4%

profile of v15, /device:TPU:0, one launch (start us, length us, event | category | flops | bytes accessed | tf_op | source)
XLA Modules:
  0.0 24.7 jit_solution(3568983748903273433)
XLA Ops:
  1.9 1.5 %shard_map.94 = (bf16[16,128]{1,0:T(8,128)(2,1)S(1)}, f32[16,128]{1,0:T(8,128)S(1)}, f32[16,2048]{1,0:T(8,128)S(1)}, bf16[16,2560]{1,0:T(8,128)(2,1)S(1)}, bf16[...) custom-call(bf16[2,4096]{1,0:T(2,128)(2,1)} %tokens_hbm.1, bf16[4096]{0:T(1024)(128)(2,1)} %bias_hbm.1, ...), custom_call_target="tpu_custom_call" | custom-call | flops 1000000 | bytes 1048576 | tf_op jit(solution)/shard_map/pallas_call | solution.py:133
  3.5 4.1 %collective-permute-start.1 = (bf16[16,2560]{1,0:T(8,128)(2,1)S(1)}, bf16[16,2560]{1,0:T(8,128)(2,1)S(1)}, u32[]{:S(2)}, u32[]{:S(2)}) collective-permute-start(bf16[16,2560]{1,0:T(8,128)(2,1)S(1)} %get-tuple-element.34.own_ref), channel_id=1, source_target_pairs={{0,8},{1,3},{2,10},{3,1},{4,12},{5,7},{6,14},{7,5},{8,0},{9,11},{1... | collective-permute-start | bytes 245768 | tf_op jit(solution)/shard_map/ppermute | solution.py:55
  7.6 0.2 shard_map.95
  7.7 0.1 collective-permute-start
  7.8 2.2 %collective-permute-done.1.arrived_ref = bf16[16,2560]{1,0:T(8,128)(2,1)S(1)} collective-permute-done((bf16[16,2560]{1,0:T(8,128)(2,1)S(1)}, bf16[16,2560]{1,0:T(8,128)(2,1)S(1)}, u32[]{:S(2)}, u32[]{:S(2)}) %collective-permute-start.1) | collective-permute-done | bytes 81952 | tf_op jit(solution)/shard_map/ppermute | solution.py:55
  10.0 1.9 %collective-permute-start.3 = (bf16[16,3072]{1,0:T(8,128)(2,1)S(1)}, bf16[16,3072]{1,0:T(8,128)(2,1)S(1)}, u32[]{:S(2)}, u32[]{:S(2)}) collective-permute-start(bf16[16,3072]{1,0:T(8,128)(2,1)S(1)} %get-tuple-element.35.after_ref.own_ref), channel_id=1, source_target_pairs={{0,2},{1,5},{2,0},{3,7},{4,6},{5,1},{6,4},{7,3},{8,10},{9,13},{10,... | collective-permute-start | bytes 294920 | tf_op jit(solution)/shard_map/ppermute | solution.py:55
  11.9 1.1 %collective-permute-done.arrived_ref = bf16[16,2048]{1,0:T(8,128)(2,1)S(1)} collective-permute-done((bf16[16,2048]{1,0:T(8,128)(2,1)S(1)}, bf16[16,2048]{1,0:T(8,128)(2,1)S(1)}, u32[]{:S(2)}, u32[]{:S(2)}) %collective-permute-start) | collective-permute-done | bytes 65568 | tf_op jit(solution)/shard_map/ppermute | solution.py:55
  13.1 1.6 %collective-permute-start.2 = (bf16[16,2048]{1,0:T(8,128)(2,1)S(1)}, bf16[16,2048]{1,0:T(8,128)(2,1)S(1)}, u32[]{:S(2)}, u32[]{:S(2)}) collective-permute-start(bf16[16,2048]{1,0:T(8,128)(2,1)S(1)} %get-tuple-element.37.after_ref.own_ref), channel_id=1, source_target_pairs={{0,2},{1,5},{2,0},{3,7},{4,6},{5,1},{6,4},{7,3},{8,10},{9,13},{10,... | collective-permute-start | bytes 196616 | tf_op jit(solution)/shard_map/ppermute | solution.py:55
  14.7 0.0 collective-permute-done.3.arrived_ref
  14.7 2.7 %collective-permute-start.5 = (bf16[16,4096]{1,0:T(8,128)(2,1)S(1)}, bf16[16,4096]{1,0:T(8,128)(2,1)S(1)}, u32[]{:S(2)}, u32[]{:S(2)}) collective-permute-start(bf16[16,4096]{1,0:T(8,128)(2,1)S(1)} %get-tuple-element.39.after_ref.own_ref), channel_id=1, source_target_pairs={{0,4},{1,9},{2,6},{3,11},{4,0},{5,13},{6,2},{7,15},{8,12},{9,1},{1... | collective-permute-start | bytes 393224 | tf_op jit(solution)/shard_map/ppermute | solution.py:55
  17.4 0.0 collective-permute-done.2.arrived_ref
  17.4 2.2 %collective-permute-start.4 = (bf16[16,2048]{1,0:T(8,128)(2,1)S(1)}, bf16[16,2048]{1,0:T(8,128)(2,1)S(1)}, u32[]{:S(2)}, u32[]{:S(2)}) collective-permute-start(bf16[16,2048]{1,0:T(8,128)(2,1)S(1)} %get-tuple-element.41), channel_id=1, source_target_pairs={{0,4},{1,9},{2,6},{3,11},{4,0},{5,13},{6,2},{7,15},{8,12},{9,1},{1... | collective-permute-start | bytes 196616 | tf_op jit(solution)/shard_map/ppermute | solution.py:55
  19.6 1.4 %collective-permute-done.5.arrived_ref = bf16[16,4096]{1,0:T(8,128)(2,1)S(1)} collective-permute-done((bf16[16,4096]{1,0:T(8,128)(2,1)S(1)}, bf16[16,4096]{1,0:T(8,128)(2,1)S(1)}, u32[]{:S(2)}, u32[]{:S(2)}) %collective-permute-start.5) | collective-permute-done | bytes 131104 | tf_op jit(solution)/shard_map/ppermute | solution.py:55
  21.0 0.2 shard_map.100
  21.3 0.6 %collective-permute-done.4.arrived_ref = bf16[16,2048]{1,0:T(8,128)(2,1)S(1)} collective-permute-done((bf16[16,2048]{1,0:T(8,128)(2,1)S(1)}, bf16[16,2048]{1,0:T(8,128)(2,1)S(1)}, u32[]{:S(2)}, u32[]{:S(2)}) %collective-permute-start.4) | collective-permute-done | bytes 65568 | tf_op jit(solution)/shard_map/ppermute | solution.py:55
  21.9 0.2 shard_map.101
  22.1 0.0 collective-permute-start.6
  22.1 0.5 %shard_map.103.rows_ref = bf16[128,4096]{1,0:T(8,128)(2,1)S(1)} custom-call(bf16[16,128]{1,0:T(8,128)(2,1)S(1)} %get-tuple-element.28.code_ref, bf16[16,2048]{1,0:T(8,128)(2,1)S(1)} %get-tuple-element.46.first_ref, bf16[16,2048]{1,0:T(8,128)(2,1)S(1)} %get-tuple-element.47.second_ref), custom_call_target="tpu_custom_call" | custom-call | flops 1000000 | bytes 1048576 | tf_op jit(solution)/shard_map/pallas_call | solution.py:300
  22.6 0.1 shard_map.102.turned_ref
  22.7 0.6 %collective-permute-done.6.theirs_ref = f32[16,128]{1,0:T(8,128)S(1)} collective-permute-done((f32[16,128]{1,0:T(8,128)S(1)}, f32[16,128]{1,0:T(8,128)S(1)}, u32[]{:S(2)}, u32[]{:S(2)}) %collective-permute-start.6) | collective-permute-done | bytes 8224 | tf_op jit(solution)/shard_map/ppermute | solution.py:412
  23.3 1.4 %shard_map.104 = (bf16[128,4096]{1,0:T(8,128)(2,1)}, bf16[4096,128]{1,0:T(8,128)(2,1)}, f32[1,128]{1,0:T(1,128)}) custom-call(f32[16,128]{1,0:T(8,128)S(1)} %get-tuple-element.27.raw_ref, f32[16,128]{1,0:T(8,128)S(1)} %get-tuple-element.44.mine_ref, f32[16,128]{1,0:T(8,128)S(1)} %collective-permute-done.6.theirs_ref, ...), custom_call_target="tpu_custom_call" | custom-call | flops 1000000 | bytes 1048576 | tf_op jit(solution)/shard_map/pallas_call | solution.py:367
  (4 shorter events, 0.1 us)
Async XLA Ops:
  3.5 6.5 %collective-permute-start.1 = (bf16[16,2560]{1,0:T(8,128)(2,1)S(1)}, bf16[16,2560]{1,0:T(8,128)(2,1)S(1)}, u32[]{:S(2)}, u32[]{:S(2)}) collective-permute-start(bf16[16,2560]{1,0:T(8,128)(2,1)S(1)} %get-tuple-element.34.own_ref), channel_id=1, source_target_pairs={{0,8},{1,3},{2,10},{3,1},{4,12},{5,7},{6,14},{7,5},{8,0},{9,11},{1... | collective-permute-start | bytes 245768 | tf_op jit(solution)/shard_map/ppermute | solution.py:55
  7.7 5.3 %collective-permute-start = (bf16[16,2048]{1,0:T(8,128)(2,1)S(1)}, bf16[16,2048]{1,0:T(8,128)(2,1)S(1)}, u32[]{:S(2)}, u32[]{:S(2)}) collective-permute-start(bf16[16,2048]{1,0:T(8,128)(2,1)S(1)} %get-tuple-element.32.after_ref.own_ref), channel_id=1, source_target_pairs={{0,8},{1,3},{2,10},{3,1},{4,12},{5,7},{6,14},{7,5},{8,0},{9,11},{1... | collective-permute-start | bytes 196616 | tf_op jit(solution)/shard_map/ppermute | solution.py:55
  10.0 4.7 %collective-permute-start.3 = (bf16[16,3072]{1,0:T(8,128)(2,1)S(1)}, bf16[16,3072]{1,0:T(8,128)(2,1)S(1)}, u32[]{:S(2)}, u32[]{:S(2)}) collective-permute-start(bf16[16,3072]{1,0:T(8,128)(2,1)S(1)} %get-tuple-element.35.after_ref.own_ref), channel_id=1, source_target_pairs={{0,2},{1,5},{2,0},{3,7},{4,6},{5,1},{6,4},{7,3},{8,10},{9,13},{10,... | collective-permute-start | bytes 294920 | tf_op jit(solution)/shard_map/ppermute | solution.py:55
  13.1 4.3 %collective-permute-start.2 = (bf16[16,2048]{1,0:T(8,128)(2,1)S(1)}, bf16[16,2048]{1,0:T(8,128)(2,1)S(1)}, u32[]{:S(2)}, u32[]{:S(2)}) collective-permute-start(bf16[16,2048]{1,0:T(8,128)(2,1)S(1)} %get-tuple-element.37.after_ref.own_ref), channel_id=1, source_target_pairs={{0,2},{1,5},{2,0},{3,7},{4,6},{5,1},{6,4},{7,3},{8,10},{9,13},{10,... | collective-permute-start | bytes 196616 | tf_op jit(solution)/shard_map/ppermute | solution.py:55
  14.7 6.3 %collective-permute-start.5 = (bf16[16,4096]{1,0:T(8,128)(2,1)S(1)}, bf16[16,4096]{1,0:T(8,128)(2,1)S(1)}, u32[]{:S(2)}, u32[]{:S(2)}) collective-permute-start(bf16[16,4096]{1,0:T(8,128)(2,1)S(1)} %get-tuple-element.39.after_ref.own_ref), channel_id=1, source_target_pairs={{0,4},{1,9},{2,6},{3,11},{4,0},{5,13},{6,2},{7,15},{8,12},{9,1},{1... | collective-permute-start | bytes 393224 | tf_op jit(solution)/shard_map/ppermute | solution.py:55
  17.4 4.4 %collective-permute-start.4 = (bf16[16,2048]{1,0:T(8,128)(2,1)S(1)}, bf16[16,2048]{1,0:T(8,128)(2,1)S(1)}, u32[]{:S(2)}, u32[]{:S(2)}) collective-permute-start(bf16[16,2048]{1,0:T(8,128)(2,1)S(1)} %get-tuple-element.41), channel_id=1, source_target_pairs={{0,4},{1,9},{2,6},{3,11},{4,0},{5,13},{6,2},{7,15},{8,12},{9,1},{1... | collective-permute-start | bytes 196616 | tf_op jit(solution)/shard_map/ppermute | solution.py:55
  22.1 1.2 %collective-permute-start.6 = (f32[16,128]{1,0:T(8,128)S(1)}, f32[16,128]{1,0:T(8,128)S(1)}, u32[]{:S(2)}, u32[]{:S(2)}) collective-permute-start(f32[16,128]{1,0:T(8,128)S(1)} %get-tuple-element.44.mine_ref), channel_id=1, source_target_pairs={{0,1},{1,0},{2,3},{3,2},{4,5},{5,4},{6,7},{7,6},{8,9},{9,8},{10,11... | collective-permute-start | bytes 24584 | tf_op jit(solution)/shard_map/ppermute | solution.py:412

commit v16 on v15

--- a/solution.py
+++ b/solution.py
@@ -12,6 +12,7 @@
 HBM = pl.BlockSpec(memory_space=pltpu.HBM)
 ANY = pl.BlockSpec(memory_space=pl.ANY)
 EARLY = 10**9
+PARTS = 4
 ROWS = 16
 
 
@@ -40,15 +41,19 @@
     return (lax.axis_size("feat") - 1).bit_length()
 
 
-def bit_of(step, core):
+def bit_of(step, core, chunk):
     bits = list(range(feat_bits()))
-    return (bits[-1:] + bits[:-1] if core == 0 else bits)[step]
-
-
-def swapped(shard, step):
+    if core == 0:
+        order = bits[-1:] + bits[:-1] if chunk == 0 else bits[:1] + bits[:0:-1]
+    else:
+        order = bits[1:] + bits[:1] if chunk == 0 else bits
+    return order[step]
+
+
+def swapped(shard, step, chunk):
     cores = lax.axis_size("tok")
     pairs = [
-        (f * cores + c, (f ^ 1 << bit_of(step, c)) * cores + c)
+        (f * cores + c, (f ^ 1 << bit_of(step, c, chunk)) * cores + c)
         for f in range(lax.axis_size("feat"))
         for c in range(cores)
     ]
@@ -72,6 +77,16 @@
     for i in range(rows):
         total -= jnp.where(token == first + i, centered[i : i + 1, :], 0.0)
     return total
+
+
+def row_parts(rows_ref):
+    slots, width = rows_ref.shape
+    first, rows = first_width(width), slots // PARTS
+    return [
+        (pl.ds(i * rows, rows), columns)
+        for columns in (pl.ds(0, first), pl.ds(first, width - first))
+        for i in range(PARTS)
+    ]
 
 
 def front_kernel(
@@ -87,7 +102,7 @@
                 (pre_hbm, pre_ref),
                 (tokens_hbm, tokens_ref),
                 (bias_hbm, bias_flat),
-                (rows_hbm, rows_ref),
+                *((rows_hbm.at[part], rows_ref.at[part]) for part in row_parts(rows_ref)),
             )
         )
     ]
@@ -114,7 +129,8 @@
     bias_ref[...] = bias
     centered_ref[...] = (tokens - bias).astype(jnp.bfloat16).astype(jnp.float32)
 
-    copies[4].wait()
+    for copy in copies[4 : 4 + PARTS]:
+        copy.wait()
     total = share(code, rows_ref, centered_ref, 0, total_ref.shape[1])
     total_ref[...] = total
     width = total.shape[1]
@@ -124,6 +140,8 @@
         cut[0][...] = block
     else:
         sent_ref[:, width:] = block
+    for copy in copies[4 + PARTS :]:
+        copy.wait()
 
 
 def front(tokens, b_pre, pre_codes, top_idx, blocks, counts, dict_rows, merged):
@@ -150,7 +168,7 @@
             pltpu.VMEM(b_pre.shape, b_pre.dtype),
             pltpu.VMEM(pre_codes.shape, pre_codes.dtype),
             pltpu.VMEM(top_idx.shape, top_idx.dtype),
-            pltpu.SemaphoreType.DMA((5,)),
+            pltpu.SemaphoreType.DMA((4 + 2 * PARTS,)),
         ],
     )(
         *(
@@ -337,7 +355,7 @@
     distance = jnp.zeros_like(place)
     for step in range(feat_bits()):
         bit = sum(
-            jnp.where(core == c, bit_of(step, c), 0) for c in range(lax.axis_size("tok"))
+            jnp.where(core == c, bit_of(step, c, 0), 0) for c in range(lax.axis_size("tok"))
         )
         distance |= (block >> step & 1) << bit
     source = (lax.axis_index("feat") ^ distance) * rows + place % rows
@@ -387,17 +405,17 @@
         tokens, b_pre, pre_codes, top_idx, blocks, counts, dict_rows, merged
     )
     for step in range(steps):
-        arrived = swapped(sent, step)
+        arrived = swapped(sent, step, 0)
         if step == 0:
             total_second, sent_second = second(code, dict_rows, centered)
         else:
             total_second, sent_second = added(
                 total_second, sent_second, arrived_second, sent, False, EARLY
             )
-        arrived_second = swapped(sent_second, step)
+        arrived_second = swapped(sent_second, step, 1)
         if not merged:
             own_block = joined(own_block, arrived_block, sent_second) if step else block[0]
-            arrived_block = swapped(own_block, step)
+            arrived_block = swapped(own_block, step, 0)
         if step < steps - 1:
             total, sent = added(total, sent, arrived, sent_second, merged)
     skip = 0

time: 25 us -> 25.2 us (level); the launches traced: 24.7 us -> 24.7 us
  waiting for transfers between devices: 5.91 us -> 3.79 us
  starting transfers between devices: 12.6 us -> 14.6 us
    ppermute x6, waiting for transfers between devices: 5.34 us -> 3.21 us  [swapped(): return lax.ppermute(shard, ('feat', 'tok'), pairs)]
    ppermute x6, starting transfers between devices: 12.5 us -> 14.6 us  [swapped(): return lax.ppermute(shard, ('feat', 'tok'), pairs)]
  transfers between devices with their start and end apart: 7 -> 7, of which waited for: 5 -> 6; matrix products, arithmetic and copies ran while one was open for 0% -> 0% of each run, Pallas kernels for 4% -> 4%
where the time goes in v16:
time: 25.2 us; the launch traced here: 24.7 us
  starting transfers between devices  14.6 us (58%)
  Pallas kernels  4.28 us (17%)
  waiting for transfers between devices  3.79 us (15%)
  between operations  1.97 us (8%)
    ppermute x6, starting transfers between devices, swapped(): return lax.ppermute(shard, ('feat', 'tok'), pairs)  14.6 us
    ppermute x6, waiting for transfers between devices, swapped(): return lax.ppermute(shard, ('feat', 'tok'), pairs)  3.21 us
    pallas_call x1, Pallas kernels, front(): kernel_call(front_kernel, (shape(count, slots), shape(count, slots, dtype...  1.53 us
    pallas_call x1, Pallas kernels, final(): kernel_call(functools.partial(final_kernel, rows), (shape(*grad_rows.shap...  1.44 us
    ppermute x1, waiting for transfers between devices, local(): theirs = lax.ppermute(code_half, 'tok', [(i, 1 - i) for i in range(2)])  0.58 us
  transfers between devices with their start and end apart: 7, of which 6 were waited for; matrix products, arithmetic and copies ran while one was open for 0% of the time, Pallas kernels for 4%

profile of v16, /device:TPU:0, one launch (start us, length us, event | category | flops | bytes accessed | tf_op | source)
XLA Modules:
  0.0 24.7 jit_solution(5787160565602805186)
XLA Ops:
  1.9 1.5 %shard_map.94 = (bf16[16,128]{1,0:T(8,128)(2,1)S(1)}, f32[16,128]{1,0:T(8,128)S(1)}, f32[16,2048]{1,0:T(8,128)S(1)}, bf16[16,2560]{1,0:T(8,128)(2,1)S(1)}, bf16[...) custom-call(bf16[2,4096]{1,0:T(2,128)(2,1)} %tokens_hbm.1, bf16[4096]{0:T(1024)(128)(2,1)} %bias_hbm.1, ...), custom_call_target="tpu_custom_call" | custom-call | flops 1000000 | bytes 1048576 | tf_op jit(solution)/shard_map/pallas_call | solution.py:151
  3.5 4.1 %collective-permute-start.1 = (bf16[16,2560]{1,0:T(8,128)(2,1)S(1)}, bf16[16,2560]{1,0:T(8,128)(2,1)S(1)}, u32[]{:S(2)}, u32[]{:S(2)}) collective-permute-start(bf16[16,2560]{1,0:T(8,128)(2,1)S(1)} %get-tuple-element.34.own_ref), channel_id=1, source_target_pairs={{0,8},{1,5},{2,10},{3,7},{4,12},{5,1},{6,14},{7,3},{8,0},{9,13},{1... | collective-permute-start | bytes 245768 | tf_op jit(solution)/shard_map/ppermute | solution.py:60
  7.6 0.2 shard_map.95
  7.7 1.6 %collective-permute-start = (bf16[16,2048]{1,0:T(8,128)(2,1)S(1)}, bf16[16,2048]{1,0:T(8,128)(2,1)S(1)}, u32[]{:S(2)}, u32[]{:S(2)}) collective-permute-start(bf16[16,2048]{1,0:T(8,128)(2,1)S(1)} %get-tuple-element.32.after_ref.own_ref), channel_id=1, source_target_pairs={{0,2},{1,3},{2,0},{3,1},{4,6},{5,7},{6,4},{7,5},{8,10},{9,11},{10,... | collective-permute-start | bytes 196616 | tf_op jit(solution)/shard_map/ppermute | solution.py:60
  9.3 0.7 %collective-permute-done.1.arrived_ref = bf16[16,2560]{1,0:T(8,128)(2,1)S(1)} collective-permute-done((bf16[16,2560]{1,0:T(8,128)(2,1)S(1)}, bf16[16,2560]{1,0:T(8,128)(2,1)S(1)}, u32[]{:S(2)}, u32[]{:S(2)}) %collective-permute-start.1) | collective-permute-done | bytes 81952 | tf_op jit(solution)/shard_map/ppermute | solution.py:60
  10.0 1.9 %collective-permute-start.3 = (bf16[16,3072]{1,0:T(8,128)(2,1)S(1)}, bf16[16,3072]{1,0:T(8,128)(2,1)S(1)}, u32[]{:S(2)}, u32[]{:S(2)}) collective-permute-start(bf16[16,3072]{1,0:T(8,128)(2,1)S(1)} %get-tuple-element.35.after_ref.own_ref), channel_id=1, source_target_pairs={{0,2},{1,9},{2,0},{3,11},{4,6},{5,13},{6,4},{7,15},{8,10},{9,1},{1... | collective-permute-start | bytes 294920 | tf_op jit(solution)/shard_map/ppermute | solution.py:60
  11.9 0.2 collective-permute-done.arrived_ref
  12.1 2.6 %collective-permute-start.2 = (bf16[16,2048]{1,0:T(8,128)(2,1)S(1)}, bf16[16,2048]{1,0:T(8,128)(2,1)S(1)}, u32[]{:S(2)}, u32[]{:S(2)}) collective-permute-start(bf16[16,2048]{1,0:T(8,128)(2,1)S(1)} %get-tuple-element.37.after_ref.own_ref), channel_id=1, source_target_pairs={{0,8},{1,5},{2,10},{3,7},{4,12},{5,1},{6,14},{7,3},{8,0},{9,13},{1... | collective-permute-start | bytes 196616 | tf_op jit(solution)/shard_map/ppermute | solution.py:60
  14.7 0.0 collective-permute-done.3.arrived_ref
  14.7 2.3 %collective-permute-start.5 = (bf16[16,4096]{1,0:T(8,128)(2,1)S(1)}, bf16[16,4096]{1,0:T(8,128)(2,1)S(1)}, u32[]{:S(2)}, u32[]{:S(2)}) collective-permute-start(bf16[16,4096]{1,0:T(8,128)(2,1)S(1)} %get-tuple-element.39.after_ref.own_ref), channel_id=1, source_target_pairs={{0,4},{1,3},{2,6},{3,1},{4,0},{5,7},{6,2},{7,5},{8,12},{9,11},{10,... | collective-permute-start | bytes 393224 | tf_op jit(solution)/shard_map/ppermute | solution.py:60
  17.0 0.3 %collective-permute-done.2.arrived_ref = bf16[16,2048]{1,0:T(8,128)(2,1)S(1)} collective-permute-done((bf16[16,2048]{1,0:T(8,128)(2,1)S(1)}, bf16[16,2048]{1,0:T(8,128)(2,1)S(1)}, u32[]{:S(2)}, u32[]{:S(2)}) %collective-permute-start.2) | collective-permute-done | bytes 65568 | tf_op jit(solution)/shard_map/ppermute | solution.py:60
  17.3 2.2 %collective-permute-start.4 = (bf16[16,2048]{1,0:T(8,128)(2,1)S(1)}, bf16[16,2048]{1,0:T(8,128)(2,1)S(1)}, u32[]{:S(2)}, u32[]{:S(2)}) collective-permute-start(bf16[16,2048]{1,0:T(8,128)(2,1)S(1)} %get-tuple-element.41), channel_id=1, source_target_pairs={{0,4},{1,9},{2,6},{3,11},{4,0},{5,13},{6,2},{7,15},{8,12},{9,1},{1... | collective-permute-start | bytes 196616 | tf_op jit(solution)/shard_map/ppermute | solution.py:60
  19.6 0.7 %collective-permute-done.5.arrived_ref = bf16[16,4096]{1,0:T(8,128)(2,1)S(1)} collective-permute-done((bf16[16,4096]{1,0:T(8,128)(2,1)S(1)}, bf16[16,4096]{1,0:T(8,128)(2,1)S(1)}, u32[]{:S(2)}, u32[]{:S(2)}) %collective-permute-start.5) | collective-permute-done | bytes 131104 | tf_op jit(solution)/shard_map/ppermute | solution.py:60
  20.2 0.2 shard_map.100
  20.5 1.3 %collective-permute-done.4.arrived_ref = bf16[16,2048]{1,0:T(8,128)(2,1)S(1)} collective-permute-done((bf16[16,2048]{1,0:T(8,128)(2,1)S(1)}, bf16[16,2048]{1,0:T(8,128)(2,1)S(1)}, u32[]{:S(2)}, u32[]{:S(2)}) %collective-permute-start.4) | collective-permute-done | bytes 65568 | tf_op jit(solution)/shard_map/ppermute | solution.py:60
  21.8 0.2 shard_map.101
  22.0 0.0 collective-permute-start.6
  22.1 0.5 %shard_map.103.rows_ref = bf16[128,4096]{1,0:T(8,128)(2,1)S(1)} custom-call(bf16[16,128]{1,0:T(8,128)(2,1)S(1)} %get-tuple-element.28.code_ref, bf16[16,2048]{1,0:T(8,128)(2,1)S(1)} %get-tuple-element.46.first_ref, bf16[16,2048]{1,0:T(8,128)(2,1)S(1)} %get-tuple-element.47.second_ref), custom_call_target="tpu_custom_call" | custom-call | flops 1000000 | bytes 1048576 | tf_op jit(solution)/shard_map/pallas_call | solution.py:318
  22.5 0.1 shard_map.102.turned_ref
  22.7 0.6 %collective-permute-done.6.theirs_ref = f32[16,128]{1,0:T(8,128)S(1)} collective-permute-done((f32[16,128]{1,0:T(8,128)S(1)}, f32[16,128]{1,0:T(8,128)S(1)}, u32[]{:S(2)}, u32[]{:S(2)}) %collective-permute-start.6) | collective-permute-done | bytes 8224 | tf_op jit(solution)/shard_map/ppermute | solution.py:430
  23.2 1.4 %shard_map.104 = (bf16[128,4096]{1,0:T(8,128)(2,1)}, bf16[4096,128]{1,0:T(8,128)(2,1)}, f32[1,128]{1,0:T(1,128)}) custom-call(f32[16,128]{1,0:T(8,128)S(1)} %get-tuple-element.27.raw_ref, f32[16,128]{1,0:T(8,128)S(1)} %get-tuple-element.44.mine_ref, f32[16,128]{1,0:T(8,128)S(1)} %collective-permute-done.6.theirs_ref, ...), custom_call_target="tpu_custom_call" | custom-call | flops 1000000 | bytes 1048576 | tf_op jit(solution)/shard_map/pallas_call | solution.py:385
  (4 shorter events, 0.1 us)
Async XLA Ops:
  3.5 6.5 %collective-permute-start.1 = (bf16[16,2560]{1,0:T(8,128)(2,1)S(1)}, bf16[16,2560]{1,0:T(8,128)(2,1)S(1)}, u32[]{:S(2)}, u32[]{:S(2)}) collective-permute-start(bf16[16,2560]{1,0:T(8,128)(2,1)S(1)} %get-tuple-element.34.own_ref), channel_id=1, source_target_pairs={{0,8},{1,5},{2,10},{3,7},{4,12},{5,1},{6,14},{7,3},{8,0},{9,13},{1... | collective-permute-start | bytes 245768 | tf_op jit(solution)/shard_map/ppermute | solution.py:60
  7.7 4.3 %collective-permute-start = (bf16[16,2048]{1,0:T(8,128)(2,1)S(1)}, bf16[16,2048]{1,0:T(8,128)(2,1)S(1)}, u32[]{:S(2)}, u32[]{:S(2)}) collective-permute-start(bf16[16,2048]{1,0:T(8,128)(2,1)S(1)} %get-tuple-element.32.after_ref.own_ref), channel_id=1, source_target_pairs={{0,2},{1,3},{2,0},{3,1},{4,6},{5,7},{6,4},{7,5},{8,10},{9,11},{10,... | collective-permute-start | bytes 196616 | tf_op jit(solution)/shard_map/ppermute | solution.py:60
  10.0 4.7 %collective-permute-start.3 = (bf16[16,3072]{1,0:T(8,128)(2,1)S(1)}, bf16[16,3072]{1,0:T(8,128)(2,1)S(1)}, u32[]{:S(2)}, u32[]{:S(2)}) collective-permute-start(bf16[16,3072]{1,0:T(8,128)(2,1)S(1)} %get-tuple-element.35.after_ref.own_ref), channel_id=1, source_target_pairs={{0,2},{1,9},{2,0},{3,11},{4,6},{5,13},{6,4},{7,15},{8,10},{9,1},{1... | collective-permute-start | bytes 294920 | tf_op jit(solution)/shard_map/ppermute | solution.py:60
  12.1 5.2 %collective-permute-start.2 = (bf16[16,2048]{1,0:T(8,128)(2,1)S(1)}, bf16[16,2048]{1,0:T(8,128)(2,1)S(1)}, u32[]{:S(2)}, u32[]{:S(2)}) collective-permute-start(bf16[16,2048]{1,0:T(8,128)(2,1)S(1)} %get-tuple-element.37.after_ref.own_ref), channel_id=1, source_target_pairs={{0,8},{1,5},{2,10},{3,7},{4,12},{5,1},{6,14},{7,3},{8,0},{9,13},{1... | collective-permute-start | bytes 196616 | tf_op jit(solution)/shard_map/ppermute | solution.py:60
  14.7 5.5 %collective-permute-start.5 = (bf16[16,4096]{1,0:T(8,128)(2,1)S(1)}, bf16[16,4096]{1,0:T(8,128)(2,1)S(1)}, u32[]{:S(2)}, u32[]{:S(2)}) collective-permute-start(bf16[16,4096]{1,0:T(8,128)(2,1)S(1)} %get-tuple-element.39.after_ref.own_ref), channel_id=1, source_target_pairs={{0,4},{1,3},{2,6},{3,1},{4,0},{5,7},{6,2},{7,5},{8,12},{9,11},{10,... | collective-permute-start | bytes 393224 | tf_op jit(solution)/shard_map/ppermute | solution.py:60
  17.3 4.5 %collective-permute-start.4 = (bf16[16,2048]{1,0:T(8,128)(2,1)S(1)}, bf16[16,2048]{1,0:T(8,128)(2,1)S(1)}, u32[]{:S(2)}, u32[]{:S(2)}) collective-permute-start(bf16[16,2048]{1,0:T(8,128)(2,1)S(1)} %get-tuple-element.41), channel_id=1, source_target_pairs={{0,4},{1,9},{2,6},{3,11},{4,0},{5,13},{6,2},{7,15},{8,12},{9,1},{1... | collective-permute-start | bytes 196616 | tf_op jit(solution)/shard_map/ppermute | solution.py:60
  22.0 1.2 %collective-permute-start.6 = (f32[16,128]{1,0:T(8,128)S(1)}, f32[16,128]{1,0:T(8,128)S(1)}, u32[]{:S(2)}, u32[]{:S(2)}) collective-permute-start(f32[16,128]{1,0:T(8,128)S(1)} %get-tuple-element.44.mine_ref), channel_id=1, source_target_pairs={{0,1},{1,0},{2,3},{3,2},{4,5},{5,4},{6,7},{7,6},{8,9},{9,8},{10,11... | collective-permute-start | bytes 24584 | tf_op jit(solution)/shard_map/ppermute | solution.py:430

commit v17 on v15

--- a/solution.py
+++ b/solution.py
@@ -74,27 +74,36 @@
     return total
 
 
+def order_kernel(rows, order_ref):
+    place = lax.broadcasted_iota(jnp.int32, order_ref.shape, 0)
+    token = lax.broadcasted_iota(jnp.int32, order_ref.shape, 1)
+    core = lax.axis_index("tok")
+    block = place // ROWS
+    distance = jnp.zeros_like(place)
+    for step in range(feat_bits()):
+        bit = sum(
+            jnp.where(core == c, bit_of(step, c), 0) for c in range(lax.axis_size("tok"))
+        )
+        distance |= (block >> step & 1) << bit
+    source = (lax.axis_index("feat") ^ distance) * rows + place % rows
+    order_ref[...] = jnp.where(token == source, 1.0, 0.0).astype(jnp.bfloat16)
+
+
+def order_of(rows, count):
+    return kernel_call(
+        functools.partial(order_kernel, rows),
+        shape(ROWS * lax.axis_size("feat"), count),
+        [],
+        VMEM,
+        count,
+        flops=EARLY,
+    )()
+
+
 def front_kernel(
-    tokens_hbm, bias_hbm, pre_hbm, top_hbm, rows_hbm, block_ref, count_ref, *refs
+    tokens_ref, bias_flat, pre_ref, top_ref, rows_ref, block_ref, count_ref, after_ref, *refs
 ):
-    code_ref, raw_ref, total_ref, sent_ref, rows_ref, centered_ref, bias_ref, *cut = refs[:-5]
-    tokens_ref, bias_flat, pre_ref, top_ref, sems = refs[-5:]
-    copies = [
-        pltpu.make_async_copy(source, target, sems.at[i])
-        for i, (source, target) in enumerate(
-            (
-                (top_hbm, top_ref),
-                (pre_hbm, pre_ref),
-                (tokens_hbm, tokens_ref),
-                (bias_hbm, bias_flat),
-                (rows_hbm, rows_ref),
-            )
-        )
-    ]
-    for copy in copies:
-        copy.start()
-    for copy in copies[:2]:
-        copy.wait()
+    code_ref, raw_ref, total_ref, sent_ref, centered_ref, bias_ref, *cut = refs
     count, latents = top_ref.shape
     slots, width = rows_ref.shape
     offsets = lax.broadcasted_iota(jnp.int32, (1, slots), 1)
@@ -107,14 +116,11 @@
     code = jnp.maximum(raw, 0.0).astype(jnp.bfloat16)
     code_ref[...] = code
 
-    for copy in copies[2:4]:
-        copy.wait()
     tokens = tokens_ref[...].astype(jnp.float32)
     bias = bias_flat[...].astype(jnp.float32).reshape(1, width)
     bias_ref[...] = bias
     centered_ref[...] = (tokens - bias).astype(jnp.bfloat16).astype(jnp.float32)
 
-    copies[4].wait()
     total = share(code, rows_ref, centered_ref, 0, total_ref.shape[1])
     total_ref[...] = total
     width = total.shape[1]
@@ -126,7 +132,7 @@
         sent_ref[:, width:] = block
 
 
-def front(tokens, b_pre, pre_codes, top_idx, blocks, counts, dict_rows, merged):
+def front(tokens, b_pre, pre_codes, top_idx, blocks, counts, dict_rows, after, merged):
     count = top_idx.shape[0]
     slots, width = dict_rows.shape
     chunk, block = first_width(width), tokens.shape[0] * width // ROWS
@@ -137,29 +143,14 @@
             shape(count, slots, dtype=jnp.float32),
             shape(count, chunk, dtype=jnp.float32),
             shape(count, chunk + (block if merged else 0)),
-            shape(slots, width),
             shape(*tokens.shape, dtype=jnp.float32),
             shape(1, width, dtype=jnp.float32),
             *([] if merged else [shape(ROWS, block)]),
         ),
-        [HBM] * 5 + [SMEM] * 2,
-        (VMEM,) * (7 if merged else 8),
-        count,
-        [
-            pltpu.VMEM(tokens.shape, tokens.dtype),
-            pltpu.VMEM(b_pre.shape, b_pre.dtype),
-            pltpu.VMEM(pre_codes.shape, pre_codes.dtype),
-            pltpu.VMEM(top_idx.shape, top_idx.dtype),
-            pltpu.SemaphoreType.DMA((5,)),
-        ],
-    )(
-        *(
-            pltpu.with_memory_space_constraint(array, pltpu.HBM)
-            for array in (tokens, b_pre, pre_codes, top_idx, dict_rows)
-        ),
-        blocks,
-        counts,
-    )
+        [VMEM] * 5 + [SMEM] * 2 + [ANY],
+        (VMEM,) * (6 if merged else 7),
+        count,
+    )(tokens, b_pre, pre_codes, top_idx, dict_rows, blocks, counts, after)
 
 
 def second_kernel(code_ref, rows_ref, centered_ref, total_ref, sent_ref):
@@ -312,6 +303,7 @@
     mine_ref,
     theirs_ref,
     turned_ref,
+    order_ref,
     rows_ref,
     rows_hbm,
     enc_hbm,
@@ -330,19 +322,7 @@
     benc_ref[...] = jnp.sum(pre_grad.astype(jnp.float32), axis=0, keepdims=True)
     copies.append(pltpu.make_async_copy(benc_ref, benc_hbm, sems.at[1]))
     copies[1].start()
-    place = lax.broadcasted_iota(jnp.int32, (depth, count), 0)
-    token = lax.broadcasted_iota(jnp.int32, (depth, count), 1)
-    core = lax.axis_index("tok")
-    block = place // ROWS
-    distance = jnp.zeros_like(place)
-    for step in range(feat_bits()):
-        bit = sum(
-            jnp.where(core == c, bit_of(step, c), 0) for c in range(lax.axis_size("tok"))
-        )
-        distance |= (block >> step & 1) << bit
-    source = (lax.axis_index("feat") ^ distance) * rows + place % rows
-    order = jnp.where(token == source, 1.0, 0.0).astype(jnp.bfloat16)
-    spread = jnp.dot(order, pre_grad, preferred_element_type=jnp.float32)
+    spread = jnp.dot(order_ref[...], pre_grad, preferred_element_type=jnp.float32)
     piece = lax.broadcasted_iota(jnp.int32, (depth, slots), 0) % ROWS // rows
     for c in range(0, pieces, 2):
         pair = [jnp.where(piece == c + i, spread, 0.0).astype(jnp.bfloat16) for i in range(2)]
@@ -360,14 +340,14 @@
         copy.wait()
 
 
-def final(raw, mine, theirs, turned_tokens, grad_rows, rows):
+def final(raw, mine, theirs, turned_tokens, order, grad_rows, rows):
     count, slots = raw.shape
     pieces = ROWS // rows
     width = turned_tokens.shape[0] * pieces
     return kernel_call(
         functools.partial(final_kernel, rows),
         (shape(*grad_rows.shape), shape(width, slots), shape(1, slots, dtype=jnp.float32)),
-        [VMEM] * 5,
+        [VMEM] * 6,
         (HBM, HBM, HBM),
         count,
         [
@@ -375,7 +355,7 @@
             pltpu.VMEM((1, slots), jnp.float32),
             pltpu.SemaphoreType.DMA((pieces // 2 + 2,)),
         ],
-    )(raw, mine, theirs, turned_tokens, grad_rows)
+    )(raw, mine, theirs, turned_tokens, order, grad_rows)
 
 
 def local(tokens, b_pre, pre_codes, top_idx, blocks, counts, dict_rows):
@@ -383,8 +363,9 @@
     steps = feat_bits()
     merged = count == ROWS
 
-    code, raw, total, sent, dict_rows, centered, bias, *block = front(
-        tokens, b_pre, pre_codes, top_idx, blocks, counts, dict_rows, merged
+    order = order_of(rows, count)
+    code, raw, total, sent, centered, bias, *block = front(
+        tokens, b_pre, pre_codes, top_idx, blocks, counts, dict_rows, order, merged
     )
     for step in range(steps):
         arrived = swapped(sent, step)
@@ -412,7 +393,7 @@
     theirs = lax.ppermute(code_half, "tok", [(i, 1 - i) for i in range(2)])
     grad_rows = grad_rows_of(code, scaled, scaled_second)
     grad_rows, grad_enc, grad_benc = final(
-        raw, code_half, theirs, turned_tokens, grad_rows, rows
+        raw, code_half, theirs, turned_tokens, order, grad_rows, rows
     )
     return (grad_rows, grad_enc, grad_benc.reshape(-1))
 

time: 25 us -> 24.2 us (0.968)
  Pallas kernels: 4.29 us -> 3.4 us
    pallas_call x1, Pallas kernels: 1.53 us -> 0.61 us  [front(): kernel_call(front_kernel, (shape(count, slots), shape(count, slots, dtype...]
  transfers between devices with their start and end apart: 7 -> 7, of which waited for: 5 -> 5; matrix products, arithmetic and copies ran while one was open for 0% -> 0% of each run, Pallas kernels for 4% -> 5%
where the time goes in v17:
time: 24.2 us; the launch traced here: 24 us
  starting transfers between devices  12.6 us (52%)
  waiting for transfers between devices  5.91 us (24%)
  Pallas kernels  3.4 us (14%)
  between operations  2.13 us (9%)
    ppermute x6, starting transfers between devices, swapped(): return lax.ppermute(shard, ('feat', 'tok'), pairs)  12.5 us
    ppermute x6, waiting for transfers between devices, swapped(): return lax.ppermute(shard, ('feat', 'tok'), pairs)  5.34 us
    pallas_call x1, Pallas kernels, final(): kernel_call(functools.partial(final_kernel, rows), (shape(*grad_rows.shap...  1.41 us
    pallas_call x1, Pallas kernels, front(): kernel_call(front_kernel, (shape(count, slots), shape(count, slots, dtype...  0.61 us
    ppermute x1, waiting for transfers between devices, local(): theirs = lax.ppermute(code_half, 'tok', [(i, 1 - i) for i in range(2)])  0.57 us
  transfers between devices with their start and end apart: 7, of which 5 were waited for; matrix products, arithmetic and copies ran while one was open for 0% of the time, Pallas kernels for 5%

profile of v17, /device:TPU:0, one launch (start us, length us, event | category | flops | bytes accessed | tf_op | source)
XLA Modules:
  0.0 24.0 jit_solution(8776721190272630288)
XLA Ops:
  0.6 0.0 copy-start
  0.6 0.0 copy-start.1
  0.7 0.0 copy-start.2
  0.7 0.0 copy-start.3
  0.7 0.0 copy-start.4
  0.7 0.1 shard_map.94.after_ref.order_ref
  2.1 0.0 copy-done
  2.1 0.0 copy-done.1
  2.1 0.0 copy-done.2
  2.1 0.0 copy-done.3
  2.1 0.0 copy-done.4
  2.2 0.6 %shard_map.95 = (bf16[16,128]{1,0:T(8,128)(2,1)S(1)}, f32[16,128]{1,0:T(8,128)S(1)}, f32[16,2048]{1,0:T(8,128)S(1)}, bf16[16,2560]{1,0:T(8,128)(2,1)S(1)}, f32[2,4096]{1,0:T(2,128)S(1)}, /*index=5*/f32[1,4096]{1,0:T(1,128)S(1)}) custom-call(bf16[2,4096]{1,0:T(2,128)(2,1)S(1)} %copy-done.1, bf16[4096]{0:T(1024)(128)(2,1)S(1)} %copy-done.2, ...), custom_call_target="tpu_custom_call" | custom-call | flops 1000000 | bytes 1048576 | tf_op jit(solution)/shard_map/pallas_call | solution.py:139
  2.8 4.1 %collective-permute-start.1 = (bf16[16,2560]{1,0:T(8,128)(2,1)S(1)}, bf16[16,2560]{1,0:T(8,128)(2,1)S(1)}, u32[]{:S(2)}, u32[]{:S(2)}) collective-permute-start(bf16[16,2560]{1,0:T(8,128)(2,1)S(1)} %get-tuple-element.32.own_ref), channel_id=1, source_target_pairs={{0,8},{1,3},{2,10},{3,1},{4,12},{5,7},{6,14},{7,5},{8,0},{9,11},{1... | collective-permute-start | bytes 245768 | tf_op jit(solution)/shard_map/ppermute | solution.py:55
  6.9 0.2 shard_map.96
  7.0 0.1 collective-permute-start
  7.1 2.2 %collective-permute-done.1.arrived_ref = bf16[16,2560]{1,0:T(8,128)(2,1)S(1)} collective-permute-done((bf16[16,2560]{1,0:T(8,128)(2,1)S(1)}, bf16[16,2560]{1,0:T(8,128)(2,1)S(1)}, u32[]{:S(2)}, u32[]{:S(2)}) %collective-permute-start.1) | collective-permute-done | bytes 81952 | tf_op jit(solution)/shard_map/ppermute | solution.py:55
  9.3 1.9 %collective-permute-start.3 = (bf16[16,3072]{1,0:T(8,128)(2,1)S(1)}, bf16[16,3072]{1,0:T(8,128)(2,1)S(1)}, u32[]{:S(2)}, u32[]{:S(2)}) collective-permute-start(bf16[16,3072]{1,0:T(8,128)(2,1)S(1)} %get-tuple-element.33.after_ref.own_ref), channel_id=1, source_target_pairs={{0,2},{1,5},{2,0},{3,7},{4,6},{5,1},{6,4},{7,3},{8,10},{9,13},{10,... | collective-permute-start | bytes 294920 | tf_op jit(solution)/shard_map/ppermute | solution.py:55
  11.2 1.1 %collective-permute-done.arrived_ref = bf16[16,2048]{1,0:T(8,128)(2,1)S(1)} collective-permute-done((bf16[16,2048]{1,0:T(8,128)(2,1)S(1)}, bf16[16,2048]{1,0:T(8,128)(2,1)S(1)}, u32[]{:S(2)}, u32[]{:S(2)}) %collective-permute-start) | collective-permute-done | bytes 65568 | tf_op jit(solution)/shard_map/ppermute | solution.py:55
  12.4 1.6 %collective-permute-start.2 = (bf16[16,2048]{1,0:T(8,128)(2,1)S(1)}, bf16[16,2048]{1,0:T(8,128)(2,1)S(1)}, u32[]{:S(2)}, u32[]{:S(2)}) collective-permute-start(bf16[16,2048]{1,0:T(8,128)(2,1)S(1)} %get-tuple-element.35.after_ref.own_ref), channel_id=1, source_target_pairs={{0,2},{1,5},{2,0},{3,7},{4,6},{5,1},{6,4},{7,3},{8,10},{9,13},{10,... | collective-permute-start | bytes 196616 | tf_op jit(solution)/shard_map/ppermute | solution.py:55
  14.0 0.0 collective-permute-done.3.arrived_ref
  14.0 2.7 %collective-permute-start.5 = (bf16[16,4096]{1,0:T(8,128)(2,1)S(1)}, bf16[16,4096]{1,0:T(8,128)(2,1)S(1)}, u32[]{:S(2)}, u32[]{:S(2)}) collective-permute-start(bf16[16,4096]{1,0:T(8,128)(2,1)S(1)} %get-tuple-element.37.after_ref.own_ref), channel_id=1, source_target_pairs={{0,4},{1,9},{2,6},{3,11},{4,0},{5,13},{6,2},{7,15},{8,12},{9,1},{1... | collective-permute-start | bytes 393224 | tf_op jit(solution)/shard_map/ppermute | solution.py:55
  16.7 0.0 collective-permute-done.2.arrived_ref
  16.7 2.2 %collective-permute-start.4 = (bf16[16,2048]{1,0:T(8,128)(2,1)S(1)}, bf16[16,2048]{1,0:T(8,128)(2,1)S(1)}, u32[]{:S(2)}, u32[]{:S(2)}) collective-permute-start(bf16[16,2048]{1,0:T(8,128)(2,1)S(1)} %get-tuple-element.39), channel_id=1, source_target_pairs={{0,4},{1,9},{2,6},{3,11},{4,0},{5,13},{6,2},{7,15},{8,12},{9,1},{1... | collective-permute-start | bytes 196616 | tf_op jit(solution)/shard_map/ppermute | solution.py:55
  18.9 1.4 %collective-permute-done.5.arrived_ref = bf16[16,4096]{1,0:T(8,128)(2,1)S(1)} collective-permute-done((bf16[16,4096]{1,0:T(8,128)(2,1)S(1)}, bf16[16,4096]{1,0:T(8,128)(2,1)S(1)}, u32[]{:S(2)}, u32[]{:S(2)}) %collective-permute-start.5) | collective-permute-done | bytes 131104 | tf_op jit(solution)/shard_map/ppermute | solution.py:55
  20.3 0.2 %shard_map.101 = (bf16[16,2048]{1,0:T(8,128)(2,1)S(1)}, f32[16,128]{1,0:T(8,128)S(1)}) custom-call(f32[16,2048]{1,0:T(8,128)S(1)} %get-tuple-element.40.total_ref, bf16[16,4096]{1,0:T(8,128)(2,1)S(1)} %collective-permute-done.5.arrived_ref, bf16[128,4096]{1,0:T(8,128)(2,1)S(1)} %copy-done), custom_call_target="tpu_custom_call" | custom-call | flops 1000000 | bytes 1048576 | tf_op jit(solution)/shard_map/pallas_call | solution.py:269
  20.6 0.6 %collective-permute-done.4.arrived_ref = bf16[16,2048]{1,0:T(8,128)(2,1)S(1)} collective-permute-done((bf16[16,2048]{1,0:T(8,128)(2,1)S(1)}, bf16[16,2048]{1,0:T(8,128)(2,1)S(1)}, u32[]{:S(2)}, u32[]{:S(2)}) %collective-permute-start.4) | collective-permute-done | bytes 65568 | tf_op jit(solution)/shard_map/ppermute | solution.py:55
  21.2 0.2 shard_map.102
  21.4 0.0 collective-permute-start.6
  21.4 0.5 %shard_map.104.rows_ref = bf16[128,4096]{1,0:T(8,128)(2,1)S(1)} custom-call(bf16[16,128]{1,0:T(8,128)(2,1)S(1)} %get-tuple-element.27.code_ref, bf16[16,2048]{1,0:T(8,128)(2,1)S(1)} %get-tuple-element.44.first_ref, bf16[16,2048]{1,0:T(8,128)(2,1)S(1)} %get-tuple-element.45.second_ref), custom_call_target="tpu_custom_call" | custom-call | flops 1000000 | bytes 1048576 | tf_op jit(solution)/shard_map/pallas_call | solution.py:291
  21.9 0.1 shard_map.103.turned_ref
  22.0 0.6 %collective-permute-done.6.theirs_ref = f32[16,128]{1,0:T(8,128)S(1)} collective-permute-done((f32[16,128]{1,0:T(8,128)S(1)}, f32[16,128]{1,0:T(8,128)S(1)}, u32[]{:S(2)}, u32[]{:S(2)}) %collective-permute-start.6) | collective-permute-done | bytes 8224 | tf_op jit(solution)/shard_map/ppermute | solution.py:393
  22.6 1.4 %shard_map.105 = (bf16[128,4096]{1,0:T(8,128)(2,1)}, bf16[4096,128]{1,0:T(8,128)(2,1)}, f32[1,128]{1,0:T(1,128)}) custom-call(f32[16,128]{1,0:T(8,128)S(1)} %get-tuple-element.26.raw_ref, f32[16,128]{1,0:T(8,128)S(1)} %get-tuple-element.42.mine_ref, f32[16,128]{1,0:T(8,128)S(1)} %collective-permute-done.6.theirs_ref, ...), custom_call_target="tpu_custom_call" | custom-call | flops 1000000 | bytes 1048576 | tf_op jit(solution)/shard_map/pallas_call | solution.py:347
  (4 shorter events, 0.1 us)
Async XLA Ops:
  0.6 1.5 %copy-start = (bf16[128,4096]{1,0:T(8,128)(2,1)S(1)}, bf16[128,4096]{1,0:T(8,128)(2,1)}, u32[]{:S(2)}) copy-start(bf16[128,4096]{1,0:T(8,128)(2,1)} %rows_ref.7) | copy-start | bytes 3145732
  0.6 1.5 %copy-start.1 = (bf16[2,4096]{1,0:T(2,128)(2,1)S(1)}, bf16[2,4096]{1,0:T(2,128)(2,1)}, u32[]{:S(2)}) copy-start(bf16[2,4096]{1,0:T(2,128)(2,1)} %tokens_ref.1) | copy-start | bytes 49156
  0.7 1.5 %copy-start.2 = (bf16[4096]{0:T(1024)(128)(2,1)S(1)}, bf16[4096]{0:T(1024)(128)(2,1)}, u32[]{:S(2)}) copy-start(bf16[4096]{0:T(1024)(128)(2,1)} %bias_flat.1) | copy-start | bytes 24580
  0.7 1.5 %copy-start.3 = (f32[16,64]{1,0:T(8,128)S(1)}, f32[16,64]{1,0:T(8,128)}, u32[]{:S(2)}) copy-start(f32[16,64]{1,0:T(8,128)} %pre_ref.1) | copy-start | bytes 12292
  0.7 1.5 %copy-start.4 = (s32[16,64]{1,0:T(8,128)S(1)}, s32[16,64]{1,0:T(8,128)}, u32[]{:S(2)}) copy-start(s32[16,64]{1,0:T(8,128)} %top_ref.1) | copy-start | bytes 12292
  2.8 6.5 %collective-permute-start.1 = (bf16[16,2560]{1,0:T(8,128)(2,1)S(1)}, bf16[16,2560]{1,0:T(8,128)(2,1)S(1)}, u32[]{:S(2)}, u32[]{:S(2)}) collective-permute-start(bf16[16,2560]{1,0:T(8,128)(2,1)S(1)} %get-tuple-element.32.own_ref), channel_id=1, source_target_pairs={{0,8},{1,3},{2,10},{3,1},{4,12},{5,7},{6,14},{7,5},{8,0},{9,11},{1... | collective-permute-start | bytes 245768 | tf_op jit(solution)/shard_map/ppermute | solution.py:55
  7.0 5.3 %collective-permute-start = (bf16[16,2048]{1,0:T(8,128)(2,1)S(1)}, bf16[16,2048]{1,0:T(8,128)(2,1)S(1)}, u32[]{:S(2)}, u32[]{:S(2)}) collective-permute-start(bf16[16,2048]{1,0:T(8,128)(2,1)S(1)} %get-tuple-element.30.after_ref.own_ref), channel_id=1, source_target_pairs={{0,8},{1,3},{2,10},{3,1},{4,12},{5,7},{6,14},{7,5},{8,0},{9,11},{1... | collective-permute-start | bytes 196616 | tf_op jit(solution)/shard_map/ppermute | solution.py:55
  9.3 4.7 %collective-permute-start.3 = (bf16[16,3072]{1,0:T(8,128)(2,1)S(1)}, bf16[16,3072]{1,0:T(8,128)(2,1)S(1)}, u32[]{:S(2)}, u32[]{:S(2)}) collective-permute-start(bf16[16,3072]{1,0:T(8,128)(2,1)S(1)} %get-tuple-element.33.after_ref.own_ref), channel_id=1, source_target_pairs={{0,2},{1,5},{2,0},{3,7},{4,6},{5,1},{6,4},{7,3},{8,10},{9,13},{10,... | collective-permute-start | bytes 294920 | tf_op jit(solution)/shard_map/ppermute | solution.py:55
  12.4 4.3 %collective-permute-start.2 = (bf16[16,2048]{1,0:T(8,128)(2,1)S(1)}, bf16[16,2048]{1,0:T(8,128)(2,1)S(1)}, u32[]{:S(2)}, u32[]{:S(2)}) collective-permute-start(bf16[16,2048]{1,0:T(8,128)(2,1)S(1)} %get-tuple-element.35.after_ref.own_ref), channel_id=1, source_target_pairs={{0,2},{1,5},{2,0},{3,7},{4,6},{5,1},{6,4},{7,3},{8,10},{9,13},{10,... | collective-permute-start | bytes 196616 | tf_op jit(solution)/shard_map/ppermute | solution.py:55
  14.0 6.3 %collective-permute-start.5 = (bf16[16,4096]{1,0:T(8,128)(2,1)S(1)}, bf16[16,4096]{1,0:T(8,128)(2,1)S(1)}, u32[]{:S(2)}, u32[]{:S(2)}) collective-permute-start(bf16[16,4096]{1,0:T(8,128)(2,1)S(1)} %get-tuple-element.37.after_ref.own_ref), channel_id=1, source_target_pairs={{0,4},{1,9},{2,6},{3,11},{4,0},{5,13},{6,2},{7,15},{8,12},{9,1},{1... | collective-permute-start | bytes 393224 | tf_op jit(solution)/shard_map/ppermute | solution.py:55
  16.7 4.4 %collective-permute-start.4 = (bf16[16,2048]{1,0:T(8,128)(2,1)S(1)}, bf16[16,2048]{1,0:T(8,128)(2,1)S(1)}, u32[]{:S(2)}, u32[]{:S(2)}) collective-permute-start(bf16[16,2048]{1,0:T(8,128)(2,1)S(1)} %get-tuple-element.39), channel_id=1, source_target_pairs={{0,4},{1,9},{2,6},{3,11},{4,0},{5,13},{6,2},{7,15},{8,12},{9,1},{1... | collective-permute-start | bytes 196616 | tf_op jit(solution)/shard_map/ppermute | solution.py:55
  21.4 1.2 %collective-permute-start.6 = (f32[16,128]{1,0:T(8,128)S(1)}, f32[16,128]{1,0:T(8,128)S(1)}, u32[]{:S(2)}, u32[]{:S(2)}) collective-permute-start(f32[16,128]{1,0:T(8,128)S(1)} %get-tuple-element.42.mine_ref), channel_id=1, source_target_pairs={{0,1},{1,0},{2,3},{3,2},{4,5},{5,4},{6,7},{7,6},{8,9},{9,8},{10,11... | collective-permute-start | bytes 24584 | tf_op jit(solution)/shard_map/ppermute | solution.py:393

commit v18 on v17

--- a/solution.py
+++ b/solution.py
@@ -40,15 +40,19 @@
     return (lax.axis_size("feat") - 1).bit_length()
 
 
-def bit_of(step, core):
+def bit_of(step, core, chunk):
     bits = list(range(feat_bits()))
-    return (bits[-1:] + bits[:-1] if core == 0 else bits)[step]
-
-
-def swapped(shard, step):
+    if core == 0:
+        order = bits[-1:] + bits[:-1] if chunk == 0 else bits
+    else:
+        order = bits[1:] + bits[:1] if chunk == 0 else bits[:1] + bits[:0:-1]
+    return order[step]
+
+
+def swapped(shard, step, chunk):
     cores = lax.axis_size("tok")
     pairs = [
-        (f * cores + c, (f ^ 1 << bit_of(step, c)) * cores + c)
+        (f * cores + c, (f ^ 1 << bit_of(step, c, chunk)) * cores + c)
         for f in range(lax.axis_size("feat"))
         for c in range(cores)
     ]
@@ -82,7 +86,7 @@
     distance = jnp.zeros_like(place)
     for step in range(feat_bits()):
         bit = sum(
-            jnp.where(core == c, bit_of(step, c), 0) for c in range(lax.axis_size("tok"))
+            jnp.where(core == c, bit_of(step, c, 0), 0) for c in range(lax.axis_size("tok"))
         )
         distance |= (block >> step & 1) << bit
     source = (lax.axis_index("feat") ^ distance) * rows + place % rows
@@ -368,17 +372,17 @@
         tokens, b_pre, pre_codes, top_idx, blocks, counts, dict_rows, order, merged
     )
     for step in range(steps):
-        arrived = swapped(sent, step)
+        arrived = swapped(sent, step, 0)
         if step == 0:
             total_second, sent_second = second(code, dict_rows, centered)
         else:
             total_second, sent_second = added(
                 total_second, sent_second, arrived_second, sent, False, EARLY
             )
-        arrived_second = swapped(sent_second, step)
+        arrived_second = swapped(sent_second, step, 1)
         if not merged:
             own_block = joined(own_block, arrived_block, sent_second) if step else block[0]
-            arrived_block = swapped(own_block, step)
+            arrived_block = swapped(own_block, step, 0)
         if step < steps - 1:
             total, sent = added(total, sent, arrived, sent_second, merged)
     skip = 0

time: 24.2 us -> 24.7 us (1.021)
  starting transfers between devices: 12.6 us -> 14.6 us
  waiting for transfers between devices: 5.91 us -> 4.39 us
    ppermute x6, starting transfers between devices: 12.5 us -> 14.6 us  [swapped(): return lax.ppermute(shard, ('feat', 'tok'), pairs)]
    ppermute x6, waiting for transfers between devices: 5.34 us -> 3.82 us  [swapped(): return lax.ppermute(shard, ('feat', 'tok'), pairs)]
  transfers between devices with their start and end apart: 7 -> 7, of which waited for: 5 -> 5; matrix products, arithmetic and copies ran while one was open for 0% -> 0% of each run, Pallas kernels for 5% -> 4%
where the time goes in v18:
time: 24.7 us; the launch traced here: 24.5 us
  starting transfers between devices  14.6 us (59%)
  waiting for transfers between devices  4.39 us (18%)
  Pallas kernels  3.39 us (14%)
  between operations  2.12 us (9%)
    ppermute x6, starting transfers between devices, swapped(): return lax.ppermute(shard, ('feat', 'tok'), pairs)  14.6 us
    ppermute x6, waiting for transfers between devices, swapped(): return lax.ppermute(shard, ('feat', 'tok'), pairs)  3.82 us
    pallas_call x1, Pallas kernels, final(): kernel_call(functools.partial(final_kernel, rows), (shape(*grad_rows.shap...  1.41 us
    pallas_call x1, Pallas kernels, front(): kernel_call(front_kernel, (shape(count, slots), shape(count, slots, dtype...  0.61 us
    ppermute x1, waiting for transfers between devices, local(): theirs = lax.ppermute(code_half, 'tok', [(i, 1 - i) for i in range(2)])  0.58 us
  transfers between devices with their start and end apart: 7, of which 5 were waited for; matrix products, arithmetic and copies ran while one was open for 0% of the time, Pallas kernels for 4%

profile of v18, /device:TPU:0, one launch (start us, length us, event | category | flops | bytes accessed | tf_op | source)
XLA Modules:
  0.0 24.5 jit_solution(15807559770208928873)
XLA Ops:
  0.6 0.0 copy-start
  0.6 0.0 copy-start.1
  0.7 0.0 copy-start.2
  0.7 0.0 copy-start.3
  0.7 0.0 copy-start.4
  0.7 0.1 shard_map.94.after_ref.order_ref
  2.1 0.0 copy-done
  2.1 0.0 copy-done.1
  2.1 0.0 copy-done.2
  2.1 0.0 copy-done.3
  2.1 0.0 copy-done.4
  2.2 0.6 %shard_map.95 = (bf16[16,128]{1,0:T(8,128)(2,1)S(1)}, f32[16,128]{1,0:T(8,128)S(1)}, f32[16,2048]{1,0:T(8,128)S(1)}, bf16[16,2560]{1,0:T(8,128)(2,1)S(1)}, f32[2,4096]{1,0:T(2,128)S(1)}, /*index=5*/f32[1,4096]{1,0:T(1,128)S(1)}) custom-call(bf16[2,4096]{1,0:T(2,128)(2,1)S(1)} %copy-done.1, bf16[4096]{0:T(1024)(128)(2,1)S(1)} %copy-done.2, ...), custom_call_target="tpu_custom_call" | custom-call | flops 1000000 | bytes 1048576 | tf_op jit(solution)/shard_map/pallas_call | solution.py:143
  2.8 4.1 %collective-permute-start.1 = (bf16[16,2560]{1,0:T(8,128)(2,1)S(1)}, bf16[16,2560]{1,0:T(8,128)(2,1)S(1)}, u32[]{:S(2)}, u32[]{:S(2)}) collective-permute-start(bf16[16,2560]{1,0:T(8,128)(2,1)S(1)} %get-tuple-element.32.own_ref), channel_id=1, source_target_pairs={{0,8},{1,5},{2,10},{3,7},{4,12},{5,1},{6,14},{7,3},{8,0},{9,13},{1... | collective-permute-start | bytes 245768 | tf_op jit(solution)/shard_map/ppermute | solution.py:59
  6.9 0.2 shard_map.96
  7.0 1.6 %collective-permute-start = (bf16[16,2048]{1,0:T(8,128)(2,1)S(1)}, bf16[16,2048]{1,0:T(8,128)(2,1)S(1)}, u32[]{:S(2)}, u32[]{:S(2)}) collective-permute-start(bf16[16,2048]{1,0:T(8,128)(2,1)S(1)} %get-tuple-element.30.after_ref.own_ref), channel_id=1, source_target_pairs={{0,2},{1,3},{2,0},{3,1},{4,6},{5,7},{6,4},{7,5},{8,10},{9,11},{10,... | collective-permute-start | bytes 196616 | tf_op jit(solution)/shard_map/ppermute | solution.py:59
  8.6 0.7 %collective-permute-done.1.arrived_ref = bf16[16,2560]{1,0:T(8,128)(2,1)S(1)} collective-permute-done((bf16[16,2560]{1,0:T(8,128)(2,1)S(1)}, bf16[16,2560]{1,0:T(8,128)(2,1)S(1)}, u32[]{:S(2)}, u32[]{:S(2)}) %collective-permute-start.1) | collective-permute-done | bytes 81952 | tf_op jit(solution)/shard_map/ppermute | solution.py:59
  9.3 1.9 %collective-permute-start.3 = (bf16[16,3072]{1,0:T(8,128)(2,1)S(1)}, bf16[16,3072]{1,0:T(8,128)(2,1)S(1)}, u32[]{:S(2)}, u32[]{:S(2)}) collective-permute-start(bf16[16,3072]{1,0:T(8,128)(2,1)S(1)} %get-tuple-element.33.after_ref.own_ref), channel_id=1, source_target_pairs={{0,2},{1,9},{2,0},{3,11},{4,6},{5,13},{6,4},{7,15},{8,10},{9,1},{1... | collective-permute-start | bytes 294920 | tf_op jit(solution)/shard_map/ppermute | solution.py:59
  11.2 0.2 collective-permute-done.arrived_ref
  11.4 1.6 %collective-permute-start.2 = (bf16[16,2048]{1,0:T(8,128)(2,1)S(1)}, bf16[16,2048]{1,0:T(8,128)(2,1)S(1)}, u32[]{:S(2)}, u32[]{:S(2)}) collective-permute-start(bf16[16,2048]{1,0:T(8,128)(2,1)S(1)} %get-tuple-element.35.after_ref.own_ref), channel_id=1, source_target_pairs={{0,4},{1,9},{2,6},{3,11},{4,0},{5,13},{6,2},{7,15},{8,12},{9,1},{1... | collective-permute-start | bytes 196616 | tf_op jit(solution)/shard_map/ppermute | solution.py:59
  13.0 1.0 %collective-permute-done.3.arrived_ref = bf16[16,3072]{1,0:T(8,128)(2,1)S(1)} collective-permute-done((bf16[16,3072]{1,0:T(8,128)(2,1)S(1)}, bf16[16,3072]{1,0:T(8,128)(2,1)S(1)}, u32[]{:S(2)}, u32[]{:S(2)}) %collective-permute-start.3) | collective-permute-done | bytes 98336 | tf_op jit(solution)/shard_map/ppermute | solution.py:59
  14.0 2.0 %collective-permute-start.5 = (bf16[16,4096]{1,0:T(8,128)(2,1)S(1)}, bf16[16,4096]{1,0:T(8,128)(2,1)S(1)}, u32[]{:S(2)}, u32[]{:S(2)}) collective-permute-start(bf16[16,4096]{1,0:T(8,128)(2,1)S(1)} %get-tuple-element.37.after_ref.own_ref), channel_id=1, source_target_pairs={{0,4},{1,3},{2,6},{3,1},{4,0},{5,7},{6,2},{7,5},{8,12},{9,11},{10,... | collective-permute-start | bytes 393224 | tf_op jit(solution)/shard_map/ppermute | solution.py:59
  16.0 0.0 collective-permute-done.2.arrived_ref
  16.0 3.4 %collective-permute-start.4 = (bf16[16,2048]{1,0:T(8,128)(2,1)S(1)}, bf16[16,2048]{1,0:T(8,128)(2,1)S(1)}, u32[]{:S(2)}, u32[]{:S(2)}) collective-permute-start(bf16[16,2048]{1,0:T(8,128)(2,1)S(1)} %get-tuple-element.39), channel_id=1, source_target_pairs={{0,8},{1,5},{2,10},{3,7},{4,12},{5,1},{6,14},{7,3},{8,0},{9,13},{1... | collective-permute-start | bytes 196616 | tf_op jit(solution)/shard_map/ppermute | solution.py:59
  19.4 0.0 collective-permute-done.5.arrived_ref
  19.4 0.2 shard_map.101
  19.7 2.0 %collective-permute-done.4.arrived_ref = bf16[16,2048]{1,0:T(8,128)(2,1)S(1)} collective-permute-done((bf16[16,2048]{1,0:T(8,128)(2,1)S(1)}, bf16[16,2048]{1,0:T(8,128)(2,1)S(1)}, u32[]{:S(2)}, u32[]{:S(2)}) %collective-permute-start.4) | collective-permute-done | bytes 65568 | tf_op jit(solution)/shard_map/ppermute | solution.py:59
  21.7 0.2 shard_map.102
  21.9 0.0 collective-permute-start.6
  21.9 0.5 %shard_map.104.rows_ref = bf16[128,4096]{1,0:T(8,128)(2,1)S(1)} custom-call(bf16[16,128]{1,0:T(8,128)(2,1)S(1)} %get-tuple-element.27.code_ref, bf16[16,2048]{1,0:T(8,128)(2,1)S(1)} %get-tuple-element.44.first_ref, bf16[16,2048]{1,0:T(8,128)(2,1)S(1)} %get-tuple-element.45.second_ref), custom_call_target="tpu_custom_call" | custom-call | flops 1000000 | bytes 1048576 | tf_op jit(solution)/shard_map/pallas_call | solution.py:295
  22.4 0.1 shard_map.103.turned_ref
  22.5 0.6 %collective-permute-done.6.theirs_ref = f32[16,128]{1,0:T(8,128)S(1)} collective-permute-done((f32[16,128]{1,0:T(8,128)S(1)}, f32[16,128]{1,0:T(8,128)S(1)}, u32[]{:S(2)}, u32[]{:S(2)}) %collective-permute-start.6) | collective-permute-done | bytes 8224 | tf_op jit(solution)/shard_map/ppermute | solution.py:397
  23.1 1.4 %shard_map.105 = (bf16[128,4096]{1,0:T(8,128)(2,1)}, bf16[4096,128]{1,0:T(8,128)(2,1)}, f32[1,128]{1,0:T(1,128)}) custom-call(f32[16,128]{1,0:T(8,128)S(1)} %get-tuple-element.26.raw_ref, f32[16,128]{1,0:T(8,128)S(1)} %get-tuple-element.42.mine_ref, f32[16,128]{1,0:T(8,128)S(1)} %collective-permute-done.6.theirs_ref, ...), custom_call_target="tpu_custom_call" | custom-call | flops 1000000 | bytes 1048576 | tf_op jit(solution)/shard_map/pallas_call | solution.py:351
  (4 shorter events, 0.1 us)
Async XLA Ops:
  0.6 1.5 %copy-start = (bf16[128,4096]{1,0:T(8,128)(2,1)S(1)}, bf16[128,4096]{1,0:T(8,128)(2,1)}, u32[]{:S(2)}) copy-start(bf16[128,4096]{1,0:T(8,128)(2,1)} %rows_ref.7) | copy-start | bytes 3145732
  0.6 1.5 %copy-start.1 = (bf16[2,4096]{1,0:T(2,128)(2,1)S(1)}, bf16[2,4096]{1,0:T(2,128)(2,1)}, u32[]{:S(2)}) copy-start(bf16[2,4096]{1,0:T(2,128)(2,1)} %tokens_ref.1) | copy-start | bytes 49156
  0.7 1.5 %copy-start.2 = (bf16[4096]{0:T(1024)(128)(2,1)S(1)}, bf16[4096]{0:T(1024)(128)(2,1)}, u32[]{:S(2)}) copy-start(bf16[4096]{0:T(1024)(128)(2,1)} %bias_flat.1) | copy-start | bytes 24580
  0.7 1.5 %copy-start.3 = (f32[16,64]{1,0:T(8,128)S(1)}, f32[16,64]{1,0:T(8,128)}, u32[]{:S(2)}) copy-start(f32[16,64]{1,0:T(8,128)} %pre_ref.1) | copy-start | bytes 12292
  0.7 1.5 %copy-start.4 = (s32[16,64]{1,0:T(8,128)S(1)}, s32[16,64]{1,0:T(8,128)}, u32[]{:S(2)}) copy-start(s32[16,64]{1,0:T(8,128)} %top_ref.1) | copy-start | bytes 12292
  2.8 6.5 %collective-permute-start.1 = (bf16[16,2560]{1,0:T(8,128)(2,1)S(1)}, bf16[16,2560]{1,0:T(8,128)(2,1)S(1)}, u32[]{:S(2)}, u32[]{:S(2)}) collective-permute-start(bf16[16,2560]{1,0:T(8,128)(2,1)S(1)} %get-tuple-element.32.own_ref), channel_id=1, source_target_pairs={{0,8},{1,5},{2,10},{3,7},{4,12},{5,1},{6,14},{7,3},{8,0},{9,13},{1... | collective-permute-start | bytes 245768 | tf_op jit(solution)/shard_map/ppermute | solution.py:59
  7.0 4.3 %collective-permute-start = (bf16[16,2048]{1,0:T(8,128)(2,1)S(1)}, bf16[16,2048]{1,0:T(8,128)(2,1)S(1)}, u32[]{:S(2)}, u32[]{:S(2)}) collective-permute-start(bf16[16,2048]{1,0:T(8,128)(2,1)S(1)} %get-tuple-element.30.after_ref.own_ref), channel_id=1, source_target_pairs={{0,2},{1,3},{2,0},{3,1},{4,6},{5,7},{6,4},{7,5},{8,10},{9,11},{10,... | collective-permute-start | bytes 196616 | tf_op jit(solution)/shard_map/ppermute | solution.py:59
  9.3 4.7 %collective-permute-start.3 = (bf16[16,3072]{1,0:T(8,128)(2,1)S(1)}, bf16[16,3072]{1,0:T(8,128)(2,1)S(1)}, u32[]{:S(2)}, u32[]{:S(2)}) collective-permute-start(bf16[16,3072]{1,0:T(8,128)(2,1)S(1)} %get-tuple-element.33.after_ref.own_ref), channel_id=1, source_target_pairs={{0,2},{1,9},{2,0},{3,11},{4,6},{5,13},{6,4},{7,15},{8,10},{9,1},{1... | collective-permute-start | bytes 294920 | tf_op jit(solution)/shard_map/ppermute | solution.py:59
  11.4 4.6 %collective-permute-start.2 = (bf16[16,2048]{1,0:T(8,128)(2,1)S(1)}, bf16[16,2048]{1,0:T(8,128)(2,1)S(1)}, u32[]{:S(2)}, u32[]{:S(2)}) collective-permute-start(bf16[16,2048]{1,0:T(8,128)(2,1)S(1)} %get-tuple-element.35.after_ref.own_ref), channel_id=1, source_target_pairs={{0,4},{1,9},{2,6},{3,11},{4,0},{5,13},{6,2},{7,15},{8,12},{9,1},{1... | collective-permute-start | bytes 196616 | tf_op jit(solution)/shard_map/ppermute | solution.py:59
  14.0 5.4 %collective-permute-start.5 = (bf16[16,4096]{1,0:T(8,128)(2,1)S(1)}, bf16[16,4096]{1,0:T(8,128)(2,1)S(1)}, u32[]{:S(2)}, u32[]{:S(2)}) collective-permute-start(bf16[16,4096]{1,0:T(8,128)(2,1)S(1)} %get-tuple-element.37.after_ref.own_ref), channel_id=1, source_target_pairs={{0,4},{1,3},{2,6},{3,1},{4,0},{5,7},{6,2},{7,5},{8,12},{9,11},{10,... | collective-permute-start | bytes 393224 | tf_op jit(solution)/shard_map/ppermute | solution.py:59
  16.0 5.7 %collective-permute-start.4 = (bf16[16,2048]{1,0:T(8,128)(2,1)S(1)}, bf16[16,2048]{1,0:T(8,128)(2,1)S(1)}, u32[]{:S(2)}, u32[]{:S(2)}) collective-permute-start(bf16[16,2048]{1,0:T(8,128)(2,1)S(1)} %get-tuple-element.39), channel_id=1, source_target_pairs={{0,8},{1,5},{2,10},{3,7},{4,12},{5,1},{6,14},{7,3},{8,0},{9,13},{1... | collective-permute-start | bytes 196616 | tf_op jit(solution)/shard_map/ppermute | solution.py:59
  21.9 1.2 %collective-permute-start.6 = (f32[16,128]{1,0:T(8,128)S(1)}, f32[16,128]{1,0:T(8,128)S(1)}, u32[]{:S(2)}, u32[]{:S(2)}) collective-permute-start(f32[16,128]{1,0:T(8,128)S(1)} %get-tuple-element.42.mine_ref), channel_id=1, source_target_pairs={{0,1},{1,0},{2,3},{3,2},{4,5},{5,4},{6,7},{7,6},{8,9},{9,8},{10,11... | collective-permute-start | bytes 24584 | tf_op jit(solution)/shard_map/ppermute | solution.py:397

commit v19 on v18

--- a/solution.py
+++ b/solution.py
@@ -33,7 +33,7 @@
 
 
 def first_width(width):
-    return width // 2
+    return width * 5 // 8 // 128 * 128
 
 
 def feat_bits():

time: 24.7 us -> 25 us (1.012)
  starting transfers between devices: 14.6 us -> 14.9 us
    ppermute x6, starting transfers between devices: 14.6 us -> 14.9 us  [swapped(): return lax.ppermute(shard, ('feat', 'tok'), pairs)]
  transfers between devices with their start and end apart: 7 -> 7, of which waited for: 5 -> 4; matrix products, arithmetic and copies ran while one was open for 0% -> 0% of each run, Pallas kernels for 4% -> 4%
where the time goes in v19:
time: 25 us; the launch traced here: 24.9 us
  starting transfers between devices  14.9 us (60%)
  waiting for transfers between devices  4.41 us (18%)
  Pallas kernels  3.4 us (14%)
  between operations  2.12 us (8%)
    ppermute x6, starting transfers between devices, swapped(): return lax.ppermute(shard, ('feat', 'tok'), pairs)  14.9 us
    ppermute x6, waiting for transfers between devices, swapped(): return lax.ppermute(shard, ('feat', 'tok'), pairs)  3.84 us
    pallas_call x1, Pallas kernels, final(): kernel_call(functools.partial(final_kernel, rows), (shape(*grad_rows.shap...  1.41 us
    pallas_call x1, Pallas kernels, front(): kernel_call(front_kernel, (shape(count, slots), shape(count, slots, dtype...  0.62 us
    ppermute x1, waiting for transfers between devices, local(): theirs = lax.ppermute(code_half, 'tok', [(i, 1 - i) for i in range(2)])  0.57 us
  transfers between devices with their start and end apart: 7, of which 4 were waited for; matrix products, arithmetic and copies ran while one was open for 0% of the time, Pallas kernels for 4%

profile of v19, /device:TPU:0, one launch (start us, length us, event | category | flops | bytes accessed | tf_op | source)
XLA Modules:
  0.0 24.9 jit_solution(14334394657114125042)
XLA Ops:
  0.6 0.0 copy-start
  0.6 0.0 copy-start.1
  0.7 0.0 copy-start.2
  0.7 0.0 copy-start.3
  0.7 0.0 copy-start.4
  0.7 0.1 shard_map.94.after_ref.order_ref
  2.1 0.0 copy-done
  2.1 0.0 copy-done.1
  2.1 0.0 copy-done.2
  2.1 0.0 copy-done.3
  2.1 0.0 copy-done.4
  2.2 0.6 %shard_map.95 = (bf16[16,128]{1,0:T(8,128)(2,1)S(1)}, f32[16,128]{1,0:T(8,128)S(1)}, f32[16,2560]{1,0:T(8,128)S(1)}, bf16[16,3072]{1,0:T(8,128)(2,1)S(1)}, f32[2,4096]{1,0:T(2,128)S(1)}, /*index=5*/f32[1,4096]{1,0:T(1,128)S(1)}) custom-call(bf16[2,4096]{1,0:T(2,128)(2,1)S(1)} %copy-done.1, bf16[4096]{0:T(1024)(128)(2,1)S(1)} %copy-done.2, ...), custom_call_target="tpu_custom_call" | custom-call | flops 1000000 | bytes 1048576 | tf_op jit(solution)/shard_map/pallas_call | solution.py:143
  2.8 4.1 %collective-permute-start.1 = (bf16[16,3072]{1,0:T(8,128)(2,1)S(1)}, bf16[16,3072]{1,0:T(8,128)(2,1)S(1)}, u32[]{:S(2)}, u32[]{:S(2)}) collective-permute-start(bf16[16,3072]{1,0:T(8,128)(2,1)S(1)} %get-tuple-element.32.own_ref), channel_id=1, source_target_pairs={{0,8},{1,5},{2,10},{3,7},{4,12},{5,1},{6,14},{7,3},{8,0},{9,13},{1... | collective-permute-start | bytes 294920 | tf_op jit(solution)/shard_map/ppermute | solution.py:59
  6.9 0.2 shard_map.96
  7.0 1.6 %collective-permute-start = (bf16[16,1536]{1,0:T(8,128)(2,1)S(1)}, bf16[16,1536]{1,0:T(8,128)(2,1)S(1)}, u32[]{:S(2)}, u32[]{:S(2)}) collective-permute-start(bf16[16,1536]{1,0:T(8,128)(2,1)S(1)} %get-tuple-element.30.after_ref.own_ref), channel_id=1, source_target_pairs={{0,2},{1,3},{2,0},{3,1},{4,6},{5,7},{6,4},{7,5},{8,10},{9,11},{10,... | collective-permute-start | bytes 147464 | tf_op jit(solution)/shard_map/ppermute | solution.py:59
  8.6 0.9 %collective-permute-done.1.arrived_ref = bf16[16,3072]{1,0:T(8,128)(2,1)S(1)} collective-permute-done((bf16[16,3072]{1,0:T(8,128)(2,1)S(1)}, bf16[16,3072]{1,0:T(8,128)(2,1)S(1)}, u32[]{:S(2)}, u32[]{:S(2)}) %collective-permute-start.1) | collective-permute-done | bytes 98336 | tf_op jit(solution)/shard_map/ppermute | solution.py:59
  9.5 1.9 %collective-permute-start.3 = (bf16[16,3584]{1,0:T(8,128)(2,1)S(1)}, bf16[16,3584]{1,0:T(8,128)(2,1)S(1)}, u32[]{:S(2)}, u32[]{:S(2)}) collective-permute-start(bf16[16,3584]{1,0:T(8,128)(2,1)S(1)} %get-tuple-element.33.after_ref.own_ref), channel_id=1, source_target_pairs={{0,2},{1,9},{2,0},{3,11},{4,6},{5,13},{6,4},{7,15},{8,10},{9,1},{1... | collective-permute-start | bytes 344072 | tf_op jit(solution)/shard_map/ppermute | solution.py:59
  11.4 0.0 collective-permute-done.arrived_ref
  11.5 1.8 %collective-permute-start.2 = (bf16[16,1536]{1,0:T(8,128)(2,1)S(1)}, bf16[16,1536]{1,0:T(8,128)(2,1)S(1)}, u32[]{:S(2)}, u32[]{:S(2)}) collective-permute-start(bf16[16,1536]{1,0:T(8,128)(2,1)S(1)} %get-tuple-element.35.after_ref.own_ref), channel_id=1, source_target_pairs={{0,4},{1,9},{2,6},{3,11},{4,0},{5,13},{6,2},{7,15},{8,12},{9,1},{1... | collective-permute-start | bytes 147464 | tf_op jit(solution)/shard_map/ppermute | solution.py:59
  13.2 1.2 %collective-permute-done.3.arrived_ref = bf16[16,3584]{1,0:T(8,128)(2,1)S(1)} collective-permute-done((bf16[16,3584]{1,0:T(8,128)(2,1)S(1)}, bf16[16,3584]{1,0:T(8,128)(2,1)S(1)}, u32[]{:S(2)}, u32[]{:S(2)}) %collective-permute-start.3) | collective-permute-done | bytes 114720 | tf_op jit(solution)/shard_map/ppermute | solution.py:59
  14.4 2.1 %collective-permute-start.5 = (bf16[16,4608]{1,0:T(8,128)(2,1)S(1)}, bf16[16,4608]{1,0:T(8,128)(2,1)S(1)}, u32[]{:S(2)}, u32[]{:S(2)}) collective-permute-start(bf16[16,4608]{1,0:T(8,128)(2,1)S(1)} %get-tuple-element.37.after_ref.own_ref), channel_id=1, source_target_pairs={{0,4},{1,3},{2,6},{3,1},{4,0},{5,7},{6,2},{7,5},{8,12},{9,11},{10,... | collective-permute-start | bytes 442376 | tf_op jit(solution)/shard_map/ppermute | solution.py:59
  16.5 0.0 collective-permute-done.2.arrived_ref
  16.5 3.4 %collective-permute-start.4 = (bf16[16,1536]{1,0:T(8,128)(2,1)S(1)}, bf16[16,1536]{1,0:T(8,128)(2,1)S(1)}, u32[]{:S(2)}, u32[]{:S(2)}) collective-permute-start(bf16[16,1536]{1,0:T(8,128)(2,1)S(1)} %get-tuple-element.39), channel_id=1, source_target_pairs={{0,8},{1,5},{2,10},{3,7},{4,12},{5,1},{6,14},{7,3},{8,0},{9,13},{1... | collective-permute-start | bytes 147464 | tf_op jit(solution)/shard_map/ppermute | solution.py:59
  20.0 0.0 collective-permute-done.5.arrived_ref
  20.0 0.3 %shard_map.101 = (bf16[16,2560]{1,0:T(8,128)(2,1)S(1)}, f32[16,128]{1,0:T(8,128)S(1)}) custom-call(f32[16,2560]{1,0:T(8,128)S(1)} %get-tuple-element.40.total_ref, bf16[16,4608]{1,0:T(8,128)(2,1)S(1)} %collective-permute-done.5.arrived_ref, bf16[128,4096]{1,0:T(8,128)(2,1)S(1)} %copy-done), custom_call_target="tpu_custom_call" | custom-call | flops 1000000 | bytes 1048576 | tf_op jit(solution)/shard_map/pallas_call | solution.py:273
  20.2 1.8 %collective-permute-done.4.arrived_ref = bf16[16,1536]{1,0:T(8,128)(2,1)S(1)} collective-permute-done((bf16[16,1536]{1,0:T(8,128)(2,1)S(1)}, bf16[16,1536]{1,0:T(8,128)(2,1)S(1)}, u32[]{:S(2)}, u32[]{:S(2)}) %collective-permute-start.4) | collective-permute-done | bytes 49184 | tf_op jit(solution)/shard_map/ppermute | solution.py:59
  22.1 0.2 shard_map.102
  22.2 0.0 collective-permute-start.6
  22.3 0.5 %shard_map.104.rows_ref = bf16[128,4096]{1,0:T(8,128)(2,1)S(1)} custom-call(bf16[16,128]{1,0:T(8,128)(2,1)S(1)} %get-tuple-element.27.code_ref, bf16[16,2560]{1,0:T(8,128)(2,1)S(1)} %get-tuple-element.44.first_ref, bf16[16,1536]{1,0:T(8,128)(2,1)S(1)} %get-tuple-element.45.second_ref), custom_call_target="tpu_custom_call" | custom-call | flops 1000000 | bytes 1048576 | tf_op jit(solution)/shard_map/pallas_call | solution.py:295
  22.8 0.1 shard_map.103.turned_ref
  22.9 0.6 %collective-permute-done.6.theirs_ref = f32[16,128]{1,0:T(8,128)S(1)} collective-permute-done((f32[16,128]{1,0:T(8,128)S(1)}, f32[16,128]{1,0:T(8,128)S(1)}, u32[]{:S(2)}, u32[]{:S(2)}) %collective-permute-start.6) | collective-permute-done | bytes 8224 | tf_op jit(solution)/shard_map/ppermute | solution.py:397
  23.5 1.4 %shard_map.105 = (bf16[128,4096]{1,0:T(8,128)(2,1)}, bf16[4096,128]{1,0:T(8,128)(2,1)}, f32[1,128]{1,0:T(1,128)}) custom-call(f32[16,128]{1,0:T(8,128)S(1)} %get-tuple-element.26.raw_ref, f32[16,128]{1,0:T(8,128)S(1)} %get-tuple-element.42.mine_ref, f32[16,128]{1,0:T(8,128)S(1)} %collective-permute-done.6.theirs_ref, ...), custom_call_target="tpu_custom_call" | custom-call | flops 1000000 | bytes 1048576 | tf_op jit(solution)/shard_map/pallas_call | solution.py:351
  (4 shorter events, 0.1 us)
Async XLA Ops:
  0.6 1.5 %copy-start = (bf16[128,4096]{1,0:T(8,128)(2,1)S(1)}, bf16[128,4096]{1,0:T(8,128)(2,1)}, u32[]{:S(2)}) copy-start(bf16[128,4096]{1,0:T(8,128)(2,1)} %rows_ref.7) | copy-start | bytes 3145732
  0.6 1.5 %copy-start.1 = (bf16[2,4096]{1,0:T(2,128)(2,1)S(1)}, bf16[2,4096]{1,0:T(2,128)(2,1)}, u32[]{:S(2)}) copy-start(bf16[2,4096]{1,0:T(2,128)(2,1)} %tokens_ref.1) | copy-start | bytes 49156
  0.7 1.5 %copy-start.2 = (bf16[4096]{0:T(1024)(128)(2,1)S(1)}, bf16[4096]{0:T(1024)(128)(2,1)}, u32[]{:S(2)}) copy-start(bf16[4096]{0:T(1024)(128)(2,1)} %bias_flat.1) | copy-start | bytes 24580
  0.7 1.5 %copy-start.3 = (f32[16,64]{1,0:T(8,128)S(1)}, f32[16,64]{1,0:T(8,128)}, u32[]{:S(2)}) copy-start(f32[16,64]{1,0:T(8,128)} %pre_ref.1) | copy-start | bytes 12292
  0.7 1.5 %copy-start.4 = (s32[16,64]{1,0:T(8,128)S(1)}, s32[16,64]{1,0:T(8,128)}, u32[]{:S(2)}) copy-start(s32[16,64]{1,0:T(8,128)} %top_ref.1) | copy-start | bytes 12292
  2.8 6.7 %collective-permute-start.1 = (bf16[16,3072]{1,0:T(8,128)(2,1)S(1)}, bf16[16,3072]{1,0:T(8,128)(2,1)S(1)}, u32[]{:S(2)}, u32[]{:S(2)}) collective-permute-start(bf16[16,3072]{1,0:T(8,128)(2,1)S(1)} %get-tuple-element.32.own_ref), channel_id=1, source_target_pairs={{0,8},{1,5},{2,10},{3,7},{4,12},{5,1},{6,14},{7,3},{8,0},{9,13},{1... | collective-permute-start | bytes 294920 | tf_op jit(solution)/shard_map/ppermute | solution.py:59
  7.0 4.4 %collective-permute-start = (bf16[16,1536]{1,0:T(8,128)(2,1)S(1)}, bf16[16,1536]{1,0:T(8,128)(2,1)S(1)}, u32[]{:S(2)}, u32[]{:S(2)}) collective-permute-start(bf16[16,1536]{1,0:T(8,128)(2,1)S(1)} %get-tuple-element.30.after_ref.own_ref), channel_id=1, source_target_pairs={{0,2},{1,3},{2,0},{3,1},{4,6},{5,7},{6,4},{7,5},{8,10},{9,11},{10,... | collective-permute-start | bytes 147464 | tf_op jit(solution)/shard_map/ppermute | solution.py:59
  9.5 4.9 %collective-permute-start.3 = (bf16[16,3584]{1,0:T(8,128)(2,1)S(1)}, bf16[16,3584]{1,0:T(8,128)(2,1)S(1)}, u32[]{:S(2)}, u32[]{:S(2)}) collective-permute-start(bf16[16,3584]{1,0:T(8,128)(2,1)S(1)} %get-tuple-element.33.after_ref.own_ref), channel_id=1, source_target_pairs={{0,2},{1,9},{2,0},{3,11},{4,6},{5,13},{6,4},{7,15},{8,10},{9,1},{1... | collective-permute-start | bytes 344072 | tf_op jit(solution)/shard_map/ppermute | solution.py:59
  11.5 5.1 %collective-permute-start.2 = (bf16[16,1536]{1,0:T(8,128)(2,1)S(1)}, bf16[16,1536]{1,0:T(8,128)(2,1)S(1)}, u32[]{:S(2)}, u32[]{:S(2)}) collective-permute-start(bf16[16,1536]{1,0:T(8,128)(2,1)S(1)} %get-tuple-element.35.after_ref.own_ref), channel_id=1, source_target_pairs={{0,4},{1,9},{2,6},{3,11},{4,0},{5,13},{6,2},{7,15},{8,12},{9,1},{1... | collective-permute-start | bytes 147464 | tf_op jit(solution)/shard_map/ppermute | solution.py:59
  14.4 5.6 %collective-permute-start.5 = (bf16[16,4608]{1,0:T(8,128)(2,1)S(1)}, bf16[16,4608]{1,0:T(8,128)(2,1)S(1)}, u32[]{:S(2)}, u32[]{:S(2)}) collective-permute-start(bf16[16,4608]{1,0:T(8,128)(2,1)S(1)} %get-tuple-element.37.after_ref.own_ref), channel_id=1, source_target_pairs={{0,4},{1,3},{2,6},{3,1},{4,0},{5,7},{6,2},{7,5},{8,12},{9,11},{10,... | collective-permute-start | bytes 442376 | tf_op jit(solution)/shard_map/ppermute | solution.py:59
  16.5 5.5 %collective-permute-start.4 = (bf16[16,1536]{1,0:T(8,128)(2,1)S(1)}, bf16[16,1536]{1,0:T(8,128)(2,1)S(1)}, u32[]{:S(2)}, u32[]{:S(2)}) collective-permute-start(bf16[16,1536]{1,0:T(8,128)(2,1)S(1)} %get-tuple-element.39), channel_id=1, source_target_pairs={{0,8},{1,5},{2,10},{3,7},{4,12},{5,1},{6,14},{7,3},{8,0},{9,13},{1... | collective-permute-start | bytes 147464 | tf_op jit(solution)/shard_map/ppermute | solution.py:59
  22.2 1.2 %collective-permute-start.6 = (f32[16,128]{1,0:T(8,128)S(1)}, f32[16,128]{1,0:T(8,128)S(1)}, u32[]{:S(2)}, u32[]{:S(2)}) collective-permute-start(f32[16,128]{1,0:T(8,128)S(1)} %get-tuple-element.42.mine_ref), channel_id=1, source_target_pairs={{0,1},{1,0},{2,3},{3,2},{4,5},{5,4},{6,7},{7,6},{8,9},{9,8},{10,11... | collective-permute-start | bytes 24584 | tf_op jit(solution)/shard_map/ppermute | solution.py:397

commit v20 on v17

--- a/solution.py
+++ b/solution.py
@@ -75,8 +75,8 @@
 
 
 def order_kernel(rows, order_ref):
-    place = lax.broadcasted_iota(jnp.int32, order_ref.shape, 0)
-    token = lax.broadcasted_iota(jnp.int32, order_ref.shape, 1)
+    target = lax.broadcasted_iota(jnp.int32, order_ref.shape, 0)
+    place = lax.broadcasted_iota(jnp.int32, order_ref.shape, 1)
     core = lax.axis_index("tok")
     block = place // ROWS
     distance = jnp.zeros_like(place)
@@ -85,14 +85,17 @@
             jnp.where(core == c, bit_of(step, c), 0) for c in range(lax.axis_size("tok"))
         )
         distance |= (block >> step & 1) << bit
-    source = (lax.axis_index("feat") ^ distance) * rows + place % rows
-    order_ref[...] = jnp.where(token == source, 1.0, 0.0).astype(jnp.bfloat16)
+    token = (lax.axis_index("feat") ^ distance) * rows + place % rows
+    piece = place % ROWS // rows
+    count = rows * lax.axis_size("feat")
+    order_ref[...] = jnp.where(target == piece * count + token, 1.0, 0.0).astype(jnp.bfloat16)
 
 
 def order_of(rows, count):
+    depth = ROWS * lax.axis_size("feat")
     return kernel_call(
         functools.partial(order_kernel, rows),
-        shape(ROWS * lax.axis_size("feat"), count),
+        shape(depth, depth),
         [],
         VMEM,
         count,
@@ -215,7 +218,7 @@
     )(first, second, after)
 
 
-def turned_kernel(skip, rows, own_ref, arrived_ref, bias_ref, out_ref):
+def turned_kernel(skip, rows, own_ref, arrived_ref, bias_ref, order_ref, out_ref):
     bias = jnp.concatenate([bias_ref[...]] * rows, axis=0)
     bias = stacked(bias, ROWS // rows)
     width = bias.shape[1]
@@ -224,18 +227,21 @@
         for ref in (own_ref, arrived_ref)
         for at in range(skip, ref.shape[1], width)
     ]
-    out_ref[...] = jnp.concatenate(blocks, axis=0).astype(jnp.float32).T.astype(jnp.bfloat16)
-
-
-def turned(own, arrived, skip, bias, rows, count):
+    ordered = jnp.dot(
+        order_ref[...], jnp.concatenate(blocks, axis=0), preferred_element_type=jnp.float32
+    )
+    out_ref[...] = ordered.T.astype(jnp.bfloat16)
+
+
+def turned(own, arrived, skip, bias, order, rows, count):
     width = bias.shape[1] * rows // ROWS
     return kernel_call(
         functools.partial(turned_kernel, skip, rows),
         shape(width, 2 * (own.shape[1] - skip) // width * ROWS),
-        [VMEM] * 3,
+        [VMEM] * 4,
         VMEM,
         count,
-    )(own, arrived, bias)
+    )(own, arrived, bias, order)
 
 
 def scaled_of(total_ref, arrived_ref):
@@ -303,7 +309,6 @@
     mine_ref,
     theirs_ref,
     turned_ref,
-    order_ref,
     rows_ref,
     rows_hbm,
     enc_hbm,
@@ -315,17 +320,19 @@
     copies = [pltpu.make_async_copy(rows_ref, rows_hbm, sems.at[0])]
     copies[0].start()
     count, slots = raw_ref.shape
-    width, depth = turned_ref.shape
+    width = turned_ref.shape[0]
     pieces = ROWS // rows
     code_grad = mine_ref[...] + theirs_ref[...]
     pre_grad = jnp.where(raw_ref[...] > 0.0, code_grad, 0.0).astype(jnp.bfloat16)
     benc_ref[...] = jnp.sum(pre_grad.astype(jnp.float32), axis=0, keepdims=True)
     copies.append(pltpu.make_async_copy(benc_ref, benc_hbm, sems.at[1]))
     copies[1].start()
-    spread = jnp.dot(order_ref[...], pre_grad, preferred_element_type=jnp.float32)
-    piece = lax.broadcasted_iota(jnp.int32, (depth, slots), 0) % ROWS // rows
+    zeros = jnp.zeros_like(pre_grad)
     for c in range(0, pieces, 2):
-        pair = [jnp.where(piece == c + i, spread, 0.0).astype(jnp.bfloat16) for i in range(2)]
+        pair = [
+            jnp.concatenate([zeros] * at + [pre_grad] + [zeros] * (pieces - 1 - at), axis=0)
+            for at in (c, c + 1)
+        ]
         out = jnp.dot(
             turned_ref[...],
             jnp.concatenate(pair, axis=1),
@@ -340,14 +347,14 @@
         copy.wait()
 
 
-def final(raw, mine, theirs, turned_tokens, order, grad_rows, rows):
+def final(raw, mine, theirs, turned_tokens, grad_rows, rows):
     count, slots = raw.shape
     pieces = ROWS // rows
     width = turned_tokens.shape[0] * pieces
     return kernel_call(
         functools.partial(final_kernel, rows),
         (shape(*grad_rows.shape), shape(width, slots), shape(1, slots, dtype=jnp.float32)),
-        [VMEM] * 6,
+        [VMEM] * 5,
         (HBM, HBM, HBM),
         count,
         [
@@ -355,7 +362,7 @@
             pltpu.VMEM((1, slots), jnp.float32),
             pltpu.SemaphoreType.DMA((pieces // 2 + 2,)),
         ],
-    )(raw, mine, theirs, turned_tokens, order, grad_rows)
+    )(raw, mine, theirs, turned_tokens, grad_rows)
 
 
 def local(tokens, b_pre, pre_codes, top_idx, blocks, counts, dict_rows):
@@ -386,14 +393,14 @@
         own_block, arrived_block, skip = sent, arrived, total.shape[1]
 
     scaled, product_first = products(total, arrived, dict_rows)
-    turned_tokens = turned(own_block, arrived_block, skip, bias, rows, count)
+    turned_tokens = turned(own_block, arrived_block, skip, bias, order, rows, count)
     scaled_second, code_half = products(
         total_second, arrived_second, dict_rows, product_first
     )
     theirs = lax.ppermute(code_half, "tok", [(i, 1 - i) for i in range(2)])
     grad_rows = grad_rows_of(code, scaled, scaled_second)
     grad_rows, grad_enc, grad_benc = final(
-        raw, code_half, theirs, turned_tokens, order, grad_rows, rows
+        raw, code_half, theirs, turned_tokens, grad_rows, rows
     )
     return (grad_rows, grad_enc, grad_benc.reshape(-1))
 

time: 24.2 us -> 24.1 us (level)
  no operation moved by 1% of the time
where the time goes in v20:
time: 24.1 us; the launch traced here: 23.9 us
  starting transfers between devices  12.6 us (52%)
  waiting for transfers between devices  5.77 us (24%)
  Pallas kernels  3.46 us (14%)
  between operations  2.13 us (9%)
    ppermute x6, starting transfers between devices, swapped(): return lax.ppermute(shard, ('feat', 'tok'), pairs)  12.5 us
    ppermute x6, waiting for transfers between devices, swapped(): return lax.ppermute(shard, ('feat', 'tok'), pairs)  5.34 us
    pallas_call x1, Pallas kernels, final(): kernel_call(functools.partial(final_kernel, rows), (shape(*grad_rows.shap...  1.36 us
    pallas_call x1, Pallas kernels, front(): kernel_call(front_kernel, (shape(count, slots), shape(count, slots, dtype...  0.61 us
  transfers between devices with their start and end apart: 7, of which 5 were waited for; matrix products, arithmetic and copies ran while one was open for 0% of the time, Pallas kernels for 5%

profile of v20, /device:TPU:0, one launch (start us, length us, event | category | flops | bytes accessed | tf_op | source)
XLA Modules:
  0.0 23.9 jit_solution(6518994654663503565)
XLA Ops:
  0.6 0.0 copy-start
  0.6 0.0 copy-start.1
  0.7 0.0 copy-start.2
  0.7 0.0 copy-start.3
  0.7 0.0 copy-start.4
  2.1 0.0 copy-done
  2.1 0.0 copy-done.1
  2.1 0.0 copy-done.2
  2.1 0.0 copy-done.3
  2.1 0.0 copy-done.4
  2.1 0.6 %shard_map.95 = (bf16[16,128]{1,0:T(8,128)(2,1)S(1)}, f32[16,128]{1,0:T(8,128)S(1)}, f32[16,2048]{1,0:T(8,128)S(1)}, bf16[16,2560]{1,0:T(8,128)(2,1)S(1)}, f32[2,4096]{1,0:T(2,128)S(1)}, /*index=5*/f32[1,4096]{1,0:T(1,128)S(1)}) custom-call(bf16[2,4096]{1,0:T(2,128)(2,1)S(1)} %copy-done.1, bf16[4096]{0:T(1024)(128)(2,1)S(1)} %copy-done.2, ...), custom_call_target="tpu_custom_call" | custom-call | flops 1000000 | bytes 1048576 | tf_op jit(solution)/shard_map/pallas_call | solution.py:142
  2.7 4.1 %collective-permute-start.1 = (bf16[16,2560]{1,0:T(8,128)(2,1)S(1)}, bf16[16,2560]{1,0:T(8,128)(2,1)S(1)}, u32[]{:S(2)}, u32[]{:S(2)}) collective-permute-start(bf16[16,2560]{1,0:T(8,128)(2,1)S(1)} %get-tuple-element.32.own_ref), channel_id=1, source_target_pairs={{0,8},{1,3},{2,10},{3,1},{4,12},{5,7},{6,14},{7,5},{8,0},{9,11},{1... | collective-permute-start | bytes 245768 | tf_op jit(solution)/shard_map/ppermute | solution.py:55
  6.8 0.2 shard_map.96
  7.0 0.1 collective-permute-start
  7.1 2.2 %collective-permute-done.1.arrived_ref = bf16[16,2560]{1,0:T(8,128)(2,1)S(1)} collective-permute-done((bf16[16,2560]{1,0:T(8,128)(2,1)S(1)}, bf16[16,2560]{1,0:T(8,128)(2,1)S(1)}, u32[]{:S(2)}, u32[]{:S(2)}) %collective-permute-start.1) | collective-permute-done | bytes 81952 | tf_op jit(solution)/shard_map/ppermute | solution.py:55
  9.3 1.9 %collective-permute-start.3 = (bf16[16,3072]{1,0:T(8,128)(2,1)S(1)}, bf16[16,3072]{1,0:T(8,128)(2,1)S(1)}, u32[]{:S(2)}, u32[]{:S(2)}) collective-permute-start(bf16[16,3072]{1,0:T(8,128)(2,1)S(1)} %get-tuple-element.33.after_ref.own_ref), channel_id=1, source_target_pairs={{0,2},{1,5},{2,0},{3,7},{4,6},{5,1},{6,4},{7,3},{8,10},{9,13},{10,... | collective-permute-start | bytes 294920 | tf_op jit(solution)/shard_map/ppermute | solution.py:55
  11.2 1.1 %collective-permute-done.arrived_ref = bf16[16,2048]{1,0:T(8,128)(2,1)S(1)} collective-permute-done((bf16[16,2048]{1,0:T(8,128)(2,1)S(1)}, bf16[16,2048]{1,0:T(8,128)(2,1)S(1)}, u32[]{:S(2)}, u32[]{:S(2)}) %collective-permute-start) | collective-permute-done | bytes 65568 | tf_op jit(solution)/shard_map/ppermute | solution.py:55
  12.3 1.6 %collective-permute-start.2 = (bf16[16,2048]{1,0:T(8,128)(2,1)S(1)}, bf16[16,2048]{1,0:T(8,128)(2,1)S(1)}, u32[]{:S(2)}, u32[]{:S(2)}) collective-permute-start(bf16[16,2048]{1,0:T(8,128)(2,1)S(1)} %get-tuple-element.35.after_ref.own_ref), channel_id=1, source_target_pairs={{0,2},{1,5},{2,0},{3,7},{4,6},{5,1},{6,4},{7,3},{8,10},{9,13},{10,... | collective-permute-start | bytes 196616 | tf_op jit(solution)/shard_map/ppermute | solution.py:55
  13.9 0.0 collective-permute-done.3.arrived_ref
  14.0 2.7 %collective-permute-start.5 = (bf16[16,4096]{1,0:T(8,128)(2,1)S(1)}, bf16[16,4096]{1,0:T(8,128)(2,1)S(1)}, u32[]{:S(2)}, u32[]{:S(2)}) collective-permute-start(bf16[16,4096]{1,0:T(8,128)(2,1)S(1)} %get-tuple-element.37.after_ref.own_ref), channel_id=1, source_target_pairs={{0,4},{1,9},{2,6},{3,11},{4,0},{5,13},{6,2},{7,15},{8,12},{9,1},{1... | collective-permute-start | bytes 393224 | tf_op jit(solution)/shard_map/ppermute | solution.py:55
  16.7 0.0 collective-permute-done.2.arrived_ref
  16.7 2.2 %collective-permute-start.4 = (bf16[16,2048]{1,0:T(8,128)(2,1)S(1)}, bf16[16,2048]{1,0:T(8,128)(2,1)S(1)}, u32[]{:S(2)}, u32[]{:S(2)}) collective-permute-start(bf16[16,2048]{1,0:T(8,128)(2,1)S(1)} %get-tuple-element.39), channel_id=1, source_target_pairs={{0,4},{1,9},{2,6},{3,11},{4,0},{5,13},{6,2},{7,15},{8,12},{9,1},{1... | collective-permute-start | bytes 196616 | tf_op jit(solution)/shard_map/ppermute | solution.py:55
  18.9 1.4 %collective-permute-done.5.arrived_ref = bf16[16,4096]{1,0:T(8,128)(2,1)S(1)} collective-permute-done((bf16[16,4096]{1,0:T(8,128)(2,1)S(1)}, bf16[16,4096]{1,0:T(8,128)(2,1)S(1)}, u32[]{:S(2)}, u32[]{:S(2)}) %collective-permute-start.5) | collective-permute-done | bytes 131104 | tf_op jit(solution)/shard_map/ppermute | solution.py:55
  20.3 0.2 %shard_map.101 = (bf16[16,2048]{1,0:T(8,128)(2,1)S(1)}, f32[16,128]{1,0:T(8,128)S(1)}) custom-call(f32[16,2048]{1,0:T(8,128)S(1)} %get-tuple-element.40.total_ref, bf16[16,4096]{1,0:T(8,128)(2,1)S(1)} %collective-permute-done.5.arrived_ref, bf16[128,4096]{1,0:T(8,128)(2,1)S(1)} %copy-done), custom_call_target="tpu_custom_call" | custom-call | flops 1000000 | bytes 1048576 | tf_op jit(solution)/shard_map/pallas_call | solution.py:275
  20.5 0.6 %collective-permute-done.4.arrived_ref = bf16[16,2048]{1,0:T(8,128)(2,1)S(1)} collective-permute-done((bf16[16,2048]{1,0:T(8,128)(2,1)S(1)}, bf16[16,2048]{1,0:T(8,128)(2,1)S(1)}, u32[]{:S(2)}, u32[]{:S(2)}) %collective-permute-start.4) | collective-permute-done | bytes 65568 | tf_op jit(solution)/shard_map/ppermute | solution.py:55
  21.1 0.2 shard_map.102
  21.4 0.0 collective-permute-start.6
  21.4 0.5 %shard_map.104.rows_ref = bf16[128,4096]{1,0:T(8,128)(2,1)S(1)} custom-call(bf16[16,128]{1,0:T(8,128)(2,1)S(1)} %get-tuple-element.27.code_ref, bf16[16,2048]{1,0:T(8,128)(2,1)S(1)} %get-tuple-element.44.first_ref, bf16[16,2048]{1,0:T(8,128)(2,1)S(1)} %get-tuple-element.45.second_ref), custom_call_target="tpu_custom_call" | custom-call | flops 1000000 | bytes 1048576 | tf_op jit(solution)/shard_map/pallas_call | solution.py:297
  21.9 0.3 %shard_map.103.turned_ref = bf16[512,128]{1,0:T(8,128)(2,1)S(1)} custom-call(bf16[16,4096]{1,0:T(8,128)(2,1)S(1)} %get-tuple-element.37.after_ref.own_ref, bf16[16,4096]{1,0:T(8,128)(2,1)S(1)} %collective-permute-done.5.arrived_ref, f32[1,4096]{1,0:T(1,128)S(1)} %get-tuple-element.43.bias_ref, bf16[128,128]{1,0:T(8,128)(2,1)S(1)} %shard_map.94.after_ref.order_ref), custom_call_target="tpu_custom_call" | custom-call | flops 1000000 | bytes 1048576 | tf_op jit(solution)/shard_map/pallas_call | solution.py:238
  22.1 0.4 %collective-permute-done.6.theirs_ref = f32[16,128]{1,0:T(8,128)S(1)} collective-permute-done((f32[16,128]{1,0:T(8,128)S(1)}, f32[16,128]{1,0:T(8,128)S(1)}, u32[]{:S(2)}, u32[]{:S(2)}) %collective-permute-start.6) | collective-permute-done | bytes 8224 | tf_op jit(solution)/shard_map/ppermute | solution.py:400
  22.6 1.4 %shard_map.105 = (bf16[128,4096]{1,0:T(8,128)(2,1)}, bf16[4096,128]{1,0:T(8,128)(2,1)}, f32[1,128]{1,0:T(1,128)}) custom-call(f32[16,128]{1,0:T(8,128)S(1)} %get-tuple-element.26.raw_ref, f32[16,128]{1,0:T(8,128)S(1)} %get-tuple-element.42.mine_ref, f32[16,128]{1,0:T(8,128)S(1)} %collective-permute-done.6.theirs_ref, ...), custom_call_target="tpu_custom_call" | custom-call | flops 1000000 | bytes 1048576 | tf_op jit(solution)/shard_map/pallas_call | solution.py:354
  (5 shorter events, 0.1 us)
Async XLA Ops:
  0.6 1.5 %copy-start = (bf16[128,4096]{1,0:T(8,128)(2,1)S(1)}, bf16[128,4096]{1,0:T(8,128)(2,1)}, u32[]{:S(2)}) copy-start(bf16[128,4096]{1,0:T(8,128)(2,1)} %rows_ref.7) | copy-start | bytes 3145732
  0.6 1.5 %copy-start.1 = (bf16[2,4096]{1,0:T(2,128)(2,1)S(1)}, bf16[2,4096]{1,0:T(2,128)(2,1)}, u32[]{:S(2)}) copy-start(bf16[2,4096]{1,0:T(2,128)(2,1)} %tokens_ref.1) | copy-start | bytes 49156
  0.7 1.5 %copy-start.2 = (bf16[4096]{0:T(1024)(128)(2,1)S(1)}, bf16[4096]{0:T(1024)(128)(2,1)}, u32[]{:S(2)}) copy-start(bf16[4096]{0:T(1024)(128)(2,1)} %bias_flat.1) | copy-start | bytes 24580
  0.7 1.5 %copy-start.3 = (f32[16,64]{1,0:T(8,128)S(1)}, f32[16,64]{1,0:T(8,128)}, u32[]{:S(2)}) copy-start(f32[16,64]{1,0:T(8,128)} %pre_ref.1) | copy-start | bytes 12292
  0.7 1.5 %copy-start.4 = (s32[16,64]{1,0:T(8,128)S(1)}, s32[16,64]{1,0:T(8,128)}, u32[]{:S(2)}) copy-start(s32[16,64]{1,0:T(8,128)} %top_ref.1) | copy-start | bytes 12292
  2.7 6.5 %collective-permute-start.1 = (bf16[16,2560]{1,0:T(8,128)(2,1)S(1)}, bf16[16,2560]{1,0:T(8,128)(2,1)S(1)}, u32[]{:S(2)}, u32[]{:S(2)}) collective-permute-start(bf16[16,2560]{1,0:T(8,128)(2,1)S(1)} %get-tuple-element.32.own_ref), channel_id=1, source_target_pairs={{0,8},{1,3},{2,10},{3,1},{4,12},{5,7},{6,14},{7,5},{8,0},{9,11},{1... | collective-permute-start | bytes 245768 | tf_op jit(solution)/shard_map/ppermute | solution.py:55
  7.0 5.3 %collective-permute-start = (bf16[16,2048]{1,0:T(8,128)(2,1)S(1)}, bf16[16,2048]{1,0:T(8,128)(2,1)S(1)}, u32[]{:S(2)}, u32[]{:S(2)}) collective-permute-start(bf16[16,2048]{1,0:T(8,128)(2,1)S(1)} %get-tuple-element.30.after_ref.own_ref), channel_id=1, source_target_pairs={{0,8},{1,3},{2,10},{3,1},{4,12},{5,7},{6,14},{7,5},{8,0},{9,11},{1... | collective-permute-start | bytes 196616 | tf_op jit(solution)/shard_map/ppermute | solution.py:55
  9.3 4.7 %collective-permute-start.3 = (bf16[16,3072]{1,0:T(8,128)(2,1)S(1)}, bf16[16,3072]{1,0:T(8,128)(2,1)S(1)}, u32[]{:S(2)}, u32[]{:S(2)}) collective-permute-start(bf16[16,3072]{1,0:T(8,128)(2,1)S(1)} %get-tuple-element.33.after_ref.own_ref), channel_id=1, source_target_pairs={{0,2},{1,5},{2,0},{3,7},{4,6},{5,1},{6,4},{7,3},{8,10},{9,13},{10,... | collective-permute-start | bytes 294920 | tf_op jit(solution)/shard_map/ppermute | solution.py:55
  12.3 4.3 %collective-permute-start.2 = (bf16[16,2048]{1,0:T(8,128)(2,1)S(1)}, bf16[16,2048]{1,0:T(8,128)(2,1)S(1)}, u32[]{:S(2)}, u32[]{:S(2)}) collective-permute-start(bf16[16,2048]{1,0:T(8,128)(2,1)S(1)} %get-tuple-element.35.after_ref.own_ref), channel_id=1, source_target_pairs={{0,2},{1,5},{2,0},{3,7},{4,6},{5,1},{6,4},{7,3},{8,10},{9,13},{10,... | collective-permute-start | bytes 196616 | tf_op jit(solution)/shard_map/ppermute | solution.py:55
  14.0 6.3 %collective-permute-start.5 = (bf16[16,4096]{1,0:T(8,128)(2,1)S(1)}, bf16[16,4096]{1,0:T(8,128)(2,1)S(1)}, u32[]{:S(2)}, u32[]{:S(2)}) collective-permute-start(bf16[16,4096]{1,0:T(8,128)(2,1)S(1)} %get-tuple-element.37.after_ref.own_ref), channel_id=1, source_target_pairs={{0,4},{1,9},{2,6},{3,11},{4,0},{5,13},{6,2},{7,15},{8,12},{9,1},{1... | collective-permute-start | bytes 393224 | tf_op jit(solution)/shard_map/ppermute | solution.py:55
  16.7 4.4 %collective-permute-start.4 = (bf16[16,2048]{1,0:T(8,128)(2,1)S(1)}, bf16[16,2048]{1,0:T(8,128)(2,1)S(1)}, u32[]{:S(2)}, u32[]{:S(2)}) collective-permute-start(bf16[16,2048]{1,0:T(8,128)(2,1)S(1)} %get-tuple-element.39), channel_id=1, source_target_pairs={{0,4},{1,9},{2,6},{3,11},{4,0},{5,13},{6,2},{7,15},{8,12},{9,1},{1... | collective-permute-start | bytes 196616 | tf_op jit(solution)/shard_map/ppermute | solution.py:55
  21.4 1.2 %collective-permute-start.6 = (f32[16,128]{1,0:T(8,128)S(1)}, f32[16,128]{1,0:T(8,128)S(1)}, u32[]{:S(2)}, u32[]{:S(2)}) collective-permute-start(f32[16,128]{1,0:T(8,128)S(1)} %get-tuple-element.42.mine_ref), channel_id=1, source_target_pairs={{0,1},{1,0},{2,3},{3,2},{4,5},{5,4},{6,7},{7,6},{8,9},{9,8},{10,11... | collective-permute-start | bytes 24584 | tf_op jit(solution)/shard_map/ppermute | solution.py:400

commit v21 on v20

--- a/solution.py
+++ b/solution.py
@@ -264,7 +264,9 @@
     half_ref[...] = product(scaled, rows_ref, 0)
 
 
-def second_product_kernel(total_ref, arrived_ref, rows_ref, first_ref, scaled_ref, half_ref):
+def second_product_kernel(
+    total_ref, arrived_ref, rows_ref, first_ref, after_ref, scaled_ref, half_ref
+):
     scaled = scaled_of(total_ref, arrived_ref)
     scaled_ref[...] = scaled
     half_ref[...] = first_ref[...] + product(scaled, rows_ref, rows_ref.shape[1] - scaled.shape[1])
@@ -275,7 +277,7 @@
     return kernel_call(
         second_product_kernel if first else first_product_kernel,
         (shape(count, width), shape(count, dict_rows.shape[0], dtype=jnp.float32)),
-        [VMEM] * (3 + len(first)),
+        [VMEM] * 3 + ([VMEM, ANY] if first else []),
         (VMEM, VMEM),
         count,
     )(total, arrived, dict_rows, *first)
@@ -286,20 +288,31 @@
     return jnp.dot(code, scaled, preferred_element_type=jnp.float32).astype(jnp.bfloat16)
 
 
-def grad_rows_kernel(code_ref, first_ref, second_ref, out_ref):
-    chunk = first_ref.shape[1]
-    out_ref[:, :chunk] = outer(code_ref, first_ref[...])
-    out_ref[:, chunk:] = outer(code_ref, second_ref[...])
+def grad_rows_kernel(code_ref, first_ref, second_ref, out_hbm, out_ref, sems):
+    at = 0
+    copies = []
+    for i, ref in enumerate((first_ref, second_ref)):
+        part = pl.ds(at, ref.shape[1])
+        out_ref[:, part] = outer(code_ref, ref[...])
+        copies.append(
+            pltpu.make_async_copy(out_ref.at[:, part], out_hbm.at[:, part], sems.at[i])
+        )
+        copies[-1].start()
+        at += ref.shape[1]
+    for copy in copies:
+        copy.wait()
 
 
 def grad_rows_of(code, first, second):
     count, slots = code.shape
+    width = first.shape[1] + second.shape[1]
     return kernel_call(
         grad_rows_kernel,
-        shape(slots, first.shape[1] + second.shape[1]),
+        shape(slots, width),
         [VMEM] * 3,
-        VMEM,
-        count,
+        HBM,
+        count,
+        [pltpu.VMEM((slots, width), jnp.bfloat16), pltpu.SemaphoreType.DMA((2,))],
     )(code, first, second)
 
 
@@ -309,60 +322,60 @@
     mine_ref,
     theirs_ref,
     turned_ref,
-    rows_ref,
-    rows_hbm,
     enc_hbm,
     benc_hbm,
     enc_ref,
     benc_ref,
     sems,
 ):
-    copies = [pltpu.make_async_copy(rows_ref, rows_hbm, sems.at[0])]
-    copies[0].start()
     count, slots = raw_ref.shape
     width = turned_ref.shape[0]
     pieces = ROWS // rows
     code_grad = mine_ref[...] + theirs_ref[...]
     pre_grad = jnp.where(raw_ref[...] > 0.0, code_grad, 0.0).astype(jnp.bfloat16)
     benc_ref[...] = jnp.sum(pre_grad.astype(jnp.float32), axis=0, keepdims=True)
-    copies.append(pltpu.make_async_copy(benc_ref, benc_hbm, sems.at[1]))
-    copies[1].start()
+    copies = [pltpu.make_async_copy(benc_ref, benc_hbm, sems.at[0])]
+    copies[0].start()
     zeros = jnp.zeros_like(pre_grad)
-    for c in range(0, pieces, 2):
-        pair = [
+    group = pieces // 2
+    for c in range(0, pieces, group):
+        placed = [
             jnp.concatenate([zeros] * at + [pre_grad] + [zeros] * (pieces - 1 - at), axis=0)
-            for at in (c, c + 1)
+            for at in range(c, c + group)
         ]
         out = jnp.dot(
             turned_ref[...],
-            jnp.concatenate(pair, axis=1),
+            jnp.concatenate(placed, axis=1),
             preferred_element_type=jnp.float32,
         ).astype(jnp.bfloat16)
-        for i in range(2):
+        for i in range(group):
             enc_ref[(c + i) * width : (c + i + 1) * width, :] = out[:, i * slots : (i + 1) * slots]
-        part = pl.ds(c * width, 2 * width)
-        copies.append(pltpu.make_async_copy(enc_ref.at[part], enc_hbm.at[part], sems.at[c // 2 + 2]))
-        copies[-1].start()
+        for i in range(0, group, 2):
+            part = pl.ds((c + i) * width, 2 * width)
+            copies.append(
+                pltpu.make_async_copy(enc_ref.at[part], enc_hbm.at[part], sems.at[(c + i) // 2 + 1])
+            )
+            copies[-1].start()
     for copy in copies:
         copy.wait()
 
 
-def final(raw, mine, theirs, turned_tokens, grad_rows, rows):
+def final(raw, mine, theirs, turned_tokens, rows):
     count, slots = raw.shape
     pieces = ROWS // rows
     width = turned_tokens.shape[0] * pieces
     return kernel_call(
         functools.partial(final_kernel, rows),
-        (shape(*grad_rows.shape), shape(width, slots), shape(1, slots, dtype=jnp.float32)),
-        [VMEM] * 5,
-        (HBM, HBM, HBM),
+        (shape(width, slots), shape(1, slots, dtype=jnp.float32)),
+        [VMEM] * 4,
+        (HBM, HBM),
         count,
         [
             pltpu.VMEM((width, slots), jnp.bfloat16),
             pltpu.VMEM((1, slots), jnp.float32),
-            pltpu.SemaphoreType.DMA((pieces // 2 + 2,)),
+            pltpu.SemaphoreType.DMA((pieces // 2 + 1,)),
         ],
-    )(raw, mine, theirs, turned_tokens, grad_rows)
+    )(raw, mine, theirs, turned_tokens)
 
 
 def local(tokens, b_pre, pre_codes, top_idx, blocks, counts, dict_rows):
@@ -395,13 +408,11 @@
     scaled, product_first = products(total, arrived, dict_rows)
     turned_tokens = turned(own_block, arrived_block, skip, bias, order, rows, count)
     scaled_second, code_half = products(
-        total_second, arrived_second, dict_rows, product_first
+        total_second, arrived_second, dict_rows, product_first, turned_tokens
     )
     theirs = lax.ppermute(code_half, "tok", [(i, 1 - i) for i in range(2)])
     grad_rows = grad_rows_of(code, scaled, scaled_second)
-    grad_rows, grad_enc, grad_benc = final(
-        raw, code_half, theirs, turned_tokens, grad_rows, rows
-    )
+    grad_enc, grad_benc = final(raw, code_half, theirs, turned_tokens, rows)
     return (grad_rows, grad_enc, grad_benc.reshape(-1))
 
 

time: 24.1 us -> 24.2 us (level)
  Pallas kernels: 3.46 us -> 4.24 us
  waiting for transfers between devices: 5.77 us -> 5.06 us
    pallas_call x2, Pallas kernels: 1.83 us -> 2.6 us  [the longest x1 1.32 us: grad_rows_of(): kernel_call(grad_rows_kernel, shape(slots, width), [VMEM] * 3, HBM, count...]
    ppermute x1, waiting for transfers between devices: 0.43 us -> 0.01 us  [local(): theirs = lax.ppermute(code_half, 'tok', [(i, 1 - i) for i in range(2)])]
    ppermute x6, waiting for transfers between devices: 5.34 us -> 5.06 us  [swapped(): return lax.ppermute(shard, ('feat', 'tok'), pairs)]
  transfers between devices with their start and end apart: 7 -> 7, of which waited for: 5 -> 4; matrix products, arithmetic and copies ran while one was open for 0% -> 0% of each run, Pallas kernels for 5% -> 9%
where the time goes in v21:
time: 24.2 us; the launch traced here: 24 us
  starting transfers between devices  12.6 us (52%)
  waiting for transfers between devices  5.06 us (21%)
  Pallas kernels  4.24 us (18%)
  between operations  2.14 us (9%)
    ppermute x6, starting transfers between devices, swapped(): return lax.ppermute(shard, ('feat', 'tok'), pairs)  12.5 us
    ppermute x6, waiting for transfers between devices, swapped(): return lax.ppermute(shard, ('feat', 'tok'), pairs)  5.06 us
    pallas_call x1, Pallas kernels, grad_rows_of(): kernel_call(grad_rows_kernel, shape(slots, width), [VMEM] * 3, HBM, count...  1.32 us
    pallas_call x1, Pallas kernels, final(): kernel_call(functools.partial(final_kernel, rows), (shape(width, slots),...  1.28 us
    pallas_call x1, Pallas kernels, front(): kernel_call(front_kernel, (shape(count, slots), shape(count, slots, dtype...  0.61 us
  transfers between devices with their start and end apart: 7, of which 4 were waited for; matrix products, arithmetic and copies ran while one was open for 0% of the time, Pallas kernels for 9%

profile of v21, /device:TPU:0, one launch (start us, length us, event | category | flops | bytes accessed | tf_op | source)
XLA Modules:
  0.0 24.0 jit_solution(6735054949538178382)
XLA Ops:
  0.6 0.0 copy-start
  0.6 0.0 copy-start.1
  0.7 0.0 copy-start.2
  0.7 0.0 copy-start.3
  0.7 0.0 copy-start.4
  2.1 0.0 copy-done
  2.1 0.0 copy-done.1
  2.1 0.0 copy-done.2
  2.1 0.0 copy-done.3
  2.1 0.0 copy-done.4
  2.1 0.6 %shard_map.95 = (bf16[16,128]{1,0:T(8,128)(2,1)S(1)}, f32[16,128]{1,0:T(8,128)S(1)}, f32[16,2048]{1,0:T(8,128)S(1)}, bf16[16,2560]{1,0:T(8,128)(2,1)S(1)}, f32[2,4096]{1,0:T(2,128)S(1)}, /*index=5*/f32[1,4096]{1,0:T(1,128)S(1)}) custom-call(bf16[2,4096]{1,0:T(2,128)(2,1)S(1)} %copy-done.1, bf16[4096]{0:T(1024)(128)(2,1)S(1)} %copy-done.2, ...), custom_call_target="tpu_custom_call" | custom-call | flops 1000000 | bytes 1048576 | tf_op jit(solution)/shard_map/pallas_call | solution.py:142
  2.7 4.1 %collective-permute-start = (bf16[16,2560]{1,0:T(8,128)(2,1)S(1)}, bf16[16,2560]{1,0:T(8,128)(2,1)S(1)}, u32[]{:S(2)}, u32[]{:S(2)}) collective-permute-start(bf16[16,2560]{1,0:T(8,128)(2,1)S(1)} %get-tuple-element.27.own_ref), channel_id=1, source_target_pairs={{0,8},{1,3},{2,10},{3,1},{4,12},{5,7},{6,14},{7,5},{8,0},{9,11},{1... | collective-permute-start | bytes 245768 | tf_op jit(solution)/shard_map/ppermute | solution.py:55
  6.8 0.2 shard_map.96
  7.0 0.1 collective-permute-start.2
  7.1 2.2 %collective-permute-done.arrived_ref = bf16[16,2560]{1,0:T(8,128)(2,1)S(1)} collective-permute-done((bf16[16,2560]{1,0:T(8,128)(2,1)S(1)}, bf16[16,2560]{1,0:T(8,128)(2,1)S(1)}, u32[]{:S(2)}, u32[]{:S(2)}) %collective-permute-start) | collective-permute-done | bytes 81952 | tf_op jit(solution)/shard_map/ppermute | solution.py:55
  9.3 1.9 %collective-permute-start.1 = (bf16[16,3072]{1,0:T(8,128)(2,1)S(1)}, bf16[16,3072]{1,0:T(8,128)(2,1)S(1)}, u32[]{:S(2)}, u32[]{:S(2)}) collective-permute-start(bf16[16,3072]{1,0:T(8,128)(2,1)S(1)} %get-tuple-element.31.after_ref.own_ref), channel_id=1, source_target_pairs={{0,2},{1,5},{2,0},{3,7},{4,6},{5,1},{6,4},{7,3},{8,10},{9,13},{10,... | collective-permute-start | bytes 294920 | tf_op jit(solution)/shard_map/ppermute | solution.py:55
  11.2 1.1 %collective-permute-done.2.arrived_ref = bf16[16,2048]{1,0:T(8,128)(2,1)S(1)} collective-permute-done((bf16[16,2048]{1,0:T(8,128)(2,1)S(1)}, bf16[16,2048]{1,0:T(8,128)(2,1)S(1)}, u32[]{:S(2)}, u32[]{:S(2)}) %collective-permute-start.2) | collective-permute-done | bytes 65568 | tf_op jit(solution)/shard_map/ppermute | solution.py:55
  12.3 1.6 %collective-permute-start.4 = (bf16[16,2048]{1,0:T(8,128)(2,1)S(1)}, bf16[16,2048]{1,0:T(8,128)(2,1)S(1)}, u32[]{:S(2)}, u32[]{:S(2)}) collective-permute-start(bf16[16,2048]{1,0:T(8,128)(2,1)S(1)} %get-tuple-element.33.after_ref.own_ref), channel_id=1, source_target_pairs={{0,2},{1,5},{2,0},{3,7},{4,6},{5,1},{6,4},{7,3},{8,10},{9,13},{10,... | collective-permute-start | bytes 196616 | tf_op jit(solution)/shard_map/ppermute | solution.py:55
  13.9 0.0 collective-permute-done.1.arrived_ref
  14.0 2.7 %collective-permute-start.3 = (bf16[16,4096]{1,0:T(8,128)(2,1)S(1)}, bf16[16,4096]{1,0:T(8,128)(2,1)S(1)}, u32[]{:S(2)}, u32[]{:S(2)}) collective-permute-start(bf16[16,4096]{1,0:T(8,128)(2,1)S(1)} %get-tuple-element.35.after_ref.own_ref), channel_id=1, source_target_pairs={{0,4},{1,9},{2,6},{3,11},{4,0},{5,13},{6,2},{7,15},{8,12},{9,1},{1... | collective-permute-start | bytes 393224 | tf_op jit(solution)/shard_map/ppermute | solution.py:55
  16.7 0.0 collective-permute-done.4.arrived_ref
  16.7 2.2 %collective-permute-start.5 = (bf16[16,2048]{1,0:T(8,128)(2,1)S(1)}, bf16[16,2048]{1,0:T(8,128)(2,1)S(1)}, u32[]{:S(2)}, u32[]{:S(2)}) collective-permute-start(bf16[16,2048]{1,0:T(8,128)(2,1)S(1)} %get-tuple-element.39), channel_id=1, source_target_pairs={{0,4},{1,9},{2,6},{3,11},{4,0},{5,13},{6,2},{7,15},{8,12},{9,1},{1... | collective-permute-start | bytes 196616 | tf_op jit(solution)/shard_map/ppermute | solution.py:55
  18.9 1.4 %collective-permute-done.3.arrived_ref = bf16[16,4096]{1,0:T(8,128)(2,1)S(1)} collective-permute-done((bf16[16,4096]{1,0:T(8,128)(2,1)S(1)}, bf16[16,4096]{1,0:T(8,128)(2,1)S(1)}, u32[]{:S(2)}, u32[]{:S(2)}) %collective-permute-start.3) | collective-permute-done | bytes 131104 | tf_op jit(solution)/shard_map/ppermute | solution.py:55
  20.3 0.2 shard_map.100
  20.5 0.3 %shard_map.102.after_ref.turned_ref = bf16[512,128]{1,0:T(8,128)(2,1)S(1)} custom-call(bf16[16,4096]{1,0:T(8,128)(2,1)S(1)} %get-tuple-element.35.after_ref.own_ref, bf16[16,4096]{1,0:T(8,128)(2,1)S(1)} %collective-permute-done.3.arrived_ref, f32[1,4096]{1,0:T(1,128)S(1)} %get-tuple-element.41.bias_ref, bf16[128,128]{1,0:T(8,128)(2,1)S(1)} %shard_map.94.after_ref.order_ref), custom_call_target="tpu_custom_call" | custom-call | flops 1000000 | bytes 1048576 | tf_op jit(solution)/shard_map/pallas_call | solution.py:238
  20.8 0.3 %collective-permute-done.5.arrived_ref = bf16[16,2048]{1,0:T(8,128)(2,1)S(1)} collective-permute-done((bf16[16,2048]{1,0:T(8,128)(2,1)S(1)}, bf16[16,2048]{1,0:T(8,128)(2,1)S(1)}, u32[]{:S(2)}, u32[]{:S(2)}) %collective-permute-start.5) | collective-permute-done | bytes 65568 | tf_op jit(solution)/shard_map/ppermute | solution.py:55
  21.1 0.2 shard_map.103
  21.4 0.0 collective-permute-start.6
  21.4 1.3 %shard_map.104 = bf16[128,4096]{1,0:T(8,128)(2,1)} custom-call(bf16[16,128]{1,0:T(8,128)(2,1)S(1)} %get-tuple-element.25.code_ref, bf16[16,2048]{1,0:T(8,128)(2,1)S(1)} %get-tuple-element.36.first_ref, bf16[16,2048]{1,0:T(8,128)(2,1)S(1)} %get-tuple-element.42.second_ref), custom_call_target="tpu_custom_call" | custom-call | flops 1000000 | bytes 1048576 | tf_op jit(solution)/shard_map/pallas_call | solution.py:309
  22.7 0.0 collective-permute-done.6.theirs_ref
  22.7 1.3 %shard_map.105 = (bf16[4096,128]{1,0:T(8,128)(2,1)}, f32[1,128]{1,0:T(1,128)}) custom-call(f32[16,128]{1,0:T(8,128)S(1)} %get-tuple-element.43.raw_ref, f32[16,128]{1,0:T(8,128)S(1)} %get-tuple-element.44.mine_ref, f32[16,128]{1,0:T(8,128)S(1)} %collective-permute-done.6.theirs_ref, bf16[512,128]{1,0:T(8,128)(2,1)S(1)} %shard_map.102.after_ref.turned_ref), custom_call_target="tpu_custom_call" | custom-call | flops 1000000 | bytes 1048576 | tf_op jit(solution)/shard_map/pallas_call | solution.py:367
  (5 shorter events, 0.1 us)
Async XLA Ops:
  0.6 1.5 %copy-start = (bf16[128,4096]{1,0:T(8,128)(2,1)S(1)}, bf16[128,4096]{1,0:T(8,128)(2,1)}, u32[]{:S(2)}) copy-start(bf16[128,4096]{1,0:T(8,128)(2,1)} %rows_ref.7) | copy-start | bytes 3145732
  0.6 1.5 %copy-start.1 = (bf16[2,4096]{1,0:T(2,128)(2,1)S(1)}, bf16[2,4096]{1,0:T(2,128)(2,1)}, u32[]{:S(2)}) copy-start(bf16[2,4096]{1,0:T(2,128)(2,1)} %tokens_ref.1) | copy-start | bytes 49156
  0.7 1.5 %copy-start.2 = (bf16[4096]{0:T(1024)(128)(2,1)S(1)}, bf16[4096]{0:T(1024)(128)(2,1)}, u32[]{:S(2)}) copy-start(bf16[4096]{0:T(1024)(128)(2,1)} %bias_flat.1) | copy-start | bytes 24580
  0.7 1.5 %copy-start.3 = (f32[16,64]{1,0:T(8,128)S(1)}, f32[16,64]{1,0:T(8,128)}, u32[]{:S(2)}) copy-start(f32[16,64]{1,0:T(8,128)} %pre_ref.1) | copy-start | bytes 12292
  0.7 1.5 %copy-start.4 = (s32[16,64]{1,0:T(8,128)S(1)}, s32[16,64]{1,0:T(8,128)}, u32[]{:S(2)}) copy-start(s32[16,64]{1,0:T(8,128)} %top_ref.1) | copy-start | bytes 12292
  2.7 6.5 %collective-permute-start = (bf16[16,2560]{1,0:T(8,128)(2,1)S(1)}, bf16[16,2560]{1,0:T(8,128)(2,1)S(1)}, u32[]{:S(2)}, u32[]{:S(2)}) collective-permute-start(bf16[16,2560]{1,0:T(8,128)(2,1)S(1)} %get-tuple-element.27.own_ref), channel_id=1, source_target_pairs={{0,8},{1,3},{2,10},{3,1},{4,12},{5,7},{6,14},{7,5},{8,0},{9,11},{1... | collective-permute-start | bytes 245768 | tf_op jit(solution)/shard_map/ppermute | solution.py:55
  7.0 5.3 %collective-permute-start.2 = (bf16[16,2048]{1,0:T(8,128)(2,1)S(1)}, bf16[16,2048]{1,0:T(8,128)(2,1)S(1)}, u32[]{:S(2)}, u32[]{:S(2)}) collective-permute-start(bf16[16,2048]{1,0:T(8,128)(2,1)S(1)} %get-tuple-element.29.after_ref.own_ref), channel_id=1, source_target_pairs={{0,8},{1,3},{2,10},{3,1},{4,12},{5,7},{6,14},{7,5},{8,0},{9,11},{1... | collective-permute-start | bytes 196616 | tf_op jit(solution)/shard_map/ppermute | solution.py:55
  9.3 4.7 %collective-permute-start.1 = (bf16[16,3072]{1,0:T(8,128)(2,1)S(1)}, bf16[16,3072]{1,0:T(8,128)(2,1)S(1)}, u32[]{:S(2)}, u32[]{:S(2)}) collective-permute-start(bf16[16,3072]{1,0:T(8,128)(2,1)S(1)} %get-tuple-element.31.after_ref.own_ref), channel_id=1, source_target_pairs={{0,2},{1,5},{2,0},{3,7},{4,6},{5,1},{6,4},{7,3},{8,10},{9,13},{10,... | collective-permute-start | bytes 294920 | tf_op jit(solution)/shard_map/ppermute | solution.py:55
  12.3 4.3 %collective-permute-start.4 = (bf16[16,2048]{1,0:T(8,128)(2,1)S(1)}, bf16[16,2048]{1,0:T(8,128)(2,1)S(1)}, u32[]{:S(2)}, u32[]{:S(2)}) collective-permute-start(bf16[16,2048]{1,0:T(8,128)(2,1)S(1)} %get-tuple-element.33.after_ref.own_ref), channel_id=1, source_target_pairs={{0,2},{1,5},{2,0},{3,7},{4,6},{5,1},{6,4},{7,3},{8,10},{9,13},{10,... | collective-permute-start | bytes 196616 | tf_op jit(solution)/shard_map/ppermute | solution.py:55
  14.0 6.3 %collective-permute-start.3 = (bf16[16,4096]{1,0:T(8,128)(2,1)S(1)}, bf16[16,4096]{1,0:T(8,128)(2,1)S(1)}, u32[]{:S(2)}, u32[]{:S(2)}) collective-permute-start(bf16[16,4096]{1,0:T(8,128)(2,1)S(1)} %get-tuple-element.35.after_ref.own_ref), channel_id=1, source_target_pairs={{0,4},{1,9},{2,6},{3,11},{4,0},{5,13},{6,2},{7,15},{8,12},{9,1},{1... | collective-permute-start | bytes 393224 | tf_op jit(solution)/shard_map/ppermute | solution.py:55
  16.7 4.4 %collective-permute-start.5 = (bf16[16,2048]{1,0:T(8,128)(2,1)S(1)}, bf16[16,2048]{1,0:T(8,128)(2,1)S(1)}, u32[]{:S(2)}, u32[]{:S(2)}) collective-permute-start(bf16[16,2048]{1,0:T(8,128)(2,1)S(1)} %get-tuple-element.39), channel_id=1, source_target_pairs={{0,4},{1,9},{2,6},{3,11},{4,0},{5,13},{6,2},{7,15},{8,12},{9,1},{1... | collective-permute-start | bytes 196616 | tf_op jit(solution)/shard_map/ppermute | solution.py:55
  21.4 1.4 %collective-permute-start.6 = (f32[16,128]{1,0:T(8,128)S(1)}, f32[16,128]{1,0:T(8,128)S(1)}, u32[]{:S(2)}, u32[]{:S(2)}) collective-permute-start(f32[16,128]{1,0:T(8,128)S(1)} %get-tuple-element.44.mine_ref), channel_id=1, source_target_pairs={{0,1},{1,0},{2,3},{3,2},{4,5},{5,4},{6,7},{7,6},{8,9},{9,8},{10,11... | collective-permute-start | bytes 24584 | tf_op jit(solution)/shard_map/ppermute | solution.py:413

commit v22 on v20

--- a/solution.py
+++ b/solution.py
@@ -42,7 +42,7 @@
 
 def bit_of(step, core):
     bits = list(range(feat_bits()))
-    return (bits[-1:] + bits[:-1] if core == 0 else bits)[step]
+    return (bits[-1:] + bits[:-1] if core == 0 else bits[:1] + bits[:0:-1])[step]
 
 
 def swapped(shard, step):
@@ -264,7 +264,9 @@
     half_ref[...] = product(scaled, rows_ref, 0)
 
 
-def second_product_kernel(total_ref, arrived_ref, rows_ref, first_ref, scaled_ref, half_ref):
+def second_product_kernel(
+    total_ref, arrived_ref, rows_ref, first_ref, after_ref, scaled_ref, half_ref
+):
     scaled = scaled_of(total_ref, arrived_ref)
     scaled_ref[...] = scaled
     half_ref[...] = first_ref[...] + product(scaled, rows_ref, rows_ref.shape[1] - scaled.shape[1])
@@ -275,7 +277,7 @@
     return kernel_call(
         second_product_kernel if first else first_product_kernel,
         (shape(count, width), shape(count, dict_rows.shape[0], dtype=jnp.float32)),
-        [VMEM] * (3 + len(first)),
+        [VMEM] * 3 + ([VMEM, ANY] if first else []),
         (VMEM, VMEM),
         count,
     )(total, arrived, dict_rows, *first)
@@ -328,21 +330,25 @@
     copies.append(pltpu.make_async_copy(benc_ref, benc_hbm, sems.at[1]))
     copies[1].start()
     zeros = jnp.zeros_like(pre_grad)
-    for c in range(0, pieces, 2):
-        pair = [
+    group = pieces // 2
+    for c in range(0, pieces, group):
+        placed = [
             jnp.concatenate([zeros] * at + [pre_grad] + [zeros] * (pieces - 1 - at), axis=0)
-            for at in (c, c + 1)
+            for at in range(c, c + group)
         ]
         out = jnp.dot(
             turned_ref[...],
-            jnp.concatenate(pair, axis=1),
+            jnp.concatenate(placed, axis=1),
             preferred_element_type=jnp.float32,
         ).astype(jnp.bfloat16)
-        for i in range(2):
+        for i in range(group):
             enc_ref[(c + i) * width : (c + i + 1) * width, :] = out[:, i * slots : (i + 1) * slots]
-        part = pl.ds(c * width, 2 * width)
-        copies.append(pltpu.make_async_copy(enc_ref.at[part], enc_hbm.at[part], sems.at[c // 2 + 2]))
-        copies[-1].start()
+        for i in range(0, group, 2):
+            part = pl.ds((c + i) * width, 2 * width)
+            copies.append(
+                pltpu.make_async_copy(enc_ref.at[part], enc_hbm.at[part], sems.at[(c + i) // 2 + 2])
+            )
+            copies[-1].start()
     for copy in copies:
         copy.wait()
 
@@ -395,7 +401,7 @@
     scaled, product_first = products(total, arrived, dict_rows)
     turned_tokens = turned(own_block, arrived_block, skip, bias, order, rows, count)
     scaled_second, code_half = products(
-        total_second, arrived_second, dict_rows, product_first
+        total_second, arrived_second, dict_rows, product_first, turned_tokens
     )
     theirs = lax.ppermute(code_half, "tok", [(i, 1 - i) for i in range(2)])
     grad_rows = grad_rows_of(code, scaled, scaled_second)

time: 24.1 us -> 27 us (1.12)
  waiting for transfers between devices: 5.77 us -> 13.4 us
  starting transfers between devices: 12.6 us -> 7.81 us
    ppermute x6, waiting for transfers between devices: 5.34 us -> 12.7 us  [swapped(): return lax.ppermute(shard, ('feat', 'tok'), pairs)]
    ppermute x6, starting transfers between devices: 12.5 us -> 7.78 us  [swapped(): return lax.ppermute(shard, ('feat', 'tok'), pairs)]
  transfers between devices with their start and end apart: 7 -> 7, of which waited for: 5 -> 6; matrix products, arithmetic and copies ran while one was open for 0% -> 0% of each run, Pallas kernels for 5% -> 5%
where the time goes in v22:
time: 27 us; the launch traced here: 26.9 us
  waiting for transfers between devices  13.4 us (50%)
  starting transfers between devices  7.81 us (29%)
  Pallas kernels  3.47 us (13%)
  between operations  2.14 us (8%)
    ppermute x6, waiting for transfers between devices, swapped(): return lax.ppermute(shard, ('feat', 'tok'), pairs)  12.7 us
    ppermute x6, starting transfers between devices, swapped(): return lax.ppermute(shard, ('feat', 'tok'), pairs)  7.78 us
    pallas_call x1, Pallas kernels, final(): kernel_call(functools.partial(final_kernel, rows), (shape(*grad_rows.shap...  1.36 us
    ppermute x1, waiting for transfers between devices, local(): theirs = lax.ppermute(code_half, 'tok', [(i, 1 - i) for i in range(2)])  0.69 us
    pallas_call x1, Pallas kernels, front(): kernel_call(front_kernel, (shape(count, slots), shape(count, slots, dtype...  0.61 us
  transfers between devices with their start and end apart: 7, of which 6 were waited for; matrix products, arithmetic and copies ran while one was open for 0% of the time, Pallas kernels for 5%

profile of v22, /device:TPU:0, one launch (start us, length us, event | category | flops | bytes accessed | tf_op | source)
XLA Modules:
  0.0 26.9 jit_solution(11562115163625628798)
XLA Ops:
  0.6 0.0 copy-start
  0.6 0.0 copy-start.1
  0.7 0.0 copy-start.2
  0.7 0.0 copy-start.3
  0.7 0.0 copy-start.4
  2.1 0.0 copy-done
  2.1 0.0 copy-done.1
  2.1 0.0 copy-done.2
  2.1 0.0 copy-done.3
  2.1 0.0 copy-done.4
  2.1 0.6 %shard_map.95 = (bf16[16,128]{1,0:T(8,128)(2,1)S(1)}, f32[16,128]{1,0:T(8,128)S(1)}, f32[16,2048]{1,0:T(8,128)S(1)}, bf16[16,2560]{1,0:T(8,128)(2,1)S(1)}, f32[2,4096]{1,0:T(2,128)S(1)}, /*index=5*/f32[1,4096]{1,0:T(1,128)S(1)}) custom-call(bf16[2,4096]{1,0:T(2,128)(2,1)S(1)} %copy-done.1, bf16[4096]{0:T(1024)(128)(2,1)S(1)} %copy-done.2, ...), custom_call_target="tpu_custom_call" | custom-call | flops 1000000 | bytes 1048576 | tf_op jit(solution)/shard_map/pallas_call | solution.py:142
  2.7 4.1 %collective-permute-start.1 = (bf16[16,2560]{1,0:T(8,128)(2,1)S(1)}, bf16[16,2560]{1,0:T(8,128)(2,1)S(1)}, u32[]{:S(2)}, u32[]{:S(2)}) collective-permute-start(bf16[16,2560]{1,0:T(8,128)(2,1)S(1)} %get-tuple-element.32.own_ref), channel_id=1, source_target_pairs={{0,8},{1,3},{2,10},{3,1},{4,12},{5,7},{6,14},{7,5},{8,0},{9,11},{1... | collective-permute-start | bytes 245768 | tf_op jit(solution)/shard_map/ppermute | solution.py:55
  6.8 0.2 shard_map.96
  7.0 0.1 collective-permute-start
  7.1 2.2 %collective-permute-done.1.arrived_ref = bf16[16,2560]{1,0:T(8,128)(2,1)S(1)} collective-permute-done((bf16[16,2560]{1,0:T(8,128)(2,1)S(1)}, bf16[16,2560]{1,0:T(8,128)(2,1)S(1)}, u32[]{:S(2)}, u32[]{:S(2)}) %collective-permute-start.1) | collective-permute-done | bytes 81952 | tf_op jit(solution)/shard_map/ppermute | solution.py:55
  9.3 1.9 %collective-permute-start.3 = (bf16[16,3072]{1,0:T(8,128)(2,1)S(1)}, bf16[16,3072]{1,0:T(8,128)(2,1)S(1)}, u32[]{:S(2)}, u32[]{:S(2)}) collective-permute-start(bf16[16,3072]{1,0:T(8,128)(2,1)S(1)} %get-tuple-element.33.after_ref.own_ref), channel_id=1, source_target_pairs={{0,2},{1,9},{2,0},{3,11},{4,6},{5,13},{6,4},{7,15},{8,10},{9,1},{1... | collective-permute-start | bytes 294920 | tf_op jit(solution)/shard_map/ppermute | solution.py:55
  11.2 4.2 %collective-permute-done.arrived_ref = bf16[16,2048]{1,0:T(8,128)(2,1)S(1)} collective-permute-done((bf16[16,2048]{1,0:T(8,128)(2,1)S(1)}, bf16[16,2048]{1,0:T(8,128)(2,1)S(1)}, u32[]{:S(2)}, u32[]{:S(2)}) %collective-permute-start) | collective-permute-done | bytes 65568 | tf_op jit(solution)/shard_map/ppermute | solution.py:55
  15.4 1.6 %collective-permute-start.2 = (bf16[16,2048]{1,0:T(8,128)(2,1)S(1)}, bf16[16,2048]{1,0:T(8,128)(2,1)S(1)}, u32[]{:S(2)}, u32[]{:S(2)}) collective-permute-start(bf16[16,2048]{1,0:T(8,128)(2,1)S(1)} %get-tuple-element.35.after_ref.own_ref), channel_id=1, source_target_pairs={{0,2},{1,9},{2,0},{3,11},{4,6},{5,13},{6,4},{7,15},{8,10},{9,1},{1... | collective-permute-start | bytes 196616 | tf_op jit(solution)/shard_map/ppermute | solution.py:55
  17.0 0.0 collective-permute-done.3.arrived_ref
  17.0 0.1 collective-permute-start.5
  17.1 2.6 %collective-permute-done.2.arrived_ref = bf16[16,2048]{1,0:T(8,128)(2,1)S(1)} collective-permute-done((bf16[16,2048]{1,0:T(8,128)(2,1)S(1)}, bf16[16,2048]{1,0:T(8,128)(2,1)S(1)}, u32[]{:S(2)}, u32[]{:S(2)}) %collective-permute-start.2) | collective-permute-done | bytes 65568 | tf_op jit(solution)/shard_map/ppermute | solution.py:55
  19.7 0.1 collective-permute-start.4
  19.8 2.2 %collective-permute-done.5.arrived_ref = bf16[16,4096]{1,0:T(8,128)(2,1)S(1)} collective-permute-done((bf16[16,4096]{1,0:T(8,128)(2,1)S(1)}, bf16[16,4096]{1,0:T(8,128)(2,1)S(1)}, u32[]{:S(2)}, u32[]{:S(2)}) %collective-permute-start.5) | collective-permute-done | bytes 131104 | tf_op jit(solution)/shard_map/ppermute | solution.py:55
  22.0 0.2 shard_map.101
  22.3 0.3 %shard_map.102.after_ref.turned_ref = bf16[512,128]{1,0:T(8,128)(2,1)S(1)} custom-call(bf16[16,4096]{1,0:T(8,128)(2,1)S(1)} %get-tuple-element.37.after_ref.own_ref, bf16[16,4096]{1,0:T(8,128)(2,1)S(1)} %collective-permute-done.5.arrived_ref, f32[1,4096]{1,0:T(1,128)S(1)} %get-tuple-element.42.bias_ref, bf16[128,128]{1,0:T(8,128)(2,1)S(1)} %shard_map.94.after_ref.order_ref), custom_call_target="tpu_custom_call" | custom-call | flops 1000000 | bytes 1048576 | tf_op jit(solution)/shard_map/pallas_call | solution.py:238
  22.5 1.5 %collective-permute-done.4.arrived_ref = bf16[16,2048]{1,0:T(8,128)(2,1)S(1)} collective-permute-done((bf16[16,2048]{1,0:T(8,128)(2,1)S(1)}, bf16[16,2048]{1,0:T(8,128)(2,1)S(1)}, u32[]{:S(2)}, u32[]{:S(2)}) %collective-permute-start.4) | collective-permute-done | bytes 65568 | tf_op jit(solution)/shard_map/ppermute | solution.py:55
  24.1 0.2 shard_map.103
  24.3 0.0 collective-permute-start.6
  24.3 0.5 %shard_map.104.rows_ref = bf16[128,4096]{1,0:T(8,128)(2,1)S(1)} custom-call(bf16[16,128]{1,0:T(8,128)(2,1)S(1)} %get-tuple-element.27.code_ref, bf16[16,2048]{1,0:T(8,128)(2,1)S(1)} %get-tuple-element.44.first_ref, bf16[16,2048]{1,0:T(8,128)(2,1)S(1)} %get-tuple-element.45.second_ref), custom_call_target="tpu_custom_call" | custom-call | flops 1000000 | bytes 1048576 | tf_op jit(solution)/shard_map/pallas_call | solution.py:299
  24.8 0.7 %collective-permute-done.6.theirs_ref = f32[16,128]{1,0:T(8,128)S(1)} collective-permute-done((f32[16,128]{1,0:T(8,128)S(1)}, f32[16,128]{1,0:T(8,128)S(1)}, u32[]{:S(2)}, u32[]{:S(2)}) %collective-permute-start.6) | collective-permute-done | bytes 8224 | tf_op jit(solution)/shard_map/ppermute | solution.py:406
  25.5 1.4 %shard_map.105 = (bf16[128,4096]{1,0:T(8,128)(2,1)}, bf16[4096,128]{1,0:T(8,128)(2,1)}, f32[1,128]{1,0:T(1,128)}) custom-call(f32[16,128]{1,0:T(8,128)S(1)} %get-tuple-element.26.raw_ref, f32[16,128]{1,0:T(8,128)S(1)} %get-tuple-element.43.mine_ref, f32[16,128]{1,0:T(8,128)S(1)} %collective-permute-done.6.theirs_ref, ...), custom_call_target="tpu_custom_call" | custom-call | flops 1000000 | bytes 1048576 | tf_op jit(solution)/shard_map/pallas_call | solution.py:360
  (5 shorter events, 0.1 us)
Async XLA Ops:
  0.6 1.5 %copy-start = (bf16[128,4096]{1,0:T(8,128)(2,1)S(1)}, bf16[128,4096]{1,0:T(8,128)(2,1)}, u32[]{:S(2)}) copy-start(bf16[128,4096]{1,0:T(8,128)(2,1)} %rows_ref.7) | copy-start | bytes 3145732
  0.6 1.5 %copy-start.1 = (bf16[2,4096]{1,0:T(2,128)(2,1)S(1)}, bf16[2,4096]{1,0:T(2,128)(2,1)}, u32[]{:S(2)}) copy-start(bf16[2,4096]{1,0:T(2,128)(2,1)} %tokens_ref.1) | copy-start | bytes 49156
  0.7 1.5 %copy-start.2 = (bf16[4096]{0:T(1024)(128)(2,1)S(1)}, bf16[4096]{0:T(1024)(128)(2,1)}, u32[]{:S(2)}) copy-start(bf16[4096]{0:T(1024)(128)(2,1)} %bias_flat.1) | copy-start | bytes 24580
  0.7 1.5 %copy-start.3 = (f32[16,64]{1,0:T(8,128)S(1)}, f32[16,64]{1,0:T(8,128)}, u32[]{:S(2)}) copy-start(f32[16,64]{1,0:T(8,128)} %pre_ref.1) | copy-start | bytes 12292
  0.7 1.5 %copy-start.4 = (s32[16,64]{1,0:T(8,128)S(1)}, s32[16,64]{1,0:T(8,128)}, u32[]{:S(2)}) copy-start(s32[16,64]{1,0:T(8,128)} %top_ref.1) | copy-start | bytes 12292
  2.7 6.5 %collective-permute-start.1 = (bf16[16,2560]{1,0:T(8,128)(2,1)S(1)}, bf16[16,2560]{1,0:T(8,128)(2,1)S(1)}, u32[]{:S(2)}, u32[]{:S(2)}) collective-permute-start(bf16[16,2560]{1,0:T(8,128)(2,1)S(1)} %get-tuple-element.32.own_ref), channel_id=1, source_target_pairs={{0,8},{1,3},{2,10},{3,1},{4,12},{5,7},{6,14},{7,5},{8,0},{9,11},{1... | collective-permute-start | bytes 245768 | tf_op jit(solution)/shard_map/ppermute | solution.py:55
  7.0 8.3 %collective-permute-start = (bf16[16,2048]{1,0:T(8,128)(2,1)S(1)}, bf16[16,2048]{1,0:T(8,128)(2,1)S(1)}, u32[]{:S(2)}, u32[]{:S(2)}) collective-permute-start(bf16[16,2048]{1,0:T(8,128)(2,1)S(1)} %get-tuple-element.30.after_ref.own_ref), channel_id=1, source_target_pairs={{0,8},{1,3},{2,10},{3,1},{4,12},{5,7},{6,14},{7,5},{8,0},{9,11},{1... | collective-permute-start | bytes 196616 | tf_op jit(solution)/shard_map/ppermute | solution.py:55
  9.3 7.7 %collective-permute-start.3 = (bf16[16,3072]{1,0:T(8,128)(2,1)S(1)}, bf16[16,3072]{1,0:T(8,128)(2,1)S(1)}, u32[]{:S(2)}, u32[]{:S(2)}) collective-permute-start(bf16[16,3072]{1,0:T(8,128)(2,1)S(1)} %get-tuple-element.33.after_ref.own_ref), channel_id=1, source_target_pairs={{0,2},{1,9},{2,0},{3,11},{4,6},{5,13},{6,4},{7,15},{8,10},{9,1},{1... | collective-permute-start | bytes 294920 | tf_op jit(solution)/shard_map/ppermute | solution.py:55
  15.4 4.3 %collective-permute-start.2 = (bf16[16,2048]{1,0:T(8,128)(2,1)S(1)}, bf16[16,2048]{1,0:T(8,128)(2,1)S(1)}, u32[]{:S(2)}, u32[]{:S(2)}) collective-permute-start(bf16[16,2048]{1,0:T(8,128)(2,1)S(1)} %get-tuple-element.35.after_ref.own_ref), channel_id=1, source_target_pairs={{0,2},{1,9},{2,0},{3,11},{4,6},{5,13},{6,4},{7,15},{8,10},{9,1},{1... | collective-permute-start | bytes 196616 | tf_op jit(solution)/shard_map/ppermute | solution.py:55
  17.0 5.0 %collective-permute-start.5 = (bf16[16,4096]{1,0:T(8,128)(2,1)S(1)}, bf16[16,4096]{1,0:T(8,128)(2,1)S(1)}, u32[]{:S(2)}, u32[]{:S(2)}) collective-permute-start(bf16[16,4096]{1,0:T(8,128)(2,1)S(1)} %get-tuple-element.37.after_ref.own_ref), channel_id=1, source_target_pairs={{0,4},{1,5},{2,6},{3,7},{4,0},{5,1},{6,2},{7,3},{8,12},{9,13},{10,... | collective-permute-start | bytes 393224 | tf_op jit(solution)/shard_map/ppermute | solution.py:55
  19.7 4.3 %collective-permute-start.4 = (bf16[16,2048]{1,0:T(8,128)(2,1)S(1)}, bf16[16,2048]{1,0:T(8,128)(2,1)S(1)}, u32[]{:S(2)}, u32[]{:S(2)}) collective-permute-start(bf16[16,2048]{1,0:T(8,128)(2,1)S(1)} %get-tuple-element.39), channel_id=1, source_target_pairs={{0,4},{1,5},{2,6},{3,7},{4,0},{5,1},{6,2},{7,3},{8,12},{9,13},{10,... | collective-permute-start | bytes 196616 | tf_op jit(solution)/shard_map/ppermute | solution.py:55
  24.3 1.2 %collective-permute-start.6 = (f32[16,128]{1,0:T(8,128)S(1)}, f32[16,128]{1,0:T(8,128)S(1)}, u32[]{:S(2)}, u32[]{:S(2)}) collective-permute-start(f32[16,128]{1,0:T(8,128)S(1)} %get-tuple-element.43.mine_ref), channel_id=1, source_target_pairs={{0,1},{1,0},{2,3},{3,2},{4,5},{5,4},{6,7},{7,6},{8,9},{9,8},{10,11... | collective-permute-start | bytes 24584 | tf_op jit(solution)/shard_map/ppermute | solution.py:406

commit v23 on v22

--- a/solution.py
+++ b/solution.py
@@ -15,7 +15,7 @@
 ROWS = 16
 
 
-def kernel_call(kernel, out_shape, in_specs, out_specs, tokens, scratch_shapes=(), flops=10**6):
+def kernel_call(kernel, out_shape, in_specs, out_specs, tokens, scratch_shapes=(), aliases={}, flops=10**6):
     limit = (16 if tokens <= ROWS else 40) * 2**20
     return pl.pallas_call(
         kernel,
@@ -23,6 +23,7 @@
         in_specs=in_specs,
         out_specs=out_specs,
         scratch_shapes=scratch_shapes,
+        input_output_aliases=aliases,
         compiler_params=pltpu.CompilerParams(vmem_limit_bytes=limit),
         cost_estimate=pl.CostEstimate(flops=flops, bytes_accessed=2**20, transcendentals=0),
     )
@@ -33,7 +34,7 @@
 
 
 def first_width(width):
-    return width // 2
+    return width * 9 // 16 // 128 * 128
 
 
 def feat_bits():
@@ -42,7 +43,7 @@
 
 def bit_of(step, core):
     bits = list(range(feat_bits()))
-    return (bits[-1:] + bits[:-1] if core == 0 else bits[:1] + bits[:0:-1])[step]
+    return (bits[-1:] + bits[:-1] if core == 0 else bits)[step]
 
 
 def swapped(shard, step):
@@ -288,20 +289,25 @@
     return jnp.dot(code, scaled, preferred_element_type=jnp.float32).astype(jnp.bfloat16)
 
 
-def grad_rows_kernel(code_ref, first_ref, second_ref, out_ref):
+def grad_rows_kernel(code_ref, first_ref, second_ref, out_hbm, last_ref, out_ref, sem):
     chunk = first_ref.shape[1]
-    out_ref[:, :chunk] = outer(code_ref, first_ref[...])
-    out_ref[:, chunk:] = outer(code_ref, second_ref[...])
+    out_ref[...] = outer(code_ref, first_ref[...])
+    copy = pltpu.make_async_copy(out_ref, out_hbm.at[:, pl.ds(0, chunk)], sem)
+    copy.start()
+    last_ref[...] = outer(code_ref, second_ref[...])
+    copy.wait()
 
 
 def grad_rows_of(code, first, second):
     count, slots = code.shape
+    chunk, rest = first.shape[1], second.shape[1]
     return kernel_call(
         grad_rows_kernel,
-        shape(slots, first.shape[1] + second.shape[1]),
+        (shape(slots, chunk + rest), shape(slots, rest)),
         [VMEM] * 3,
-        VMEM,
-        count,
+        (HBM, VMEM),
+        count,
+        [pltpu.VMEM((slots, chunk), jnp.bfloat16), pltpu.SemaphoreType.DMA],
     )(code, first, second)
 
 
@@ -311,7 +317,8 @@
     mine_ref,
     theirs_ref,
     turned_ref,
-    rows_ref,
+    last_ref,
+    written_hbm,
     rows_hbm,
     enc_hbm,
     benc_hbm,
@@ -319,7 +326,9 @@
     benc_ref,
     sems,
 ):
-    copies = [pltpu.make_async_copy(rows_ref, rows_hbm, sems.at[0])]
+    rest = last_ref.shape[1]
+    features = pl.ds(rows_hbm.shape[1] - rest, rest)
+    copies = [pltpu.make_async_copy(last_ref, rows_hbm.at[:, features], sems.at[0])]
     copies[0].start()
     count, slots = raw_ref.shape
     width = turned_ref.shape[0]
@@ -353,14 +362,14 @@
         copy.wait()
 
 
-def final(raw, mine, theirs, turned_tokens, grad_rows, rows):
+def final(raw, mine, theirs, turned_tokens, last, written, rows):
     count, slots = raw.shape
     pieces = ROWS // rows
     width = turned_tokens.shape[0] * pieces
     return kernel_call(
         functools.partial(final_kernel, rows),
-        (shape(*grad_rows.shape), shape(width, slots), shape(1, slots, dtype=jnp.float32)),
-        [VMEM] * 5,
+        (shape(*written.shape), shape(width, slots), shape(1, slots, dtype=jnp.float32)),
+        [VMEM] * 5 + [HBM],
         (HBM, HBM, HBM),
         count,
         [
@@ -368,7 +377,8 @@
             pltpu.VMEM((1, slots), jnp.float32),
             pltpu.SemaphoreType.DMA((pieces // 2 + 2,)),
         ],
-    )(raw, mine, theirs, turned_tokens, grad_rows)
+        aliases={5: 0},
+    )(raw, mine, theirs, turned_tokens, last, written)
 
 
 def local(tokens, b_pre, pre_codes, top_idx, blocks, counts, dict_rows):
@@ -404,9 +414,9 @@
         total_second, arrived_second, dict_rows, product_first, turned_tokens
     )
     theirs = lax.ppermute(code_half, "tok", [(i, 1 - i) for i in range(2)])
-    grad_rows = grad_rows_of(code, scaled, scaled_second)
+    written, last = grad_rows_of(code, scaled, scaled_second)
     grad_rows, grad_enc, grad_benc = final(
-        raw, code_half, theirs, turned_tokens, grad_rows, rows
+        raw, code_half, theirs, turned_tokens, last, written, rows
     )
     return (grad_rows, grad_enc, grad_benc.reshape(-1))
 

time: 27 us -> 24.2 us (0.90)
  waiting for transfers between devices: 13.4 us -> 5.49 us
  starting transfers between devices: 7.81 us -> 12.1 us
  Pallas kernels: 3.47 us -> 4.18 us
    ppermute x6, waiting for transfers between devices: 12.7 us -> 5.48 us  [swapped(): return lax.ppermute(shard, ('feat', 'tok'), pairs)]
    ppermute x6, starting transfers between devices: 7.78 us -> 12 us  [swapped(): return lax.ppermute(shard, ('feat', 'tok'), pairs)]
    ppermute x1, waiting for transfers between devices: 0.69 us -> 0.01 us  [local(): theirs = lax.ppermute(code_half, 'tok', [(i, 1 - i) for i in range(2)])]
    pallas_call x2, Pallas kernels: 1.84 us -> 2.49 us  [the longest x1 1.29 us: final(): kernel_call(functools.partial(final_kernel, rows), (shape(*written.shape)...]
  transfers between devices with their start and end apart: 7 -> 7, of which waited for: 6 -> 5; matrix products, arithmetic and copies ran while one was open for 0% -> 0% of each run, Pallas kernels for 5% -> 8%
where the time goes in v23:
time: 24.2 us; the launch traced here: 23.9 us
  starting transfers between devices  12.1 us (50%)
  waiting for transfers between devices  5.49 us (23%)
  Pallas kernels  4.18 us (17%)
  between operations  2.14 us (9%)
    ppermute x6, starting transfers between devices, swapped(): return lax.ppermute(shard, ('feat', 'tok'), pairs)  12 us
    ppermute x6, waiting for transfers between devices, swapped(): return lax.ppermute(shard, ('feat', 'tok'), pairs)  5.48 us
    pallas_call x1, Pallas kernels, final(): kernel_call(functools.partial(final_kernel, rows), (shape(*written.shape)...  1.29 us
    pallas_call x1, Pallas kernels, grad_rows_of(): kernel_call(grad_rows_kernel, (shape(slots, chunk + rest), shape(slots, r...  1.2 us
    pallas_call x1, Pallas kernels, front(): kernel_call(front_kernel, (shape(count, slots), shape(count, slots, dtype...  0.62 us
  transfers between devices with their start and end apart: 7, of which 5 were waited for; matrix products, arithmetic and copies ran while one was open for 0% of the time, Pallas kernels for 8%

profile of v23, /device:TPU:0, one launch (start us, length us, event | category | flops | bytes accessed | tf_op | source)
XLA Modules:
  0.0 23.9 jit_solution(11772606592986799099)
XLA Ops:
  0.6 0.0 copy-start
  0.6 0.0 copy-start.1
  0.7 0.0 copy-start.2
  0.7 0.0 copy-start.3
  0.7 0.0 copy-start.4
  2.1 0.0 copy-done
  2.1 0.0 copy-done.1
  2.1 0.0 copy-done.2
  2.1 0.0 copy-done.3
  2.1 0.0 copy-done.4
  2.1 0.6 %shard_map.95 = (bf16[16,128]{1,0:T(8,128)(2,1)S(1)}, f32[16,128]{1,0:T(8,128)S(1)}, f32[16,2304]{1,0:T(8,128)S(1)}, bf16[16,2816]{1,0:T(8,128)(2,1)S(1)}, f32[2,4096]{1,0:T(2,128)S(1)}, /*index=5*/f32[1,4096]{1,0:T(1,128)S(1)}) custom-call(bf16[2,4096]{1,0:T(2,128)(2,1)S(1)} %copy-done.1, bf16[4096]{0:T(1024)(128)(2,1)S(1)} %copy-done.2, ...), custom_call_target="tpu_custom_call" | custom-call | flops 1000000 | bytes 1048576 | tf_op jit(solution)/shard_map/pallas_call | solution.py:143
  2.8 4.1 %collective-permute-start.1 = (bf16[16,2816]{1,0:T(8,128)(2,1)S(1)}, bf16[16,2816]{1,0:T(8,128)(2,1)S(1)}, u32[]{:S(2)}, u32[]{:S(2)}) collective-permute-start(bf16[16,2816]{1,0:T(8,128)(2,1)S(1)} %get-tuple-element.34.own_ref), channel_id=1, source_target_pairs={{0,8},{1,3},{2,10},{3,1},{4,12},{5,7},{6,14},{7,5},{8,0},{9,11},{1... | collective-permute-start | bytes 270344 | tf_op jit(solution)/shard_map/ppermute | solution.py:56
  6.9 0.2 shard_map.96
  7.0 0.1 collective-permute-start
  7.1 2.2 %collective-permute-done.1.arrived_ref = bf16[16,2816]{1,0:T(8,128)(2,1)S(1)} collective-permute-done((bf16[16,2816]{1,0:T(8,128)(2,1)S(1)}, bf16[16,2816]{1,0:T(8,128)(2,1)S(1)}, u32[]{:S(2)}, u32[]{:S(2)}) %collective-permute-start.1) | collective-permute-done | bytes 90144 | tf_op jit(solution)/shard_map/ppermute | solution.py:56
  9.4 1.9 %collective-permute-start.3 = (bf16[16,3328]{1,0:T(8,128)(2,1)S(1)}, bf16[16,3328]{1,0:T(8,128)(2,1)S(1)}, u32[]{:S(2)}, u32[]{:S(2)}) collective-permute-start(bf16[16,3328]{1,0:T(8,128)(2,1)S(1)} %get-tuple-element.35.after_ref.own_ref), channel_id=1, source_target_pairs={{0,2},{1,5},{2,0},{3,7},{4,6},{5,1},{6,4},{7,3},{8,10},{9,13},{10,... | collective-permute-start | bytes 319496 | tf_op jit(solution)/shard_map/ppermute | solution.py:56
  11.3 1.0 %collective-permute-done.arrived_ref = bf16[16,1792]{1,0:T(8,128)(2,1)S(1)} collective-permute-done((bf16[16,1792]{1,0:T(8,128)(2,1)S(1)}, bf16[16,1792]{1,0:T(8,128)(2,1)S(1)}, u32[]{:S(2)}, u32[]{:S(2)}) %collective-permute-start) | collective-permute-done | bytes 57376 | tf_op jit(solution)/shard_map/ppermute | solution.py:56
  12.3 1.6 %collective-permute-start.2 = (bf16[16,1792]{1,0:T(8,128)(2,1)S(1)}, bf16[16,1792]{1,0:T(8,128)(2,1)S(1)}, u32[]{:S(2)}, u32[]{:S(2)}) collective-permute-start(bf16[16,1792]{1,0:T(8,128)(2,1)S(1)} %get-tuple-element.37.after_ref.own_ref), channel_id=1, source_target_pairs={{0,2},{1,5},{2,0},{3,7},{4,6},{5,1},{6,4},{7,3},{8,10},{9,13},{10,... | collective-permute-start | bytes 172040 | tf_op jit(solution)/shard_map/ppermute | solution.py:56
  13.9 0.3 %collective-permute-done.3.arrived_ref = bf16[16,3328]{1,0:T(8,128)(2,1)S(1)} collective-permute-done((bf16[16,3328]{1,0:T(8,128)(2,1)S(1)}, bf16[16,3328]{1,0:T(8,128)(2,1)S(1)}, u32[]{:S(2)}, u32[]{:S(2)}) %collective-permute-start.3) | collective-permute-done | bytes 106528 | tf_op jit(solution)/shard_map/ppermute | solution.py:56
  14.2 2.6 %collective-permute-start.5 = (bf16[16,4352]{1,0:T(8,128)(2,1)S(1)}, bf16[16,4352]{1,0:T(8,128)(2,1)S(1)}, u32[]{:S(2)}, u32[]{:S(2)}) collective-permute-start(bf16[16,4352]{1,0:T(8,128)(2,1)S(1)} %get-tuple-element.39.after_ref.own_ref), channel_id=1, source_target_pairs={{0,4},{1,9},{2,6},{3,11},{4,0},{5,13},{6,2},{7,15},{8,12},{9,1},{1... | collective-permute-start | bytes 417800 | tf_op jit(solution)/shard_map/ppermute | solution.py:56
  16.8 0.0 collective-permute-done.2.arrived_ref
  16.9 1.8 %collective-permute-start.4 = (bf16[16,1792]{1,0:T(8,128)(2,1)S(1)}, bf16[16,1792]{1,0:T(8,128)(2,1)S(1)}, u32[]{:S(2)}, u32[]{:S(2)}) collective-permute-start(bf16[16,1792]{1,0:T(8,128)(2,1)S(1)} %get-tuple-element.41), channel_id=1, source_target_pairs={{0,4},{1,9},{2,6},{3,11},{4,0},{5,13},{6,2},{7,15},{8,12},{9,1},{1... | collective-permute-start | bytes 172040 | tf_op jit(solution)/shard_map/ppermute | solution.py:56
  18.6 1.8 %collective-permute-done.5.arrived_ref = bf16[16,4352]{1,0:T(8,128)(2,1)S(1)} collective-permute-done((bf16[16,4352]{1,0:T(8,128)(2,1)S(1)}, bf16[16,4352]{1,0:T(8,128)(2,1)S(1)}, u32[]{:S(2)}, u32[]{:S(2)}) %collective-permute-start.5) | collective-permute-done | bytes 139296 | tf_op jit(solution)/shard_map/ppermute | solution.py:56
  20.5 0.2 shard_map.101
  20.7 0.3 %shard_map.102.after_ref.turned_ref = bf16[512,128]{1,0:T(8,128)(2,1)S(1)} custom-call(bf16[16,4352]{1,0:T(8,128)(2,1)S(1)} %get-tuple-element.39.after_ref.own_ref, bf16[16,4352]{1,0:T(8,128)(2,1)S(1)} %collective-permute-done.5.arrived_ref, f32[1,4096]{1,0:T(1,128)S(1)} %get-tuple-element.44.bias_ref, bf16[128,128]{1,0:T(8,128)(2,1)S(1)} %shard_map.94.after_ref.order_ref), custom_call_target="tpu_custom_call" | custom-call | flops 1000000 | bytes 1048576 | tf_op jit(solution)/shard_map/pallas_call | solution.py:239
  21.0 0.1 collective-permute-done.4.arrived_ref
  21.1 0.2 shard_map.103
  21.3 0.0 collective-permute-start.6
  21.4 1.2 %shard_map.104 = (bf16[128,4096]{1,0:T(8,128)(2,1)}, bf16[128,1792]{1,0:T(8,128)(2,1)S(1)}) custom-call(bf16[16,128]{1,0:T(8,128)(2,1)S(1)} %get-tuple-element.29.code_ref, bf16[16,2304]{1,0:T(8,128)(2,1)S(1)} %get-tuple-element.46.first_ref, bf16[16,1792]{1,0:T(8,128)(2,1)S(1)} %get-tuple-element.47.second_ref), custom_call_target="tpu_custom_call" | custom-call | flops 1000000 | bytes 1048576 | tf_op jit(solution)/shard_map/pallas_call | solution.py:304
  22.6 0.0 collective-permute-done.6.theirs_ref
  22.6 1.3 %shard_map.105 = (bf16[128,4096]{1,0:T(8,128)(2,1)}, bf16[4096,128]{1,0:T(8,128)(2,1)}, f32[1,128]{1,0:T(1,128)}) custom-call(f32[16,128]{1,0:T(8,128)S(1)} %get-tuple-element.28.raw_ref, f32[16,128]{1,0:T(8,128)S(1)} %get-tuple-element.45.mine_ref, f32[16,128]{1,0:T(8,128)S(1)} %collective-permute-done.6.theirs_ref, ...), custom_call_target="tpu_custom_call", output_to_operand_aliasing={{0}: (5, {})} | custom-call | flops 1000000 | bytes 1048576 | tf_op jit(solution)/shard_map/pallas_call | solution.py:369
  (5 shorter events, 0.1 us)
Async XLA Ops:
  0.6 1.5 %copy-start = (bf16[128,4096]{1,0:T(8,128)(2,1)S(1)}, bf16[128,4096]{1,0:T(8,128)(2,1)}, u32[]{:S(2)}) copy-start(bf16[128,4096]{1,0:T(8,128)(2,1)} %rows_ref.7) | copy-start | bytes 3145732
  0.6 1.5 %copy-start.1 = (bf16[2,4096]{1,0:T(2,128)(2,1)S(1)}, bf16[2,4096]{1,0:T(2,128)(2,1)}, u32[]{:S(2)}) copy-start(bf16[2,4096]{1,0:T(2,128)(2,1)} %tokens_ref.1) | copy-start | bytes 49156
  0.7 1.5 %copy-start.2 = (bf16[4096]{0:T(1024)(128)(2,1)S(1)}, bf16[4096]{0:T(1024)(128)(2,1)}, u32[]{:S(2)}) copy-start(bf16[4096]{0:T(1024)(128)(2,1)} %bias_flat.1) | copy-start | bytes 24580
  0.7 1.5 %copy-start.3 = (f32[16,64]{1,0:T(8,128)S(1)}, f32[16,64]{1,0:T(8,128)}, u32[]{:S(2)}) copy-start(f32[16,64]{1,0:T(8,128)} %pre_ref.1) | copy-start | bytes 12292
  0.7 1.5 %copy-start.4 = (s32[16,64]{1,0:T(8,128)S(1)}, s32[16,64]{1,0:T(8,128)}, u32[]{:S(2)}) copy-start(s32[16,64]{1,0:T(8,128)} %top_ref.1) | copy-start | bytes 12292
  2.8 6.6 %collective-permute-start.1 = (bf16[16,2816]{1,0:T(8,128)(2,1)S(1)}, bf16[16,2816]{1,0:T(8,128)(2,1)S(1)}, u32[]{:S(2)}, u32[]{:S(2)}) collective-permute-start(bf16[16,2816]{1,0:T(8,128)(2,1)S(1)} %get-tuple-element.34.own_ref), channel_id=1, source_target_pairs={{0,8},{1,3},{2,10},{3,1},{4,12},{5,7},{6,14},{7,5},{8,0},{9,11},{1... | collective-permute-start | bytes 270344 | tf_op jit(solution)/shard_map/ppermute | solution.py:56
  7.0 5.2 %collective-permute-start = (bf16[16,1792]{1,0:T(8,128)(2,1)S(1)}, bf16[16,1792]{1,0:T(8,128)(2,1)S(1)}, u32[]{:S(2)}, u32[]{:S(2)}) collective-permute-start(bf16[16,1792]{1,0:T(8,128)(2,1)S(1)} %get-tuple-element.32.after_ref.own_ref), channel_id=1, source_target_pairs={{0,8},{1,3},{2,10},{3,1},{4,12},{5,7},{6,14},{7,5},{8,0},{9,11},{1... | collective-permute-start | bytes 172040 | tf_op jit(solution)/shard_map/ppermute | solution.py:56
  9.4 4.8 %collective-permute-start.3 = (bf16[16,3328]{1,0:T(8,128)(2,1)S(1)}, bf16[16,3328]{1,0:T(8,128)(2,1)S(1)}, u32[]{:S(2)}, u32[]{:S(2)}) collective-permute-start(bf16[16,3328]{1,0:T(8,128)(2,1)S(1)} %get-tuple-element.35.after_ref.own_ref), channel_id=1, source_target_pairs={{0,2},{1,5},{2,0},{3,7},{4,6},{5,1},{6,4},{7,3},{8,10},{9,13},{10,... | collective-permute-start | bytes 319496 | tf_op jit(solution)/shard_map/ppermute | solution.py:56
  12.3 4.5 %collective-permute-start.2 = (bf16[16,1792]{1,0:T(8,128)(2,1)S(1)}, bf16[16,1792]{1,0:T(8,128)(2,1)S(1)}, u32[]{:S(2)}, u32[]{:S(2)}) collective-permute-start(bf16[16,1792]{1,0:T(8,128)(2,1)S(1)} %get-tuple-element.37.after_ref.own_ref), channel_id=1, source_target_pairs={{0,2},{1,5},{2,0},{3,7},{4,6},{5,1},{6,4},{7,3},{8,10},{9,13},{10,... | collective-permute-start | bytes 172040 | tf_op jit(solution)/shard_map/ppermute | solution.py:56
  14.2 6.3 %collective-permute-start.5 = (bf16[16,4352]{1,0:T(8,128)(2,1)S(1)}, bf16[16,4352]{1,0:T(8,128)(2,1)S(1)}, u32[]{:S(2)}, u32[]{:S(2)}) collective-permute-start(bf16[16,4352]{1,0:T(8,128)(2,1)S(1)} %get-tuple-element.39.after_ref.own_ref), channel_id=1, source_target_pairs={{0,4},{1,9},{2,6},{3,11},{4,0},{5,13},{6,2},{7,15},{8,12},{9,1},{1... | collective-permute-start | bytes 417800 | tf_op jit(solution)/shard_map/ppermute | solution.py:56
  16.9 4.2 %collective-permute-start.4 = (bf16[16,1792]{1,0:T(8,128)(2,1)S(1)}, bf16[16,1792]{1,0:T(8,128)(2,1)S(1)}, u32[]{:S(2)}, u32[]{:S(2)}) collective-permute-start(bf16[16,1792]{1,0:T(8,128)(2,1)S(1)} %get-tuple-element.41), channel_id=1, source_target_pairs={{0,4},{1,9},{2,6},{3,11},{4,0},{5,13},{6,2},{7,15},{8,12},{9,1},{1... | collective-permute-start | bytes 172040 | tf_op jit(solution)/shard_map/ppermute | solution.py:56
  21.3 1.2 %collective-permute-start.6 = (f32[16,128]{1,0:T(8,128)S(1)}, f32[16,128]{1,0:T(8,128)S(1)}, u32[]{:S(2)}, u32[]{:S(2)}) collective-permute-start(f32[16,128]{1,0:T(8,128)S(1)} %get-tuple-element.45.mine_ref), channel_id=1, source_target_pairs={{0,1},{1,0},{2,3},{3,2},{4,5},{5,4},{6,7},{7,6},{8,9},{9,8},{10,11... | collective-permute-start | bytes 24584 | tf_op jit(solution)/shard_map/ppermute | solution.py:416

commit v24 on v20

--- a/solution.py
+++ b/solution.py
@@ -40,15 +40,17 @@
     return (lax.axis_size("feat") - 1).bit_length()
 
 
-def bit_of(step, core):
+def bit_of(step, core, chunk):
     bits = list(range(feat_bits()))
-    return (bits[-1:] + bits[:-1] if core == 0 else bits)[step]
-
-
-def swapped(shard, step):
+    if core == 0:
+        return (bits[-1:] + bits[:-1] if chunk == 0 else bits[::-1])[step]
+    return bits[step]
+
+
+def swapped(shard, step, chunk):
     cores = lax.axis_size("tok")
     pairs = [
-        (f * cores + c, (f ^ 1 << bit_of(step, c)) * cores + c)
+        (f * cores + c, (f ^ 1 << bit_of(step, c, chunk)) * cores + c)
         for f in range(lax.axis_size("feat"))
         for c in range(cores)
     ]
@@ -82,7 +84,7 @@
     distance = jnp.zeros_like(place)
     for step in range(feat_bits()):
         bit = sum(
-            jnp.where(core == c, bit_of(step, c), 0) for c in range(lax.axis_size("tok"))
+            jnp.where(core == c, bit_of(step, c, 0), 0) for c in range(lax.axis_size("tok"))
         )
         distance |= (block >> step & 1) << bit
     token = (lax.axis_index("feat") ^ distance) * rows + place % rows
@@ -375,17 +377,17 @@
         tokens, b_pre, pre_codes, top_idx, blocks, counts, dict_rows, order, merged
     )
     for step in range(steps):
-        arrived = swapped(sent, step)
+        arrived = swapped(sent, step, 0)
         if step == 0:
             total_second, sent_second = second(code, dict_rows, centered)
         else:
             total_second, sent_second = added(
                 total_second, sent_second, arrived_second, sent, False, EARLY
             )
-        arrived_second = swapped(sent_second, step)
+        arrived_second = swapped(sent_second, step, 1)
         if not merged:
             own_block = joined(own_block, arrived_block, sent_second) if step else block[0]
-            arrived_block = swapped(own_block, step)
+            arrived_block = swapped(own_block, step, 0)
         if step < steps - 1:
             total, sent = added(total, sent, arrived, sent_second, merged)
     skip = 0

time: 24.1 us -> 24.8 us (1.029)
  waiting for transfers between devices: 5.77 us -> 7.03 us
  starting transfers between devices: 12.6 us -> 12 us
    ppermute x6, waiting for transfers between devices: 5.34 us -> 6.6 us  [swapped(): return lax.ppermute(shard, ('feat', 'tok'), pairs)]
    ppermute x6, starting transfers between devices: 12.5 us -> 11.9 us  [swapped(): return lax.ppermute(shard, ('feat', 'tok'), pairs)]
  transfers between devices with their start and end apart: 7 -> 7, of which waited for: 5 -> 6; matrix products, arithmetic and copies ran while one was open for 0% -> 0% of each run, Pallas kernels for 5% -> 5%
where the time goes in v24:
time: 24.8 us; the launch traced here: 24.6 us
  starting transfers between devices  12 us (48%)
  waiting for transfers between devices  7.03 us (28%)
  Pallas kernels  3.46 us (14%)
  between operations  2.13 us (9%)
    ppermute x6, starting transfers between devices, swapped(): return lax.ppermute(shard, ('feat', 'tok'), pairs)  11.9 us
    ppermute x6, waiting for transfers between devices, swapped(): return lax.ppermute(shard, ('feat', 'tok'), pairs)  6.6 us
    pallas_call x1, Pallas kernels, final(): kernel_call(functools.partial(final_kernel, rows), (shape(*grad_rows.shap...  1.36 us
    pallas_call x1, Pallas kernels, front(): kernel_call(front_kernel, (shape(count, slots), shape(count, slots, dtype...  0.61 us
  transfers between devices with their start and end apart: 7, of which 6 were waited for; matrix products, arithmetic and copies ran while one was open for 0% of the time, Pallas kernels for 5%

profile of v24, /device:TPU:0, one launch (start us, length us, event | category | flops | bytes accessed | tf_op | source)
XLA Modules:
  0.0 24.6 jit_solution(16980479821887835450)
XLA Ops:
  0.6 0.0 copy-start
  0.6 0.0 copy-start.1
  0.7 0.0 copy-start.2
  0.7 0.0 copy-start.3
  0.7 0.0 copy-start.4
  2.1 0.0 copy-done
  2.1 0.0 copy-done.1
  2.1 0.0 copy-done.2
  2.1 0.0 copy-done.3
  2.1 0.0 copy-done.4
  2.1 0.6 %shard_map.95 = (bf16[16,128]{1,0:T(8,128)(2,1)S(1)}, f32[16,128]{1,0:T(8,128)S(1)}, f32[16,2048]{1,0:T(8,128)S(1)}, bf16[16,2560]{1,0:T(8,128)(2,1)S(1)}, f32[2,4096]{1,0:T(2,128)S(1)}, /*index=5*/f32[1,4096]{1,0:T(1,128)S(1)}) custom-call(bf16[2,4096]{1,0:T(2,128)(2,1)S(1)} %copy-done.1, bf16[4096]{0:T(1024)(128)(2,1)S(1)} %copy-done.2, ...), custom_call_target="tpu_custom_call" | custom-call | flops 1000000 | bytes 1048576 | tf_op jit(solution)/shard_map/pallas_call | solution.py:144
  2.7 4.1 %collective-permute-start.1 = (bf16[16,2560]{1,0:T(8,128)(2,1)S(1)}, bf16[16,2560]{1,0:T(8,128)(2,1)S(1)}, u32[]{:S(2)}, u32[]{:S(2)}) collective-permute-start(bf16[16,2560]{1,0:T(8,128)(2,1)S(1)} %get-tuple-element.32.own_ref), channel_id=1, source_target_pairs={{0,8},{1,3},{2,10},{3,1},{4,12},{5,7},{6,14},{7,5},{8,0},{9,11},{1... | collective-permute-start | bytes 245768 | tf_op jit(solution)/shard_map/ppermute | solution.py:57
  6.8 0.2 shard_map.96
  7.0 0.1 collective-permute-start
  7.1 2.2 %collective-permute-done.1.arrived_ref = bf16[16,2560]{1,0:T(8,128)(2,1)S(1)} collective-permute-done((bf16[16,2560]{1,0:T(8,128)(2,1)S(1)}, bf16[16,2560]{1,0:T(8,128)(2,1)S(1)}, u32[]{:S(2)}, u32[]{:S(2)}) %collective-permute-start.1) | collective-permute-done | bytes 81952 | tf_op jit(solution)/shard_map/ppermute | solution.py:57
  9.3 1.9 %collective-permute-start.3 = (bf16[16,3072]{1,0:T(8,128)(2,1)S(1)}, bf16[16,3072]{1,0:T(8,128)(2,1)S(1)}, u32[]{:S(2)}, u32[]{:S(2)}) collective-permute-start(bf16[16,3072]{1,0:T(8,128)(2,1)S(1)} %get-tuple-element.33.after_ref.own_ref), channel_id=1, source_target_pairs={{0,2},{1,5},{2,0},{3,7},{4,6},{5,1},{6,4},{7,3},{8,10},{9,13},{10,... | collective-permute-start | bytes 294920 | tf_op jit(solution)/shard_map/ppermute | solution.py:57
  11.2 1.1 %collective-permute-done.arrived_ref = bf16[16,2048]{1,0:T(8,128)(2,1)S(1)} collective-permute-done((bf16[16,2048]{1,0:T(8,128)(2,1)S(1)}, bf16[16,2048]{1,0:T(8,128)(2,1)S(1)}, u32[]{:S(2)}, u32[]{:S(2)}) %collective-permute-start) | collective-permute-done | bytes 65568 | tf_op jit(solution)/shard_map/ppermute | solution.py:57
  12.3 2.2 %collective-permute-start.2 = (bf16[16,2048]{1,0:T(8,128)(2,1)S(1)}, bf16[16,2048]{1,0:T(8,128)(2,1)S(1)}, u32[]{:S(2)}, u32[]{:S(2)}) collective-permute-start(bf16[16,2048]{1,0:T(8,128)(2,1)S(1)} %get-tuple-element.35.after_ref.own_ref), channel_id=1, source_target_pairs={{0,4},{1,5},{2,6},{3,7},{4,0},{5,1},{6,2},{7,3},{8,12},{9,13},{10,... | collective-permute-start | bytes 196616 | tf_op jit(solution)/shard_map/ppermute | solution.py:57
  14.5 0.0 collective-permute-done.3.arrived_ref
  14.6 2.1 %collective-permute-start.5 = (bf16[16,4096]{1,0:T(8,128)(2,1)S(1)}, bf16[16,4096]{1,0:T(8,128)(2,1)S(1)}, u32[]{:S(2)}, u32[]{:S(2)}) collective-permute-start(bf16[16,4096]{1,0:T(8,128)(2,1)S(1)} %get-tuple-element.37.after_ref.own_ref), channel_id=1, source_target_pairs={{0,4},{1,9},{2,6},{3,11},{4,0},{5,13},{6,2},{7,15},{8,12},{9,1},{1... | collective-permute-start | bytes 393224 | tf_op jit(solution)/shard_map/ppermute | solution.py:57
  16.7 0.8 %collective-permute-done.2.arrived_ref = bf16[16,2048]{1,0:T(8,128)(2,1)S(1)} collective-permute-done((bf16[16,2048]{1,0:T(8,128)(2,1)S(1)}, bf16[16,2048]{1,0:T(8,128)(2,1)S(1)}, u32[]{:S(2)}, u32[]{:S(2)}) %collective-permute-start.2) | collective-permute-done | bytes 65568 | tf_op jit(solution)/shard_map/ppermute | solution.py:57
  17.5 1.6 %collective-permute-start.4 = (bf16[16,2048]{1,0:T(8,128)(2,1)S(1)}, bf16[16,2048]{1,0:T(8,128)(2,1)S(1)}, u32[]{:S(2)}, u32[]{:S(2)}) collective-permute-start(bf16[16,2048]{1,0:T(8,128)(2,1)S(1)} %get-tuple-element.39), channel_id=1, source_target_pairs={{0,2},{1,9},{2,0},{3,11},{4,6},{5,13},{6,4},{7,15},{8,10},{9,1},{1... | collective-permute-start | bytes 196616 | tf_op jit(solution)/shard_map/ppermute | solution.py:57
  19.0 1.2 %collective-permute-done.5.arrived_ref = bf16[16,4096]{1,0:T(8,128)(2,1)S(1)} collective-permute-done((bf16[16,4096]{1,0:T(8,128)(2,1)S(1)}, bf16[16,4096]{1,0:T(8,128)(2,1)S(1)}, u32[]{:S(2)}, u32[]{:S(2)}) %collective-permute-start.5) | collective-permute-done | bytes 131104 | tf_op jit(solution)/shard_map/ppermute | solution.py:57
  20.2 0.2 shard_map.101
  20.5 1.4 %collective-permute-done.4.arrived_ref = bf16[16,2048]{1,0:T(8,128)(2,1)S(1)} collective-permute-done((bf16[16,2048]{1,0:T(8,128)(2,1)S(1)}, bf16[16,2048]{1,0:T(8,128)(2,1)S(1)}, u32[]{:S(2)}, u32[]{:S(2)}) %collective-permute-start.4) | collective-permute-done | bytes 65568 | tf_op jit(solution)/shard_map/ppermute | solution.py:57
  21.8 0.2 shard_map.102
  22.0 0.0 collective-permute-start.6
  22.1 0.5 %shard_map.104.rows_ref = bf16[128,4096]{1,0:T(8,128)(2,1)S(1)} custom-call(bf16[16,128]{1,0:T(8,128)(2,1)S(1)} %get-tuple-element.27.code_ref, bf16[16,2048]{1,0:T(8,128)(2,1)S(1)} %get-tuple-element.44.first_ref, bf16[16,2048]{1,0:T(8,128)(2,1)S(1)} %get-tuple-element.45.second_ref), custom_call_target="tpu_custom_call" | custom-call | flops 1000000 | bytes 1048576 | tf_op jit(solution)/shard_map/pallas_call | solution.py:299
  22.5 0.3 %shard_map.103.turned_ref = bf16[512,128]{1,0:T(8,128)(2,1)S(1)} custom-call(bf16[16,4096]{1,0:T(8,128)(2,1)S(1)} %get-tuple-element.37.after_ref.own_ref, bf16[16,4096]{1,0:T(8,128)(2,1)S(1)} %collective-permute-done.5.arrived_ref, f32[1,4096]{1,0:T(1,128)S(1)} %get-tuple-element.43.bias_ref, bf16[128,128]{1,0:T(8,128)(2,1)S(1)} %shard_map.94.after_ref.order_ref), custom_call_target="tpu_custom_call" | custom-call | flops 1000000 | bytes 1048576 | tf_op jit(solution)/shard_map/pallas_call | solution.py:240
  22.8 0.4 %collective-permute-done.6.theirs_ref = f32[16,128]{1,0:T(8,128)S(1)} collective-permute-done((f32[16,128]{1,0:T(8,128)S(1)}, f32[16,128]{1,0:T(8,128)S(1)}, u32[]{:S(2)}, u32[]{:S(2)}) %collective-permute-start.6) | collective-permute-done | bytes 8224 | tf_op jit(solution)/shard_map/ppermute | solution.py:402
  23.2 1.4 %shard_map.105 = (bf16[128,4096]{1,0:T(8,128)(2,1)}, bf16[4096,128]{1,0:T(8,128)(2,1)}, f32[1,128]{1,0:T(1,128)}) custom-call(f32[16,128]{1,0:T(8,128)S(1)} %get-tuple-element.26.raw_ref, f32[16,128]{1,0:T(8,128)S(1)} %get-tuple-element.42.mine_ref, f32[16,128]{1,0:T(8,128)S(1)} %collective-permute-done.6.theirs_ref, ...), custom_call_target="tpu_custom_call" | custom-call | flops 1000000 | bytes 1048576 | tf_op jit(solution)/shard_map/pallas_call | solution.py:356
  (5 shorter events, 0.1 us)
Async XLA Ops:
  0.6 1.5 %copy-start = (bf16[128,4096]{1,0:T(8,128)(2,1)S(1)}, bf16[128,4096]{1,0:T(8,128)(2,1)}, u32[]{:S(2)}) copy-start(bf16[128,4096]{1,0:T(8,128)(2,1)} %rows_ref.7) | copy-start | bytes 3145732
  0.6 1.5 %copy-start.1 = (bf16[2,4096]{1,0:T(2,128)(2,1)S(1)}, bf16[2,4096]{1,0:T(2,128)(2,1)}, u32[]{:S(2)}) copy-start(bf16[2,4096]{1,0:T(2,128)(2,1)} %tokens_ref.1) | copy-start | bytes 49156
  0.7 1.5 %copy-start.2 = (bf16[4096]{0:T(1024)(128)(2,1)S(1)}, bf16[4096]{0:T(1024)(128)(2,1)}, u32[]{:S(2)}) copy-start(bf16[4096]{0:T(1024)(128)(2,1)} %bias_flat.1) | copy-start | bytes 24580
  0.7 1.5 %copy-start.3 = (f32[16,64]{1,0:T(8,128)S(1)}, f32[16,64]{1,0:T(8,128)}, u32[]{:S(2)}) copy-start(f32[16,64]{1,0:T(8,128)} %pre_ref.1) | copy-start | bytes 12292
  0.7 1.5 %copy-start.4 = (s32[16,64]{1,0:T(8,128)S(1)}, s32[16,64]{1,0:T(8,128)}, u32[]{:S(2)}) copy-start(s32[16,64]{1,0:T(8,128)} %top_ref.1) | copy-start | bytes 12292
  2.7 6.5 %collective-permute-start.1 = (bf16[16,2560]{1,0:T(8,128)(2,1)S(1)}, bf16[16,2560]{1,0:T(8,128)(2,1)S(1)}, u32[]{:S(2)}, u32[]{:S(2)}) collective-permute-start(bf16[16,2560]{1,0:T(8,128)(2,1)S(1)} %get-tuple-element.32.own_ref), channel_id=1, source_target_pairs={{0,8},{1,3},{2,10},{3,1},{4,12},{5,7},{6,14},{7,5},{8,0},{9,11},{1... | collective-permute-start | bytes 245768 | tf_op jit(solution)/shard_map/ppermute | solution.py:57
  7.0 5.3 %collective-permute-start = (bf16[16,2048]{1,0:T(8,128)(2,1)S(1)}, bf16[16,2048]{1,0:T(8,128)(2,1)S(1)}, u32[]{:S(2)}, u32[]{:S(2)}) collective-permute-start(bf16[16,2048]{1,0:T(8,128)(2,1)S(1)} %get-tuple-element.30.after_ref.own_ref), channel_id=1, source_target_pairs={{0,8},{1,3},{2,10},{3,1},{4,12},{5,7},{6,14},{7,5},{8,0},{9,11},{1... | collective-permute-start | bytes 196616 | tf_op jit(solution)/shard_map/ppermute | solution.py:57
  9.3 5.3 %collective-permute-start.3 = (bf16[16,3072]{1,0:T(8,128)(2,1)S(1)}, bf16[16,3072]{1,0:T(8,128)(2,1)S(1)}, u32[]{:S(2)}, u32[]{:S(2)}) collective-permute-start(bf16[16,3072]{1,0:T(8,128)(2,1)S(1)} %get-tuple-element.33.after_ref.own_ref), channel_id=1, source_target_pairs={{0,2},{1,5},{2,0},{3,7},{4,6},{5,1},{6,4},{7,3},{8,10},{9,13},{10,... | collective-permute-start | bytes 294920 | tf_op jit(solution)/shard_map/ppermute | solution.py:57
  12.3 5.1 %collective-permute-start.2 = (bf16[16,2048]{1,0:T(8,128)(2,1)S(1)}, bf16[16,2048]{1,0:T(8,128)(2,1)S(1)}, u32[]{:S(2)}, u32[]{:S(2)}) collective-permute-start(bf16[16,2048]{1,0:T(8,128)(2,1)S(1)} %get-tuple-element.35.after_ref.own_ref), channel_id=1, source_target_pairs={{0,4},{1,5},{2,6},{3,7},{4,0},{5,1},{6,2},{7,3},{8,12},{9,13},{10,... | collective-permute-start | bytes 196616 | tf_op jit(solution)/shard_map/ppermute | solution.py:57
  14.6 5.6 %collective-permute-start.5 = (bf16[16,4096]{1,0:T(8,128)(2,1)S(1)}, bf16[16,4096]{1,0:T(8,128)(2,1)S(1)}, u32[]{:S(2)}, u32[]{:S(2)}) collective-permute-start(bf16[16,4096]{1,0:T(8,128)(2,1)S(1)} %get-tuple-element.37.after_ref.own_ref), channel_id=1, source_target_pairs={{0,4},{1,9},{2,6},{3,11},{4,0},{5,13},{6,2},{7,15},{8,12},{9,1},{1... | collective-permute-start | bytes 393224 | tf_op jit(solution)/shard_map/ppermute | solution.py:57
  17.5 4.3 %collective-permute-start.4 = (bf16[16,2048]{1,0:T(8,128)(2,1)S(1)}, bf16[16,2048]{1,0:T(8,128)(2,1)S(1)}, u32[]{:S(2)}, u32[]{:S(2)}) collective-permute-start(bf16[16,2048]{1,0:T(8,128)(2,1)S(1)} %get-tuple-element.39), channel_id=1, source_target_pairs={{0,2},{1,9},{2,0},{3,11},{4,6},{5,13},{6,4},{7,15},{8,10},{9,1},{1... | collective-permute-start | bytes 196616 | tf_op jit(solution)/shard_map/ppermute | solution.py:57
  22.0 1.2 %collective-permute-start.6 = (f32[16,128]{1,0:T(8,128)S(1)}, f32[16,128]{1,0:T(8,128)S(1)}, u32[]{:S(2)}, u32[]{:S(2)}) collective-permute-start(f32[16,128]{1,0:T(8,128)S(1)} %get-tuple-element.42.mine_ref), channel_id=1, source_target_pairs={{0,1},{1,0},{2,3},{3,2},{4,5},{5,4},{6,7},{7,6},{8,9},{9,8},{10,11... | collective-permute-start | bytes 24584 | tf_op jit(solution)/shard_map/ppermute | solution.py:402

commit v25 on v20

--- a/solution.py
+++ b/solution.py
@@ -42,7 +42,7 @@
 
 def bit_of(step, core):
     bits = list(range(feat_bits()))
-    return (bits[-1:] + bits[:-1] if core == 0 else bits)[step]
+    return (bits[::-1] if core == 0 else bits)[step]
 
 
 def swapped(shard, step):

time: 24.1 us -> 24.8 us (1.029)
  waiting for transfers between devices: 5.77 us -> 6.79 us
  starting transfers between devices: 12.6 us -> 12.2 us
    ppermute x6, waiting for transfers between devices: 5.34 us -> 6.36 us  [swapped(): return lax.ppermute(shard, ('feat', 'tok'), pairs)]
    ppermute x6, starting transfers between devices: 12.5 us -> 12.2 us  [swapped(): return lax.ppermute(shard, ('feat', 'tok'), pairs)]
  transfers between devices with their start and end apart: 7 -> 7, of which waited for: 5 -> 6; matrix products, arithmetic and copies ran while one was open for 0% -> 0% of each run, Pallas kernels for 5% -> 5%
where the time goes in v25:
time: 24.8 us; the launch traced here: 24.6 us
  starting transfers between devices  12.2 us (49%)
  waiting for transfers between devices  6.79 us (27%)
  Pallas kernels  3.46 us (14%)
  between operations  2.13 us (9%)
    ppermute x6, starting transfers between devices, swapped(): return lax.ppermute(shard, ('feat', 'tok'), pairs)  12.2 us
    ppermute x6, waiting for transfers between devices, swapped(): return lax.ppermute(shard, ('feat', 'tok'), pairs)  6.36 us
    pallas_call x1, Pallas kernels, final(): kernel_call(functools.partial(final_kernel, rows), (shape(*grad_rows.shap...  1.36 us
    pallas_call x1, Pallas kernels, front(): kernel_call(front_kernel, (shape(count, slots), shape(count, slots, dtype...  0.61 us
  transfers between devices with their start and end apart: 7, of which 6 were waited for; matrix products, arithmetic and copies ran while one was open for 0% of the time, Pallas kernels for 5%

profile of v25, /device:TPU:0, one launch (start us, length us, event | category | flops | bytes accessed | tf_op | source)
XLA Modules:
  0.0 24.6 jit_solution(10632096985063014642)
XLA Ops:
  0.6 0.0 copy-start
  0.6 0.0 copy-start.1
  0.7 0.0 copy-start.2
  0.7 0.0 copy-start.3
  0.7 0.0 copy-start.4
  2.1 0.0 copy-done
  2.1 0.0 copy-done.1
  2.1 0.0 copy-done.2
  2.1 0.0 copy-done.3
  2.1 0.0 copy-done.4
  2.1 0.6 %shard_map.95 = (bf16[16,128]{1,0:T(8,128)(2,1)S(1)}, f32[16,128]{1,0:T(8,128)S(1)}, f32[16,2048]{1,0:T(8,128)S(1)}, bf16[16,2560]{1,0:T(8,128)(2,1)S(1)}, f32[2,4096]{1,0:T(2,128)S(1)}, /*index=5*/f32[1,4096]{1,0:T(1,128)S(1)}) custom-call(bf16[2,4096]{1,0:T(2,128)(2,1)S(1)} %copy-done.1, bf16[4096]{0:T(1024)(128)(2,1)S(1)} %copy-done.2, ...), custom_call_target="tpu_custom_call" | custom-call | flops 1000000 | bytes 1048576 | tf_op jit(solution)/shard_map/pallas_call | solution.py:142
  2.7 4.1 %collective-permute-start.1 = (bf16[16,2560]{1,0:T(8,128)(2,1)S(1)}, bf16[16,2560]{1,0:T(8,128)(2,1)S(1)}, u32[]{:S(2)}, u32[]{:S(2)}) collective-permute-start(bf16[16,2560]{1,0:T(8,128)(2,1)S(1)} %get-tuple-element.32.own_ref), channel_id=1, source_target_pairs={{0,8},{1,3},{2,10},{3,1},{4,12},{5,7},{6,14},{7,5},{8,0},{9,11},{1... | collective-permute-start | bytes 245768 | tf_op jit(solution)/shard_map/ppermute | solution.py:55
  6.8 0.2 shard_map.96
  7.0 0.1 collective-permute-start
  7.1 2.2 %collective-permute-done.1.arrived_ref = bf16[16,2560]{1,0:T(8,128)(2,1)S(1)} collective-permute-done((bf16[16,2560]{1,0:T(8,128)(2,1)S(1)}, bf16[16,2560]{1,0:T(8,128)(2,1)S(1)}, u32[]{:S(2)}, u32[]{:S(2)}) %collective-permute-start.1) | collective-permute-done | bytes 81952 | tf_op jit(solution)/shard_map/ppermute | solution.py:55
  9.3 2.7 %collective-permute-start.3 = (bf16[16,3072]{1,0:T(8,128)(2,1)S(1)}, bf16[16,3072]{1,0:T(8,128)(2,1)S(1)}, u32[]{:S(2)}, u32[]{:S(2)}) collective-permute-start(bf16[16,3072]{1,0:T(8,128)(2,1)S(1)} %get-tuple-element.33.after_ref.own_ref), channel_id=1, source_target_pairs={{0,4},{1,5},{2,6},{3,7},{4,0},{5,1},{6,2},{7,3},{8,12},{9,13},{10,... | collective-permute-start | bytes 294920 | tf_op jit(solution)/shard_map/ppermute | solution.py:55
  12.0 0.3 %collective-permute-done.arrived_ref = bf16[16,2048]{1,0:T(8,128)(2,1)S(1)} collective-permute-done((bf16[16,2048]{1,0:T(8,128)(2,1)S(1)}, bf16[16,2048]{1,0:T(8,128)(2,1)S(1)}, u32[]{:S(2)}, u32[]{:S(2)}) %collective-permute-start) | collective-permute-done | bytes 65568 | tf_op jit(solution)/shard_map/ppermute | solution.py:55
  12.3 2.2 %collective-permute-start.2 = (bf16[16,2048]{1,0:T(8,128)(2,1)S(1)}, bf16[16,2048]{1,0:T(8,128)(2,1)S(1)}, u32[]{:S(2)}, u32[]{:S(2)}) collective-permute-start(bf16[16,2048]{1,0:T(8,128)(2,1)S(1)} %get-tuple-element.35.after_ref.own_ref), channel_id=1, source_target_pairs={{0,4},{1,5},{2,6},{3,7},{4,0},{5,1},{6,2},{7,3},{8,12},{9,13},{10,... | collective-permute-start | bytes 196616 | tf_op jit(solution)/shard_map/ppermute | solution.py:55
  14.5 0.0 collective-permute-done.3.arrived_ref
  14.6 1.6 %collective-permute-start.5 = (bf16[16,4096]{1,0:T(8,128)(2,1)S(1)}, bf16[16,4096]{1,0:T(8,128)(2,1)S(1)}, u32[]{:S(2)}, u32[]{:S(2)}) collective-permute-start(bf16[16,4096]{1,0:T(8,128)(2,1)S(1)} %get-tuple-element.37.after_ref.own_ref), channel_id=1, source_target_pairs={{0,2},{1,9},{2,0},{3,11},{4,6},{5,13},{6,4},{7,15},{8,10},{9,1},{1... | collective-permute-start | bytes 393224 | tf_op jit(solution)/shard_map/ppermute | solution.py:55
  16.1 1.3 %collective-permute-done.2.arrived_ref = bf16[16,2048]{1,0:T(8,128)(2,1)S(1)} collective-permute-done((bf16[16,2048]{1,0:T(8,128)(2,1)S(1)}, bf16[16,2048]{1,0:T(8,128)(2,1)S(1)}, u32[]{:S(2)}, u32[]{:S(2)}) %collective-permute-start.2) | collective-permute-done | bytes 65568 | tf_op jit(solution)/shard_map/ppermute | solution.py:55
  17.5 1.6 %collective-permute-start.4 = (bf16[16,2048]{1,0:T(8,128)(2,1)S(1)}, bf16[16,2048]{1,0:T(8,128)(2,1)S(1)}, u32[]{:S(2)}, u32[]{:S(2)}) collective-permute-start(bf16[16,2048]{1,0:T(8,128)(2,1)S(1)} %get-tuple-element.39), channel_id=1, source_target_pairs={{0,2},{1,9},{2,0},{3,11},{4,6},{5,13},{6,4},{7,15},{8,10},{9,1},{1... | collective-permute-start | bytes 196616 | tf_op jit(solution)/shard_map/ppermute | solution.py:55
  19.0 0.6 %collective-permute-done.5.arrived_ref = bf16[16,4096]{1,0:T(8,128)(2,1)S(1)} collective-permute-done((bf16[16,4096]{1,0:T(8,128)(2,1)S(1)}, bf16[16,4096]{1,0:T(8,128)(2,1)S(1)}, u32[]{:S(2)}, u32[]{:S(2)}) %collective-permute-start.5) | collective-permute-done | bytes 131104 | tf_op jit(solution)/shard_map/ppermute | solution.py:55
  19.6 0.2 shard_map.101
  19.9 1.9 %collective-permute-done.4.arrived_ref = bf16[16,2048]{1,0:T(8,128)(2,1)S(1)} collective-permute-done((bf16[16,2048]{1,0:T(8,128)(2,1)S(1)}, bf16[16,2048]{1,0:T(8,128)(2,1)S(1)}, u32[]{:S(2)}, u32[]{:S(2)}) %collective-permute-start.4) | collective-permute-done | bytes 65568 | tf_op jit(solution)/shard_map/ppermute | solution.py:55
  21.8 0.2 shard_map.102
  22.0 0.0 collective-permute-start.6
  22.1 0.5 %shard_map.104.rows_ref = bf16[128,4096]{1,0:T(8,128)(2,1)S(1)} custom-call(bf16[16,128]{1,0:T(8,128)(2,1)S(1)} %get-tuple-element.27.code_ref, bf16[16,2048]{1,0:T(8,128)(2,1)S(1)} %get-tuple-element.44.first_ref, bf16[16,2048]{1,0:T(8,128)(2,1)S(1)} %get-tuple-element.45.second_ref), custom_call_target="tpu_custom_call" | custom-call | flops 1000000 | bytes 1048576 | tf_op jit(solution)/shard_map/pallas_call | solution.py:297
  22.5 0.3 %shard_map.103.turned_ref = bf16[512,128]{1,0:T(8,128)(2,1)S(1)} custom-call(bf16[16,4096]{1,0:T(8,128)(2,1)S(1)} %get-tuple-element.37.after_ref.own_ref, bf16[16,4096]{1,0:T(8,128)(2,1)S(1)} %collective-permute-done.5.arrived_ref, f32[1,4096]{1,0:T(1,128)S(1)} %get-tuple-element.43.bias_ref, bf16[128,128]{1,0:T(8,128)(2,1)S(1)} %shard_map.94.after_ref.order_ref), custom_call_target="tpu_custom_call" | custom-call | flops 1000000 | bytes 1048576 | tf_op jit(solution)/shard_map/pallas_call | solution.py:238
  22.8 0.4 %collective-permute-done.6.theirs_ref = f32[16,128]{1,0:T(8,128)S(1)} collective-permute-done((f32[16,128]{1,0:T(8,128)S(1)}, f32[16,128]{1,0:T(8,128)S(1)}, u32[]{:S(2)}, u32[]{:S(2)}) %collective-permute-start.6) | collective-permute-done | bytes 8224 | tf_op jit(solution)/shard_map/ppermute | solution.py:400
  23.2 1.4 %shard_map.105 = (bf16[128,4096]{1,0:T(8,128)(2,1)}, bf16[4096,128]{1,0:T(8,128)(2,1)}, f32[1,128]{1,0:T(1,128)}) custom-call(f32[16,128]{1,0:T(8,128)S(1)} %get-tuple-element.26.raw_ref, f32[16,128]{1,0:T(8,128)S(1)} %get-tuple-element.42.mine_ref, f32[16,128]{1,0:T(8,128)S(1)} %collective-permute-done.6.theirs_ref, ...), custom_call_target="tpu_custom_call" | custom-call | flops 1000000 | bytes 1048576 | tf_op jit(solution)/shard_map/pallas_call | solution.py:354
  (5 shorter events, 0.1 us)
Async XLA Ops:
  0.6 1.5 %copy-start = (bf16[128,4096]{1,0:T(8,128)(2,1)S(1)}, bf16[128,4096]{1,0:T(8,128)(2,1)}, u32[]{:S(2)}) copy-start(bf16[128,4096]{1,0:T(8,128)(2,1)} %rows_ref.7) | copy-start | bytes 3145732
  0.6 1.5 %copy-start.1 = (bf16[2,4096]{1,0:T(2,128)(2,1)S(1)}, bf16[2,4096]{1,0:T(2,128)(2,1)}, u32[]{:S(2)}) copy-start(bf16[2,4096]{1,0:T(2,128)(2,1)} %tokens_ref.1) | copy-start | bytes 49156
  0.7 1.5 %copy-start.2 = (bf16[4096]{0:T(1024)(128)(2,1)S(1)}, bf16[4096]{0:T(1024)(128)(2,1)}, u32[]{:S(2)}) copy-start(bf16[4096]{0:T(1024)(128)(2,1)} %bias_flat.1) | copy-start | bytes 24580
  0.7 1.5 %copy-start.3 = (f32[16,64]{1,0:T(8,128)S(1)}, f32[16,64]{1,0:T(8,128)}, u32[]{:S(2)}) copy-start(f32[16,64]{1,0:T(8,128)} %pre_ref.1) | copy-start | bytes 12292
  0.7 1.5 %copy-start.4 = (s32[16,64]{1,0:T(8,128)S(1)}, s32[16,64]{1,0:T(8,128)}, u32[]{:S(2)}) copy-start(s32[16,64]{1,0:T(8,128)} %top_ref.1) | copy-start | bytes 12292
  2.7 6.5 %collective-permute-start.1 = (bf16[16,2560]{1,0:T(8,128)(2,1)S(1)}, bf16[16,2560]{1,0:T(8,128)(2,1)S(1)}, u32[]{:S(2)}, u32[]{:S(2)}) collective-permute-start(bf16[16,2560]{1,0:T(8,128)(2,1)S(1)} %get-tuple-element.32.own_ref), channel_id=1, source_target_pairs={{0,8},{1,3},{2,10},{3,1},{4,12},{5,7},{6,14},{7,5},{8,0},{9,11},{1... | collective-permute-start | bytes 245768 | tf_op jit(solution)/shard_map/ppermute | solution.py:55
  7.0 5.3 %collective-permute-start = (bf16[16,2048]{1,0:T(8,128)(2,1)S(1)}, bf16[16,2048]{1,0:T(8,128)(2,1)S(1)}, u32[]{:S(2)}, u32[]{:S(2)}) collective-permute-start(bf16[16,2048]{1,0:T(8,128)(2,1)S(1)} %get-tuple-element.30.after_ref.own_ref), channel_id=1, source_target_pairs={{0,8},{1,3},{2,10},{3,1},{4,12},{5,7},{6,14},{7,5},{8,0},{9,11},{1... | collective-permute-start | bytes 196616 | tf_op jit(solution)/shard_map/ppermute | solution.py:55
  9.3 5.3 %collective-permute-start.3 = (bf16[16,3072]{1,0:T(8,128)(2,1)S(1)}, bf16[16,3072]{1,0:T(8,128)(2,1)S(1)}, u32[]{:S(2)}, u32[]{:S(2)}) collective-permute-start(bf16[16,3072]{1,0:T(8,128)(2,1)S(1)} %get-tuple-element.33.after_ref.own_ref), channel_id=1, source_target_pairs={{0,4},{1,5},{2,6},{3,7},{4,0},{5,1},{6,2},{7,3},{8,12},{9,13},{10,... | collective-permute-start | bytes 294920 | tf_op jit(solution)/shard_map/ppermute | solution.py:55
  12.3 5.1 %collective-permute-start.2 = (bf16[16,2048]{1,0:T(8,128)(2,1)S(1)}, bf16[16,2048]{1,0:T(8,128)(2,1)S(1)}, u32[]{:S(2)}, u32[]{:S(2)}) collective-permute-start(bf16[16,2048]{1,0:T(8,128)(2,1)S(1)} %get-tuple-element.35.after_ref.own_ref), channel_id=1, source_target_pairs={{0,4},{1,5},{2,6},{3,7},{4,0},{5,1},{6,2},{7,3},{8,12},{9,13},{10,... | collective-permute-start | bytes 196616 | tf_op jit(solution)/shard_map/ppermute | solution.py:55
  14.6 5.0 %collective-permute-start.5 = (bf16[16,4096]{1,0:T(8,128)(2,1)S(1)}, bf16[16,4096]{1,0:T(8,128)(2,1)S(1)}, u32[]{:S(2)}, u32[]{:S(2)}) collective-permute-start(bf16[16,4096]{1,0:T(8,128)(2,1)S(1)} %get-tuple-element.37.after_ref.own_ref), channel_id=1, source_target_pairs={{0,2},{1,9},{2,0},{3,11},{4,6},{5,13},{6,4},{7,15},{8,10},{9,1},{1... | collective-permute-start | bytes 393224 | tf_op jit(solution)/shard_map/ppermute | solution.py:55
  17.5 4.3 %collective-permute-start.4 = (bf16[16,2048]{1,0:T(8,128)(2,1)S(1)}, bf16[16,2048]{1,0:T(8,128)(2,1)S(1)}, u32[]{:S(2)}, u32[]{:S(2)}) collective-permute-start(bf16[16,2048]{1,0:T(8,128)(2,1)S(1)} %get-tuple-element.39), channel_id=1, source_target_pairs={{0,2},{1,9},{2,0},{3,11},{4,6},{5,13},{6,4},{7,15},{8,10},{9,1},{1... | collective-permute-start | bytes 196616 | tf_op jit(solution)/shard_map/ppermute | solution.py:55
  22.0 1.2 %collective-permute-start.6 = (f32[16,128]{1,0:T(8,128)S(1)}, f32[16,128]{1,0:T(8,128)S(1)}, u32[]{:S(2)}, u32[]{:S(2)}) collective-permute-start(f32[16,128]{1,0:T(8,128)S(1)} %get-tuple-element.42.mine_ref), channel_id=1, source_target_pairs={{0,1},{1,0},{2,3},{3,2},{4,5},{5,4},{6,7},{7,6},{8,9},{9,8},{10,11... | collective-permute-start | bytes 24584 | tf_op jit(solution)/shard_map/ppermute | solution.py:400

commit v26 on v25

--- a/solution.py
+++ b/solution.py
@@ -42,7 +42,8 @@
 
 def bit_of(step, core):
     bits = list(range(feat_bits()))
-    return (bits[::-1] if core == 0 else bits)[step]
+    first = bits[-1:] + bits[:-1]
+    return (first if core == 0 else bits[1:2] + bits[:1] + bits[2:])[step]
 
 
 def swapped(shard, step):

time: 24.8 us -> 24 us (0.968)
  starting transfers between devices: 12.2 us -> 11.8 us
  waiting for transfers between devices: 6.79 us -> 6.4 us
    ppermute x6, starting transfers between devices: 12.2 us -> 11.8 us  [swapped(): return lax.ppermute(shard, ('feat', 'tok'), pairs)]
    ppermute x6, waiting for transfers between devices: 6.36 us -> 5.97 us  [swapped(): return lax.ppermute(shard, ('feat', 'tok'), pairs)]
where the time goes in v26:
time: 24 us; the launch traced here: 23.8 us
  starting transfers between devices  11.8 us (49%)
  waiting for transfers between devices  6.4 us (27%)
  Pallas kernels  3.47 us (14%)
  between operations  2.13 us (9%)
    ppermute x6, starting transfers between devices, swapped(): return lax.ppermute(shard, ('feat', 'tok'), pairs)  11.8 us
    ppermute x6, waiting for transfers between devices, swapped(): return lax.ppermute(shard, ('feat', 'tok'), pairs)  5.97 us
    pallas_call x1, Pallas kernels, final(): kernel_call(functools.partial(final_kernel, rows), (shape(*grad_rows.shap...  1.36 us
    pallas_call x1, Pallas kernels, front(): kernel_call(front_kernel, (shape(count, slots), shape(count, slots, dtype...  0.61 us
  transfers between devices with their start and end apart: 7, of which 6 were waited for; matrix products, arithmetic and copies ran while one was open for 0% of the time, Pallas kernels for 5%

profile of v26, /device:TPU:0, one launch (start us, length us, event | category | flops | bytes accessed | tf_op | source)
XLA Modules:
  0.0 23.8 jit_solution(12604988552571984301)
XLA Ops:
  0.6 0.0 copy-start
  0.6 0.0 copy-start.1
  0.7 0.0 copy-start.2
  0.7 0.0 copy-start.3
  0.7 0.0 copy-start.4
  2.1 0.0 copy-done
  2.1 0.0 copy-done.1
  2.1 0.0 copy-done.2
  2.1 0.0 copy-done.3
  2.1 0.0 copy-done.4
  2.1 0.6 %shard_map.95 = (bf16[16,128]{1,0:T(8,128)(2,1)S(1)}, f32[16,128]{1,0:T(8,128)S(1)}, f32[16,2048]{1,0:T(8,128)S(1)}, bf16[16,2560]{1,0:T(8,128)(2,1)S(1)}, f32[2,4096]{1,0:T(2,128)S(1)}, /*index=5*/f32[1,4096]{1,0:T(1,128)S(1)}) custom-call(bf16[2,4096]{1,0:T(2,128)(2,1)S(1)} %copy-done.1, bf16[4096]{0:T(1024)(128)(2,1)S(1)} %copy-done.2, ...), custom_call_target="tpu_custom_call" | custom-call | flops 1000000 | bytes 1048576 | tf_op jit(solution)/shard_map/pallas_call | solution.py:143
  2.7 4.1 %collective-permute-start.1 = (bf16[16,2560]{1,0:T(8,128)(2,1)S(1)}, bf16[16,2560]{1,0:T(8,128)(2,1)S(1)}, u32[]{:S(2)}, u32[]{:S(2)}) collective-permute-start(bf16[16,2560]{1,0:T(8,128)(2,1)S(1)} %get-tuple-element.32.own_ref), channel_id=1, source_target_pairs={{0,8},{1,5},{2,10},{3,7},{4,12},{5,1},{6,14},{7,3},{8,0},{9,13},{1... | collective-permute-start | bytes 245768 | tf_op jit(solution)/shard_map/ppermute | solution.py:56
  6.8 0.2 shard_map.96
  7.0 0.1 collective-permute-start
  7.1 2.3 %collective-permute-done.1.arrived_ref = bf16[16,2560]{1,0:T(8,128)(2,1)S(1)} collective-permute-done((bf16[16,2560]{1,0:T(8,128)(2,1)S(1)}, bf16[16,2560]{1,0:T(8,128)(2,1)S(1)}, u32[]{:S(2)}, u32[]{:S(2)}) %collective-permute-start.1) | collective-permute-done | bytes 81952 | tf_op jit(solution)/shard_map/ppermute | solution.py:56
  9.4 1.9 %collective-permute-start.3 = (bf16[16,3072]{1,0:T(8,128)(2,1)S(1)}, bf16[16,3072]{1,0:T(8,128)(2,1)S(1)}, u32[]{:S(2)}, u32[]{:S(2)}) collective-permute-start(bf16[16,3072]{1,0:T(8,128)(2,1)S(1)} %get-tuple-element.33.after_ref.own_ref), channel_id=1, source_target_pairs={{0,2},{1,3},{2,0},{3,1},{4,6},{5,7},{6,4},{7,5},{8,10},{9,11},{10,... | collective-permute-start | bytes 294920 | tf_op jit(solution)/shard_map/ppermute | solution.py:56
  11.3 1.0 %collective-permute-done.arrived_ref = bf16[16,2048]{1,0:T(8,128)(2,1)S(1)} collective-permute-done((bf16[16,2048]{1,0:T(8,128)(2,1)S(1)}, bf16[16,2048]{1,0:T(8,128)(2,1)S(1)}, u32[]{:S(2)}, u32[]{:S(2)}) %collective-permute-start) | collective-permute-done | bytes 65568 | tf_op jit(solution)/shard_map/ppermute | solution.py:56
  12.3 1.6 %collective-permute-start.2 = (bf16[16,2048]{1,0:T(8,128)(2,1)S(1)}, bf16[16,2048]{1,0:T(8,128)(2,1)S(1)}, u32[]{:S(2)}, u32[]{:S(2)}) collective-permute-start(bf16[16,2048]{1,0:T(8,128)(2,1)S(1)} %get-tuple-element.35.after_ref.own_ref), channel_id=1, source_target_pairs={{0,2},{1,3},{2,0},{3,1},{4,6},{5,7},{6,4},{7,5},{8,10},{9,11},{10,... | collective-permute-start | bytes 196616 | tf_op jit(solution)/shard_map/ppermute | solution.py:56
  13.8 0.2 %collective-permute-done.3.arrived_ref = bf16[16,3072]{1,0:T(8,128)(2,1)S(1)} collective-permute-done((bf16[16,3072]{1,0:T(8,128)(2,1)S(1)}, bf16[16,3072]{1,0:T(8,128)(2,1)S(1)}, u32[]{:S(2)}, u32[]{:S(2)}) %collective-permute-start.3) | collective-permute-done | bytes 98336 | tf_op jit(solution)/shard_map/ppermute | solution.py:56
  14.1 2.5 %collective-permute-start.5 = (bf16[16,4096]{1,0:T(8,128)(2,1)S(1)}, bf16[16,4096]{1,0:T(8,128)(2,1)S(1)}, u32[]{:S(2)}, u32[]{:S(2)}) collective-permute-start(bf16[16,4096]{1,0:T(8,128)(2,1)S(1)} %get-tuple-element.37.after_ref.own_ref), channel_id=1, source_target_pairs={{0,4},{1,9},{2,6},{3,11},{4,0},{5,13},{6,2},{7,15},{8,12},{9,1},{1... | collective-permute-start | bytes 393224 | tf_op jit(solution)/shard_map/ppermute | solution.py:56
  16.6 0.0 collective-permute-done.2.arrived_ref
  16.7 1.6 %collective-permute-start.4 = (bf16[16,2048]{1,0:T(8,128)(2,1)S(1)}, bf16[16,2048]{1,0:T(8,128)(2,1)S(1)}, u32[]{:S(2)}, u32[]{:S(2)}) collective-permute-start(bf16[16,2048]{1,0:T(8,128)(2,1)S(1)} %get-tuple-element.39), channel_id=1, source_target_pairs={{0,4},{1,9},{2,6},{3,11},{4,0},{5,13},{6,2},{7,15},{8,12},{9,1},{1... | collective-permute-start | bytes 196616 | tf_op jit(solution)/shard_map/ppermute | solution.py:56
  18.3 1.3 %collective-permute-done.5.arrived_ref = bf16[16,4096]{1,0:T(8,128)(2,1)S(1)} collective-permute-done((bf16[16,4096]{1,0:T(8,128)(2,1)S(1)}, bf16[16,4096]{1,0:T(8,128)(2,1)S(1)}, u32[]{:S(2)}, u32[]{:S(2)}) %collective-permute-start.5) | collective-permute-done | bytes 131104 | tf_op jit(solution)/shard_map/ppermute | solution.py:56
  19.6 0.2 %shard_map.101 = (bf16[16,2048]{1,0:T(8,128)(2,1)S(1)}, f32[16,128]{1,0:T(8,128)S(1)}) custom-call(f32[16,2048]{1,0:T(8,128)S(1)} %get-tuple-element.40.total_ref, bf16[16,4096]{1,0:T(8,128)(2,1)S(1)} %collective-permute-done.5.arrived_ref, bf16[128,4096]{1,0:T(8,128)(2,1)S(1)} %copy-done), custom_call_target="tpu_custom_call" | custom-call | flops 1000000 | bytes 1048576 | tf_op jit(solution)/shard_map/pallas_call | solution.py:276
  19.8 1.2 %collective-permute-done.4.arrived_ref = bf16[16,2048]{1,0:T(8,128)(2,1)S(1)} collective-permute-done((bf16[16,2048]{1,0:T(8,128)(2,1)S(1)}, bf16[16,2048]{1,0:T(8,128)(2,1)S(1)}, u32[]{:S(2)}, u32[]{:S(2)}) %collective-permute-start.4) | collective-permute-done | bytes 65568 | tf_op jit(solution)/shard_map/ppermute | solution.py:56
  21.0 0.2 shard_map.102
  21.2 0.0 collective-permute-start.6
  21.3 0.5 %shard_map.104.rows_ref = bf16[128,4096]{1,0:T(8,128)(2,1)S(1)} custom-call(bf16[16,128]{1,0:T(8,128)(2,1)S(1)} %get-tuple-element.27.code_ref, bf16[16,2048]{1,0:T(8,128)(2,1)S(1)} %get-tuple-element.44.first_ref, bf16[16,2048]{1,0:T(8,128)(2,1)S(1)} %get-tuple-element.45.second_ref), custom_call_target="tpu_custom_call" | custom-call | flops 1000000 | bytes 1048576 | tf_op jit(solution)/shard_map/pallas_call | solution.py:298
  21.7 0.3 %shard_map.103.turned_ref = bf16[512,128]{1,0:T(8,128)(2,1)S(1)} custom-call(bf16[16,4096]{1,0:T(8,128)(2,1)S(1)} %get-tuple-element.37.after_ref.own_ref, bf16[16,4096]{1,0:T(8,128)(2,1)S(1)} %collective-permute-done.5.arrived_ref, f32[1,4096]{1,0:T(1,128)S(1)} %get-tuple-element.43.bias_ref, bf16[128,128]{1,0:T(8,128)(2,1)S(1)} %shard_map.94.after_ref.order_ref), custom_call_target="tpu_custom_call" | custom-call | flops 1000000 | bytes 1048576 | tf_op jit(solution)/shard_map/pallas_call | solution.py:239
  22.0 0.4 %collective-permute-done.6.theirs_ref = f32[16,128]{1,0:T(8,128)S(1)} collective-permute-done((f32[16,128]{1,0:T(8,128)S(1)}, f32[16,128]{1,0:T(8,128)S(1)}, u32[]{:S(2)}, u32[]{:S(2)}) %collective-permute-start.6) | collective-permute-done | bytes 8224 | tf_op jit(solution)/shard_map/ppermute | solution.py:401
  22.4 1.4 %shard_map.105 = (bf16[128,4096]{1,0:T(8,128)(2,1)}, bf16[4096,128]{1,0:T(8,128)(2,1)}, f32[1,128]{1,0:T(1,128)}) custom-call(f32[16,128]{1,0:T(8,128)S(1)} %get-tuple-element.26.raw_ref, f32[16,128]{1,0:T(8,128)S(1)} %get-tuple-element.42.mine_ref, f32[16,128]{1,0:T(8,128)S(1)} %collective-permute-done.6.theirs_ref, ...), custom_call_target="tpu_custom_call" | custom-call | flops 1000000 | bytes 1048576 | tf_op jit(solution)/shard_map/pallas_call | solution.py:355
  (5 shorter events, 0.1 us)
Async XLA Ops:
  0.6 1.5 %copy-start = (bf16[128,4096]{1,0:T(8,128)(2,1)S(1)}, bf16[128,4096]{1,0:T(8,128)(2,1)}, u32[]{:S(2)}) copy-start(bf16[128,4096]{1,0:T(8,128)(2,1)} %rows_ref.7) | copy-start | bytes 3145732
  0.6 1.5 %copy-start.1 = (bf16[2,4096]{1,0:T(2,128)(2,1)S(1)}, bf16[2,4096]{1,0:T(2,128)(2,1)}, u32[]{:S(2)}) copy-start(bf16[2,4096]{1,0:T(2,128)(2,1)} %tokens_ref.1) | copy-start | bytes 49156
  0.7 1.5 %copy-start.2 = (bf16[4096]{0:T(1024)(128)(2,1)S(1)}, bf16[4096]{0:T(1024)(128)(2,1)}, u32[]{:S(2)}) copy-start(bf16[4096]{0:T(1024)(128)(2,1)} %bias_flat.1) | copy-start | bytes 24580
  0.7 1.5 %copy-start.3 = (f32[16,64]{1,0:T(8,128)S(1)}, f32[16,64]{1,0:T(8,128)}, u32[]{:S(2)}) copy-start(f32[16,64]{1,0:T(8,128)} %pre_ref.1) | copy-start | bytes 12292
  0.7 1.5 %copy-start.4 = (s32[16,64]{1,0:T(8,128)S(1)}, s32[16,64]{1,0:T(8,128)}, u32[]{:S(2)}) copy-start(s32[16,64]{1,0:T(8,128)} %top_ref.1) | copy-start | bytes 12292
  2.7 6.6 %collective-permute-start.1 = (bf16[16,2560]{1,0:T(8,128)(2,1)S(1)}, bf16[16,2560]{1,0:T(8,128)(2,1)S(1)}, u32[]{:S(2)}, u32[]{:S(2)}) collective-permute-start(bf16[16,2560]{1,0:T(8,128)(2,1)S(1)} %get-tuple-element.32.own_ref), channel_id=1, source_target_pairs={{0,8},{1,5},{2,10},{3,7},{4,12},{5,1},{6,14},{7,3},{8,0},{9,13},{1... | collective-permute-start | bytes 245768 | tf_op jit(solution)/shard_map/ppermute | solution.py:56
  7.0 5.2 %collective-permute-start = (bf16[16,2048]{1,0:T(8,128)(2,1)S(1)}, bf16[16,2048]{1,0:T(8,128)(2,1)S(1)}, u32[]{:S(2)}, u32[]{:S(2)}) collective-permute-start(bf16[16,2048]{1,0:T(8,128)(2,1)S(1)} %get-tuple-element.30.after_ref.own_ref), channel_id=1, source_target_pairs={{0,8},{1,5},{2,10},{3,7},{4,12},{5,1},{6,14},{7,3},{8,0},{9,13},{1... | collective-permute-start | bytes 196616 | tf_op jit(solution)/shard_map/ppermute | solution.py:56
  9.4 4.7 %collective-permute-start.3 = (bf16[16,3072]{1,0:T(8,128)(2,1)S(1)}, bf16[16,3072]{1,0:T(8,128)(2,1)S(1)}, u32[]{:S(2)}, u32[]{:S(2)}) collective-permute-start(bf16[16,3072]{1,0:T(8,128)(2,1)S(1)} %get-tuple-element.33.after_ref.own_ref), channel_id=1, source_target_pairs={{0,2},{1,3},{2,0},{3,1},{4,6},{5,7},{6,4},{7,5},{8,10},{9,11},{10,... | collective-permute-start | bytes 294920 | tf_op jit(solution)/shard_map/ppermute | solution.py:56
  12.3 4.4 %collective-permute-start.2 = (bf16[16,2048]{1,0:T(8,128)(2,1)S(1)}, bf16[16,2048]{1,0:T(8,128)(2,1)S(1)}, u32[]{:S(2)}, u32[]{:S(2)}) collective-permute-start(bf16[16,2048]{1,0:T(8,128)(2,1)S(1)} %get-tuple-element.35.after_ref.own_ref), channel_id=1, source_target_pairs={{0,2},{1,3},{2,0},{3,1},{4,6},{5,7},{6,4},{7,5},{8,10},{9,11},{10,... | collective-permute-start | bytes 196616 | tf_op jit(solution)/shard_map/ppermute | solution.py:56
  14.1 5.5 %collective-permute-start.5 = (bf16[16,4096]{1,0:T(8,128)(2,1)S(1)}, bf16[16,4096]{1,0:T(8,128)(2,1)S(1)}, u32[]{:S(2)}, u32[]{:S(2)}) collective-permute-start(bf16[16,4096]{1,0:T(8,128)(2,1)S(1)} %get-tuple-element.37.after_ref.own_ref), channel_id=1, source_target_pairs={{0,4},{1,9},{2,6},{3,11},{4,0},{5,13},{6,2},{7,15},{8,12},{9,1},{1... | collective-permute-start | bytes 393224 | tf_op jit(solution)/shard_map/ppermute | solution.py:56
  16.7 4.3 %collective-permute-start.4 = (bf16[16,2048]{1,0:T(8,128)(2,1)S(1)}, bf16[16,2048]{1,0:T(8,128)(2,1)S(1)}, u32[]{:S(2)}, u32[]{:S(2)}) collective-permute-start(bf16[16,2048]{1,0:T(8,128)(2,1)S(1)} %get-tuple-element.39), channel_id=1, source_target_pairs={{0,4},{1,9},{2,6},{3,11},{4,0},{5,13},{6,2},{7,15},{8,12},{9,1},{1... | collective-permute-start | bytes 196616 | tf_op jit(solution)/shard_map/ppermute | solution.py:56
  21.2 1.2 %collective-permute-start.6 = (f32[16,128]{1,0:T(8,128)S(1)}, f32[16,128]{1,0:T(8,128)S(1)}, u32[]{:S(2)}, u32[]{:S(2)}) collective-permute-start(f32[16,128]{1,0:T(8,128)S(1)} %get-tuple-element.42.mine_ref), channel_id=1, source_target_pairs={{0,1},{1,0},{2,3},{3,2},{4,5},{5,4},{6,7},{7,6},{8,9},{9,8},{10,11... | collective-permute-start | bytes 24584 | tf_op jit(solution)/shard_map/ppermute | solution.py:401

commit v27 on v26

--- a/solution.py
+++ b/solution.py
@@ -33,7 +33,7 @@
 
 
 def first_width(width):
-    return width // 2
+    return width * 7 // 16 // 128 * 128
 
 
 def feat_bits():

time: 24 us -> 24.2 us (level)
  waiting for transfers between devices: 6.4 us -> 6.82 us
    ppermute x6, waiting for transfers between devices: 5.97 us -> 6.39 us  [swapped(): return lax.ppermute(shard, ('feat', 'tok'), pairs)]
  transfers between devices with their start and end apart: 7 -> 7, of which waited for: 6 -> 7; matrix products, arithmetic and copies ran while one was open for 0% -> 0% of each run, Pallas kernels for 5% -> 5%
where the time goes in v27:
time: 24.2 us; the launch traced here: 24.1 us
  starting transfers between devices  11.6 us (48%)
  waiting for transfers between devices  6.82 us (28%)
  Pallas kernels  3.47 us (14%)
  between operations  2.13 us (9%)
    ppermute x6, starting transfers between devices, swapped(): return lax.ppermute(shard, ('feat', 'tok'), pairs)  11.6 us
    ppermute x6, waiting for transfers between devices, swapped(): return lax.ppermute(shard, ('feat', 'tok'), pairs)  6.39 us
    pallas_call x1, Pallas kernels, final(): kernel_call(functools.partial(final_kernel, rows), (shape(*grad_rows.shap...  1.36 us
    pallas_call x1, Pallas kernels, front(): kernel_call(front_kernel, (shape(count, slots), shape(count, slots, dtype...  0.61 us
  transfers between devices with their start and end apart: 7, of which 7 were waited for; matrix products, arithmetic and copies ran while one was open for 0% of the time, Pallas kernels for 5%

profile of v27, /device:TPU:0, one launch (start us, length us, event | category | flops | bytes accessed | tf_op | source)
XLA Modules:
  0.0 24.1 jit_solution(15453684340015010359)
XLA Ops:
  0.6 0.0 copy-start
  0.6 0.0 copy-start.1
  0.7 0.0 copy-start.2
  0.7 0.0 copy-start.3
  0.7 0.0 copy-start.4
  2.1 0.0 copy-done
  2.1 0.0 copy-done.1
  2.1 0.0 copy-done.2
  2.1 0.0 copy-done.3
  2.1 0.0 copy-done.4
  2.1 0.6 %shard_map.95 = (bf16[16,128]{1,0:T(8,128)(2,1)S(1)}, f32[16,128]{1,0:T(8,128)S(1)}, f32[16,1792]{1,0:T(8,128)S(1)}, bf16[16,2304]{1,0:T(8,128)(2,1)S(1)}, f32[2,4096]{1,0:T(2,128)S(1)}, /*index=5*/f32[1,4096]{1,0:T(1,128)S(1)}) custom-call(bf16[2,4096]{1,0:T(2,128)(2,1)S(1)} %copy-done.1, bf16[4096]{0:T(1024)(128)(2,1)S(1)} %copy-done.2, ...), custom_call_target="tpu_custom_call" | custom-call | flops 1000000 | bytes 1048576 | tf_op jit(solution)/shard_map/pallas_call | solution.py:143
  2.7 4.1 %collective-permute-start.1 = (bf16[16,2304]{1,0:T(8,128)(2,1)S(1)}, bf16[16,2304]{1,0:T(8,128)(2,1)S(1)}, u32[]{:S(2)}, u32[]{:S(2)}) collective-permute-start(bf16[16,2304]{1,0:T(8,128)(2,1)S(1)} %get-tuple-element.32.own_ref), channel_id=1, source_target_pairs={{0,8},{1,5},{2,10},{3,7},{4,12},{5,1},{6,14},{7,3},{8,0},{9,13},{1... | collective-permute-start | bytes 221192 | tf_op jit(solution)/shard_map/ppermute | solution.py:56
  6.8 0.2 shard_map.96
  7.0 0.1 collective-permute-start
  7.1 2.2 %collective-permute-done.1.arrived_ref = bf16[16,2304]{1,0:T(8,128)(2,1)S(1)} collective-permute-done((bf16[16,2304]{1,0:T(8,128)(2,1)S(1)}, bf16[16,2304]{1,0:T(8,128)(2,1)S(1)}, u32[]{:S(2)}, u32[]{:S(2)}) %collective-permute-start.1) | collective-permute-done | bytes 73760 | tf_op jit(solution)/shard_map/ppermute | solution.py:56
  9.3 1.9 %collective-permute-start.3 = (bf16[16,2816]{1,0:T(8,128)(2,1)S(1)}, bf16[16,2816]{1,0:T(8,128)(2,1)S(1)}, u32[]{:S(2)}, u32[]{:S(2)}) collective-permute-start(bf16[16,2816]{1,0:T(8,128)(2,1)S(1)} %get-tuple-element.33.after_ref.own_ref), channel_id=1, source_target_pairs={{0,2},{1,3},{2,0},{3,1},{4,6},{5,7},{6,4},{7,5},{8,10},{9,11},{10,... | collective-permute-start | bytes 270344 | tf_op jit(solution)/shard_map/ppermute | solution.py:56
  11.2 1.2 %collective-permute-done.arrived_ref = bf16[16,2304]{1,0:T(8,128)(2,1)S(1)} collective-permute-done((bf16[16,2304]{1,0:T(8,128)(2,1)S(1)}, bf16[16,2304]{1,0:T(8,128)(2,1)S(1)}, u32[]{:S(2)}, u32[]{:S(2)}) %collective-permute-start) | collective-permute-done | bytes 73760 | tf_op jit(solution)/shard_map/ppermute | solution.py:56
  12.4 1.6 %collective-permute-start.2 = (bf16[16,2304]{1,0:T(8,128)(2,1)S(1)}, bf16[16,2304]{1,0:T(8,128)(2,1)S(1)}, u32[]{:S(2)}, u32[]{:S(2)}) collective-permute-start(bf16[16,2304]{1,0:T(8,128)(2,1)S(1)} %get-tuple-element.35.after_ref.own_ref), channel_id=1, source_target_pairs={{0,2},{1,3},{2,0},{3,1},{4,6},{5,7},{6,4},{7,5},{8,10},{9,11},{10,... | collective-permute-start | bytes 221192 | tf_op jit(solution)/shard_map/ppermute | solution.py:56
  13.9 0.1 collective-permute-done.3.arrived_ref
  14.1 2.4 %collective-permute-start.5 = (bf16[16,3840]{1,0:T(8,128)(2,1)S(1)}, bf16[16,3840]{1,0:T(8,128)(2,1)S(1)}, u32[]{:S(2)}, u32[]{:S(2)}) collective-permute-start(bf16[16,3840]{1,0:T(8,128)(2,1)S(1)} %get-tuple-element.37.after_ref.own_ref), channel_id=1, source_target_pairs={{0,4},{1,9},{2,6},{3,11},{4,0},{5,13},{6,2},{7,15},{8,12},{9,1},{1... | collective-permute-start | bytes 368648 | tf_op jit(solution)/shard_map/ppermute | solution.py:56
  16.5 0.3 %collective-permute-done.2.arrived_ref = bf16[16,2304]{1,0:T(8,128)(2,1)S(1)} collective-permute-done((bf16[16,2304]{1,0:T(8,128)(2,1)S(1)}, bf16[16,2304]{1,0:T(8,128)(2,1)S(1)}, u32[]{:S(2)}, u32[]{:S(2)}) %collective-permute-start.2) | collective-permute-done | bytes 73760 | tf_op jit(solution)/shard_map/ppermute | solution.py:56
  16.8 1.6 %collective-permute-start.4 = (bf16[16,2304]{1,0:T(8,128)(2,1)S(1)}, bf16[16,2304]{1,0:T(8,128)(2,1)S(1)}, u32[]{:S(2)}, u32[]{:S(2)}) collective-permute-start(bf16[16,2304]{1,0:T(8,128)(2,1)S(1)} %get-tuple-element.39), channel_id=1, source_target_pairs={{0,4},{1,9},{2,6},{3,11},{4,0},{5,13},{6,2},{7,15},{8,12},{9,1},{1... | collective-permute-start | bytes 221192 | tf_op jit(solution)/shard_map/ppermute | solution.py:56
  18.5 0.9 %collective-permute-done.5.arrived_ref = bf16[16,3840]{1,0:T(8,128)(2,1)S(1)} collective-permute-done((bf16[16,3840]{1,0:T(8,128)(2,1)S(1)}, bf16[16,3840]{1,0:T(8,128)(2,1)S(1)}, u32[]{:S(2)}, u32[]{:S(2)}) %collective-permute-start.5) | collective-permute-done | bytes 122912 | tf_op jit(solution)/shard_map/ppermute | solution.py:56
  19.3 0.2 shard_map.101
  19.5 1.7 %collective-permute-done.4.arrived_ref = bf16[16,2304]{1,0:T(8,128)(2,1)S(1)} collective-permute-done((bf16[16,2304]{1,0:T(8,128)(2,1)S(1)}, bf16[16,2304]{1,0:T(8,128)(2,1)S(1)}, u32[]{:S(2)}, u32[]{:S(2)}) %collective-permute-start.4) | collective-permute-done | bytes 73760 | tf_op jit(solution)/shard_map/ppermute | solution.py:56
  21.2 0.3 %shard_map.102 = (bf16[16,2304]{1,0:T(8,128)(2,1)S(1)}, f32[16,128]{1,0:T(8,128)S(1)}) custom-call(f32[16,2304]{1,0:T(8,128)S(1)} %get-tuple-element.38.total_ref, bf16[16,2304]{1,0:T(8,128)(2,1)S(1)} %collective-permute-done.4.arrived_ref, bf16[128,4096]{1,0:T(8,128)(2,1)S(1)} %copy-done, f32[16,128]{1,0:T(8,128)S(1)} %get-tuple-element.41.first_ref), custom_call_target="tpu_custom_call" | custom-call | flops 1000000 | bytes 1048576 | tf_op jit(solution)/shard_map/pallas_call | solution.py:276
  21.5 0.0 collective-permute-start.6
  21.5 0.5 %shard_map.104.rows_ref = bf16[128,4096]{1,0:T(8,128)(2,1)S(1)} custom-call(bf16[16,128]{1,0:T(8,128)(2,1)S(1)} %get-tuple-element.27.code_ref, bf16[16,1792]{1,0:T(8,128)(2,1)S(1)} %get-tuple-element.44.first_ref, bf16[16,2304]{1,0:T(8,128)(2,1)S(1)} %get-tuple-element.45.second_ref), custom_call_target="tpu_custom_call" | custom-call | flops 1000000 | bytes 1048576 | tf_op jit(solution)/shard_map/pallas_call | solution.py:298
  22.0 0.3 %shard_map.103.turned_ref = bf16[512,128]{1,0:T(8,128)(2,1)S(1)} custom-call(bf16[16,3840]{1,0:T(8,128)(2,1)S(1)} %get-tuple-element.37.after_ref.own_ref, bf16[16,3840]{1,0:T(8,128)(2,1)S(1)} %collective-permute-done.5.arrived_ref, f32[1,4096]{1,0:T(1,128)S(1)} %get-tuple-element.43.bias_ref, bf16[128,128]{1,0:T(8,128)(2,1)S(1)} %shard_map.94.after_ref.order_ref), custom_call_target="tpu_custom_call" | custom-call | flops 1000000 | bytes 1048576 | tf_op jit(solution)/shard_map/pallas_call | solution.py:239
  22.3 0.4 %collective-permute-done.6.theirs_ref = f32[16,128]{1,0:T(8,128)S(1)} collective-permute-done((f32[16,128]{1,0:T(8,128)S(1)}, f32[16,128]{1,0:T(8,128)S(1)}, u32[]{:S(2)}, u32[]{:S(2)}) %collective-permute-start.6) | collective-permute-done | bytes 8224 | tf_op jit(solution)/shard_map/ppermute | solution.py:401
  22.7 1.4 %shard_map.105 = (bf16[128,4096]{1,0:T(8,128)(2,1)}, bf16[4096,128]{1,0:T(8,128)(2,1)}, f32[1,128]{1,0:T(1,128)}) custom-call(f32[16,128]{1,0:T(8,128)S(1)} %get-tuple-element.26.raw_ref, f32[16,128]{1,0:T(8,128)S(1)} %get-tuple-element.42.mine_ref, f32[16,128]{1,0:T(8,128)S(1)} %collective-permute-done.6.theirs_ref, ...), custom_call_target="tpu_custom_call" | custom-call | flops 1000000 | bytes 1048576 | tf_op jit(solution)/shard_map/pallas_call | solution.py:355
  (5 shorter events, 0.1 us)
Async XLA Ops:
  0.6 1.5 %copy-start = (bf16[128,4096]{1,0:T(8,128)(2,1)S(1)}, bf16[128,4096]{1,0:T(8,128)(2,1)}, u32[]{:S(2)}) copy-start(bf16[128,4096]{1,0:T(8,128)(2,1)} %rows_ref.7) | copy-start | bytes 3145732
  0.6 1.5 %copy-start.1 = (bf16[2,4096]{1,0:T(2,128)(2,1)S(1)}, bf16[2,4096]{1,0:T(2,128)(2,1)}, u32[]{:S(2)}) copy-start(bf16[2,4096]{1,0:T(2,128)(2,1)} %tokens_ref.1) | copy-start | bytes 49156
  0.7 1.5 %copy-start.2 = (bf16[4096]{0:T(1024)(128)(2,1)S(1)}, bf16[4096]{0:T(1024)(128)(2,1)}, u32[]{:S(2)}) copy-start(bf16[4096]{0:T(1024)(128)(2,1)} %bias_flat.1) | copy-start | bytes 24580
  0.7 1.5 %copy-start.3 = (f32[16,64]{1,0:T(8,128)S(1)}, f32[16,64]{1,0:T(8,128)}, u32[]{:S(2)}) copy-start(f32[16,64]{1,0:T(8,128)} %pre_ref.1) | copy-start | bytes 12292
  0.7 1.5 %copy-start.4 = (s32[16,64]{1,0:T(8,128)S(1)}, s32[16,64]{1,0:T(8,128)}, u32[]{:S(2)}) copy-start(s32[16,64]{1,0:T(8,128)} %top_ref.1) | copy-start | bytes 12292
  2.7 6.5 %collective-permute-start.1 = (bf16[16,2304]{1,0:T(8,128)(2,1)S(1)}, bf16[16,2304]{1,0:T(8,128)(2,1)S(1)}, u32[]{:S(2)}, u32[]{:S(2)}) collective-permute-start(bf16[16,2304]{1,0:T(8,128)(2,1)S(1)} %get-tuple-element.32.own_ref), channel_id=1, source_target_pairs={{0,8},{1,5},{2,10},{3,7},{4,12},{5,1},{6,14},{7,3},{8,0},{9,13},{1... | collective-permute-start | bytes 221192 | tf_op jit(solution)/shard_map/ppermute | solution.py:56
  7.0 5.3 %collective-permute-start = (bf16[16,2304]{1,0:T(8,128)(2,1)S(1)}, bf16[16,2304]{1,0:T(8,128)(2,1)S(1)}, u32[]{:S(2)}, u32[]{:S(2)}) collective-permute-start(bf16[16,2304]{1,0:T(8,128)(2,1)S(1)} %get-tuple-element.30.after_ref.own_ref), channel_id=1, source_target_pairs={{0,8},{1,5},{2,10},{3,7},{4,12},{5,1},{6,14},{7,3},{8,0},{9,13},{1... | collective-permute-start | bytes 221192 | tf_op jit(solution)/shard_map/ppermute | solution.py:56
  9.3 4.8 %collective-permute-start.3 = (bf16[16,2816]{1,0:T(8,128)(2,1)S(1)}, bf16[16,2816]{1,0:T(8,128)(2,1)S(1)}, u32[]{:S(2)}, u32[]{:S(2)}) collective-permute-start(bf16[16,2816]{1,0:T(8,128)(2,1)S(1)} %get-tuple-element.33.after_ref.own_ref), channel_id=1, source_target_pairs={{0,2},{1,3},{2,0},{3,1},{4,6},{5,7},{6,4},{7,5},{8,10},{9,11},{10,... | collective-permute-start | bytes 270344 | tf_op jit(solution)/shard_map/ppermute | solution.py:56
  12.4 4.4 %collective-permute-start.2 = (bf16[16,2304]{1,0:T(8,128)(2,1)S(1)}, bf16[16,2304]{1,0:T(8,128)(2,1)S(1)}, u32[]{:S(2)}, u32[]{:S(2)}) collective-permute-start(bf16[16,2304]{1,0:T(8,128)(2,1)S(1)} %get-tuple-element.35.after_ref.own_ref), channel_id=1, source_target_pairs={{0,2},{1,3},{2,0},{3,1},{4,6},{5,7},{6,4},{7,5},{8,10},{9,11},{10,... | collective-permute-start | bytes 221192 | tf_op jit(solution)/shard_map/ppermute | solution.py:56
  14.1 5.2 %collective-permute-start.5 = (bf16[16,3840]{1,0:T(8,128)(2,1)S(1)}, bf16[16,3840]{1,0:T(8,128)(2,1)S(1)}, u32[]{:S(2)}, u32[]{:S(2)}) collective-permute-start(bf16[16,3840]{1,0:T(8,128)(2,1)S(1)} %get-tuple-element.37.after_ref.own_ref), channel_id=1, source_target_pairs={{0,4},{1,9},{2,6},{3,11},{4,0},{5,13},{6,2},{7,15},{8,12},{9,1},{1... | collective-permute-start | bytes 368648 | tf_op jit(solution)/shard_map/ppermute | solution.py:56
  16.8 4.4 %collective-permute-start.4 = (bf16[16,2304]{1,0:T(8,128)(2,1)S(1)}, bf16[16,2304]{1,0:T(8,128)(2,1)S(1)}, u32[]{:S(2)}, u32[]{:S(2)}) collective-permute-start(bf16[16,2304]{1,0:T(8,128)(2,1)S(1)} %get-tuple-element.39), channel_id=1, source_target_pairs={{0,4},{1,9},{2,6},{3,11},{4,0},{5,13},{6,2},{7,15},{8,12},{9,1},{1... | collective-permute-start | bytes 221192 | tf_op jit(solution)/shard_map/ppermute | solution.py:56
  21.5 1.2 %collective-permute-start.6 = (f32[16,128]{1,0:T(8,128)S(1)}, f32[16,128]{1,0:T(8,128)S(1)}, u32[]{:S(2)}, u32[]{:S(2)}) collective-permute-start(f32[16,128]{1,0:T(8,128)S(1)} %get-tuple-element.42.mine_ref), channel_id=1, source_target_pairs={{0,1},{1,0},{2,3},{3,2},{4,5},{5,4},{6,7},{7,6},{8,9},{9,8},{10,11... | collective-permute-start | bytes 24584 | tf_op jit(solution)/shard_map/ppermute | solution.py:401

commit v28 on v27

--- a/solution.py
+++ b/solution.py
@@ -33,7 +33,7 @@
 
 
 def first_width(width):
-    return width * 7 // 16 // 128 * 128
+    return width * 9 // 16 // 128 * 128
 
 
 def feat_bits():

time: 24.2 us -> 24.1 us (level)
  transfers between devices with their start and end apart: 7 -> 7, of which waited for: 7 -> 6; matrix products, arithmetic and copies ran while one was open for 0% -> 0% of each run, Pallas kernels for 5% -> 5%
where the time goes in v28:
time: 24.1 us; the launch traced here: 23.9 us
  starting transfers between devices  11.4 us (47%)
  waiting for transfers between devices  6.86 us (28%)
  Pallas kernels  3.47 us (14%)
  between operations  2.13 us (9%)
    ppermute x6, starting transfers between devices, swapped(): return lax.ppermute(shard, ('feat', 'tok'), pairs)  11.4 us
    ppermute x6, waiting for transfers between devices, swapped(): return lax.ppermute(shard, ('feat', 'tok'), pairs)  6.43 us
    pallas_call x1, Pallas kernels, final(): kernel_call(functools.partial(final_kernel, rows), (shape(*grad_rows.shap...  1.36 us
    pallas_call x1, Pallas kernels, front(): kernel_call(front_kernel, (shape(count, slots), shape(count, slots, dtype...  0.62 us
  transfers between devices with their start and end apart: 7, of which 6 were waited for; matrix products, arithmetic and copies ran while one was open for 0% of the time, Pallas kernels for 5%

profile of v28, /device:TPU:0, one launch (start us, length us, event | category | flops | bytes accessed | tf_op | source)
XLA Modules:
  0.0 23.9 jit_solution(949904961462190834)
XLA Ops:
  0.6 0.0 copy-start
  0.6 0.0 copy-start.1
  0.7 0.0 copy-start.2
  0.7 0.0 copy-start.3
  0.7 0.0 copy-start.4
  2.1 0.0 copy-done
  2.1 0.0 copy-done.1
  2.1 0.0 copy-done.2
  2.1 0.0 copy-done.3
  2.1 0.0 copy-done.4
  2.1 0.6 %shard_map.95 = (bf16[16,128]{1,0:T(8,128)(2,1)S(1)}, f32[16,128]{1,0:T(8,128)S(1)}, f32[16,2304]{1,0:T(8,128)S(1)}, bf16[16,2816]{1,0:T(8,128)(2,1)S(1)}, f32[2,4096]{1,0:T(2,128)S(1)}, /*index=5*/f32[1,4096]{1,0:T(1,128)S(1)}) custom-call(bf16[2,4096]{1,0:T(2,128)(2,1)S(1)} %copy-done.1, bf16[4096]{0:T(1024)(128)(2,1)S(1)} %copy-done.2, ...), custom_call_target="tpu_custom_call" | custom-call | flops 1000000 | bytes 1048576 | tf_op jit(solution)/shard_map/pallas_call | solution.py:143
  2.8 4.1 %collective-permute-start.1 = (bf16[16,2816]{1,0:T(8,128)(2,1)S(1)}, bf16[16,2816]{1,0:T(8,128)(2,1)S(1)}, u32[]{:S(2)}, u32[]{:S(2)}) collective-permute-start(bf16[16,2816]{1,0:T(8,128)(2,1)S(1)} %get-tuple-element.32.own_ref), channel_id=1, source_target_pairs={{0,8},{1,5},{2,10},{3,7},{4,12},{5,1},{6,14},{7,3},{8,0},{9,13},{1... | collective-permute-start | bytes 270344 | tf_op jit(solution)/shard_map/ppermute | solution.py:56
  6.9 0.2 shard_map.96
  7.0 0.1 collective-permute-start
  7.1 2.4 %collective-permute-done.1.arrived_ref = bf16[16,2816]{1,0:T(8,128)(2,1)S(1)} collective-permute-done((bf16[16,2816]{1,0:T(8,128)(2,1)S(1)}, bf16[16,2816]{1,0:T(8,128)(2,1)S(1)}, u32[]{:S(2)}, u32[]{:S(2)}) %collective-permute-start.1) | collective-permute-done | bytes 90144 | tf_op jit(solution)/shard_map/ppermute | solution.py:56
  9.5 1.9 %collective-permute-start.3 = (bf16[16,3328]{1,0:T(8,128)(2,1)S(1)}, bf16[16,3328]{1,0:T(8,128)(2,1)S(1)}, u32[]{:S(2)}, u32[]{:S(2)}) collective-permute-start(bf16[16,3328]{1,0:T(8,128)(2,1)S(1)} %get-tuple-element.33.after_ref.own_ref), channel_id=1, source_target_pairs={{0,2},{1,3},{2,0},{3,1},{4,6},{5,7},{6,4},{7,5},{8,10},{9,11},{10,... | collective-permute-start | bytes 319496 | tf_op jit(solution)/shard_map/ppermute | solution.py:56
  11.4 0.8 %collective-permute-done.arrived_ref = bf16[16,1792]{1,0:T(8,128)(2,1)S(1)} collective-permute-done((bf16[16,1792]{1,0:T(8,128)(2,1)S(1)}, bf16[16,1792]{1,0:T(8,128)(2,1)S(1)}, u32[]{:S(2)}, u32[]{:S(2)}) %collective-permute-start) | collective-permute-done | bytes 57376 | tf_op jit(solution)/shard_map/ppermute | solution.py:56
  12.2 1.6 %collective-permute-start.2 = (bf16[16,1792]{1,0:T(8,128)(2,1)S(1)}, bf16[16,1792]{1,0:T(8,128)(2,1)S(1)}, u32[]{:S(2)}, u32[]{:S(2)}) collective-permute-start(bf16[16,1792]{1,0:T(8,128)(2,1)S(1)} %get-tuple-element.35.after_ref.own_ref), channel_id=1, source_target_pairs={{0,2},{1,3},{2,0},{3,1},{4,6},{5,7},{6,4},{7,5},{8,10},{9,11},{10,... | collective-permute-start | bytes 172040 | tf_op jit(solution)/shard_map/ppermute | solution.py:56
  13.8 0.5 %collective-permute-done.3.arrived_ref = bf16[16,3328]{1,0:T(8,128)(2,1)S(1)} collective-permute-done((bf16[16,3328]{1,0:T(8,128)(2,1)S(1)}, bf16[16,3328]{1,0:T(8,128)(2,1)S(1)}, u32[]{:S(2)}, u32[]{:S(2)}) %collective-permute-start.3) | collective-permute-done | bytes 106528 | tf_op jit(solution)/shard_map/ppermute | solution.py:56
  14.3 2.5 %collective-permute-start.5 = (bf16[16,4352]{1,0:T(8,128)(2,1)S(1)}, bf16[16,4352]{1,0:T(8,128)(2,1)S(1)}, u32[]{:S(2)}, u32[]{:S(2)}) collective-permute-start(bf16[16,4352]{1,0:T(8,128)(2,1)S(1)} %get-tuple-element.37.after_ref.own_ref), channel_id=1, source_target_pairs={{0,4},{1,9},{2,6},{3,11},{4,0},{5,13},{6,2},{7,15},{8,12},{9,1},{1... | collective-permute-start | bytes 417800 | tf_op jit(solution)/shard_map/ppermute | solution.py:56
  16.8 0.0 collective-permute-done.2.arrived_ref
  16.9 1.2 %collective-permute-start.4 = (bf16[16,1792]{1,0:T(8,128)(2,1)S(1)}, bf16[16,1792]{1,0:T(8,128)(2,1)S(1)}, u32[]{:S(2)}, u32[]{:S(2)}) collective-permute-start(bf16[16,1792]{1,0:T(8,128)(2,1)S(1)} %get-tuple-element.39), channel_id=1, source_target_pairs={{0,4},{1,9},{2,6},{3,11},{4,0},{5,13},{6,2},{7,15},{8,12},{9,1},{1... | collective-permute-start | bytes 172040 | tf_op jit(solution)/shard_map/ppermute | solution.py:56
  18.1 1.8 %collective-permute-done.5.arrived_ref = bf16[16,4352]{1,0:T(8,128)(2,1)S(1)} collective-permute-done((bf16[16,4352]{1,0:T(8,128)(2,1)S(1)}, bf16[16,4352]{1,0:T(8,128)(2,1)S(1)}, u32[]{:S(2)}, u32[]{:S(2)}) %collective-permute-start.5) | collective-permute-done | bytes 139296 | tf_op jit(solution)/shard_map/ppermute | solution.py:56
  19.9 0.2 shard_map.101
  20.1 1.0 %collective-permute-done.4.arrived_ref = bf16[16,1792]{1,0:T(8,128)(2,1)S(1)} collective-permute-done((bf16[16,1792]{1,0:T(8,128)(2,1)S(1)}, bf16[16,1792]{1,0:T(8,128)(2,1)S(1)}, u32[]{:S(2)}, u32[]{:S(2)}) %collective-permute-start.4) | collective-permute-done | bytes 57376 | tf_op jit(solution)/shard_map/ppermute | solution.py:56
  21.1 0.2 shard_map.102
  21.3 0.0 collective-permute-start.6
  21.4 0.5 %shard_map.104.rows_ref = bf16[128,4096]{1,0:T(8,128)(2,1)S(1)} custom-call(bf16[16,128]{1,0:T(8,128)(2,1)S(1)} %get-tuple-element.27.code_ref, bf16[16,2304]{1,0:T(8,128)(2,1)S(1)} %get-tuple-element.44.first_ref, bf16[16,1792]{1,0:T(8,128)(2,1)S(1)} %get-tuple-element.45.second_ref), custom_call_target="tpu_custom_call" | custom-call | flops 1000000 | bytes 1048576 | tf_op jit(solution)/shard_map/pallas_call | solution.py:298
  21.8 0.3 %shard_map.103.turned_ref = bf16[512,128]{1,0:T(8,128)(2,1)S(1)} custom-call(bf16[16,4352]{1,0:T(8,128)(2,1)S(1)} %get-tuple-element.37.after_ref.own_ref, bf16[16,4352]{1,0:T(8,128)(2,1)S(1)} %collective-permute-done.5.arrived_ref, f32[1,4096]{1,0:T(1,128)S(1)} %get-tuple-element.43.bias_ref, bf16[128,128]{1,0:T(8,128)(2,1)S(1)} %shard_map.94.after_ref.order_ref), custom_call_target="tpu_custom_call" | custom-call | flops 1000000 | bytes 1048576 | tf_op jit(solution)/shard_map/pallas_call | solution.py:239
  22.1 0.4 %collective-permute-done.6.theirs_ref = f32[16,128]{1,0:T(8,128)S(1)} collective-permute-done((f32[16,128]{1,0:T(8,128)S(1)}, f32[16,128]{1,0:T(8,128)S(1)}, u32[]{:S(2)}, u32[]{:S(2)}) %collective-permute-start.6) | collective-permute-done | bytes 8224 | tf_op jit(solution)/shard_map/ppermute | solution.py:401
  22.5 1.4 %shard_map.105 = (bf16[128,4096]{1,0:T(8,128)(2,1)}, bf16[4096,128]{1,0:T(8,128)(2,1)}, f32[1,128]{1,0:T(1,128)}) custom-call(f32[16,128]{1,0:T(8,128)S(1)} %get-tuple-element.26.raw_ref, f32[16,128]{1,0:T(8,128)S(1)} %get-tuple-element.42.mine_ref, f32[16,128]{1,0:T(8,128)S(1)} %collective-permute-done.6.theirs_ref, ...), custom_call_target="tpu_custom_call" | custom-call | flops 1000000 | bytes 1048576 | tf_op jit(solution)/shard_map/pallas_call | solution.py:355
  (5 shorter events, 0.1 us)
Async XLA Ops:
  0.6 1.5 %copy-start = (bf16[128,4096]{1,0:T(8,128)(2,1)S(1)}, bf16[128,4096]{1,0:T(8,128)(2,1)}, u32[]{:S(2)}) copy-start(bf16[128,4096]{1,0:T(8,128)(2,1)} %rows_ref.7) | copy-start | bytes 3145732
  0.6 1.5 %copy-start.1 = (bf16[2,4096]{1,0:T(2,128)(2,1)S(1)}, bf16[2,4096]{1,0:T(2,128)(2,1)}, u32[]{:S(2)}) copy-start(bf16[2,4096]{1,0:T(2,128)(2,1)} %tokens_ref.1) | copy-start | bytes 49156
  0.7 1.5 %copy-start.2 = (bf16[4096]{0:T(1024)(128)(2,1)S(1)}, bf16[4096]{0:T(1024)(128)(2,1)}, u32[]{:S(2)}) copy-start(bf16[4096]{0:T(1024)(128)(2,1)} %bias_flat.1) | copy-start | bytes 24580
  0.7 1.5 %copy-start.3 = (f32[16,64]{1,0:T(8,128)S(1)}, f32[16,64]{1,0:T(8,128)}, u32[]{:S(2)}) copy-start(f32[16,64]{1,0:T(8,128)} %pre_ref.1) | copy-start | bytes 12292
  0.7 1.5 %copy-start.4 = (s32[16,64]{1,0:T(8,128)S(1)}, s32[16,64]{1,0:T(8,128)}, u32[]{:S(2)}) copy-start(s32[16,64]{1,0:T(8,128)} %top_ref.1) | copy-start | bytes 12292
  2.8 6.7 %collective-permute-start.1 = (bf16[16,2816]{1,0:T(8,128)(2,1)S(1)}, bf16[16,2816]{1,0:T(8,128)(2,1)S(1)}, u32[]{:S(2)}, u32[]{:S(2)}) collective-permute-start(bf16[16,2816]{1,0:T(8,128)(2,1)S(1)} %get-tuple-element.32.own_ref), channel_id=1, source_target_pairs={{0,8},{1,5},{2,10},{3,7},{4,12},{5,1},{6,14},{7,3},{8,0},{9,13},{1... | collective-permute-start | bytes 270344 | tf_op jit(solution)/shard_map/ppermute | solution.py:56
  7.0 5.1 %collective-permute-start = (bf16[16,1792]{1,0:T(8,128)(2,1)S(1)}, bf16[16,1792]{1,0:T(8,128)(2,1)S(1)}, u32[]{:S(2)}, u32[]{:S(2)}) collective-permute-start(bf16[16,1792]{1,0:T(8,128)(2,1)S(1)} %get-tuple-element.30.after_ref.own_ref), channel_id=1, source_target_pairs={{0,8},{1,5},{2,10},{3,7},{4,12},{5,1},{6,14},{7,3},{8,0},{9,13},{1... | collective-permute-start | bytes 172040 | tf_op jit(solution)/shard_map/ppermute | solution.py:56
  9.5 4.8 %collective-permute-start.3 = (bf16[16,3328]{1,0:T(8,128)(2,1)S(1)}, bf16[16,3328]{1,0:T(8,128)(2,1)S(1)}, u32[]{:S(2)}, u32[]{:S(2)}) collective-permute-start(bf16[16,3328]{1,0:T(8,128)(2,1)S(1)} %get-tuple-element.33.after_ref.own_ref), channel_id=1, source_target_pairs={{0,2},{1,3},{2,0},{3,1},{4,6},{5,7},{6,4},{7,5},{8,10},{9,11},{10,... | collective-permute-start | bytes 319496 | tf_op jit(solution)/shard_map/ppermute | solution.py:56
  12.2 4.6 %collective-permute-start.2 = (bf16[16,1792]{1,0:T(8,128)(2,1)S(1)}, bf16[16,1792]{1,0:T(8,128)(2,1)S(1)}, u32[]{:S(2)}, u32[]{:S(2)}) collective-permute-start(bf16[16,1792]{1,0:T(8,128)(2,1)S(1)} %get-tuple-element.35.after_ref.own_ref), channel_id=1, source_target_pairs={{0,2},{1,3},{2,0},{3,1},{4,6},{5,7},{6,4},{7,5},{8,10},{9,11},{10,... | collective-permute-start | bytes 172040 | tf_op jit(solution)/shard_map/ppermute | solution.py:56
  14.3 5.6 %collective-permute-start.5 = (bf16[16,4352]{1,0:T(8,128)(2,1)S(1)}, bf16[16,4352]{1,0:T(8,128)(2,1)S(1)}, u32[]{:S(2)}, u32[]{:S(2)}) collective-permute-start(bf16[16,4352]{1,0:T(8,128)(2,1)S(1)} %get-tuple-element.37.after_ref.own_ref), channel_id=1, source_target_pairs={{0,4},{1,9},{2,6},{3,11},{4,0},{5,13},{6,2},{7,15},{8,12},{9,1},{1... | collective-permute-start | bytes 417800 | tf_op jit(solution)/shard_map/ppermute | solution.py:56
  16.9 4.2 %collective-permute-start.4 = (bf16[16,1792]{1,0:T(8,128)(2,1)S(1)}, bf16[16,1792]{1,0:T(8,128)(2,1)S(1)}, u32[]{:S(2)}, u32[]{:S(2)}) collective-permute-start(bf16[16,1792]{1,0:T(8,128)(2,1)S(1)} %get-tuple-element.39), channel_id=1, source_target_pairs={{0,4},{1,9},{2,6},{3,11},{4,0},{5,13},{6,2},{7,15},{8,12},{9,1},{1... | collective-permute-start | bytes 172040 | tf_op jit(solution)/shard_map/ppermute | solution.py:56
  21.3 1.2 %collective-permute-start.6 = (f32[16,128]{1,0:T(8,128)S(1)}, f32[16,128]{1,0:T(8,128)S(1)}, u32[]{:S(2)}, u32[]{:S(2)}) collective-permute-start(f32[16,128]{1,0:T(8,128)S(1)} %get-tuple-element.42.mine_ref), channel_id=1, source_target_pairs={{0,1},{1,0},{2,3},{3,2},{4,5},{5,4},{6,7},{7,6},{8,9},{9,8},{10,11... | collective-permute-start | bytes 24584 | tf_op jit(solution)/shard_map/ppermute | solution.py:401

commit v29 on v22

--- a/solution.py
+++ b/solution.py
@@ -42,7 +42,8 @@
 
 def bit_of(step, core):
     bits = list(range(feat_bits()))
-    return (bits[-1:] + bits[:-1] if core == 0 else bits[:1] + bits[:0:-1])[step]
+    first = bits[-1:] + bits[:-1]
+    return (first if core == 0 else bits[1:2] + bits[:1] + bits[2:])[step]
 
 
 def swapped(shard, step):

time: 27 us -> 24 us (0.89)
  waiting for transfers between devices: 13.4 us -> 6.38 us
  starting transfers between devices: 7.81 us -> 11.8 us
    ppermute x6, waiting for transfers between devices: 12.7 us -> 5.69 us  [swapped(): return lax.ppermute(shard, ('feat', 'tok'), pairs)]
    ppermute x6, starting transfers between devices: 7.78 us -> 11.8 us  [swapped(): return lax.ppermute(shard, ('feat', 'tok'), pairs)]
where the time goes in v29:
time: 24 us; the launch traced here: 23.8 us
  starting transfers between devices  11.8 us (49%)
  waiting for transfers between devices  6.38 us (27%)
  Pallas kernels  3.47 us (14%)
  between operations  2.13 us (9%)
    ppermute x6, starting transfers between devices, swapped(): return lax.ppermute(shard, ('feat', 'tok'), pairs)  11.8 us
    ppermute x6, waiting for transfers between devices, swapped(): return lax.ppermute(shard, ('feat', 'tok'), pairs)  5.69 us
    pallas_call x1, Pallas kernels, final(): kernel_call(functools.partial(final_kernel, rows), (shape(*grad_rows.shap...  1.36 us
    ppermute x1, waiting for transfers between devices, local(): theirs = lax.ppermute(code_half, 'tok', [(i, 1 - i) for i in range(2)])  0.69 us
    pallas_call x1, Pallas kernels, front(): kernel_call(front_kernel, (shape(count, slots), shape(count, slots, dtype...  0.61 us
  transfers between devices with their start and end apart: 7, of which 6 were waited for; matrix products, arithmetic and copies ran while one was open for 0% of the time, Pallas kernels for 5%

profile of v29, /device:TPU:0, one launch (start us, length us, event | category | flops | bytes accessed | tf_op | source)
XLA Modules:
  0.0 23.8 jit_solution(11427371764266312288)
XLA Ops:
  0.6 0.0 copy-start
  0.6 0.0 copy-start.1
  0.7 0.0 copy-start.2
  0.7 0.0 copy-start.3
  0.7 0.0 copy-start.4
  2.1 0.0 copy-done
  2.1 0.0 copy-done.1
  2.1 0.0 copy-done.2
  2.1 0.0 copy-done.3
  2.1 0.0 copy-done.4
  2.1 0.6 %shard_map.95 = (bf16[16,128]{1,0:T(8,128)(2,1)S(1)}, f32[16,128]{1,0:T(8,128)S(1)}, f32[16,2048]{1,0:T(8,128)S(1)}, bf16[16,2560]{1,0:T(8,128)(2,1)S(1)}, f32[2,4096]{1,0:T(2,128)S(1)}, /*index=5*/f32[1,4096]{1,0:T(1,128)S(1)}) custom-call(bf16[2,4096]{1,0:T(2,128)(2,1)S(1)} %copy-done.1, bf16[4096]{0:T(1024)(128)(2,1)S(1)} %copy-done.2, ...), custom_call_target="tpu_custom_call" | custom-call | flops 1000000 | bytes 1048576 | tf_op jit(solution)/shard_map/pallas_call | solution.py:143
  2.7 4.1 %collective-permute-start.1 = (bf16[16,2560]{1,0:T(8,128)(2,1)S(1)}, bf16[16,2560]{1,0:T(8,128)(2,1)S(1)}, u32[]{:S(2)}, u32[]{:S(2)}) collective-permute-start(bf16[16,2560]{1,0:T(8,128)(2,1)S(1)} %get-tuple-element.32.own_ref), channel_id=1, source_target_pairs={{0,8},{1,5},{2,10},{3,7},{4,12},{5,1},{6,14},{7,3},{8,0},{9,13},{1... | collective-permute-start | bytes 245768 | tf_op jit(solution)/shard_map/ppermute | solution.py:56
  6.8 0.2 shard_map.96
  7.0 0.1 collective-permute-start
  7.1 2.3 %collective-permute-done.1.arrived_ref = bf16[16,2560]{1,0:T(8,128)(2,1)S(1)} collective-permute-done((bf16[16,2560]{1,0:T(8,128)(2,1)S(1)}, bf16[16,2560]{1,0:T(8,128)(2,1)S(1)}, u32[]{:S(2)}, u32[]{:S(2)}) %collective-permute-start.1) | collective-permute-done | bytes 81952 | tf_op jit(solution)/shard_map/ppermute | solution.py:56
  9.4 1.9 %collective-permute-start.3 = (bf16[16,3072]{1,0:T(8,128)(2,1)S(1)}, bf16[16,3072]{1,0:T(8,128)(2,1)S(1)}, u32[]{:S(2)}, u32[]{:S(2)}) collective-permute-start(bf16[16,3072]{1,0:T(8,128)(2,1)S(1)} %get-tuple-element.33.after_ref.own_ref), channel_id=1, source_target_pairs={{0,2},{1,3},{2,0},{3,1},{4,6},{5,7},{6,4},{7,5},{8,10},{9,11},{10,... | collective-permute-start | bytes 294920 | tf_op jit(solution)/shard_map/ppermute | solution.py:56
  11.3 1.0 %collective-permute-done.arrived_ref = bf16[16,2048]{1,0:T(8,128)(2,1)S(1)} collective-permute-done((bf16[16,2048]{1,0:T(8,128)(2,1)S(1)}, bf16[16,2048]{1,0:T(8,128)(2,1)S(1)}, u32[]{:S(2)}, u32[]{:S(2)}) %collective-permute-start) | collective-permute-done | bytes 65568 | tf_op jit(solution)/shard_map/ppermute | solution.py:56
  12.3 1.6 %collective-permute-start.2 = (bf16[16,2048]{1,0:T(8,128)(2,1)S(1)}, bf16[16,2048]{1,0:T(8,128)(2,1)S(1)}, u32[]{:S(2)}, u32[]{:S(2)}) collective-permute-start(bf16[16,2048]{1,0:T(8,128)(2,1)S(1)} %get-tuple-element.35.after_ref.own_ref), channel_id=1, source_target_pairs={{0,2},{1,3},{2,0},{3,1},{4,6},{5,7},{6,4},{7,5},{8,10},{9,11},{10,... | collective-permute-start | bytes 196616 | tf_op jit(solution)/shard_map/ppermute | solution.py:56
  13.8 0.2 %collective-permute-done.3.arrived_ref = bf16[16,3072]{1,0:T(8,128)(2,1)S(1)} collective-permute-done((bf16[16,3072]{1,0:T(8,128)(2,1)S(1)}, bf16[16,3072]{1,0:T(8,128)(2,1)S(1)}, u32[]{:S(2)}, u32[]{:S(2)}) %collective-permute-start.3) | collective-permute-done | bytes 98336 | tf_op jit(solution)/shard_map/ppermute | solution.py:56
  14.1 2.5 %collective-permute-start.5 = (bf16[16,4096]{1,0:T(8,128)(2,1)S(1)}, bf16[16,4096]{1,0:T(8,128)(2,1)S(1)}, u32[]{:S(2)}, u32[]{:S(2)}) collective-permute-start(bf16[16,4096]{1,0:T(8,128)(2,1)S(1)} %get-tuple-element.37.after_ref.own_ref), channel_id=1, source_target_pairs={{0,4},{1,9},{2,6},{3,11},{4,0},{5,13},{6,2},{7,15},{8,12},{9,1},{1... | collective-permute-start | bytes 393224 | tf_op jit(solution)/shard_map/ppermute | solution.py:56
  16.6 0.0 collective-permute-done.2.arrived_ref
  16.7 1.6 %collective-permute-start.4 = (bf16[16,2048]{1,0:T(8,128)(2,1)S(1)}, bf16[16,2048]{1,0:T(8,128)(2,1)S(1)}, u32[]{:S(2)}, u32[]{:S(2)}) collective-permute-start(bf16[16,2048]{1,0:T(8,128)(2,1)S(1)} %get-tuple-element.39), channel_id=1, source_target_pairs={{0,4},{1,9},{2,6},{3,11},{4,0},{5,13},{6,2},{7,15},{8,12},{9,1},{1... | collective-permute-start | bytes 196616 | tf_op jit(solution)/shard_map/ppermute | solution.py:56
  18.3 1.3 %collective-permute-done.5.arrived_ref = bf16[16,4096]{1,0:T(8,128)(2,1)S(1)} collective-permute-done((bf16[16,4096]{1,0:T(8,128)(2,1)S(1)}, bf16[16,4096]{1,0:T(8,128)(2,1)S(1)}, u32[]{:S(2)}, u32[]{:S(2)}) %collective-permute-start.5) | collective-permute-done | bytes 131104 | tf_op jit(solution)/shard_map/ppermute | solution.py:56
  19.6 0.2 shard_map.101
  19.8 0.3 %shard_map.102.after_ref.turned_ref = bf16[512,128]{1,0:T(8,128)(2,1)S(1)} custom-call(bf16[16,4096]{1,0:T(8,128)(2,1)S(1)} %get-tuple-element.37.after_ref.own_ref, bf16[16,4096]{1,0:T(8,128)(2,1)S(1)} %collective-permute-done.5.arrived_ref, f32[1,4096]{1,0:T(1,128)S(1)} %get-tuple-element.42.bias_ref, bf16[128,128]{1,0:T(8,128)(2,1)S(1)} %shard_map.94.after_ref.order_ref), custom_call_target="tpu_custom_call" | custom-call | flops 1000000 | bytes 1048576 | tf_op jit(solution)/shard_map/pallas_call | solution.py:239
  20.1 0.9 %collective-permute-done.4.arrived_ref = bf16[16,2048]{1,0:T(8,128)(2,1)S(1)} collective-permute-done((bf16[16,2048]{1,0:T(8,128)(2,1)S(1)}, bf16[16,2048]{1,0:T(8,128)(2,1)S(1)}, u32[]{:S(2)}, u32[]{:S(2)}) %collective-permute-start.4) | collective-permute-done | bytes 65568 | tf_op jit(solution)/shard_map/ppermute | solution.py:56
  21.0 0.2 shard_map.103
  21.2 0.0 collective-permute-start.6
  21.3 0.5 %shard_map.104.rows_ref = bf16[128,4096]{1,0:T(8,128)(2,1)S(1)} custom-call(bf16[16,128]{1,0:T(8,128)(2,1)S(1)} %get-tuple-element.27.code_ref, bf16[16,2048]{1,0:T(8,128)(2,1)S(1)} %get-tuple-element.44.first_ref, bf16[16,2048]{1,0:T(8,128)(2,1)S(1)} %get-tuple-element.45.second_ref), custom_call_target="tpu_custom_call" | custom-call | flops 1000000 | bytes 1048576 | tf_op jit(solution)/shard_map/pallas_call | solution.py:300
  21.7 0.7 %collective-permute-done.6.theirs_ref = f32[16,128]{1,0:T(8,128)S(1)} collective-permute-done((f32[16,128]{1,0:T(8,128)S(1)}, f32[16,128]{1,0:T(8,128)S(1)}, u32[]{:S(2)}, u32[]{:S(2)}) %collective-permute-start.6) | collective-permute-done | bytes 8224 | tf_op jit(solution)/shard_map/ppermute | solution.py:407
  22.4 1.4 %shard_map.105 = (bf16[128,4096]{1,0:T(8,128)(2,1)}, bf16[4096,128]{1,0:T(8,128)(2,1)}, f32[1,128]{1,0:T(1,128)}) custom-call(f32[16,128]{1,0:T(8,128)S(1)} %get-tuple-element.26.raw_ref, f32[16,128]{1,0:T(8,128)S(1)} %get-tuple-element.43.mine_ref, f32[16,128]{1,0:T(8,128)S(1)} %collective-permute-done.6.theirs_ref, ...), custom_call_target="tpu_custom_call" | custom-call | flops 1000000 | bytes 1048576 | tf_op jit(solution)/shard_map/pallas_call | solution.py:361
  (5 shorter events, 0.1 us)
Async XLA Ops:
  0.6 1.5 %copy-start = (bf16[128,4096]{1,0:T(8,128)(2,1)S(1)}, bf16[128,4096]{1,0:T(8,128)(2,1)}, u32[]{:S(2)}) copy-start(bf16[128,4096]{1,0:T(8,128)(2,1)} %rows_ref.7) | copy-start | bytes 3145732
  0.6 1.5 %copy-start.1 = (bf16[2,4096]{1,0:T(2,128)(2,1)S(1)}, bf16[2,4096]{1,0:T(2,128)(2,1)}, u32[]{:S(2)}) copy-start(bf16[2,4096]{1,0:T(2,128)(2,1)} %tokens_ref.1) | copy-start | bytes 49156
  0.7 1.5 %copy-start.2 = (bf16[4096]{0:T(1024)(128)(2,1)S(1)}, bf16[4096]{0:T(1024)(128)(2,1)}, u32[]{:S(2)}) copy-start(bf16[4096]{0:T(1024)(128)(2,1)} %bias_flat.1) | copy-start | bytes 24580
  0.7 1.5 %copy-start.3 = (f32[16,64]{1,0:T(8,128)S(1)}, f32[16,64]{1,0:T(8,128)}, u32[]{:S(2)}) copy-start(f32[16,64]{1,0:T(8,128)} %pre_ref.1) | copy-start | bytes 12292
  0.7 1.5 %copy-start.4 = (s32[16,64]{1,0:T(8,128)S(1)}, s32[16,64]{1,0:T(8,128)}, u32[]{:S(2)}) copy-start(s32[16,64]{1,0:T(8,128)} %top_ref.1) | copy-start | bytes 12292
  2.7 6.6 %collective-permute-start.1 = (bf16[16,2560]{1,0:T(8,128)(2,1)S(1)}, bf16[16,2560]{1,0:T(8,128)(2,1)S(1)}, u32[]{:S(2)}, u32[]{:S(2)}) collective-permute-start(bf16[16,2560]{1,0:T(8,128)(2,1)S(1)} %get-tuple-element.32.own_ref), channel_id=1, source_target_pairs={{0,8},{1,5},{2,10},{3,7},{4,12},{5,1},{6,14},{7,3},{8,0},{9,13},{1... | collective-permute-start | bytes 245768 | tf_op jit(solution)/shard_map/ppermute | solution.py:56
  7.0 5.2 %collective-permute-start = (bf16[16,2048]{1,0:T(8,128)(2,1)S(1)}, bf16[16,2048]{1,0:T(8,128)(2,1)S(1)}, u32[]{:S(2)}, u32[]{:S(2)}) collective-permute-start(bf16[16,2048]{1,0:T(8,128)(2,1)S(1)} %get-tuple-element.30.after_ref.own_ref), channel_id=1, source_target_pairs={{0,8},{1,5},{2,10},{3,7},{4,12},{5,1},{6,14},{7,3},{8,0},{9,13},{1... | collective-permute-start | bytes 196616 | tf_op jit(solution)/shard_map/ppermute | solution.py:56
  9.4 4.7 %collective-permute-start.3 = (bf16[16,3072]{1,0:T(8,128)(2,1)S(1)}, bf16[16,3072]{1,0:T(8,128)(2,1)S(1)}, u32[]{:S(2)}, u32[]{:S(2)}) collective-permute-start(bf16[16,3072]{1,0:T(8,128)(2,1)S(1)} %get-tuple-element.33.after_ref.own_ref), channel_id=1, source_target_pairs={{0,2},{1,3},{2,0},{3,1},{4,6},{5,7},{6,4},{7,5},{8,10},{9,11},{10,... | collective-permute-start | bytes 294920 | tf_op jit(solution)/shard_map/ppermute | solution.py:56
  12.3 4.4 %collective-permute-start.2 = (bf16[16,2048]{1,0:T(8,128)(2,1)S(1)}, bf16[16,2048]{1,0:T(8,128)(2,1)S(1)}, u32[]{:S(2)}, u32[]{:S(2)}) collective-permute-start(bf16[16,2048]{1,0:T(8,128)(2,1)S(1)} %get-tuple-element.35.after_ref.own_ref), channel_id=1, source_target_pairs={{0,2},{1,3},{2,0},{3,1},{4,6},{5,7},{6,4},{7,5},{8,10},{9,11},{10,... | collective-permute-start | bytes 196616 | tf_op jit(solution)/shard_map/ppermute | solution.py:56
  14.1 5.5 %collective-permute-start.5 = (bf16[16,4096]{1,0:T(8,128)(2,1)S(1)}, bf16[16,4096]{1,0:T(8,128)(2,1)S(1)}, u32[]{:S(2)}, u32[]{:S(2)}) collective-permute-start(bf16[16,4096]{1,0:T(8,128)(2,1)S(1)} %get-tuple-element.37.after_ref.own_ref), channel_id=1, source_target_pairs={{0,4},{1,9},{2,6},{3,11},{4,0},{5,13},{6,2},{7,15},{8,12},{9,1},{1... | collective-permute-start | bytes 393224 | tf_op jit(solution)/shard_map/ppermute | solution.py:56
  16.7 4.3 %collective-permute-start.4 = (bf16[16,2048]{1,0:T(8,128)(2,1)S(1)}, bf16[16,2048]{1,0:T(8,128)(2,1)S(1)}, u32[]{:S(2)}, u32[]{:S(2)}) collective-permute-start(bf16[16,2048]{1,0:T(8,128)(2,1)S(1)} %get-tuple-element.39), channel_id=1, source_target_pairs={{0,4},{1,9},{2,6},{3,11},{4,0},{5,13},{6,2},{7,15},{8,12},{9,1},{1... | collective-permute-start | bytes 196616 | tf_op jit(solution)/shard_map/ppermute | solution.py:56
  21.2 1.2 %collective-permute-start.6 = (f32[16,128]{1,0:T(8,128)S(1)}, f32[16,128]{1,0:T(8,128)S(1)}, u32[]{:S(2)}, u32[]{:S(2)}) collective-permute-start(f32[16,128]{1,0:T(8,128)S(1)} %get-tuple-element.43.mine_ref), channel_id=1, source_target_pairs={{0,1},{1,0},{2,3},{3,2},{4,5},{5,4},{6,7},{7,6},{8,9},{9,8},{10,11... | collective-permute-start | bytes 24584 | tf_op jit(solution)/shard_map/ppermute | solution.py:407
